TPU v7x, 32 devices: a whole 2x2x4 slice. The times are simulated.
32 devices in a mesh: prow: 4 (over x, core), pcol: 8 (over z, y).
Axes of the slice: x: 2, y: 2, z: 4, core: 2. Of those that a mesh axis runs over, the one named last changes fastest.
Arguments:
- matrix: bfloat16 [8, 4, 512, 4, 8, 512], P(None, 'prow', None, None, 'pcol'), may hold values from -6 to 6
- upper_inv: bfloat16 [2, 512, 512], replicated, may hold values from -4 to 4
- lower_inv: bfloat16 [2, 512, 512], replicated, may hold values from -4 to 4
- solution: bfloat16 [4, 8, 512], P(None, 'pcol'), may hold values from -0.046875 to 0.046875
- right_side: float32 [8, 4, 512], P(None, 'prow'), may hold values from -6 to 6
- diagonal_block_inverses: bfloat16 [1, 4, 512, 512], P(None, 'prow'), may hold values from -0.013671875 to 0.013671875
Outputs:
- updated: bfloat16 [8, 4, 512, 4, 8, 512], P(None, 'prow', None, None, 'pcol')
- residual: float32 [8, 4, 512], P(None, 'prow')
- precond: float32 [4, 512], replicated
All inputs are finite; a program needn't handle non-finite values.
Results may differ from a plain program's by a relative error of at most 0.0085.
Values may be sent and summed in bfloat16 or wider, within the bound.
No kernel may reach another device: no remote copies, remote signals or barrier semaphores. Data moves between devices by JAX's collectives and lax.ppermute only.
A program may use at most 128 MiB of HBM per device.

v0:
```python
import jax
import jax.numpy as jnp
from jax import lax
from jax.experimental import pallas as pl
from jax.experimental.pallas import tpu as pltpu
from jax.sharding import PartitionSpec as P

LANES = 128
VMEM_BYTES = 50 * 1024 * 1024
F32 = jnp.float32
BF16 = jnp.bfloat16


def matmul(a, b):
    return jnp.dot(a, b, preferred_element_type=F32)


class Chain:
    def __init__(self):
        self.token = None

    def __call__(self, kernel, inputs, in_specs, out_shape, out_specs, name, work, after=(), grid=None, scratch=(), aliases=None):
        deps = list(after) + ([] if self.token is None else [self.token])
        n_in, n_out, n_dep = len(inputs), len(out_shape), len(deps)
        anywhere = pl.BlockSpec(memory_space=pl.ANY)

        def body(*refs):
            outs = n_in + n_dep
            kernel(*refs[:n_in], *refs[outs : outs + n_out], *refs[outs + n_out + 1 :])

        params = {} if grid is None else {"grid": grid}
        *results, self.token = pl.pallas_call(
            body,
            in_specs=list(in_specs) + [anywhere] * n_dep,
            out_specs=list(out_specs) + [anywhere],
            out_shape=list(out_shape) + [jax.ShapeDtypeStruct((8, LANES), F32)],
            scratch_shapes=list(scratch),
            input_output_aliases=aliases or {},
            compiler_params=pltpu.CompilerParams(vmem_limit_bytes=VMEM_BYTES),
            cost_estimate=pl.CostEstimate(flops=work[0], bytes_accessed=work[1], transcendentals=0),
            name=name,
            **params,
        )(*inputs, *deps)
        return results[0] if len(results) == 1 else results

    def gate(self, values, after):
        anywhere = pl.BlockSpec(memory_space=pl.ANY)
        return self(
            lambda *refs: None,
            values,
            [anywhere] * len(values),
            [jax.ShapeDtypeStruct(v.shape, v.dtype) for v in values],
            [anywhere] * len(values),
            "gate",
            (0, 0),
            after=after,
            aliases={i: i for i in range(len(values))},
        )

    def add(self, a, b):
        def kernel(a_ref, b_ref, out_ref):
            out_ref[...] = a_ref[...] + b_ref[...]

        vmem = pl.BlockSpec(memory_space=pltpu.VMEM)
        return self(kernel, [a, b], [vmem] * 2, [jax.ShapeDtypeStruct(a.shape, a.dtype)], [vmem], "add", (a.size, 12 * a.size))

    def choose(self, index, values):
        def kernel(index_ref, *refs):
            *sources, out, sem = refs
            for i, ref in enumerate(sources):

                @pl.when(index_ref[0] == i)
                def _(ref=ref):
                    copy = pltpu.make_async_copy(ref, out, sem)
                    copy.start()
                    copy.wait()

        anywhere = pl.BlockSpec(memory_space=pl.ANY)
        value = values[0]
        return self(
            kernel,
            [index, *values],
            [pl.BlockSpec(memory_space=pltpu.SMEM)] + [anywhere] * len(values),
            [jax.ShapeDtypeStruct(value.shape, value.dtype)],
            [anywhere],
            "choose",
            (0, 4 * value.size),
            scratch=[pltpu.SemaphoreType.DMA],
        )


def transpose8(x):
    at = lax.broadcasted_iota(jnp.int32, x[0].shape, 1)
    for d in (4, 2, 1):
        low = (at & d) == 0
        y = list(x)
        for i in range(8):
            if i & d == 0:
                a, b = x[i], x[i + d]
                y[i] = jnp.where(low, a, pltpu.roll(b, d, 1))
                y[i + d] = jnp.where(low, pltpu.roll(a, 8 - d, 1), b)
        x = y
    return x


def sum8(x):
    at = lax.broadcasted_iota(jnp.int32, x[0].shape, 1)
    for d in (4, 2, 1):
        low = (at & d) == 0
        y = []
        for a, b in zip(x[:d], x[d : 2 * d]):
            gone = jnp.where(low, b, a)
            back = pltpu.roll(gone, d, 1)
            if d != 4:
                back = jnp.where(low, pltpu.roll(gone, 8 - d, 1), back)
            y.append(jnp.where(low, a, b) + back)
        x = y
    return x[0]


def extract_kernel(groups, stride, a_ref, sol_ref, col_ref, part_ref, *rest):
    wide, totals = rest[-2:]
    rows = col_ref.shape[0]
    if len(rest) > 2:
        rest[0][...] = a_ref[...]
    if groups % 16 == 0:
        sol = sol_ref[...].astype(F32)

        def one(block, carry):
            here = pl.ds(pl.multiple_of(block * 8 * groups, 8 * groups), 8 * groups)
            raw = a_ref[here, :].astype(F32)
            wide[here, :] = raw
            raw = raw.reshape(8, groups, LANES) * sol[None]
            sums = [sum(raw[r : r + 1, 8 * h : 8 * h + 8] for h in range(groups // 8)) for r in range(8)]
            totals[pl.ds(pl.multiple_of(block * 8, 8), 8), :] = sum8(sums)[0]
            return carry

        lax.fori_loop(0, rows // 8, one, 0, unroll=4)
    else:
        wide[...] = a_ref[...].astype(F32)
        total = jnp.zeros((rows, LANES), F32)
        for g in range(groups):
            total = total + wide[pl.ds(g, rows, stride=groups), :] * sol_ref[g : g + 1, :].astype(F32)
        totals[...] = total
    for g in range(0, groups, stride):
        piece = wide[pl.ds(g, rows, stride=groups), :]
        col_ref[:, pl.ds(g // stride * LANES, LANES)] = piece.astype(BF16)
    ones = jnp.ones((8, LANES), F32)
    sums = lax.dot_general(
        ones, totals[...], (((1,), (1,)), ((), ())), precision=lax.Precision.HIGHEST, preferred_element_type=F32
    )
    part_ref[...] = sums[0:1, :]


def extract(chain, flat, sol, first, rows, groups, stride, width, with_band):
    sub = min(rows, 128)
    size = sub * groups
    at = first // sub
    out_specs = [
        pl.BlockSpec((sub, width), lambda i: (i, 0)),
        pl.BlockSpec((1, sub), lambda i: (0, i)),
    ]
    out_shape = [
        jax.ShapeDtypeStruct((rows, width), BF16),
        jax.ShapeDtypeStruct((1, rows), F32),
    ]
    if with_band:
        out_specs.append(pl.BlockSpec((size, LANES), lambda i: (i, 0)))
        out_shape.append(jax.ShapeDtypeStruct((rows * groups, LANES), BF16))
    return chain(
        lambda *refs: extract_kernel(groups, stride, *refs),
        [flat, sol],
        [
            pl.BlockSpec((size, LANES), lambda i: (at + i, 0)),
            pl.BlockSpec((groups, LANES), lambda i: (0, 0)),
        ],
        out_shape,
        out_specs,
        "extract",
        (4 * rows * groups * LANES, rows * groups * LANES * 2),
        grid=(rows // sub,),
        scratch=[pltpu.VMEM((size, LANES), F32), pltpu.VMEM((sub, LANES), F32)],
    )


def factor_kernel(groups, n_x, where_ref, *refs):
    core, lane, x = where_ref[0], where_ref[1], where_ref[2]
    given, (up_ref, low_ref, v_ref, raws, bands, blocks, sems, *rest) = refs[: 4 * n_x], refs[4 * n_x :]
    width = up_ref.shape[1]
    for i in range(n_x):

        @pl.when(x == i)
        def _(i=i):
            pairs = [(raws, given[2 * i], given[2 * i + 1]), (blocks, given[2 * n_x + 2 * i], given[2 * n_x + 2 * i + 1])]
            copies = []
            for kind, (target, mine, other) in enumerate(pairs):
                copies.append(pltpu.make_async_copy(mine, target.at[core], sems.at[kind, 0]))
                copies.append(pltpu.make_async_copy(other, target.at[1 - core], sems.at[kind, 1]))
            for copy in copies:
                copy.start()
            for copy in copies:
                copy.wait()

    for slot in range(2):
        if groups % 16 == 0:

            def one(block, carry, slot=slot):
                here = pl.ds(pl.multiple_of(block * 16 * groups, 16 * groups), 16 * groups)
                raw = raws[slot, here, :].astype(F32).reshape(2, 8, groups, LANES)
                rows = pl.ds(pl.multiple_of(block * 16, 16), 16)
                for h in range(groups // 8):
                    turned = transpose8([raw[:, r, 8 * h : 8 * h + 8] for r in range(8)])
                    for g in range(8):
                        at = pl.ds((8 * h + g) * LANES, LANES)
                        bands[slot, rows, at] = turned[g].reshape(16, LANES).astype(BF16)
                return carry

            lax.fori_loop(0, width // 16, one, 0, unroll=2)
        else:
            wide = rest[0]
            wide[...] = raws[slot].astype(F32)
            for g in range(groups):
                at = pl.ds(g * LANES, LANES)
                bands[slot, :, at] = wide[pl.ds(g, width, stride=groups), :].astype(BF16)
    row = lax.broadcasted_iota(jnp.int32, (width, width), 0)
    col = lax.broadcasted_iota(jnp.int32, (width, width), 1)
    zero = jnp.zeros((width, width), BF16)
    upper = [jnp.where(row <= col, up_ref[s], zero) for s in range(2)]
    lower = [jnp.where(row >= col, low_ref[s], zero) for s in range(2)]
    top_01 = matmul(lower[0], blocks[0]).astype(BF16)
    left_10 = matmul(blocks[1], upper[0]).astype(BF16)
    piece = min(groups * LANES, 1024)
    for n in range(groups * LANES // piece):
        at = slice(n * piece, (n + 1) * piece)
        top_0 = matmul(lower[0], bands[0, :, at]).astype(BF16)
        rest_1 = (bands[1, :, at].astype(F32) - matmul(left_10, top_0)).astype(BF16)
        top_1 = matmul(lower[1], rest_1).astype(BF16)
        v_1 = matmul(upper[1], top_1).astype(BF16)
        mixed = (top_0.astype(F32) - matmul(top_01, v_1)).astype(BF16)
        v_0 = matmul(upper[0], mixed).astype(BF16)
        v_ref[pl.ds(pl.multiple_of(lane * width, width), width), at] = v_0
        v_ref[pl.ds(pl.multiple_of((1 - lane) * width, width), width), at] = v_1


def factors(chain, where, bands, blocks, upper, lower, groups):
    width = upper.shape[1]
    cols = groups * LANES
    n_x = len(bands) // 2
    vmem = pl.BlockSpec(memory_space=pltpu.VMEM)
    anywhere = pl.BlockSpec(memory_space=pl.ANY)
    scratch = [
        pltpu.VMEM((2, width * groups, LANES), BF16),
        pltpu.VMEM((2, width, cols), BF16),
        pltpu.VMEM((2, width, width), BF16),
        pltpu.SemaphoreType.DMA((2, 2)),
    ]
    if groups % 16:
        scratch.append(pltpu.VMEM((width * groups, LANES), F32))
    return chain(
        lambda *refs: factor_kernel(groups, n_x, *refs),
        [where, *bands, *blocks, upper, lower],
        [pl.BlockSpec(memory_space=pltpu.SMEM)] + [anywhere] * (4 * n_x) + [vmem] * 2,
        [jax.ShapeDtypeStruct((2 * width, cols), BF16)],
        [vmem],
        "factors",
        (12 * width * width * cols, 12 * width * cols),
        scratch=scratch,
    )


def update_kernel(groups, a_ref, mine_ref, other_ref, v_ref, *rest):
    rows = mine_ref.shape[0]
    both = jnp.concatenate([mine_ref[...], other_ref[...]], axis=1)
    if groups % 16 == 0:
        out_ref, value = rest[-2:]
        part = min(rows, 128)
        for p in range(rows // part):
            value[p] = matmul(both[p * part : (p + 1) * part], v_ref[...])

            def one(block, carry, p=p):
                at = pl.ds(pl.multiple_of(block * 8, 8), 8)
                halves = [
                    transpose8([value[p, at, (8 * h + g) * LANES : (8 * h + g + 1) * LANES][None] for g in range(8)])
                    for h in range(groups // 8)
                ]
                for r in range(8):
                    here = pl.ds(pl.multiple_of((p * part + block * 8 + r) * groups, groups), groups)
                    change = jnp.concatenate([half[r][0] for half in halves], axis=0)
                    out_ref[here, :] = (a_ref[here, :].astype(F32) - change).astype(BF16)
                return carry

            lax.fori_loop(0, part // 8, one, 0, unroll=part // 8)
        return
    out_ref, wide = rest[-2:]
    value = matmul(both, v_ref[...])
    for g in range(groups):
        wide[pl.ds(g, rows, stride=groups), :] = value[:, g * LANES : (g + 1) * LANES]
    out_ref[...] = (a_ref[...].astype(F32) - wide[...]).astype(BF16)


def update(chain, flat, mine, other, v, out, first, groups):
    rows, width = mine.shape
    sub = min(rows, 256)
    size = sub * groups
    base = first // sub
    cols = groups * LANES
    in_specs = [
        pl.BlockSpec((size, LANES), lambda i: (base + i, 0)),
        pl.BlockSpec((sub, width), lambda i: (i, 0)),
        pl.BlockSpec((sub, width), lambda i: (i, 0)),
        pl.BlockSpec(memory_space=pltpu.VMEM),
    ]
    args = [flat, mine, other, v]
    aliases = {}
    if out is not None:
        in_specs.append(pl.BlockSpec(memory_space=pl.ANY))
        args.append(out)
        aliases = {4: 0}
    return chain(
        lambda *refs: update_kernel(groups, *refs),
        args,
        in_specs,
        [jax.ShapeDtypeStruct(flat.shape, BF16)],
        [pl.BlockSpec((size, LANES), lambda i: (base + i, 0))],
        "update",
        (4 * rows * width * cols, 4 * rows * cols + 4 * rows * width),
        grid=(rows // sub,),
        scratch=[pltpu.VMEM((size, LANES), F32) if groups % 16 else pltpu.VMEM((sub // 128, 128, cols), F32)],
        aliases=aliases,
    )


def solve_kernel(place_ref, state_ref, res_ref, inv_ref, *rest):
    cols, out_ref = rest[:-1], rest[-1]
    place = place_ref[0]
    width = inv_ref.shape[0]
    nt = (((1,), (1,)), ((), ()))
    pending = jnp.zeros((8, width), F32)
    for j, col in enumerate(cols):
        known = jnp.where(j < place, state_ref[j : j + 1, :], 0.0)
        pending = pending + lax.dot_general(
            jnp.broadcast_to(known, (8, width)).astype(BF16), col[...], nt, preferred_element_type=F32
        )
    left = res_ref[...] - pending[0:1, :]
    high = left.astype(BF16)
    rest_1 = left - high.astype(F32)
    mid = rest_1.astype(BF16)
    low = (rest_1 - mid.astype(F32)).astype(BF16)
    total = jnp.zeros((8, width), F32)
    for piece in (low, mid, high):
        wide = jnp.broadcast_to(piece.astype(F32), (8, width)).astype(BF16)
        total = total + lax.dot_general(wide, inv_ref[...], nt, preferred_element_type=F32)
    row = lax.broadcasted_iota(jnp.int32, state_ref.shape, 0)
    out_ref[...] = jnp.where(row == place, jnp.broadcast_to(total[0:1, :], state_ref.shape), state_ref[...])


def solve_step(chain, place, state, res, inv, cols):
    vmem = pl.BlockSpec(memory_space=pltpu.VMEM)
    return chain(
        solve_kernel,
        [place, state, res, inv, *cols],
        [pl.BlockSpec(memory_space=pltpu.SMEM)] + [vmem] * (3 + len(cols)),
        [jax.ShapeDtypeStruct(state.shape, F32)],
        [vmem],
        "solve",
        (2 * inv.size * (len(cols) + 3), 2 * inv.size * (len(cols) + 1)),
    )


def shards(matrix, upper_inv, lower_inv, solution, right_side, diagonal_block_inverses):
    slots, _, width, col_slots, _, _ = matrix.shape
    n_prow = lax.axis_size("prow")
    n_pcol = lax.axis_size("pcol")
    ny = n_prow // 2
    nz = n_pcol // ny
    prow = lax.axis_index("prow")
    pcol = lax.axis_index("pcol")
    z, y = pcol // ny, pcol % ny
    core, lane = prow % 2, y % 2
    lane_tiles = width // LANES
    groups = lane_tiles * col_slots
    rows = slots * width
    flat = matrix.reshape(rows, col_slots, lane_tiles, LANES).transpose(0, 2, 1, 3).reshape(rows * groups, LANES)
    sol = solution.reshape(col_slots, lane_tiles, LANES).transpose(1, 0, 2).reshape(groups, LANES)

    chain = Chain()

    def spread(value, axis, size):
        values = [value]
        for s in range(2, size, 2):
            pairs = [(s - 2, s), (s - 1, s + 1), (s, s - 2), (s + 1, s - 1)]
            values.append(lax.ppermute(values[-1], axis, pairs))
        return values

    def swap(value, axis, size, bit=1):
        return lax.ppermute(value, axis, [(i, i ^ bit) for i in range(size)])

    def along_z(pairs, keep=True, extra=()):
        pairs = [*pairs, *extra]
        if keep:
            busy = {i for pair in pairs for i in pair}
            pairs = pairs + [(i, i) for i in range(nz) if i not in busy]
        return [(a * ny + k, b * ny + k) for a, b in pairs for k in range(ny if keep else 2)]

    stages = [[[(0, nz // 2)]]]
    held, step = [nz // 2], nz // 4
    while step:
        stages.append([[(m, m - step) for m in held], [(m, m + step) for m in held]])
        held = [b for moves in stages[-1] for _, b in moves]
        step //= 2

    def picked(got, moves, value):
        mask = z == moves[0][1]
        for _, b in moves[1:]:
            mask = mask | (z == b)
        return jnp.where(mask, got, value)

    def first_stage(local):
        return lax.ppermute(local, "pcol", along_z(stages[0][0]))

    def second_stage(arrived):
        left, right = stages[1]
        back = [(b, a) for a, b in right]
        return [
            lax.ppermute(arrived, "pcol", along_z(left)),
            lax.ppermute(arrived, "pcol", along_z(right, extra=back)),
        ]

    source = jnp.zeros((), jnp.int32)
    for i, moves in enumerate(stages[0] + stages[1]):
        for _, b in moves:
            source = jnp.where(z == b, i + 1, source)
    source = source.astype(jnp.int32).reshape(1)

    def settle(local, arrived, outward):
        value = chain.choose(source, [local, arrived, *outward])
        for stage in stages[2:]:
            gots = [lax.ppermute(value, "pcol", along_z(moves)) for moves in stage]
            for got, moves in zip(gots, stage):
                value = picked(got, moves, value)
        for s in range(2, ny, 2):
            pairs = [(a * ny + s - 2 + k, a * ny + s + k) for a in range(nz) for k in range(2)]
            got = lax.ppermute(value, "pcol", pairs)
            value = jnp.where(y // 2 == s // 2, got, value)
        return value

    count = n_prow * diagonal_block_inverses.shape[0]
    assert diagonal_block_inverses.shape[0] == 1
    home = count - 2
    inv = diagonal_block_inverses.reshape(width, width)
    place = prow.astype(jnp.int32).reshape(1)
    where = jnp.stack([core, lane, prow // 2]).astype(jnp.int32)
    flag = jnp.where(core != lane, 0, 1).astype(jnp.int32).reshape(1)
    bits = [1 << b for b in range(n_pcol.bit_length() - 1)]

    cuts = [(c * width, width) for c in range(slots - 1)]
    cuts += [((slots - 1) * width + h * width // 2, width // 2) for h in range(2)]
    chunks = len(cuts)
    column, parts, first, outward, mine, other, box = {}, {}, {}, {}, {}, {}, {"out": None}
    for c in [0, 2, 3, 1, *range(4, slots)]:
        col, part, *band = extract(chain, flat, sol, c * width, width, groups, col_slots, width, c == 0)
        parts[c] = part
        if c < slots - 1:
            column[c] = col
        else:
            column[c], column[c + 1] = col[: width // 2], col[width // 2 :]
        if c < 2:
            first[c] = first_stage(col)
        if c == 0:
            box["bands"] = spread(band[0], "prow", n_prow)

    def total_step(bit):
        def run():
            if bit == 1:
                box["total"] = jnp.concatenate([parts[c] for c in range(slots)], axis=0)
            box["total"] = chain.add(box["total"], swap(box["total"], "pcol", n_pcol, bit))
            if bit == bits[-1]:
                box["residual"] = right_side.reshape(slots, width) - box["total"]

        return run

    def solve(k):
        def run():
            if k == 0:
                a, b = mine[0], other[0]
                needed = [jnp.where(lane == 0, a, b), jnp.where(lane == 0, b, a)]
                for j in range(2, home):
                    needed.append(lax.ppermute(column[0], "pcol", [(j, home)]))
                box["needed"] = needed + [column[0]]
                state = jnp.zeros((count, width), F32)
            else:
                state = lax.ppermute(box["state"], "prow", [(i, i + 1) for i in range(n_prow - 1)])
            state = solve_step(chain, place, state, box["residual"][0:1], inv, box["needed"])
            if k == count - 1:
                state = jnp.where((prow == n_prow - 1) & (pcol == home), state, 0.0)
            box["state"] = state

        return run

    def share(axis, size, bit):
        def run():
            box["state"] = chain.add(box["state"], swap(box["state"], axis, size, bit))

        return run

    def blocks_out():
        box["blks"] = spread(chain.choose(flag, [mine[0], other[0]]), "prow", n_prow)
        box["bands"] = [v for b in box["bands"] for v in (b, swap(b, "prow", n_prow))]

    def blocks_swap():
        box["blks"] = [v for b in box["blks"] for v in (b, swap(b, "prow", n_prow))]

    def make_factors():
        box["v"] = factors(chain, where, box["bands"], box["blks"], upper_inv, lower_inv, groups)

    def updates(c):
        def run():
            box["out"] = update(chain, flat, mine[c], other[c], box["v"], box["out"], cuts[c][0], groups)

        return run

    def take(c):
        mine[c] = settle(column[c], first[c], outward[c])
        other[c] = swap(mine[c], "pcol", n_pcol)

    total = [total_step(b) for b in bits]
    line = [solve(k) for k in range(count)]
    line += [share("prow", n_prow, 1 << b) for b in range(n_prow.bit_length() - 1)]
    line += [share("pcol", n_pcol, b) for b in bits]
    if slots == 8 and len(line) == 9:
        plan = {
            0: total[:2],
            1: total[2:],
            2: [blocks_out, line[0]],
            3: [blocks_swap, line[1], make_factors],
            4: [updates(0), line[2], updates(1), updates(2)],
            5: [line[3], updates(3), line[4]],
            6: [updates(4), line[5]],
            7: [updates(5), line[6]],
            8: [updates(6), line[7]],
        }
        tail = []
    else:
        plan = {0: total, slots - 1: [blocks_out, blocks_swap, make_factors] + line}
        tail = [updates(c) for c in range(chunks - 2)]
        line = []

    for k in range(chunks):
        ahead = [column[k + 2]] if k + 2 < chunks else []
        got = chain.gate([first[k], *ahead], [])
        first[k] = got[0] if ahead else got
        outward[k] = second_stage(first[k])
        if ahead:
            column[k + 2] = got[1]
            first[k + 2] = first_stage(column[k + 2])
        if k:
            take(k - 1)
        for task in plan.get(k, []):
            task()
    for task in tail:
        task()
    updates(chunks - 2)()
    take(chunks - 1)
    if line:
        line[-1]()
    updates(chunks - 1)()
    residual, out, state = box["residual"], box["out"], box["state"]
    updated = out.reshape(rows, lane_tiles, col_slots, LANES).transpose(0, 2, 1, 3).reshape(matrix.shape)
    return (updated, residual.reshape(right_side.shape), state)


def solution(mesh):
    return jax.shard_map(
        shards,
        mesh=mesh,
        in_specs=(
            P(None, "prow", None, None, "pcol", None),
            P(),
            P(),
            P(None, "pcol", None),
            P(None, "prow", None),
            P(None, "prow", None, None),
        ),
        out_specs=(P(None, "prow", None, None, "pcol", None), P(None, "prow", None), P()),
        check_vma=False,
    )
```

profile of v0, /device:TPU:0, one launch (start us, length us, event | category | flops | bytes accessed | tf_op | source)
XLA Modules:
  0.0 255.7 jit_solution(12117159512539760818)
XLA Ops:
  1.3 4.4 %extract.8 = (bf16[512,512]{1,0:T(8,128)(2,1)S(1)}, f32[1,512]{1,0:T(1,128)S(1)}, bf16[8192,128]{1,0:T(8,128)(2,1)}, f32[8,128]{1,0:T(8,128)S(1)}) custom-call(bf16[65536,128]{1,0:T(8,128)(2,1)} %bitcast.37, bf16[16,128]{1,0:T(8,128)(2,1)S(1)} %bitcast.29), custom_call_target="tpu_custom_call" | custom-call | flops 4194304 | bytes 2097152 | tf_op jit(solution)/shard_map/extract/pallas_call | solution.py:32
  5.7 2.9 %collective-permute-start.10 = (bf16[8192,128]{1,0:T(8,128)(2,1)}, bf16[8192,128]{1,0:T(8,128)(2,1)}, u32[]{:S(2)}, u32[]{:S(2)}) collective-permute-start(bf16[8192,128]{1,0:T(8,128)(2,1)} %get-tuple-element.149.refs_1_), channel_id=1, source_target_pairs={{0,16},{8,24},{16,0},{24,8},{1,17},{9,25},{17,1},{25,9},{2,18},{10... | collective-permute-start | bytes 6291464 | tf_op jit(solution)/shard_map/ppermute | solution.py:392
  8.6 4.5 %collective-permute-start = (bf16[512,512]{1,0:T(8,128)(2,1)S(1)}, bf16[512,512]{1,0:T(8,128)(2,1)S(1)}, u32[]{:S(2)}, u32[]{:S(2)}) collective-permute-start(bf16[512,512]{1,0:T(8,128)(2,1)S(1)} %get-tuple-element.116.refs_1_.refs_6_), channel_id=1, source_target_pairs={{0,4},{1,5},{2,2},{3,3},{6,6},{7,7},{8,12},{9,13},{10,10},{11,11},... | collective-permute-start | bytes 1572872 | tf_op jit(solution)/shard_map/ppermute | solution.py:419
  13.1 3.6 %extract.9 = (bf16[512,512]{1,0:T(8,128)(2,1)S(1)}, f32[1,512]{1,0:T(1,128)S(1)}, f32[8,128]{1,0:T(8,128)S(1)}) custom-call(bf16[65536,128]{1,0:T(8,128)(2,1)} %bitcast.38, bf16[16,128]{1,0:T(8,128)(2,1)S(1)} %bitcast.30, f32[8,128]{1,0:T(8,128)S(1)} %get-tuple-element.117.refs_2_), custom_call_target="tpu_custom_call" | custom-call | flops 4194304 | bytes 2097152 | tf_op jit(solution)/shard_map/extract/pallas_call | solution.py:32
  16.8 3.6 %extract.10 = (bf16[512,512]{1,0:T(8,128)(2,1)S(1)}, f32[1,512]{1,0:T(1,128)S(1)}, f32[8,128]{1,0:T(8,128)S(1)}) custom-call(bf16[65536,128]{1,0:T(8,128)(2,1)} %bitcast.39, bf16[16,128]{1,0:T(8,128)(2,1)S(1)} %bitcast.31, f32[8,128]{1,0:T(8,128)S(1)} %get-tuple-element.119.refs_2_), custom_call_target="tpu_custom_call" | custom-call | flops 4194304 | bytes 2097152 | tf_op jit(solution)/shard_map/extract/pallas_call | solution.py:32
  20.4 4.2 %extract.11 = (bf16[512,512]{1,0:T(8,128)(2,1)}, f32[1,512]{1,0:T(1,128)S(1)}, f32[8,128]{1,0:T(8,128)S(1)}) custom-call(bf16[65536,128]{1,0:T(8,128)(2,1)} %bitcast.40, bf16[16,128]{1,0:T(8,128)(2,1)S(1)} %bitcast.32, f32[8,128]{1,0:T(8,128)S(1)} %get-tuple-element.120.refs_2_), custom_call_target="tpu_custom_call" | custom-call | flops 4194304 | bytes 2097152 | tf_op jit(solution)/shard_map/extract/pallas_call | solution.py:32
  25.9 4.2 %extract.12 = (bf16[512,512]{1,0:T(8,128)(2,1)}, f32[1,512]{1,0:T(1,128)S(1)}, f32[8,128]{1,0:T(8,128)S(1)}) custom-call(bf16[65536,128]{1,0:T(8,128)(2,1)} %bitcast.41, bf16[16,128]{1,0:T(8,128)(2,1)S(1)} %bitcast.33, f32[8,128]{1,0:T(8,128)S(1)} %get-tuple-element.121.refs_2_), custom_call_target="tpu_custom_call" | custom-call | flops 4194304 | bytes 2097152 | tf_op jit(solution)/shard_map/extract/pallas_call | solution.py:32
  30.1 3.6 %extract.13 = (bf16[512,512]{1,0:T(8,128)(2,1)S(1)}, f32[1,512]{1,0:T(1,128)S(1)}, f32[8,128]{1,0:T(8,128)S(1)}) custom-call(bf16[65536,128]{1,0:T(8,128)(2,1)} %bitcast.42, bf16[16,128]{1,0:T(8,128)(2,1)S(1)} %bitcast.34, f32[8,128]{1,0:T(8,128)S(1)} %get-tuple-element.122.refs_2_), custom_call_target="tpu_custom_call" | custom-call | flops 4194304 | bytes 2097152 | tf_op jit(solution)/shard_map/extract/pallas_call | solution.py:32
  34.5 3.6 %extract.14 = (bf16[512,512]{1,0:T(8,128)(2,1)S(1)}, f32[1,512]{1,0:T(1,128)S(1)}, f32[8,128]{1,0:T(8,128)S(1)}) custom-call(bf16[65536,128]{1,0:T(8,128)(2,1)} %bitcast.43, bf16[16,128]{1,0:T(8,128)(2,1)S(1)} %bitcast.35, f32[8,128]{1,0:T(8,128)S(1)} %get-tuple-element.123.refs_2_), custom_call_target="tpu_custom_call" | custom-call | flops 4194304 | bytes 2097152 | tf_op jit(solution)/shard_map/extract/pallas_call | solution.py:32
  38.9 3.7 %extract.15 = (bf16[512,512]{1,0:T(8,128)(2,1)S(1)}, f32[1,512]{1,0:T(1,128)S(1)}, f32[8,128]{1,0:T(8,128)S(1)}) custom-call(bf16[65536,128]{1,0:T(8,128)(2,1)} %bitcast.44, bf16[16,128]{1,0:T(8,128)(2,1)S(1)} %bitcast.36, f32[8,128]{1,0:T(8,128)S(1)} %get-tuple-element.124.refs_2_), custom_call_target="tpu_custom_call" | custom-call | flops 4194304 | bytes 2097152 | tf_op jit(solution)/shard_map/extract/pallas_call | solution.py:32
  43.4 1.5 collective-permute-start.5
  46.3 1.6 collective-permute-start.2
  47.9 2.2 collective-permute-done.2.refs_1_
  50.2 3.7 %collective-permute-done.3.refs_1_ = f32[8,512]{1,0:T(8,128)S(1)} collective-permute-done((f32[8,512]{1,0:T(8,128)S(1)}, f32[8,512]{1,0:T(8,128)S(1)}, u32[]{:S(2)}, u32[]{:S(2)}) %collective-permute-start.3) | collective-permute-done | bytes 16416 | tf_op jit(solution)/shard_map/ppermute | solution.py:396
  53.9 7.2 %collective-permute-start.4 = (f32[8,512]{1,0:T(8,128)S(1)}, f32[8,512]{1,0:T(8,128)S(1)}, u32[]{:S(2)}, u32[]{:S(2)}) collective-permute-start(f32[8,512]{1,0:T(8,128)S(1)} %get-tuple-element.139.refs_0_), channel_id=1, source_target_pairs={{0,4},{1,5},{2,6},{3,7},{4,0},{5,1},{6,2},{7,3},{8,12},{9,13},{10,... | collective-permute-start | bytes 49160 | tf_op jit(solution)/shard_map/ppermute | solution.py:396
  61.1 2.7 %collective-permute-start.1 = (bf16[512,512]{1,0:T(8,128)(2,1)S(1)}, bf16[512,512]{1,0:T(8,128)(2,1)}, u32[]{:S(2)}, u32[]{:S(2)}) collective-permute-start(bf16[512,512]{1,0:T(8,128)(2,1)S(1)} %get-tuple-element.126.refs_1_), channel_id=1, source_target_pairs={{0,4},{1,5},{2,2},{3,3},{6,6},{7,7},{8,12},{9,13},{10,10},{11,11},... | collective-permute-start | bytes 1572872 | tf_op jit(solution)/shard_map/ppermute | solution.py:419
  67.2 5.7 %collective-permute-done.1.refs_0_ = bf16[512,512]{1,0:T(8,128)(2,1)} collective-permute-done((bf16[512,512]{1,0:T(8,128)(2,1)S(1)}, bf16[512,512]{1,0:T(8,128)(2,1)}, u32[]{:S(2)}, u32[]{:S(2)}) %collective-permute-start.1) | collective-permute-done | bytes 524320 | tf_op jit(solution)/shard_map/ppermute | solution.py:419
  72.9 6.2 %collective-permute-start.21 = (bf16[512,512]{1,0:T(8,128)(2,1)S(1)}, bf16[512,512]{1,0:T(8,128)(2,1)}, u32[]{:S(2)}, u32[]{:S(2)}) collective-permute-start(bf16[512,512]{1,0:T(8,128)(2,1)S(1)} %get-tuple-element.159.refs_1_), channel_id=1, source_target_pairs={{0,4},{1,5},{2,2},{3,3},{6,6},{7,7},{8,12},{9,13},{10,10},{11,11},... | collective-permute-start | bytes 1572872 | tf_op jit(solution)/shard_map/ppermute | solution.py:419
  79.2 1.6 collective-permute-start.12
  80.8 5.4 %collective-permute-start.19 = (bf16[512,512]{1,0:T(8,128)(2,1)}, bf16[512,512]{1,0:T(8,128)(2,1)}, u32[]{:S(2)}, u32[]{:S(2)}) collective-permute-start(bf16[512,512]{1,0:T(8,128)(2,1)} %get-tuple-element.158.refs_2_), channel_id=1, source_target_pairs={{4,2},{5,3},{0,0},{1,1},{6,6},{7,7},{12,10},{13,11},{8,8},{9,9},{1... | collective-permute-start | bytes 1572872 | tf_op jit(solution)/shard_map/ppermute | solution.py:425
  87.3 5.3 %collective-permute-start.20 = (bf16[512,512]{1,0:T(8,128)(2,1)}, bf16[512,512]{1,0:T(8,128)(2,1)}, u32[]{:S(2)}, u32[]{:S(2)}) collective-permute-start(bf16[512,512]{1,0:T(8,128)(2,1)} %get-tuple-element.158.refs_2_), channel_id=1, source_target_pairs={{4,6},{5,7},{6,4},{7,5},{0,0},{1,1},{2,2},{3,3},{12,14},{13,15},{1... | collective-permute-start | bytes 1572872 | tf_op jit(solution)/shard_map/ppermute | solution.py:426
  92.7 2.8 %collective-permute-start.8 = (bf16[512,512]{1,0:T(8,128)(2,1)}, bf16[512,512]{1,0:T(8,128)(2,1)}, u32[]{:S(2)}, u32[]{:S(2)}) collective-permute-start(bf16[512,512]{1,0:T(8,128)(2,1)} %get-tuple-element.147.refs_1_), channel_id=1, source_target_pairs={{0,4},{1,5},{2,2},{3,3},{6,6},{7,7},{8,12},{9,13},{10,10},{11,11},... | collective-permute-start | bytes 1572872 | tf_op jit(solution)/shard_map/ppermute | solution.py:419
  101.2 3.9 %collective-permute-done.8.refs_0_ = bf16[512,512]{1,0:T(8,128)(2,1)} collective-permute-done((bf16[512,512]{1,0:T(8,128)(2,1)}, bf16[512,512]{1,0:T(8,128)(2,1)}, u32[]{:S(2)}, u32[]{:S(2)}) %collective-permute-start.8) | collective-permute-done | bytes 524320 | tf_op jit(solution)/shard_map/ppermute | solution.py:419
  106.9 5.4 %collective-permute-start.24 = (bf16[512,512]{1,0:T(8,128)(2,1)}, bf16[512,512]{1,0:T(8,128)(2,1)}, u32[]{:S(2)}, u32[]{:S(2)}) collective-permute-start(bf16[512,512]{1,0:T(8,128)(2,1)} %get-tuple-element.170.refs_2_), channel_id=1, source_target_pairs={{4,2},{5,3},{0,0},{1,1},{6,6},{7,7},{12,10},{13,11},{8,8},{9,9},{1... | collective-permute-start | bytes 1572872 | tf_op jit(solution)/shard_map/ppermute | solution.py:425
  116.1 1.5 collective-permute-start.31
  117.6 1.7 collective-permute-start.25
  119.8 7.6 %collective-permute-start.29 = (bf16[512,512]{1,0:T(8,128)(2,1)}, bf16[512,512]{1,0:T(8,128)(2,1)S(1)}, u32[]{:S(2)}, u32[]{:S(2)}) collective-permute-start(bf16[512,512]{1,0:T(8,128)(2,1)} %copy-done.5), channel_id=1, source_target_pairs={{0,4},{1,5},{2,2},{3,3},{6,6},{7,7},{8,12},{9,13},{10,10},{11,11},... | collective-permute-start | bytes 1572872 | tf_op jit(solution)/shard_map/ppermute | solution.py:419
  130.0 15.5 %factors.1 = (bf16[1024,2048]{1,0:T(8,128)(2,1)}, f32[8,128]{1,0:T(8,128)S(1)}) custom-call(s32[3]{0:T(128)S(1)} %pad_add_fusion.refs_0_, bf16[8192,128]{1,0:T(8,128)(2,1)} %get-tuple-element.149.refs_1_, bf16[8192,128]{1,0:T(8,128)(2,1)} %collective-permute-done.9.refs_2_, bf16[8192,128]{1,0:T(8,128)(2,1)} %collective-permute-done.10.refs_3_, ...), custom_call_target="tpu_custom_call" | custom-call | flops 6442450944 | bytes 12582912 | tf_op jit(solution)/shard_map/factors/pallas_call | solution.py:32
  145.5 1.8 collective-permute-start.27
  147.5 1.7 collective-permute-start.28
  149.2 7.3 %update.9 = (bf16[65536,128]{1,0:T(8,128)(2,1)}, f32[8,128]{1,0:T(8,128)S(1)}) custom-call(bf16[65536,128]{1,0:T(8,128)(2,1)} %bitcast.45, bf16[512,512]{1,0:T(8,128)(2,1)S(1)} %get-tuple-element.150.refs_1_, bf16[512,512]{1,0:T(8,128)(2,1)S(1)} %collective-permute-done.12.refs_2_, bf16[1024,2048]{1,0:T(8,128)(2,1)} %get-tuple-element.169.refs_3_, ...), custom_call_target="tpu_custom_call" | custom-call | flops 2147483648 | bytes 5242880 | tf_op jit(solution)/shard_map/update/pallas_call | solution.py:32
  158.0 7.5 %update.10 = (bf16[65536,128]{1,0:T(8,128)(2,1)}, f32[8,128]{1,0:T(8,128)S(1)}) custom-call(bf16[65536,128]{1,0:T(8,128)(2,1)} %bitcast.46, bf16[512,512]{1,0:T(8,128)(2,1)S(1)} %copy-done.12, bf16[512,512]{1,0:T(8,128)(2,1)S(1)} %collective-permute-done.31.refs_2_, bf16[1024,2048]{1,0:T(8,128)(2,1)} %get-tuple-element.169.refs_3_, ...), custom_call_target="tpu_custom_call", output_to_operand_aliasing={{0}: (4, {})} | custom-call | flops 2147483648 | bytes 5242880 | tf_op jit(solution)/shard_map/update/pallas_call | solution.py:32
  165.4 3.0 %collective-permute-start.26 = (f32[4,512]{1,0:T(4,128)S(1)}, f32[4,512]{1,0:T(4,128)S(1)}, u32[]{:S(2)}, u32[]{:S(2)}) collective-permute-start(f32[4,512]{1,0:T(4,128)S(1)} %get-tuple-element.174), channel_id=1, source_target_pairs={{0,8},{8,16},{16,24},{1,9},{9,17},{17,25},{2,10},{10,18},{18,26},{... | collective-permute-start | bytes 24584 | tf_op jit(solution)/shard_map/ppermute | solution.py:492
  168.5 5.4 %collective-permute-start.22 = (bf16[512,512]{1,0:T(8,128)(2,1)S(1)}, bf16[512,512]{1,0:T(8,128)(2,1)S(1)}, u32[]{:S(2)}, u32[]{:S(2)}) collective-permute-start(bf16[512,512]{1,0:T(8,128)(2,1)S(1)} %get-tuple-element.166.refs_1_), channel_id=1, source_target_pairs={{0,4},{1,5},{2,2},{3,3},{6,6},{7,7},{8,12},{9,13},{10,10},{11,11},... | collective-permute-start | bytes 1572872 | tf_op jit(solution)/shard_map/ppermute | solution.py:419
  173.9 7.5 %update.11 = (bf16[65536,128]{1,0:T(8,128)(2,1)}, f32[8,128]{1,0:T(8,128)S(1)}) custom-call(bf16[65536,128]{1,0:T(8,128)(2,1)} %bitcast.47, bf16[512,512]{1,0:T(8,128)(2,1)S(1)} %get-tuple-element.177.refs_1_, bf16[512,512]{1,0:T(8,128)(2,1)S(1)} %collective-permute-done.30.refs_2_, ...), custom_call_target="tpu_custom_call", output_to_operand_aliasing={{0}: (4, {})} | custom-call | flops 2147483648 | bytes 5242880 | tf_op jit(solution)/shard_map/update/pallas_call | solution.py:32
  185.2 1.5 collective-permute-start.36
  186.8 7.5 %update.12 = (bf16[65536,128]{1,0:T(8,128)(2,1)}, f32[8,128]{1,0:T(8,128)S(1)}) custom-call(bf16[65536,128]{1,0:T(8,128)(2,1)} %bitcast.48, bf16[512,512]{1,0:T(8,128)(2,1)S(1)} %get-tuple-element.187.refs_1_, bf16[512,512]{1,0:T(8,128)(2,1)S(1)} %collective-permute-done.33.refs_2_, ...), custom_call_target="tpu_custom_call", output_to_operand_aliasing={{0}: (4, {})} | custom-call | flops 2147483648 | bytes 5242880 | tf_op jit(solution)/shard_map/update/pallas_call | solution.py:32
  196.4 5.7 %collective-permute-start.43 = (bf16[256,512]{1,0:T(8,128)(2,1)S(1)}, bf16[256,512]{1,0:T(8,128)(2,1)S(1)}, u32[]{:S(2)}, u32[]{:S(2)}) collective-permute-start(bf16[256,512]{1,0:T(8,128)(2,1)S(1)} %get-tuple-element.204.refs_1_), channel_id=1, source_target_pairs={{0,4},{1,5},{2,2},{3,3},{6,6},{7,7},{8,12},{9,13},{10,10},{11,11},... | collective-permute-start | bytes 786440 | tf_op jit(solution)/shard_map/ppermute | solution.py:419
  202.5 7.3 %update.13 = (bf16[65536,128]{1,0:T(8,128)(2,1)}, f32[8,128]{1,0:T(8,128)S(1)}) custom-call(bf16[65536,128]{1,0:T(8,128)(2,1)} %bitcast.49, bf16[512,512]{1,0:T(8,128)(2,1)S(1)} %get-tuple-element.194.refs_1_, bf16[512,512]{1,0:T(8,128)(2,1)S(1)} %collective-permute-done.36.refs_2_, ...), custom_call_target="tpu_custom_call", output_to_operand_aliasing={{0}: (4, {})} | custom-call | flops 2147483648 | bytes 5242880 | tf_op jit(solution)/shard_map/update/pallas_call | solution.py:32
  209.9 1.6 collective-permute-start.49
  211.5 4.1 %collective-permute-start.34 = (bf16[256,512]{1,0:T(8,128)(2,1)S(1)}, bf16[256,512]{1,0:T(8,128)(2,1)S(1)}, u32[]{:S(2)}, u32[]{:S(2)}) collective-permute-start(bf16[256,512]{1,0:T(8,128)(2,1)S(1)} %get-tuple-element.192.refs_1_), channel_id=1, source_target_pairs={{0,4},{1,5},{2,2},{3,3},{6,6},{7,7},{8,12},{9,13},{10,10},{11,11},... | collective-permute-start | bytes 786440 | tf_op jit(solution)/shard_map/ppermute | solution.py:419
  217.3 1.6 collective-permute-start.39
  218.9 7.5 %update.14 = (bf16[65536,128]{1,0:T(8,128)(2,1)}, f32[8,128]{1,0:T(8,128)S(1)}) custom-call(bf16[65536,128]{1,0:T(8,128)(2,1)} %bitcast.50, bf16[512,512]{1,0:T(8,128)(2,1)S(1)} %get-tuple-element.201.refs_1_, bf16[512,512]{1,0:T(8,128)(2,1)S(1)} %collective-permute-done.40.refs_2_, ...), custom_call_target="tpu_custom_call", output_to_operand_aliasing={{0}: (4, {})} | custom-call | flops 2147483648 | bytes 5242880 | tf_op jit(solution)/shard_map/update/pallas_call | solution.py:32
  228.5 7.4 %update.15 = (bf16[65536,128]{1,0:T(8,128)(2,1)}, f32[8,128]{1,0:T(8,128)S(1)}) custom-call(bf16[65536,128]{1,0:T(8,128)(2,1)} %bitcast.51, bf16[512,512]{1,0:T(8,128)(2,1)S(1)} %get-tuple-element.214.refs_1_, bf16[512,512]{1,0:T(8,128)(2,1)S(1)} %collective-permute-done.49.refs_2_, ...), custom_call_target="tpu_custom_call", output_to_operand_aliasing={{0}: (4, {})} | custom-call | flops 2147483648 | bytes 5242880 | tf_op jit(solution)/shard_map/update/pallas_call | solution.py:32
  235.9 5.4 %update.16 = (bf16[65536,128]{1,0:T(8,128)(2,1)}, f32[8,128]{1,0:T(8,128)S(1)}) custom-call(bf16[65536,128]{1,0:T(8,128)(2,1)} %bitcast.52, bf16[256,512]{1,0:T(8,128)(2,1)S(1)} %get-tuple-element.213.refs_1_, bf16[256,512]{1,0:T(8,128)(2,1)S(1)} %collective-permute-done.48.refs_2_, ...), custom_call_target="tpu_custom_call", output_to_operand_aliasing={{0}: (4, {})} | custom-call | flops 1073741824 | bytes 2621440 | tf_op jit(solution)/shard_map/update/pallas_call | solution.py:32
  241.4 1.6 collective-permute-start.51
  243.0 5.1 %collective-permute-start.52 = (f32[4,512]{1,0:T(4,128)S(1)}, f32[4,512]{1,0:T(4,128)S(1)}, u32[]{:S(2)}, u32[]{:S(2)}) collective-permute-start(f32[4,512]{1,0:T(4,128)S(1)} %get-tuple-element.224.refs_0_), channel_id=1, source_target_pairs={{0,4},{1,5},{2,6},{3,7},{4,0},{5,1},{6,2},{7,3},{8,12},{9,13},{10,... | collective-permute-start | bytes 24584 | tf_op jit(solution)/shard_map/ppermute | solution.py:396
  250.3 5.4 %update.17 = (bf16[65536,128]{1,0:T(8,128)(2,1)}, f32[8,128]{1,0:T(8,128)}) custom-call(bf16[65536,128]{1,0:T(8,128)(2,1)} %bitcast.53, bf16[256,512]{1,0:T(8,128)(2,1)S(1)} %get-tuple-element.222.refs_1_, bf16[256,512]{1,0:T(8,128)(2,1)S(1)} %collective-permute-done.51.refs_2_, ...), custom_call_target="tpu_custom_call", output_to_operand_aliasing={{0}: (4, {})} | custom-call | flops 1073741824 | bytes 2621440 | tf_op jit(solution)/shard_map/update/pallas_call | solution.py:32
  (152 shorter events, 38.7 us)
Async XLA Ops:
  5.7 61.0 %collective-permute-start.10 = (bf16[8192,128]{1,0:T(8,128)(2,1)}, bf16[8192,128]{1,0:T(8,128)(2,1)}, u32[]{:S(2)}, u32[]{:S(2)}) collective-permute-start(bf16[8192,128]{1,0:T(8,128)(2,1)} %get-tuple-element.149.refs_1_), channel_id=1, source_target_pairs={{0,16},{8,24},{16,0},{24,8},{1,17},{9,25},{17,1},{25,9},{2,18},{10... | collective-permute-start | bytes 6291464 | tf_op jit(solution)/shard_map/ppermute | solution.py:392
  8.6 34.0 %collective-permute-start = (bf16[512,512]{1,0:T(8,128)(2,1)S(1)}, bf16[512,512]{1,0:T(8,128)(2,1)S(1)}, u32[]{:S(2)}, u32[]{:S(2)}) collective-permute-start(bf16[512,512]{1,0:T(8,128)(2,1)S(1)} %get-tuple-element.116.refs_1_.refs_6_), channel_id=1, source_target_pairs={{0,4},{1,5},{2,2},{3,3},{6,6},{7,7},{8,12},{9,13},{10,10},{11,11},... | collective-permute-start | bytes 1572872 | tf_op jit(solution)/shard_map/ppermute | solution.py:419
  24.6 36.5 %collective-permute-start.7 = (bf16[512,512]{1,0:T(8,128)(2,1)}, bf16[512,512]{1,0:T(8,128)(2,1)S(1)}, u32[]{:S(2)}, u32[]{:S(2)}) collective-permute-start(bf16[512,512]{1,0:T(8,128)(2,1)} %get-tuple-element.141.refs_1_), channel_id=1, source_target_pairs={{0,4},{1,5},{2,2},{3,3},{6,6},{7,7},{8,12},{9,13},{10,10},{11,11},... | collective-permute-start | bytes 1572872 | tf_op jit(solution)/shard_map/ppermute | solution.py:419
  43.4 21.8 %collective-permute-start.5 = (bf16[512,512]{1,0:T(8,128)(2,1)S(1)}, bf16[512,512]{1,0:T(8,128)(2,1)}, u32[]{:S(2)}, u32[]{:S(2)}) collective-permute-start(bf16[512,512]{1,0:T(8,128)(2,1)S(1)} %get-tuple-element.140.refs_2_), channel_id=1, source_target_pairs={{4,2},{5,3},{0,0},{1,1},{6,6},{7,7},{12,10},{13,11},{8,8},{9,9},{1... | collective-permute-start | bytes 1572872 | tf_op jit(solution)/shard_map/ppermute | solution.py:425
  44.9 20.4 %collective-permute-start.6 = (bf16[512,512]{1,0:T(8,128)(2,1)S(1)}, bf16[512,512]{1,0:T(8,128)(2,1)}, u32[]{:S(2)}, u32[]{:S(2)}) collective-permute-start(bf16[512,512]{1,0:T(8,128)(2,1)S(1)} %get-tuple-element.140.refs_2_), channel_id=1, source_target_pairs={{4,6},{5,7},{6,4},{7,5},{0,0},{1,1},{2,2},{3,3},{12,14},{13,15},{1... | collective-permute-start | bytes 1572872 | tf_op jit(solution)/shard_map/ppermute | solution.py:426
  53.9 9.9 %collective-permute-start.4 = (f32[8,512]{1,0:T(8,128)S(1)}, f32[8,512]{1,0:T(8,128)S(1)}, u32[]{:S(2)}, u32[]{:S(2)}) collective-permute-start(f32[8,512]{1,0:T(8,128)S(1)} %get-tuple-element.139.refs_0_), channel_id=1, source_target_pairs={{0,4},{1,5},{2,6},{3,7},{4,0},{5,1},{6,2},{7,3},{8,12},{9,13},{10,... | collective-permute-start | bytes 49160 | tf_op jit(solution)/shard_map/ppermute | solution.py:396
  61.1 11.9 %collective-permute-start.1 = (bf16[512,512]{1,0:T(8,128)(2,1)S(1)}, bf16[512,512]{1,0:T(8,128)(2,1)}, u32[]{:S(2)}, u32[]{:S(2)}) collective-permute-start(bf16[512,512]{1,0:T(8,128)(2,1)S(1)} %get-tuple-element.126.refs_1_), channel_id=1, source_target_pairs={{0,4},{1,5},{2,2},{3,3},{6,6},{7,7},{8,12},{9,13},{10,10},{11,11},... | collective-permute-start | bytes 1572872 | tf_op jit(solution)/shard_map/ppermute | solution.py:419
  63.8 15.4 %collective-permute-start.13 = (bf16[512,512]{1,0:T(8,128)(2,1)S(1)}, bf16[512,512]{1,0:T(8,128)(2,1)}, u32[]{:S(2)}, u32[]{:S(2)}) collective-permute-start(bf16[512,512]{1,0:T(8,128)(2,1)S(1)} %get-tuple-element.151.refs_2_), channel_id=1, source_target_pairs={{4,2},{5,3},{0,0},{1,1},{6,6},{7,7},{12,10},{13,11},{8,8},{9,9},{1... | collective-permute-start | bytes 1572872 | tf_op jit(solution)/shard_map/ppermute | solution.py:425
  65.2 52.4 %collective-permute-start.9 = (bf16[8192,128]{1,0:T(8,128)(2,1)}, bf16[8192,128]{1,0:T(8,128)(2,1)}, u32[]{:S(2)}, u32[]{:S(2)}) collective-permute-start(bf16[8192,128]{1,0:T(8,128)(2,1)} %get-tuple-element.149.refs_1_), channel_id=1, source_target_pairs={{0,8},{8,0},{16,24},{24,16},{1,9},{9,1},{17,25},{25,17},{2,10},{10... | collective-permute-start | bytes 6291464 | tf_op jit(solution)/shard_map/ppermute | solution.py:396
  65.3 15.5 %collective-permute-start.14 = (bf16[512,512]{1,0:T(8,128)(2,1)S(1)}, bf16[512,512]{1,0:T(8,128)(2,1)}, u32[]{:S(2)}, u32[]{:S(2)}) collective-permute-start(bf16[512,512]{1,0:T(8,128)(2,1)S(1)} %get-tuple-element.151.refs_2_), channel_id=1, source_target_pairs={{4,6},{5,7},{6,4},{7,5},{0,0},{1,1},{2,2},{3,3},{12,14},{13,15},{1... | collective-permute-start | bytes 1572872 | tf_op jit(solution)/shard_map/ppermute | solution.py:426
  66.7 60.8 %collective-permute-start.11 = (bf16[8192,128]{1,0:T(8,128)(2,1)}, bf16[8192,128]{1,0:T(8,128)(2,1)}, u32[]{:S(2)}, u32[]{:S(2)}) collective-permute-start(bf16[8192,128]{1,0:T(8,128)(2,1)} %collective-permute-done.10.refs_3_), channel_id=1, source_target_pairs={{0,8},{8,0},{16,24},{24,16},{1,9},{9,1},{17,25},{25,17},{2,10},{10... | collective-permute-start | bytes 6291464 | tf_op jit(solution)/shard_map/ppermute | solution.py:396
  72.9 14.4 %collective-permute-start.21 = (bf16[512,512]{1,0:T(8,128)(2,1)S(1)}, bf16[512,512]{1,0:T(8,128)(2,1)}, u32[]{:S(2)}, u32[]{:S(2)}) collective-permute-start(bf16[512,512]{1,0:T(8,128)(2,1)S(1)} %get-tuple-element.159.refs_1_), channel_id=1, source_target_pairs={{0,4},{1,5},{2,2},{3,3},{6,6},{7,7},{8,12},{9,13},{10,10},{11,11},... | collective-permute-start | bytes 1572872 | tf_op jit(solution)/shard_map/ppermute | solution.py:419
  79.2 13.5 %collective-permute-start.12 = (bf16[512,512]{1,0:T(8,128)(2,1)S(1)}, bf16[512,512]{1,0:T(8,128)(2,1)S(1)}, u32[]{:S(2)}, u32[]{:S(2)}) collective-permute-start(bf16[512,512]{1,0:T(8,128)(2,1)S(1)} %get-tuple-element.150.refs_1_), channel_id=1, source_target_pairs={{0,1},{1,0},{2,3},{3,2},{4,5},{5,4},{6,7},{7,6},{8,9},{9,8},{10,11... | collective-permute-start | bytes 1572872 | tf_op jit(solution)/shard_map/ppermute | solution.py:396
  80.8 17.4 %collective-permute-start.19 = (bf16[512,512]{1,0:T(8,128)(2,1)}, bf16[512,512]{1,0:T(8,128)(2,1)}, u32[]{:S(2)}, u32[]{:S(2)}) collective-permute-start(bf16[512,512]{1,0:T(8,128)(2,1)} %get-tuple-element.158.refs_2_), channel_id=1, source_target_pairs={{4,2},{5,3},{0,0},{1,1},{6,6},{7,7},{12,10},{13,11},{8,8},{9,9},{1... | collective-permute-start | bytes 1572872 | tf_op jit(solution)/shard_map/ppermute | solution.py:425
  87.3 12.6 %collective-permute-start.20 = (bf16[512,512]{1,0:T(8,128)(2,1)}, bf16[512,512]{1,0:T(8,128)(2,1)}, u32[]{:S(2)}, u32[]{:S(2)}) collective-permute-start(bf16[512,512]{1,0:T(8,128)(2,1)} %get-tuple-element.158.refs_2_), channel_id=1, source_target_pairs={{4,6},{5,7},{6,4},{7,5},{0,0},{1,1},{2,2},{3,3},{12,14},{13,15},{1... | collective-permute-start | bytes 1572872 | tf_op jit(solution)/shard_map/ppermute | solution.py:426
  92.7 12.4 %collective-permute-start.8 = (bf16[512,512]{1,0:T(8,128)(2,1)}, bf16[512,512]{1,0:T(8,128)(2,1)}, u32[]{:S(2)}, u32[]{:S(2)}) collective-permute-start(bf16[512,512]{1,0:T(8,128)(2,1)} %get-tuple-element.147.refs_1_), channel_id=1, source_target_pairs={{0,4},{1,5},{2,2},{3,3},{6,6},{7,7},{8,12},{9,13},{10,10},{11,11},... | collective-permute-start | bytes 1572872 | tf_op jit(solution)/shard_map/ppermute | solution.py:419
  98.2 14.1 %collective-permute-start.16 = (bf16[512,512]{1,0:T(8,128)(2,1)}, bf16[512,512]{1,0:T(8,128)(2,1)}, u32[]{:S(2)}, u32[]{:S(2)}) collective-permute-start(bf16[512,512]{1,0:T(8,128)(2,1)} %get-tuple-element.154.refs_5_), channel_id=1, source_target_pairs={{0,16},{8,24},{16,0},{24,8},{1,17},{9,25},{17,1},{25,9},{2,18},{10... | collective-permute-start | bytes 1572872 | tf_op jit(solution)/shard_map/ppermute | solution.py:392
  105.0 11.0 %collective-permute-start.15 = (bf16[512,512]{1,0:T(8,128)(2,1)}, bf16[512,512]{1,0:T(8,128)(2,1)}, u32[]{:S(2)}, u32[]{:S(2)}) collective-permute-start(bf16[512,512]{1,0:T(8,128)(2,1)} %get-tuple-element.154.refs_5_), channel_id=1, source_target_pairs={{0,8},{8,0},{16,24},{24,16},{1,9},{9,1},{17,25},{25,17},{2,10},{10... | collective-permute-start | bytes 1572872 | tf_op jit(solution)/shard_map/ppermute | solution.py:396
  106.9 12.4 %collective-permute-start.24 = (bf16[512,512]{1,0:T(8,128)(2,1)}, bf16[512,512]{1,0:T(8,128)(2,1)}, u32[]{:S(2)}, u32[]{:S(2)}) collective-permute-start(bf16[512,512]{1,0:T(8,128)(2,1)} %get-tuple-element.170.refs_2_), channel_id=1, source_target_pairs={{4,2},{5,3},{0,0},{1,1},{6,6},{7,7},{12,10},{13,11},{8,8},{9,9},{1... | collective-permute-start | bytes 1572872 | tf_op jit(solution)/shard_map/ppermute | solution.py:425
  112.3 7.6 %collective-permute-start.17 = (bf16[512,512]{1,0:T(8,128)(2,1)}, bf16[512,512]{1,0:T(8,128)(2,1)}, u32[]{:S(2)}, u32[]{:S(2)}) collective-permute-start(bf16[512,512]{1,0:T(8,128)(2,1)} %collective-permute-done.16.refs_7_), channel_id=1, source_target_pairs={{0,8},{8,0},{16,24},{24,16},{1,9},{9,1},{17,25},{25,17},{2,10},{10... | collective-permute-start | bytes 1572872 | tf_op jit(solution)/shard_map/ppermute | solution.py:396
  116.1 41.3 %collective-permute-start.31 = (bf16[512,512]{1,0:T(8,128)(2,1)}, bf16[512,512]{1,0:T(8,128)(2,1)S(1)}, u32[]{:S(2)}, u32[]{:S(2)}) collective-permute-start(bf16[512,512]{1,0:T(8,128)(2,1)} %copy-done.11), channel_id=1, source_target_pairs={{0,1},{1,0},{2,3},{3,2},{4,5},{5,4},{6,7},{7,6},{8,9},{9,8},{10,11... | collective-permute-start | bytes 1572872 | tf_op jit(solution)/shard_map/ppermute | solution.py:396
  117.6 27.9 %collective-permute-start.25 = (bf16[512,512]{1,0:T(8,128)(2,1)}, bf16[512,512]{1,0:T(8,128)(2,1)S(1)}, u32[]{:S(2)}, u32[]{:S(2)}) collective-permute-start(bf16[512,512]{1,0:T(8,128)(2,1)} %get-tuple-element.170.refs_2_), channel_id=1, source_target_pairs={{4,6},{5,7},{6,4},{7,5},{0,0},{1,1},{2,2},{3,3},{12,14},{13,15},{1... | collective-permute-start | bytes 1572872 | tf_op jit(solution)/shard_map/ppermute | solution.py:426
  119.3 46.1 %collective-permute-start.30 = (bf16[512,512]{1,0:T(8,128)(2,1)S(1)}, bf16[512,512]{1,0:T(8,128)(2,1)S(1)}, u32[]{:S(2)}, u32[]{:S(2)}) collective-permute-start(bf16[512,512]{1,0:T(8,128)(2,1)S(1)} %get-tuple-element.177.refs_1_), channel_id=1, source_target_pairs={{0,1},{1,0},{2,3},{3,2},{4,5},{5,4},{6,7},{7,6},{8,9},{9,8},{10,11... | collective-permute-start | bytes 1572872 | tf_op jit(solution)/shard_map/ppermute | solution.py:396
  119.8 48.6 %collective-permute-start.29 = (bf16[512,512]{1,0:T(8,128)(2,1)}, bf16[512,512]{1,0:T(8,128)(2,1)S(1)}, u32[]{:S(2)}, u32[]{:S(2)}) collective-permute-start(bf16[512,512]{1,0:T(8,128)(2,1)} %copy-done.5), channel_id=1, source_target_pairs={{0,4},{1,5},{2,2},{3,3},{6,6},{7,7},{8,12},{9,13},{10,10},{11,11},... | collective-permute-start | bytes 1572872 | tf_op jit(solution)/shard_map/ppermute | solution.py:419
  127.5 20.0 %collective-permute-start.23 = (f32[4,512]{1,0:T(4,128)S(1)}, f32[4,512]{1,0:T(4,128)S(1)}, u32[]{:S(2)}, u32[]{:S(2)}) collective-permute-start(f32[4,512]{1,0:T(4,128)S(1)} %get-tuple-element.168), channel_id=1, source_target_pairs={{0,8},{8,16},{16,24},{1,9},{9,17},{17,25},{2,10},{10,18},{18,26},{... | collective-permute-start | bytes 24584 | tf_op jit(solution)/shard_map/ppermute | solution.py:492
  145.5 35.9 %collective-permute-start.27 = (bf16[512,512]{1,0:T(8,128)(2,1)}, bf16[512,512]{1,0:T(8,128)(2,1)S(1)}, u32[]{:S(2)}, u32[]{:S(2)}) collective-permute-start(bf16[512,512]{1,0:T(8,128)(2,1)} %get-tuple-element.175.refs_2_), channel_id=1, source_target_pairs={{4,2},{5,3},{0,0},{1,1},{6,6},{7,7},{12,10},{13,11},{8,8},{9,9},{1... | collective-permute-start | bytes 1572872 | tf_op jit(solution)/shard_map/ppermute | solution.py:425
  147.5 34.7 %collective-permute-start.28 = (bf16[512,512]{1,0:T(8,128)(2,1)}, bf16[512,512]{1,0:T(8,128)(2,1)S(1)}, u32[]{:S(2)}, u32[]{:S(2)}) collective-permute-start(bf16[512,512]{1,0:T(8,128)(2,1)} %get-tuple-element.175.refs_2_), channel_id=1, source_target_pairs={{4,6},{5,7},{6,4},{7,5},{0,0},{1,1},{2,2},{3,3},{12,14},{13,15},{1... | collective-permute-start | bytes 1572872 | tf_op jit(solution)/shard_map/ppermute | solution.py:426
  157.4 27.8 %collective-permute-start.33 = (bf16[512,512]{1,0:T(8,128)(2,1)S(1)}, bf16[512,512]{1,0:T(8,128)(2,1)S(1)}, u32[]{:S(2)}, u32[]{:S(2)}) collective-permute-start(bf16[512,512]{1,0:T(8,128)(2,1)S(1)} %get-tuple-element.187.refs_1_), channel_id=1, source_target_pairs={{0,1},{1,0},{2,3},{3,2},{4,5},{5,4},{6,7},{7,6},{8,9},{9,8},{10,11... | collective-permute-start | bytes 1572872 | tf_op jit(solution)/shard_map/ppermute | solution.py:396
  165.4 18.5 %collective-permute-start.26 = (f32[4,512]{1,0:T(4,128)S(1)}, f32[4,512]{1,0:T(4,128)S(1)}, u32[]{:S(2)}, u32[]{:S(2)}) collective-permute-start(f32[4,512]{1,0:T(4,128)S(1)} %get-tuple-element.174), channel_id=1, source_target_pairs={{0,8},{8,16},{16,24},{1,9},{9,17},{17,25},{2,10},{10,18},{18,26},{... | collective-permute-start | bytes 24584 | tf_op jit(solution)/shard_map/ppermute | solution.py:492
  168.5 25.8 %collective-permute-start.22 = (bf16[512,512]{1,0:T(8,128)(2,1)S(1)}, bf16[512,512]{1,0:T(8,128)(2,1)S(1)}, u32[]{:S(2)}, u32[]{:S(2)}) collective-permute-start(bf16[512,512]{1,0:T(8,128)(2,1)S(1)} %get-tuple-element.166.refs_1_), channel_id=1, source_target_pairs={{0,4},{1,5},{2,2},{3,3},{6,6},{7,7},{8,12},{9,13},{10,10},{11,11},... | collective-permute-start | bytes 1572872 | tf_op jit(solution)/shard_map/ppermute | solution.py:419
  181.4 14.3 %collective-permute-start.37 = (bf16[512,512]{1,0:T(8,128)(2,1)S(1)}, bf16[512,512]{1,0:T(8,128)(2,1)S(1)}, u32[]{:S(2)}, u32[]{:S(2)}) collective-permute-start(bf16[512,512]{1,0:T(8,128)(2,1)S(1)} %get-tuple-element.196.refs_2_), channel_id=1, source_target_pairs={{4,2},{5,3},{0,0},{1,1},{6,6},{7,7},{12,10},{13,11},{8,8},{9,9},{1... | collective-permute-start | bytes 1572872 | tf_op jit(solution)/shard_map/ppermute | solution.py:425
  182.1 13.6 %collective-permute-start.38 = (bf16[512,512]{1,0:T(8,128)(2,1)S(1)}, bf16[512,512]{1,0:T(8,128)(2,1)S(1)}, u32[]{:S(2)}, u32[]{:S(2)}) collective-permute-start(bf16[512,512]{1,0:T(8,128)(2,1)S(1)} %get-tuple-element.196.refs_2_), channel_id=1, source_target_pairs={{4,6},{5,7},{6,4},{7,5},{0,0},{1,1},{2,2},{3,3},{12,14},{13,15},{1... | collective-permute-start | bytes 1572872 | tf_op jit(solution)/shard_map/ppermute | solution.py:426
  184.9 9.4 %collective-permute-start.32 = (f32[4,512]{1,0:T(4,128)S(1)}, f32[4,512]{1,0:T(4,128)S(1)}, u32[]{:S(2)}, u32[]{:S(2)}) collective-permute-start(f32[4,512]{1,0:T(4,128)S(1)} %broadcast_select_fusion.2.refs_0_), channel_id=1, source_target_pairs={{0,8},{8,0},{16,24},{24,16},{1,9},{9,1},{17,25},{25,17},{2,10},{10... | collective-permute-start | bytes 24584 | tf_op jit(solution)/shard_map/ppermute | solution.py:396
  185.2 16.9 %collective-permute-start.36 = (bf16[512,512]{1,0:T(8,128)(2,1)S(1)}, bf16[512,512]{1,0:T(8,128)(2,1)S(1)}, u32[]{:S(2)}, u32[]{:S(2)}) collective-permute-start(bf16[512,512]{1,0:T(8,128)(2,1)S(1)} %get-tuple-element.194.refs_1_), channel_id=1, source_target_pairs={{0,1},{1,0},{2,3},{3,2},{4,5},{5,4},{6,7},{7,6},{8,9},{9,8},{10,11... | collective-permute-start | bytes 1572872 | tf_op jit(solution)/shard_map/ppermute | solution.py:396
  194.3 15.5 %collective-permute-start.41 = (bf16[512,512]{1,0:T(8,128)(2,1)S(1)}, bf16[512,512]{1,0:T(8,128)(2,1)S(1)}, u32[]{:S(2)}, u32[]{:S(2)}) collective-permute-start(bf16[512,512]{1,0:T(8,128)(2,1)S(1)} %get-tuple-element.203.refs_2_), channel_id=1, source_target_pairs={{4,2},{5,3},{0,0},{1,1},{6,6},{7,7},{12,10},{13,11},{8,8},{9,9},{1... | collective-permute-start | bytes 1572872 | tf_op jit(solution)/shard_map/ppermute | solution.py:425
  195.0 14.8 %collective-permute-start.42 = (bf16[512,512]{1,0:T(8,128)(2,1)S(1)}, bf16[512,512]{1,0:T(8,128)(2,1)S(1)}, u32[]{:S(2)}, u32[]{:S(2)}) collective-permute-start(bf16[512,512]{1,0:T(8,128)(2,1)S(1)} %get-tuple-element.203.refs_2_), channel_id=1, source_target_pairs={{4,6},{5,7},{6,4},{7,5},{0,0},{1,1},{2,2},{3,3},{12,14},{13,15},{1... | collective-permute-start | bytes 1572872 | tf_op jit(solution)/shard_map/ppermute | solution.py:426
  195.8 21.4 %collective-permute-start.40 = (bf16[512,512]{1,0:T(8,128)(2,1)S(1)}, bf16[512,512]{1,0:T(8,128)(2,1)S(1)}, u32[]{:S(2)}, u32[]{:S(2)}) collective-permute-start(bf16[512,512]{1,0:T(8,128)(2,1)S(1)} %get-tuple-element.201.refs_1_), channel_id=1, source_target_pairs={{0,1},{1,0},{2,3},{3,2},{4,5},{5,4},{6,7},{7,6},{8,9},{9,8},{10,11... | collective-permute-start | bytes 1572872 | tf_op jit(solution)/shard_map/ppermute | solution.py:396
  196.4 13.4 %collective-permute-start.43 = (bf16[256,512]{1,0:T(8,128)(2,1)S(1)}, bf16[256,512]{1,0:T(8,128)(2,1)S(1)}, u32[]{:S(2)}, u32[]{:S(2)}) collective-permute-start(bf16[256,512]{1,0:T(8,128)(2,1)S(1)} %get-tuple-element.204.refs_1_), channel_id=1, source_target_pairs={{0,4},{1,5},{2,2},{3,3},{6,6},{7,7},{8,12},{9,13},{10,10},{11,11},... | collective-permute-start | bytes 786440 | tf_op jit(solution)/shard_map/ppermute | solution.py:419
  202.2 7.7 %collective-permute-start.35 = (f32[4,512]{1,0:T(4,128)S(1)}, f32[4,512]{1,0:T(4,128)S(1)}, u32[]{:S(2)}, u32[]{:S(2)}) collective-permute-start(f32[4,512]{1,0:T(4,128)S(1)} %get-tuple-element.193.refs_0_), channel_id=1, source_target_pairs={{0,16},{8,24},{16,0},{24,8},{1,17},{9,25},{17,1},{25,9},{2,18},{10... | collective-permute-start | bytes 24584 | tf_op jit(solution)/shard_map/ppermute | solution.py:396
  209.9 18.5 %collective-permute-start.49 = (bf16[512,512]{1,0:T(8,128)(2,1)S(1)}, bf16[512,512]{1,0:T(8,128)(2,1)S(1)}, u32[]{:S(2)}, u32[]{:S(2)}) collective-permute-start(bf16[512,512]{1,0:T(8,128)(2,1)S(1)} %get-tuple-element.214.refs_1_), channel_id=1, source_target_pairs={{0,1},{1,0},{2,3},{3,2},{4,5},{5,4},{6,7},{7,6},{8,9},{9,8},{10,11... | collective-permute-start | bytes 1572872 | tf_op jit(solution)/shard_map/ppermute | solution.py:396
  211.5 14.9 %collective-permute-start.34 = (bf16[256,512]{1,0:T(8,128)(2,1)S(1)}, bf16[256,512]{1,0:T(8,128)(2,1)S(1)}, u32[]{:S(2)}, u32[]{:S(2)}) collective-permute-start(bf16[256,512]{1,0:T(8,128)(2,1)S(1)} %get-tuple-element.192.refs_1_), channel_id=1, source_target_pairs={{0,4},{1,5},{2,2},{3,3},{6,6},{7,7},{8,12},{9,13},{10,10},{11,11},... | collective-permute-start | bytes 786440 | tf_op jit(solution)/shard_map/ppermute | solution.py:419
  215.7 10.7 %collective-permute-start.46 = (bf16[256,512]{1,0:T(8,128)(2,1)S(1)}, bf16[256,512]{1,0:T(8,128)(2,1)S(1)}, u32[]{:S(2)}, u32[]{:S(2)}) collective-permute-start(bf16[256,512]{1,0:T(8,128)(2,1)S(1)} %get-tuple-element.211.refs_2_), channel_id=1, source_target_pairs={{4,2},{5,3},{0,0},{1,1},{6,6},{7,7},{12,10},{13,11},{8,8},{9,9},{1... | collective-permute-start | bytes 786440 | tf_op jit(solution)/shard_map/ppermute | solution.py:425
  216.4 10.0 %collective-permute-start.47 = (bf16[256,512]{1,0:T(8,128)(2,1)S(1)}, bf16[256,512]{1,0:T(8,128)(2,1)S(1)}, u32[]{:S(2)}, u32[]{:S(2)}) collective-permute-start(bf16[256,512]{1,0:T(8,128)(2,1)S(1)} %get-tuple-element.211.refs_2_), channel_id=1, source_target_pairs={{4,6},{5,7},{6,4},{7,5},{0,0},{1,1},{2,2},{3,3},{12,14},{13,15},{1... | collective-permute-start | bytes 786440 | tf_op jit(solution)/shard_map/ppermute | solution.py:426
  217.3 9.1 %collective-permute-start.39 = (f32[4,512]{1,0:T(4,128)S(1)}, f32[4,512]{1,0:T(4,128)S(1)}, u32[]{:S(2)}, u32[]{:S(2)}) collective-permute-start(f32[4,512]{1,0:T(4,128)S(1)} %get-tuple-element.200.refs_0_), channel_id=1, source_target_pairs={{0,1},{1,0},{2,3},{3,2},{4,5},{5,4},{6,7},{7,6},{8,9},{9,8},{10,11... | collective-permute-start | bytes 24584 | tf_op jit(solution)/shard_map/ppermute | solution.py:396
  226.5 9.4 %collective-permute-start.48 = (bf16[256,512]{1,0:T(8,128)(2,1)S(1)}, bf16[256,512]{1,0:T(8,128)(2,1)S(1)}, u32[]{:S(2)}, u32[]{:S(2)}) collective-permute-start(bf16[256,512]{1,0:T(8,128)(2,1)S(1)} %get-tuple-element.213.refs_1_), channel_id=1, source_target_pairs={{0,1},{1,0},{2,3},{3,2},{4,5},{5,4},{6,7},{7,6},{8,9},{9,8},{10,11... | collective-permute-start | bytes 786440 | tf_op jit(solution)/shard_map/ppermute | solution.py:396
  227.0 14.3 %collective-permute-start.44 = (bf16[256,512]{1,0:T(8,128)(2,1)S(1)}, bf16[256,512]{1,0:T(8,128)(2,1)S(1)}, u32[]{:S(2)}, u32[]{:S(2)}) collective-permute-start(bf16[256,512]{1,0:T(8,128)(2,1)S(1)} %get-tuple-element.210.refs_2_), channel_id=1, source_target_pairs={{4,2},{5,3},{0,0},{1,1},{6,6},{7,7},{12,10},{13,11},{8,8},{9,9},{1... | collective-permute-start | bytes 786440 | tf_op jit(solution)/shard_map/ppermute | solution.py:425
  227.7 13.6 %collective-permute-start.45 = (bf16[256,512]{1,0:T(8,128)(2,1)S(1)}, bf16[256,512]{1,0:T(8,128)(2,1)S(1)}, u32[]{:S(2)}, u32[]{:S(2)}) collective-permute-start(bf16[256,512]{1,0:T(8,128)(2,1)S(1)} %get-tuple-element.210.refs_2_), channel_id=1, source_target_pairs={{4,6},{5,7},{6,4},{7,5},{0,0},{1,1},{2,2},{3,3},{12,14},{13,15},{1... | collective-permute-start | bytes 786440 | tf_op jit(solution)/shard_map/ppermute | solution.py:426
  241.4 8.9 %collective-permute-start.51 = (bf16[256,512]{1,0:T(8,128)(2,1)S(1)}, bf16[256,512]{1,0:T(8,128)(2,1)S(1)}, u32[]{:S(2)}, u32[]{:S(2)}) collective-permute-start(bf16[256,512]{1,0:T(8,128)(2,1)S(1)} %get-tuple-element.222.refs_1_), channel_id=1, source_target_pairs={{0,1},{1,0},{2,3},{3,2},{4,5},{5,4},{6,7},{7,6},{8,9},{9,8},{10,11... | collective-permute-start | bytes 786440 | tf_op jit(solution)/shard_map/ppermute | solution.py:396
  (23 other events, 324.2 us)
where the time goes:
time: 258 us; the launch traced here: 256 us
  Pallas kernels  117 us (45%)
  starting transfers between devices  110 us (43%)
  waiting for transfers between devices  17.8 us (7%)
  local copies, waits for them, and re-layouts  9.9 us (4%)
    pallas_call x49, Pallas kernels, __call__(): pl.pallas_call(body, in_specs=list(in_specs) + [anywhere] * n_dep, out_sp...  117 us
    ppermute x9, starting transfers between devices, first_stage(): return lax.ppermute(local, 'pcol', along_z(stages[0][0]))  40.5 us
    ppermute x21, starting transfers between devices, swap(): return lax.ppermute(value, axis, [(i, i ^ bit) for i in range(size)])  27.2 us
    ppermute x9, starting transfers between devices, second_stage(): lax.ppermute(arrived, 'pcol', along_z(left))  18.2 us
    ppermute x9, starting transfers between devices, second_stage(): lax.ppermute(arrived, 'pcol', along_z(right, extra=back))  14.6 us
    ppermute x9, waiting for transfers between devices, first_stage(): return lax.ppermute(local, 'pcol', along_z(stages[0][0]))  10.8 us
    unnamed x37, local copies, waits for them, and re-layouts  8.72 us
    ppermute x21, waiting for transfers between devices, swap(): return lax.ppermute(value, axis, [(i, i ^ bit) for i in range(size)])  7 us
  transfers between devices with their start and end apart: 53, of which 6 were waited for; matrix products, arithmetic and copies ran while one was open for 1% of the time, Pallas kernels for 42%

commit v1 on v0

--- a/solution.py
+++ b/solution.py
@@ -119,35 +119,33 @@
 
 
 def extract_kernel(groups, stride, a_ref, sol_ref, col_ref, part_ref, *rest):
-    wide, totals = rest[-2:]
+    wide = rest[-1]
     rows = col_ref.shape[0]
-    if len(rest) > 2:
+    if len(rest) > 1:
         rest[0][...] = a_ref[...]
+    wide[...] = a_ref[...].astype(F32)
+    for g in range(0, groups, stride):
+        piece = wide[pl.ds(g, rows, stride=groups), :]
+        col_ref[:, pl.ds(g // stride * LANES, LANES)] = piece.astype(BF16)
     if groups % 16 == 0:
         sol = sol_ref[...].astype(F32)
-
-        def one(block, carry):
-            here = pl.ds(pl.multiple_of(block * 8 * groups, 8 * groups), 8 * groups)
-            raw = a_ref[here, :].astype(F32)
-            wide[here, :] = raw
-            raw = raw.reshape(8, groups, LANES) * sol[None]
-            sums = [sum(raw[r : r + 1, 8 * h : 8 * h + 8] for h in range(groups // 8)) for r in range(8)]
-            totals[pl.ds(pl.multiple_of(block * 8, 8), 8), :] = sum8(sums)[0]
-            return carry
-
-        lax.fori_loop(0, rows // 8, one, 0, unroll=4)
+        totals = []
+        for block in range(rows // 8):
+            sums = []
+            for r in range(8):
+                base = (block * 8 + r) * groups
+                sums.append(
+                    sum(wide[pl.ds(base + 8 * h, 8), :] * sol[8 * h : 8 * h + 8] for h in range(groups // 8))[None]
+                )
+            totals.append(sum8(sums)[0])
+        total = jnp.concatenate(totals, axis=0)
     else:
-        wide[...] = a_ref[...].astype(F32)
         total = jnp.zeros((rows, LANES), F32)
         for g in range(groups):
             total = total + wide[pl.ds(g, rows, stride=groups), :] * sol_ref[g : g + 1, :].astype(F32)
-        totals[...] = total
-    for g in range(0, groups, stride):
-        piece = wide[pl.ds(g, rows, stride=groups), :]
-        col_ref[:, pl.ds(g // stride * LANES, LANES)] = piece.astype(BF16)
     ones = jnp.ones((8, LANES), F32)
     sums = lax.dot_general(
-        ones, totals[...], (((1,), (1,)), ((), ())), precision=lax.Precision.HIGHEST, preferred_element_type=F32
+        ones, total, (((1,), (1,)), ((), ())), precision=lax.Precision.HIGHEST, preferred_element_type=F32
     )
     part_ref[...] = sums[0:1, :]
 
@@ -179,7 +177,7 @@
         "extract",
         (4 * rows * groups * LANES, rows * groups * LANES * 2),
         grid=(rows // sub,),
-        scratch=[pltpu.VMEM((size, LANES), F32), pltpu.VMEM((sub, LANES), F32)],
+        scratch=[pltpu.VMEM((size, LANES), F32)],
     )
 
 
@@ -268,76 +266,82 @@
     )
 
 
-def update_kernel(groups, a_ref, mine_ref, other_ref, v_ref, *rest):
-    rows = mine_ref.shape[0]
-    both = jnp.concatenate([mine_ref[...], other_ref[...]], axis=1)
+def update_kernel(groups, chunks, steps, a_ref, v_ref, *rest):
+    out_ref, both, *wide = rest[-3 if groups % 16 else -2 :]
+    rows, width = both.shape[0], both.shape[1] // 2
+    i = pl.program_id(0)
+    for c in range(chunks):
+
+        @pl.when(i // steps == c)
+        def _(c=c):
+            both[:, :width] = rest[2 * c][...]
+            both[:, width:] = rest[2 * c + 1][...]
+
     if groups % 16 == 0:
-        out_ref, value = rest[-2:]
         part = min(rows, 128)
         for p in range(rows // part):
-            value[p] = matmul(both[p * part : (p + 1) * part], v_ref[...])
-
-            def one(block, carry, p=p):
-                at = pl.ds(pl.multiple_of(block * 8, 8), 8)
+            value = matmul(both[p * part : (p + 1) * part, :], v_ref[...])
+            for block in range(part // 8):
+                cut = value[block * 8 : block * 8 + 8, :]
                 halves = [
-                    transpose8([value[p, at, (8 * h + g) * LANES : (8 * h + g + 1) * LANES][None] for g in range(8)])
+                    transpose8([cut[:, (8 * h + g) * LANES : (8 * h + g + 1) * LANES][None] for g in range(8)])
                     for h in range(groups // 8)
                 ]
                 for r in range(8):
-                    here = pl.ds(pl.multiple_of((p * part + block * 8 + r) * groups, groups), groups)
+                    here = pl.ds((p * part + block * 8 + r) * groups, groups)
                     change = jnp.concatenate([half[r][0] for half in halves], axis=0)
                     out_ref[here, :] = (a_ref[here, :].astype(F32) - change).astype(BF16)
-                return carry
-
-            lax.fori_loop(0, part // 8, one, 0, unroll=part // 8)
         return
-    out_ref, wide = rest[-2:]
-    value = matmul(both, v_ref[...])
+    value = matmul(both[...], v_ref[...])
     for g in range(groups):
-        wide[pl.ds(g, rows, stride=groups), :] = value[:, g * LANES : (g + 1) * LANES]
-    out_ref[...] = (a_ref[...].astype(F32) - wide[...]).astype(BF16)
+        wide[0][pl.ds(g, rows, stride=groups), :] = value[:, g * LANES : (g + 1) * LANES]
+    out_ref[...] = (a_ref[...].astype(F32) - wide[0][...]).astype(BF16)
 
 
 def update(chain, flat, mine, other, v, out, first, groups):
-    rows, width = mine.shape
+    rows, width = mine[0].shape
+    chunks = len(mine)
     sub = min(rows, 256)
+    steps = rows // sub
     size = sub * groups
     base = first // sub
     cols = groups * LANES
-    in_specs = [
-        pl.BlockSpec((size, LANES), lambda i: (base + i, 0)),
-        pl.BlockSpec((sub, width), lambda i: (i, 0)),
-        pl.BlockSpec((sub, width), lambda i: (i, 0)),
-        pl.BlockSpec(memory_space=pltpu.VMEM),
-    ]
-    args = [flat, mine, other, v]
+    in_specs = [pl.BlockSpec((size, LANES), lambda i: (base + i, 0)), pl.BlockSpec(memory_space=pltpu.VMEM)]
+    args = [flat, v]
+    for c in range(chunks):
+        args += [mine[c], other[c]]
+        in_specs += [pl.BlockSpec((sub, width), lambda i, c=c: (jnp.clip(i - c * steps, 0, steps - 1), 0))] * 2
     aliases = {}
     if out is not None:
+        aliases = {len(args): 0}
         in_specs.append(pl.BlockSpec(memory_space=pl.ANY))
         args.append(out)
-        aliases = {4: 0}
+    scratch = [pltpu.VMEM((sub, 2 * width), BF16)]
+    if groups % 16:
+        scratch.append(pltpu.VMEM((size, LANES), F32))
     return chain(
-        lambda *refs: update_kernel(groups, *refs),
+        lambda *refs: update_kernel(groups, chunks, steps, *refs),
         args,
         in_specs,
         [jax.ShapeDtypeStruct(flat.shape, BF16)],
         [pl.BlockSpec((size, LANES), lambda i: (base + i, 0))],
         "update",
-        (4 * rows * width * cols, 4 * rows * cols + 4 * rows * width),
-        grid=(rows // sub,),
-        scratch=[pltpu.VMEM((size, LANES), F32) if groups % 16 else pltpu.VMEM((sub // 128, 128, cols), F32)],
+        (4 * chunks * rows * width * cols, chunks * (4 * rows * cols + 4 * rows * width)),
+        grid=(chunks * steps,),
+        scratch=scratch,
         aliases=aliases,
     )
 
 
 def solve_kernel(place_ref, state_ref, res_ref, inv_ref, *rest):
     cols, out_ref = rest[:-1], rest[-1]
-    place = place_ref[0]
+    place, lane = place_ref[0], place_ref[1]
     width = inv_ref.shape[0]
     nt = (((1,), (1,)), ((), ()))
     pending = jnp.zeros((8, width), F32)
     for j, col in enumerate(cols):
-        known = jnp.where(j < place, state_ref[j : j + 1, :], 0.0)
+        at = (j + lane) % 2 if j < 2 else j
+        known = jnp.where(at < place, state_ref[pl.ds(at, 1), :], 0.0)
         pending = pending + lax.dot_general(
             jnp.broadcast_to(known, (8, width)).astype(BF16), col[...], nt, preferred_element_type=F32
         )
@@ -395,12 +399,8 @@
     def swap(value, axis, size, bit=1):
         return lax.ppermute(value, axis, [(i, i ^ bit) for i in range(size)])
 
-    def along_z(pairs, keep=True, extra=()):
-        pairs = [*pairs, *extra]
-        if keep:
-            busy = {i for pair in pairs for i in pair}
-            pairs = pairs + [(i, i) for i in range(nz) if i not in busy]
-        return [(a * ny + k, b * ny + k) for a, b in pairs for k in range(ny if keep else 2)]
+    def along_z(pairs):
+        return [(a * ny + k, b * ny + k) for a, b in pairs for k in range(2)]
 
     stages = [[[(0, nz // 2)]]]
     held, step = [nz // 2], nz // 4
@@ -419,12 +419,7 @@
         return lax.ppermute(local, "pcol", along_z(stages[0][0]))
 
     def second_stage(arrived):
-        left, right = stages[1]
-        back = [(b, a) for a, b in right]
-        return [
-            lax.ppermute(arrived, "pcol", along_z(left)),
-            lax.ppermute(arrived, "pcol", along_z(right, extra=back)),
-        ]
+        return [lax.ppermute(arrived, "pcol", along_z(moves)) for moves in stages[1]]
 
     source = jnp.zeros((), jnp.int32)
     for i, moves in enumerate(stages[0] + stages[1]):
@@ -448,7 +443,7 @@
     assert diagonal_block_inverses.shape[0] == 1
     home = count - 2
     inv = diagonal_block_inverses.reshape(width, width)
-    place = prow.astype(jnp.int32).reshape(1)
+    place = jnp.stack([prow, lane]).astype(jnp.int32)
     where = jnp.stack([core, lane, prow // 2]).astype(jnp.int32)
     flag = jnp.where(core != lane, 0, 1).astype(jnp.int32).reshape(1)
     bits = [1 << b for b in range(n_pcol.bit_length() - 1)]
@@ -482,8 +477,7 @@
     def solve(k):
         def run():
             if k == 0:
-                a, b = mine[0], other[0]
-                needed = [jnp.where(lane == 0, a, b), jnp.where(lane == 0, b, a)]
+                needed = [mine[0], other[0]]
                 for j in range(2, home):
                     needed.append(lax.ppermute(column[0], "pcol", [(j, home)]))
                 box["needed"] = needed + [column[0]]
@@ -513,9 +507,10 @@
     def make_factors():
         box["v"] = factors(chain, where, box["bands"], box["blks"], upper_inv, lower_inv, groups)
 
-    def updates(c):
+    def updates(*which):
         def run():
-            box["out"] = update(chain, flat, mine[c], other[c], box["v"], box["out"], cuts[c][0], groups)
+            args = [mine[c] for c in which], [other[c] for c in which]
+            box["out"] = update(chain, flat, *args, box["v"], box["out"], cuts[which[0]][0], groups)
 
         return run
 
@@ -529,14 +524,14 @@
     line += [share("pcol", n_pcol, b) for b in bits]
     if slots == 8 and len(line) == 9:
         plan = {
-            0: total[:2],
-            1: total[2:],
-            2: [blocks_out, line[0]],
-            3: [blocks_swap, line[1], make_factors],
-            4: [updates(0), line[2], updates(1), updates(2)],
-            5: [line[3], updates(3), line[4]],
-            6: [updates(4), line[5]],
-            7: [updates(5), line[6]],
+            0: total[:1],
+            1: total[1:2],
+            2: [blocks_out, total[2]],
+            3: [blocks_swap, line[0]],
+            4: [make_factors, line[1], updates(0, 1, 2)],
+            5: [line[2], updates(3), line[3]],
+            6: [line[4], updates(4, 5)],
+            7: [line[5], line[6]],
             8: [updates(6), line[7]],
         }
         tail = []

time: 258 us -> 264 us (1.023)
  waiting for transfers between devices: 17.8 us -> 30.2 us
  Pallas kernels: 117 us -> 106 us
  local copies, waits for them, and re-layouts: 9.9 us -> 13.6 us
    ppermute x9, starting transfers between devices: 40.5 us -> 57.9 us  [first_stage(): return lax.ppermute(local, 'pcol', along_z(stages[0][0]))]
    ppermute x18, starting transfers between devices: 32.7 us -> 17.2 us  [second_stage(): lax.ppermute(arrived, 'pcol', along_z(moves))]
    pallas_call x49 -> x46, Pallas kernels: 117 us -> 106 us  [__call__(): pl.pallas_call(body, in_specs=list(in_specs) + [anywhere] * n_dep, out_sp...]
    ppermute x21, waiting for transfers between devices: 7 us -> 15.7 us  [swap(): return lax.ppermute(value, axis, [(i, i ^ bit) for i in range(size)])]
    unnamed x37 -> x45, local copies, waits for them, and re-layouts: 8.72 us -> 12.4 us
    ppermute x2, waiting for transfers between devices: 0.01 us -> 3.11 us  [spread(): values.append(lax.ppermute(values[-1], axis, pairs))]
  transfers between devices with their start and end apart: 53 -> 53, of which waited for: 6 -> 10; matrix products, arithmetic and copies ran while one was open for 1% -> 1% of each run, Pallas kernels for 42% -> 37%
where the time goes in v1:
time: 264 us; the launch traced here: 263 us
  starting transfers between devices  111 us (42%)
  Pallas kernels  106 us (40%)
  waiting for transfers between devices  30.2 us (11%)
  local copies, waits for them, and re-layouts  13.6 us (5%)
    pallas_call x46, Pallas kernels, __call__(): pl.pallas_call(body, in_specs=list(in_specs) + [anywhere] * n_dep, out_sp...  106 us
    ppermute x9, starting transfers between devices, first_stage(): return lax.ppermute(local, 'pcol', along_z(stages[0][0]))  57.9 us
    ppermute x21, starting transfers between devices, swap(): return lax.ppermute(value, axis, [(i, i ^ bit) for i in range(size)])  25.2 us
    ppermute x18, starting transfers between devices, second_stage(): lax.ppermute(arrived, 'pcol', along_z(moves))  17.2 us
    ppermute x21, waiting for transfers between devices, swap(): return lax.ppermute(value, axis, [(i, i ^ bit) for i in range(size)])  15.7 us
    unnamed x45, local copies, waits for them, and re-layouts  12.4 us
    ppermute x9, waiting for transfers between devices, first_stage(): return lax.ppermute(local, 'pcol', along_z(stages[0][0]))  11.4 us
    ppermute x3, starting transfers between devices, run(): lax.ppermute(box['state'], 'prow', [(i, i + 1) for i in range(n_prow - 1)])  7.23 us
  transfers between devices with their start and end apart: 53, of which 10 were waited for; matrix products, arithmetic and copies ran while one was open for 1% of the time, Pallas kernels for 37%

profile of v1, /device:TPU:0, one launch (start us, length us, event | category | flops | bytes accessed | tf_op | source)
XLA Modules:
  0.0 262.5 jit_solution(17842334748096708575)
XLA Ops:
  1.3 4.4 %extract.8 = (bf16[512,512]{1,0:T(8,128)(2,1)S(1)}, f32[1,512]{1,0:T(1,128)S(1)}, bf16[8192,128]{1,0:T(8,128)(2,1)}, f32[8,128]{1,0:T(8,128)S(1)}) custom-call(bf16[65536,128]{1,0:T(8,128)(2,1)} %bitcast.37, bf16[16,128]{1,0:T(8,128)(2,1)S(1)} %bitcast.29), custom_call_target="tpu_custom_call" | custom-call | flops 4194304 | bytes 2097152 | tf_op jit(solution)/shard_map/extract/pallas_call | solution.py:32
  5.7 2.9 %collective-permute-start.1 = (bf16[8192,128]{1,0:T(8,128)(2,1)}, bf16[8192,128]{1,0:T(8,128)(2,1)}, u32[]{:S(2)}, u32[]{:S(2)}) collective-permute-start(bf16[8192,128]{1,0:T(8,128)(2,1)} %get-tuple-element.110.refs_1_), channel_id=1, source_target_pairs={{0,16},{8,24},{16,0},{24,8},{1,17},{9,25},{17,1},{25,9},{2,18},{10... | collective-permute-start | bytes 6291464 | tf_op jit(solution)/shard_map/ppermute | solution.py:396
  8.6 4.5 %collective-permute-start.3 = (bf16[512,512]{1,0:T(8,128)(2,1)S(1)}, bf16[512,512]{1,0:T(8,128)(2,1)S(1)}, u32[]{:S(2)}, u32[]{:S(2)}) collective-permute-start(bf16[512,512]{1,0:T(8,128)(2,1)S(1)} %get-tuple-element.111.refs_1_.refs_6_), channel_id=1, source_target_pairs={{0,4},{1,5},{8,12},{9,13},{16,20},{17,21},{24,28},{25,29}} | collective-permute-start | bytes 1572872 | tf_op jit(solution)/shard_map/ppermute | solution.py:419
  13.2 3.4 %extract.9 = (bf16[512,512]{1,0:T(8,128)(2,1)S(1)}, f32[1,512]{1,0:T(1,128)S(1)}, f32[8,128]{1,0:T(8,128)S(1)}) custom-call(bf16[65536,128]{1,0:T(8,128)(2,1)} %bitcast.38, bf16[16,128]{1,0:T(8,128)(2,1)S(1)} %bitcast.30, f32[8,128]{1,0:T(8,128)S(1)} %get-tuple-element.112.refs_2_), custom_call_target="tpu_custom_call" | custom-call | flops 4194304 | bytes 2097152 | tf_op jit(solution)/shard_map/extract/pallas_call | solution.py:32
  16.6 3.5 %extract.10 = (bf16[512,512]{1,0:T(8,128)(2,1)S(1)}, f32[1,512]{1,0:T(1,128)S(1)}, f32[8,128]{1,0:T(8,128)S(1)}) custom-call(bf16[65536,128]{1,0:T(8,128)(2,1)} %bitcast.39, bf16[16,128]{1,0:T(8,128)(2,1)S(1)} %bitcast.31, f32[8,128]{1,0:T(8,128)S(1)} %get-tuple-element.114.refs_2_), custom_call_target="tpu_custom_call" | custom-call | flops 4194304 | bytes 2097152 | tf_op jit(solution)/shard_map/extract/pallas_call | solution.py:32
  20.1 3.9 %extract.11 = (bf16[512,512]{1,0:T(8,128)(2,1)}, f32[1,512]{1,0:T(1,128)S(1)}, f32[8,128]{1,0:T(8,128)S(1)}) custom-call(bf16[65536,128]{1,0:T(8,128)(2,1)} %bitcast.40, bf16[16,128]{1,0:T(8,128)(2,1)S(1)} %bitcast.32, f32[8,128]{1,0:T(8,128)S(1)} %get-tuple-element.115.refs_2_), custom_call_target="tpu_custom_call" | custom-call | flops 4194304 | bytes 2097152 | tf_op jit(solution)/shard_map/extract/pallas_call | solution.py:32
  24.0 2.1 collective-permute-start.6
  26.2 3.4 %extract.12 = (bf16[512,512]{1,0:T(8,128)(2,1)S(1)}, f32[1,512]{1,0:T(1,128)S(1)}, f32[8,128]{1,0:T(8,128)S(1)}) custom-call(bf16[65536,128]{1,0:T(8,128)(2,1)} %bitcast.41, bf16[16,128]{1,0:T(8,128)(2,1)S(1)} %bitcast.33, f32[8,128]{1,0:T(8,128)S(1)} %get-tuple-element.116.refs_2_), custom_call_target="tpu_custom_call" | custom-call | flops 4194304 | bytes 2097152 | tf_op jit(solution)/shard_map/extract/pallas_call | solution.py:32
  30.4 3.4 %extract.13 = (bf16[512,512]{1,0:T(8,128)(2,1)S(1)}, f32[1,512]{1,0:T(1,128)S(1)}, f32[8,128]{1,0:T(8,128)S(1)}) custom-call(bf16[65536,128]{1,0:T(8,128)(2,1)} %bitcast.42, bf16[16,128]{1,0:T(8,128)(2,1)S(1)} %bitcast.34, f32[8,128]{1,0:T(8,128)S(1)} %get-tuple-element.117.refs_2_), custom_call_target="tpu_custom_call" | custom-call | flops 4194304 | bytes 2097152 | tf_op jit(solution)/shard_map/extract/pallas_call | solution.py:32
  33.9 3.5 %extract.14 = (bf16[512,512]{1,0:T(8,128)(2,1)S(1)}, f32[1,512]{1,0:T(1,128)S(1)}, f32[8,128]{1,0:T(8,128)S(1)}) custom-call(bf16[65536,128]{1,0:T(8,128)(2,1)} %bitcast.43, bf16[16,128]{1,0:T(8,128)(2,1)S(1)} %bitcast.35, f32[8,128]{1,0:T(8,128)S(1)} %get-tuple-element.118.refs_2_), custom_call_target="tpu_custom_call" | custom-call | flops 4194304 | bytes 2097152 | tf_op jit(solution)/shard_map/extract/pallas_call | solution.py:32
  37.3 3.5 %extract.15 = (bf16[512,512]{1,0:T(8,128)(2,1)S(1)}, f32[1,512]{1,0:T(1,128)S(1)}, f32[8,128]{1,0:T(8,128)S(1)}) custom-call(bf16[65536,128]{1,0:T(8,128)(2,1)} %bitcast.44, bf16[16,128]{1,0:T(8,128)(2,1)S(1)} %bitcast.36, f32[8,128]{1,0:T(8,128)S(1)} %get-tuple-element.119.refs_2_), custom_call_target="tpu_custom_call" | custom-call | flops 4194304 | bytes 2097152 | tf_op jit(solution)/shard_map/extract/pallas_call | solution.py:32
  44.8 1.6 collective-permute-start.7
  46.4 2.2 collective-permute-done.7.refs_1_
  48.7 3.7 %collective-permute-start.11 = (bf16[512,512]{1,0:T(8,128)(2,1)}, bf16[512,512]{1,0:T(8,128)(2,1)}, u32[]{:S(2)}, u32[]{:S(2)}) collective-permute-start(bf16[512,512]{1,0:T(8,128)(2,1)} %copy-done.11), channel_id=1, source_target_pairs={{0,4},{1,5},{8,12},{9,13},{16,20},{17,21},{24,28},{25,29}} | collective-permute-start | bytes 1572872 | tf_op jit(solution)/shard_map/ppermute | solution.py:419
  56.1 5.8 %collective-permute-done.12.refs_1_ = f32[8,512]{1,0:T(8,128)S(1)} collective-permute-done((f32[8,512]{1,0:T(8,128)S(1)}, f32[8,512]{1,0:T(8,128)S(1)}, u32[]{:S(2)}, u32[]{:S(2)}) %collective-permute-start.12) | collective-permute-done | bytes 16416 | tf_op jit(solution)/shard_map/ppermute | solution.py:400
  61.9 1.5 collective-permute-start.8
  64.0 5.5 %collective-permute-start.17 = (f32[8,512]{1,0:T(8,128)S(1)}, f32[8,512]{1,0:T(8,128)S(1)}, u32[]{:S(2)}, u32[]{:S(2)}) collective-permute-start(f32[8,512]{1,0:T(8,128)S(1)} %get-tuple-element.147.refs_0_), channel_id=1, source_target_pairs={{0,4},{1,5},{2,6},{3,7},{4,0},{5,1},{6,2},{7,3},{8,12},{9,13},{10,... | collective-permute-start | bytes 49160 | tf_op jit(solution)/shard_map/ppermute | solution.py:400
  69.5 2.8 %collective-permute-start.16 = (bf16[512,512]{1,0:T(8,128)(2,1)}, bf16[512,512]{1,0:T(8,128)(2,1)}, u32[]{:S(2)}, u32[]{:S(2)}) collective-permute-start(bf16[512,512]{1,0:T(8,128)(2,1)} %copy-done.9), channel_id=1, source_target_pairs={{0,4},{1,5},{8,12},{9,13},{16,20},{17,21},{24,28},{25,29}} | collective-permute-start | bytes 1572872 | tf_op jit(solution)/shard_map/ppermute | solution.py:419
  79.0 4.2 %collective-permute-done.16.refs_0_ = bf16[512,512]{1,0:T(8,128)(2,1)} collective-permute-done((bf16[512,512]{1,0:T(8,128)(2,1)}, bf16[512,512]{1,0:T(8,128)(2,1)}, u32[]{:S(2)}, u32[]{:S(2)}) %collective-permute-start.16) | collective-permute-done | bytes 524320 | tf_op jit(solution)/shard_map/ppermute | solution.py:419
  83.1 6.7 %collective-permute-start.20 = (bf16[512,512]{1,0:T(8,128)(2,1)}, bf16[512,512]{1,0:T(8,128)(2,1)}, u32[]{:S(2)}, u32[]{:S(2)}) collective-permute-start(bf16[512,512]{1,0:T(8,128)(2,1)} %copy-done.5), channel_id=1, source_target_pairs={{0,4},{1,5},{8,12},{9,13},{16,20},{17,21},{24,28},{25,29}} | collective-permute-start | bytes 1572872 | tf_op jit(solution)/shard_map/ppermute | solution.py:419
  92.0 7.2 %collective-permute-done.20.refs_0_ = bf16[512,512]{1,0:T(8,128)(2,1)} collective-permute-done((bf16[512,512]{1,0:T(8,128)(2,1)}, bf16[512,512]{1,0:T(8,128)(2,1)}, u32[]{:S(2)}, u32[]{:S(2)}) %collective-permute-start.20) | collective-permute-done | bytes 524320 | tf_op jit(solution)/shard_map/ppermute | solution.py:419
  100.7 3.1 %collective-permute-done.14.refs_7_ = bf16[512,512]{1,0:T(8,128)(2,1)} collective-permute-done((bf16[512,512]{1,0:T(8,128)(2,1)}, bf16[512,512]{1,0:T(8,128)(2,1)}, u32[]{:S(2)}, u32[]{:S(2)}) %collective-permute-start.14) | collective-permute-done | bytes 524320 | tf_op jit(solution)/shard_map/ppermute | solution.py:396
  106.2 1.5 solve.4
  111.9 2.1 collective-permute-start.24
  114.0 1.6 collective-permute-start.30
  116.9 15.3 %factors.1 = (bf16[1024,2048]{1,0:T(8,128)(2,1)}, f32[8,128]{1,0:T(8,128)S(1)}) custom-call(s32[3]{0:T(128)S(1)} %pad_add_fusion.refs_0_, bf16[8192,128]{1,0:T(8,128)(2,1)} %get-tuple-element.110.refs_1_, bf16[8192,128]{1,0:T(8,128)(2,1)} %collective-permute-done.refs_2_, bf16[8192,128]{1,0:T(8,128)(2,1)} %collective-permute-done.1.refs_3_, ...), custom_call_target="tpu_custom_call" | custom-call | flops 6442450944 | bytes 12582912 | tf_op jit(solution)/shard_map/factors/pallas_call | solution.py:32
  132.2 10.5 %collective-permute-start.28 = (bf16[512,512]{1,0:T(8,128)(2,1)S(1)}, bf16[512,512]{1,0:T(8,128)(2,1)S(1)}, u32[]{:S(2)}, u32[]{:S(2)}) collective-permute-start(bf16[512,512]{1,0:T(8,128)(2,1)S(1)} %copy-done.2), channel_id=1, source_target_pairs={{0,4},{1,5},{8,12},{9,13},{16,20},{17,21},{24,28},{25,29}} | collective-permute-start | bytes 1572872 | tf_op jit(solution)/shard_map/ppermute | solution.py:419
  142.7 1.5 solve.5
  145.7 15.0 %update.6 = (bf16[65536,128]{1,0:T(8,128)(2,1)}, f32[8,128]{1,0:T(8,128)S(1)}) custom-call(bf16[65536,128]{1,0:T(8,128)(2,1)} %bitcast.45, bf16[1024,2048]{1,0:T(8,128)(2,1)} %get-tuple-element.160.refs_1_, bf16[512,512]{1,0:T(8,128)(2,1)S(1)} %get-tuple-element.135.refs_1_.refs_4_.refs_2_, ...), custom_call_target="tpu_custom_call" | custom-call | flops 6442450944 | bytes 15728640 | tf_op jit(solution)/shard_map/update/pallas_call | solution.py:32
  162.1 2.6 collective-permute-start.25
  165.6 1.8 collective-permute-start.41
  167.4 1.5 solve.6
  168.9 2.5 collective-permute-start.31
  171.4 7.3 %update.7 = (bf16[65536,128]{1,0:T(8,128)(2,1)}, f32[8,128]{1,0:T(8,128)S(1)}) custom-call(bf16[65536,128]{1,0:T(8,128)(2,1)} %bitcast.46, bf16[1024,2048]{1,0:T(8,128)(2,1)} %get-tuple-element.160.refs_1_, bf16[512,512]{1,0:T(8,128)(2,1)S(1)} %get-tuple-element.175.refs_2_, ...), custom_call_target="tpu_custom_call", output_to_operand_aliasing={{0}: (4, {})} | custom-call | flops 2147483648 | bytes 5242880 | tf_op jit(solution)/shard_map/update/pallas_call | solution.py:32
  178.7 1.5 solve.7
  183.0 2.2 collective-permute-start.34
  186.0 18.2 %collective-permute-start.40 = (bf16[256,512]{1,0:T(8,128)(2,1)S(1)}, bf16[256,512]{1,0:T(8,128)(2,1)S(1)}, u32[]{:S(2)}, u32[]{:S(2)}) collective-permute-start(bf16[256,512]{1,0:T(8,128)(2,1)S(1)} %get-tuple-element.187.refs_1_), channel_id=1, source_target_pairs={{0,4},{1,5},{8,12},{9,13},{16,20},{17,21},{24,28},{25,29}} | collective-permute-start | bytes 786440 | tf_op jit(solution)/shard_map/ppermute | solution.py:419
  204.2 11.5 %update.8 = (bf16[65536,128]{1,0:T(8,128)(2,1)}, f32[8,128]{1,0:T(8,128)S(1)}) custom-call(bf16[65536,128]{1,0:T(8,128)(2,1)} %bitcast.47, bf16[1024,2048]{1,0:T(8,128)(2,1)} %get-tuple-element.160.refs_1_, bf16[512,512]{1,0:T(8,128)(2,1)} %get-tuple-element.188.refs_2_, ...), custom_call_target="tpu_custom_call", output_to_operand_aliasing={{0}: (6, {})} | custom-call | flops 4294967296 | bytes 10485760 | tf_op jit(solution)/shard_map/update/pallas_call | solution.py:32
  215.8 1.8 collective-permute-start.49
  217.6 8.2 %collective-permute-start.33 = (bf16[256,512]{1,0:T(8,128)(2,1)S(1)}, bf16[256,512]{1,0:T(8,128)(2,1)S(1)}, u32[]{:S(2)}, u32[]{:S(2)}) collective-permute-start(bf16[256,512]{1,0:T(8,128)(2,1)S(1)} %get-tuple-element.180.refs_1_), channel_id=1, source_target_pairs={{0,4},{1,5},{8,12},{9,13},{16,20},{17,21},{24,28},{25,29}} | collective-permute-start | bytes 786440 | tf_op jit(solution)/shard_map/ppermute | solution.py:419
  227.2 3.6 %collective-permute-done.37.refs_1_ = f32[4,512]{1,0:T(4,128)S(1)} collective-permute-done((f32[4,512]{1,0:T(4,128)S(1)}, f32[4,512]{1,0:T(4,128)S(1)}, u32[]{:S(2)}, u32[]{:S(2)}) %collective-permute-start.37) | collective-permute-done | bytes 8224 | tf_op jit(solution)/shard_map/ppermute | solution.py:400
  230.9 1.7 collective-permute-start.43
  232.6 2.0 collective-permute-done.43.refs_1_
  234.7 1.8 collective-permute-start.48
  237.9 7.3 %update.9 = (bf16[65536,128]{1,0:T(8,128)(2,1)}, f32[8,128]{1,0:T(8,128)S(1)}) custom-call(bf16[65536,128]{1,0:T(8,128)(2,1)} %bitcast.48, bf16[1024,2048]{1,0:T(8,128)(2,1)} %get-tuple-element.160.refs_1_, bf16[512,512]{1,0:T(8,128)(2,1)S(1)} %get-tuple-element.202.refs_2_, ...), custom_call_target="tpu_custom_call", output_to_operand_aliasing={{0}: (4, {})} | custom-call | flops 2147483648 | bytes 5242880 | tf_op jit(solution)/shard_map/update/pallas_call | solution.py:32
  245.3 5.4 %update.10 = (bf16[65536,128]{1,0:T(8,128)(2,1)}, f32[8,128]{1,0:T(8,128)S(1)}) custom-call(bf16[65536,128]{1,0:T(8,128)(2,1)} %bitcast.49, bf16[1024,2048]{1,0:T(8,128)(2,1)} %get-tuple-element.160.refs_1_, bf16[256,512]{1,0:T(8,128)(2,1)S(1)} %get-tuple-element.201.refs_2_, ...), custom_call_target="tpu_custom_call", output_to_operand_aliasing={{0}: (4, {})} | custom-call | flops 1073741824 | bytes 2621440 | tf_op jit(solution)/shard_map/update/pallas_call | solution.py:32
  251.1 3.7 %collective-permute-start.52 = (f32[4,512]{1,0:T(4,128)S(1)}, f32[4,512]{1,0:T(4,128)S(1)}, u32[]{:S(2)}, u32[]{:S(2)}) collective-permute-start(f32[4,512]{1,0:T(4,128)S(1)} %get-tuple-element.212.refs_0_), channel_id=1, source_target_pairs={{0,4},{1,5},{2,6},{3,7},{4,0},{5,1},{6,2},{7,3},{8,12},{9,13},{10,... | collective-permute-start | bytes 24584 | tf_op jit(solution)/shard_map/ppermute | solution.py:400
  257.1 5.4 %update.11 = (bf16[65536,128]{1,0:T(8,128)(2,1)}, f32[8,128]{1,0:T(8,128)}) custom-call(bf16[65536,128]{1,0:T(8,128)(2,1)} %bitcast.50, bf16[1024,2048]{1,0:T(8,128)(2,1)} %get-tuple-element.160.refs_1_, bf16[256,512]{1,0:T(8,128)(2,1)S(1)} %get-tuple-element.210.refs_2_, ...), custom_call_target="tpu_custom_call", output_to_operand_aliasing={{0}: (4, {})} | custom-call | flops 1073741824 | bytes 2621440 | tf_op jit(solution)/shard_map/update/pallas_call | solution.py:32
  (157 shorter events, 40.7 us)
Async XLA Ops:
  5.7 57.8 %collective-permute-start.1 = (bf16[8192,128]{1,0:T(8,128)(2,1)}, bf16[8192,128]{1,0:T(8,128)(2,1)}, u32[]{:S(2)}, u32[]{:S(2)}) collective-permute-start(bf16[8192,128]{1,0:T(8,128)(2,1)} %get-tuple-element.110.refs_1_), channel_id=1, source_target_pairs={{0,16},{8,24},{16,0},{24,8},{1,17},{9,25},{17,1},{25,9},{2,18},{10... | collective-permute-start | bytes 6291464 | tf_op jit(solution)/shard_map/ppermute | solution.py:396
  8.6 32.2 %collective-permute-start.3 = (bf16[512,512]{1,0:T(8,128)(2,1)S(1)}, bf16[512,512]{1,0:T(8,128)(2,1)S(1)}, u32[]{:S(2)}, u32[]{:S(2)}) collective-permute-start(bf16[512,512]{1,0:T(8,128)(2,1)S(1)} %get-tuple-element.111.refs_1_.refs_6_), channel_id=1, source_target_pairs={{0,4},{1,5},{8,12},{9,13},{16,20},{17,21},{24,28},{25,29}} | collective-permute-start | bytes 1572872 | tf_op jit(solution)/shard_map/ppermute | solution.py:419
  24.0 28.3 %collective-permute-start.6 = (bf16[512,512]{1,0:T(8,128)(2,1)}, bf16[512,512]{1,0:T(8,128)(2,1)}, u32[]{:S(2)}, u32[]{:S(2)}) collective-permute-start(bf16[512,512]{1,0:T(8,128)(2,1)} %get-tuple-element.122.refs_1_), channel_id=1, source_target_pairs={{0,4},{1,5},{8,12},{9,13},{16,20},{17,21},{24,28},{25,29}} | collective-permute-start | bytes 1572872 | tf_op jit(solution)/shard_map/ppermute | solution.py:419
  41.8 12.7 %collective-permute-start.4 = (bf16[512,512]{1,0:T(8,128)(2,1)S(1)}, bf16[512,512]{1,0:T(8,128)(2,1)}, u32[]{:S(2)}, u32[]{:S(2)}) collective-permute-start(bf16[512,512]{1,0:T(8,128)(2,1)S(1)} %get-tuple-element.121.refs_2_), channel_id=1, source_target_pairs={{4,2},{5,3},{12,10},{13,11},{20,18},{21,19},{28,26},{29,27}} | collective-permute-start | bytes 1572872 | tf_op jit(solution)/shard_map/ppermute | solution.py:422
  43.3 11.3 %collective-permute-start.5 = (bf16[512,512]{1,0:T(8,128)(2,1)S(1)}, bf16[512,512]{1,0:T(8,128)(2,1)}, u32[]{:S(2)}, u32[]{:S(2)}) collective-permute-start(bf16[512,512]{1,0:T(8,128)(2,1)S(1)} %get-tuple-element.121.refs_2_), channel_id=1, source_target_pairs={{4,6},{5,7},{12,14},{13,15},{20,22},{21,23},{28,30},{29,31}} | collective-permute-start | bytes 1572872 | tf_op jit(solution)/shard_map/ppermute | solution.py:422
  48.7 14.8 %collective-permute-start.11 = (bf16[512,512]{1,0:T(8,128)(2,1)}, bf16[512,512]{1,0:T(8,128)(2,1)}, u32[]{:S(2)}, u32[]{:S(2)}) collective-permute-start(bf16[512,512]{1,0:T(8,128)(2,1)} %copy-done.11), channel_id=1, source_target_pairs={{0,4},{1,5},{8,12},{9,13},{16,20},{17,21},{24,28},{25,29}} | collective-permute-start | bytes 1572872 | tf_op jit(solution)/shard_map/ppermute | solution.py:419
  53.1 10.8 %collective-permute-start.10 = (bf16[512,512]{1,0:T(8,128)(2,1)}, bf16[512,512]{1,0:T(8,128)(2,1)}, u32[]{:S(2)}, u32[]{:S(2)}) collective-permute-start(bf16[512,512]{1,0:T(8,128)(2,1)} %get-tuple-element.136.refs_2_), channel_id=1, source_target_pairs={{4,6},{5,7},{12,14},{13,15},{20,22},{21,23},{28,30},{29,31}} | collective-permute-start | bytes 1572872 | tf_op jit(solution)/shard_map/ppermute | solution.py:422
  54.6 7.3 %collective-permute-start.12 = (f32[8,512]{1,0:T(8,128)S(1)}, f32[8,512]{1,0:T(8,128)S(1)}, u32[]{:S(2)}, u32[]{:S(2)}) collective-permute-start(f32[8,512]{1,0:T(8,128)S(1)} %get-tuple-element.139.refs_0_), channel_id=1, source_target_pairs={{0,2},{1,3},{2,0},{3,1},{4,6},{5,7},{6,4},{7,5},{8,10},{9,11},{10,... | collective-permute-start | bytes 49160 | tf_op jit(solution)/shard_map/ppermute | solution.py:400
  54.6 14.9 %collective-permute-start.9 = (bf16[512,512]{1,0:T(8,128)(2,1)}, bf16[512,512]{1,0:T(8,128)(2,1)}, u32[]{:S(2)}, u32[]{:S(2)}) collective-permute-start(bf16[512,512]{1,0:T(8,128)(2,1)} %get-tuple-element.136.refs_2_), channel_id=1, source_target_pairs={{4,2},{5,3},{12,10},{13,11},{20,18},{21,19},{28,26},{29,27}} | collective-permute-start | bytes 1572872 | tf_op jit(solution)/shard_map/ppermute | solution.py:422
  61.9 13.7 %collective-permute-start.8 = (bf16[512,512]{1,0:T(8,128)(2,1)S(1)}, bf16[512,512]{1,0:T(8,128)(2,1)S(1)}, u32[]{:S(2)}, u32[]{:S(2)}) collective-permute-start(bf16[512,512]{1,0:T(8,128)(2,1)S(1)} %get-tuple-element.135.refs_1_.refs_4_.refs_2_), channel_id=1, source_target_pairs={{0,1},{1,0},{2,3},{3,2},{4,5},{5,4},{6,7},{7,6},{8,9},{9,8},{10,11... | collective-permute-start | bytes 1572872 | tf_op jit(solution)/shard_map/ppermute | solution.py:400
  63.4 47.7 %collective-permute-start = (bf16[8192,128]{1,0:T(8,128)(2,1)}, bf16[8192,128]{1,0:T(8,128)(2,1)}, u32[]{:S(2)}, u32[]{:S(2)}) collective-permute-start(bf16[8192,128]{1,0:T(8,128)(2,1)} %get-tuple-element.110.refs_1_), channel_id=1, source_target_pairs={{0,8},{8,0},{16,24},{24,16},{1,9},{9,1},{17,25},{25,17},{2,10},{10... | collective-permute-start | bytes 6291464 | tf_op jit(solution)/shard_map/ppermute | solution.py:400
  63.5 50.6 %collective-permute-start.2 = (bf16[8192,128]{1,0:T(8,128)(2,1)}, bf16[8192,128]{1,0:T(8,128)(2,1)}, u32[]{:S(2)}, u32[]{:S(2)}) collective-permute-start(bf16[8192,128]{1,0:T(8,128)(2,1)} %collective-permute-done.1.refs_3_), channel_id=1, source_target_pairs={{0,8},{8,0},{16,24},{24,16},{1,9},{9,1},{17,25},{25,17},{2,10},{10... | collective-permute-start | bytes 6291464 | tf_op jit(solution)/shard_map/ppermute | solution.py:400
  64.0 10.2 %collective-permute-start.17 = (f32[8,512]{1,0:T(8,128)S(1)}, f32[8,512]{1,0:T(8,128)S(1)}, u32[]{:S(2)}, u32[]{:S(2)}) collective-permute-start(f32[8,512]{1,0:T(8,128)S(1)} %get-tuple-element.147.refs_0_), channel_id=1, source_target_pairs={{0,4},{1,5},{2,6},{3,7},{4,0},{5,1},{6,2},{7,3},{8,12},{9,13},{10,... | collective-permute-start | bytes 49160 | tf_op jit(solution)/shard_map/ppermute | solution.py:400
  69.5 13.6 %collective-permute-start.16 = (bf16[512,512]{1,0:T(8,128)(2,1)}, bf16[512,512]{1,0:T(8,128)(2,1)}, u32[]{:S(2)}, u32[]{:S(2)}) collective-permute-start(bf16[512,512]{1,0:T(8,128)(2,1)} %copy-done.9), channel_id=1, source_target_pairs={{0,4},{1,5},{8,12},{9,13},{16,20},{17,21},{24,28},{25,29}} | collective-permute-start | bytes 1572872 | tf_op jit(solution)/shard_map/ppermute | solution.py:419
  74.1 16.5 %collective-permute-start.21 = (bf16[512,512]{1,0:T(8,128)(2,1)}, bf16[512,512]{1,0:T(8,128)(2,1)}, u32[]{:S(2)}, u32[]{:S(2)}) collective-permute-start(bf16[512,512]{1,0:T(8,128)(2,1)} %get-tuple-element.154.refs_2_), channel_id=1, source_target_pairs={{4,2},{5,3},{12,10},{13,11},{20,18},{21,19},{28,26},{29,27}} | collective-permute-start | bytes 1572872 | tf_op jit(solution)/shard_map/ppermute | solution.py:422
  75.6 15.7 %collective-permute-start.22 = (bf16[512,512]{1,0:T(8,128)(2,1)}, bf16[512,512]{1,0:T(8,128)(2,1)}, u32[]{:S(2)}, u32[]{:S(2)}) collective-permute-start(bf16[512,512]{1,0:T(8,128)(2,1)} %get-tuple-element.154.refs_2_), channel_id=1, source_target_pairs={{4,6},{5,7},{12,14},{13,15},{20,22},{21,23},{28,30},{29,31}} | collective-permute-start | bytes 1572872 | tf_op jit(solution)/shard_map/ppermute | solution.py:422
  83.1 16.1 %collective-permute-start.20 = (bf16[512,512]{1,0:T(8,128)(2,1)}, bf16[512,512]{1,0:T(8,128)(2,1)}, u32[]{:S(2)}, u32[]{:S(2)}) collective-permute-start(bf16[512,512]{1,0:T(8,128)(2,1)} %copy-done.5), channel_id=1, source_target_pairs={{0,4},{1,5},{8,12},{9,13},{16,20},{17,21},{24,28},{25,29}} | collective-permute-start | bytes 1572872 | tf_op jit(solution)/shard_map/ppermute | solution.py:419
  90.6 9.3 %collective-permute-start.18 = (bf16[512,512]{1,0:T(8,128)(2,1)}, bf16[512,512]{1,0:T(8,128)(2,1)S(1)}, u32[]{:S(2)}, u32[]{:S(2)}) collective-permute-start(bf16[512,512]{1,0:T(8,128)(2,1)} %get-tuple-element.150.refs_2_), channel_id=1, source_target_pairs={{4,2},{5,3},{12,10},{13,11},{20,18},{21,19},{28,26},{29,27}} | collective-permute-start | bytes 1572872 | tf_op jit(solution)/shard_map/ppermute | solution.py:422
  91.3 12.5 %collective-permute-start.14 = (bf16[512,512]{1,0:T(8,128)(2,1)}, bf16[512,512]{1,0:T(8,128)(2,1)}, u32[]{:S(2)}, u32[]{:S(2)}) collective-permute-start(bf16[512,512]{1,0:T(8,128)(2,1)} %get-tuple-element.144.refs_5_), channel_id=1, source_target_pairs={{0,16},{8,24},{16,0},{24,8},{1,17},{9,25},{17,1},{25,9},{2,18},{10... | collective-permute-start | bytes 1572872 | tf_op jit(solution)/shard_map/ppermute | solution.py:396
  99.2 8.5 %collective-permute-start.19 = (bf16[512,512]{1,0:T(8,128)(2,1)}, bf16[512,512]{1,0:T(8,128)(2,1)S(1)}, u32[]{:S(2)}, u32[]{:S(2)}) collective-permute-start(bf16[512,512]{1,0:T(8,128)(2,1)} %get-tuple-element.150.refs_2_), channel_id=1, source_target_pairs={{4,6},{5,7},{12,14},{13,15},{20,22},{21,23},{28,30},{29,31}} | collective-permute-start | bytes 1572872 | tf_op jit(solution)/shard_map/ppermute | solution.py:422
  100.7 9.7 %collective-permute-start.13 = (bf16[512,512]{1,0:T(8,128)(2,1)}, bf16[512,512]{1,0:T(8,128)(2,1)S(1)}, u32[]{:S(2)}, u32[]{:S(2)}) collective-permute-start(bf16[512,512]{1,0:T(8,128)(2,1)} %get-tuple-element.144.refs_5_), channel_id=1, source_target_pairs={{0,8},{8,0},{16,24},{24,16},{1,9},{9,1},{17,25},{25,17},{2,10},{10... | collective-permute-start | bytes 1572872 | tf_op jit(solution)/shard_map/ppermute | solution.py:400
  103.8 8.1 %collective-permute-start.15 = (bf16[512,512]{1,0:T(8,128)(2,1)}, bf16[512,512]{1,0:T(8,128)(2,1)S(1)}, u32[]{:S(2)}, u32[]{:S(2)}) collective-permute-start(bf16[512,512]{1,0:T(8,128)(2,1)} %collective-permute-done.14.refs_7_), channel_id=1, source_target_pairs={{0,8},{8,0},{16,24},{24,16},{1,9},{9,1},{17,25},{25,17},{2,10},{10... | collective-permute-start | bytes 1572872 | tf_op jit(solution)/shard_map/ppermute | solution.py:400
  107.7 36.5 %collective-permute-start.29 = (bf16[512,512]{1,0:T(8,128)(2,1)}, bf16[512,512]{1,0:T(8,128)(2,1)S(1)}, u32[]{:S(2)}, u32[]{:S(2)}) collective-permute-start(bf16[512,512]{1,0:T(8,128)(2,1)} %copy-done.13), channel_id=1, source_target_pairs={{0,1},{1,0},{2,3},{3,2},{4,5},{5,4},{6,7},{7,6},{8,9},{9,8},{10,11... | collective-permute-start | bytes 1572872 | tf_op jit(solution)/shard_map/ppermute | solution.py:400
  110.5 51.0 %collective-permute-start.26 = (bf16[512,512]{1,0:T(8,128)(2,1)}, bf16[512,512]{1,0:T(8,128)(2,1)S(1)}, u32[]{:S(2)}, u32[]{:S(2)}) collective-permute-start(bf16[512,512]{1,0:T(8,128)(2,1)} %get-tuple-element.166.refs_2_), channel_id=1, source_target_pairs={{4,2},{5,3},{12,10},{13,11},{20,18},{21,19},{28,26},{29,27}} | collective-permute-start | bytes 1572872 | tf_op jit(solution)/shard_map/ppermute | solution.py:422
  111.2 51.0 %collective-permute-start.27 = (bf16[512,512]{1,0:T(8,128)(2,1)}, bf16[512,512]{1,0:T(8,128)(2,1)S(1)}, u32[]{:S(2)}, u32[]{:S(2)}) collective-permute-start(bf16[512,512]{1,0:T(8,128)(2,1)} %get-tuple-element.166.refs_2_), channel_id=1, source_target_pairs={{4,6},{5,7},{12,14},{13,15},{20,22},{21,23},{28,30},{29,31}} | collective-permute-start | bytes 1572872 | tf_op jit(solution)/shard_map/ppermute | solution.py:422
  111.9 20.3 %collective-permute-start.24 = (f32[4,512]{1,0:T(4,128)S(1)}, f32[4,512]{1,0:T(4,128)S(1)}, u32[]{:S(2)}, u32[]{:S(2)}) collective-permute-start(f32[4,512]{1,0:T(4,128)S(1)} %get-tuple-element.163), channel_id=1, source_target_pairs={{0,8},{8,16},{16,24},{1,9},{9,17},{17,25},{2,10},{10,18},{18,26},{... | collective-permute-start | bytes 24584 | tf_op jit(solution)/shard_map/ppermute | solution.py:486
  114.0 31.6 %collective-permute-start.30 = (bf16[512,512]{1,0:T(8,128)(2,1)S(1)}, bf16[512,512]{1,0:T(8,128)(2,1)S(1)}, u32[]{:S(2)}, u32[]{:S(2)}) collective-permute-start(bf16[512,512]{1,0:T(8,128)(2,1)S(1)} %get-tuple-element.169.refs_6_), channel_id=1, source_target_pairs={{0,1},{1,0},{2,3},{3,2},{4,5},{5,4},{6,7},{7,6},{8,9},{9,8},{10,11... | collective-permute-start | bytes 1572872 | tf_op jit(solution)/shard_map/ppermute | solution.py:400
  132.2 28.5 %collective-permute-start.28 = (bf16[512,512]{1,0:T(8,128)(2,1)S(1)}, bf16[512,512]{1,0:T(8,128)(2,1)S(1)}, u32[]{:S(2)}, u32[]{:S(2)}) collective-permute-start(bf16[512,512]{1,0:T(8,128)(2,1)S(1)} %copy-done.2), channel_id=1, source_target_pairs={{0,4},{1,5},{8,12},{9,13},{16,20},{17,21},{24,28},{25,29}} | collective-permute-start | bytes 1572872 | tf_op jit(solution)/shard_map/ppermute | solution.py:419
  144.3 35.9 %collective-permute-start.23 = (bf16[512,512]{1,0:T(8,128)(2,1)S(1)}, bf16[512,512]{1,0:T(8,128)(2,1)S(1)}, u32[]{:S(2)}, u32[]{:S(2)}) collective-permute-start(bf16[512,512]{1,0:T(8,128)(2,1)S(1)} %get-tuple-element.161.refs_1_), channel_id=1, source_target_pairs={{0,4},{1,5},{8,12},{9,13},{16,20},{17,21},{24,28},{25,29}} | collective-permute-start | bytes 1572872 | tf_op jit(solution)/shard_map/ppermute | solution.py:419
  145.6 23.3 %collective-permute-start.32 = (bf16[512,512]{1,0:T(8,128)(2,1)S(1)}, bf16[512,512]{1,0:T(8,128)(2,1)S(1)}, u32[]{:S(2)}, u32[]{:S(2)}) collective-permute-start(bf16[512,512]{1,0:T(8,128)(2,1)S(1)} %get-tuple-element.175.refs_2_), channel_id=1, source_target_pairs={{0,1},{1,0},{2,3},{3,2},{4,5},{5,4},{6,7},{7,6},{8,9},{9,8},{10,11... | collective-permute-start | bytes 1572872 | tf_op jit(solution)/shard_map/ppermute | solution.py:400
  160.7 19.5 %collective-permute-start.35 = (bf16[512,512]{1,0:T(8,128)(2,1)S(1)}, bf16[512,512]{1,0:T(8,128)(2,1)S(1)}, u32[]{:S(2)}, u32[]{:S(2)}) collective-permute-start(bf16[512,512]{1,0:T(8,128)(2,1)S(1)} %get-tuple-element.182.refs_2_), channel_id=1, source_target_pairs={{4,2},{5,3},{12,10},{13,11},{20,18},{21,19},{28,26},{29,27}} | collective-permute-start | bytes 1572872 | tf_op jit(solution)/shard_map/ppermute | solution.py:422
  161.4 18.8 %collective-permute-start.36 = (bf16[512,512]{1,0:T(8,128)(2,1)S(1)}, bf16[512,512]{1,0:T(8,128)(2,1)S(1)}, u32[]{:S(2)}, u32[]{:S(2)}) collective-permute-start(bf16[512,512]{1,0:T(8,128)(2,1)S(1)} %get-tuple-element.182.refs_2_), channel_id=1, source_target_pairs={{4,6},{5,7},{12,14},{13,15},{20,22},{21,23},{28,30},{29,31}} | collective-permute-start | bytes 1572872 | tf_op jit(solution)/shard_map/ppermute | solution.py:422
  165.6 38.5 %collective-permute-start.41 = (bf16[512,512]{1,0:T(8,128)(2,1)}, bf16[512,512]{1,0:T(8,128)(2,1)}, u32[]{:S(2)}, u32[]{:S(2)}) collective-permute-start(bf16[512,512]{1,0:T(8,128)(2,1)} %get-tuple-element.188.refs_2_), channel_id=1, source_target_pairs={{0,1},{1,0},{2,3},{3,2},{4,5},{5,4},{6,7},{7,6},{8,9},{9,8},{10,11... | collective-permute-start | bytes 1572872 | tf_op jit(solution)/shard_map/ppermute | solution.py:400
  168.9 9.8 %collective-permute-start.31 = (f32[4,512]{1,0:T(4,128)S(1)}, f32[4,512]{1,0:T(4,128)S(1)}, u32[]{:S(2)}, u32[]{:S(2)}) collective-permute-start(f32[4,512]{1,0:T(4,128)S(1)} %get-tuple-element.174), channel_id=1, source_target_pairs={{0,8},{8,16},{16,24},{1,9},{9,17},{17,25},{2,10},{10,18},{18,26},{... | collective-permute-start | bytes 24584 | tf_op jit(solution)/shard_map/ppermute | solution.py:486
  181.0 23.1 %collective-permute-start.42 = (bf16[512,512]{1,0:T(8,128)(2,1)S(1)}, bf16[512,512]{1,0:T(8,128)(2,1)S(1)}, u32[]{:S(2)}, u32[]{:S(2)}) collective-permute-start(bf16[512,512]{1,0:T(8,128)(2,1)S(1)} %get-tuple-element.189.refs_4_), channel_id=1, source_target_pairs={{0,1},{1,0},{2,3},{3,2},{4,5},{5,4},{6,7},{7,6},{8,9},{9,8},{10,11... | collective-permute-start | bytes 1572872 | tf_op jit(solution)/shard_map/ppermute | solution.py:400
  181.3 34.3 %collective-permute-start.38 = (bf16[512,512]{1,0:T(8,128)(2,1)}, bf16[512,512]{1,0:T(8,128)(2,1)S(1)}, u32[]{:S(2)}, u32[]{:S(2)}) collective-permute-start(bf16[512,512]{1,0:T(8,128)(2,1)} %copy-done.7), channel_id=1, source_target_pairs={{4,2},{5,3},{12,10},{13,11},{20,18},{21,19},{28,26},{29,27}} | collective-permute-start | bytes 1572872 | tf_op jit(solution)/shard_map/ppermute | solution.py:422
  182.0 33.6 %collective-permute-start.39 = (bf16[512,512]{1,0:T(8,128)(2,1)}, bf16[512,512]{1,0:T(8,128)(2,1)S(1)}, u32[]{:S(2)}, u32[]{:S(2)}) collective-permute-start(bf16[512,512]{1,0:T(8,128)(2,1)} %copy-done.7), channel_id=1, source_target_pairs={{4,6},{5,7},{12,14},{13,15},{20,22},{21,23},{28,30},{29,31}} | collective-permute-start | bytes 1572872 | tf_op jit(solution)/shard_map/ppermute | solution.py:422
  186.0 29.7 %collective-permute-start.40 = (bf16[256,512]{1,0:T(8,128)(2,1)S(1)}, bf16[256,512]{1,0:T(8,128)(2,1)S(1)}, u32[]{:S(2)}, u32[]{:S(2)}) collective-permute-start(bf16[256,512]{1,0:T(8,128)(2,1)S(1)} %get-tuple-element.187.refs_1_), channel_id=1, source_target_pairs={{0,4},{1,5},{8,12},{9,13},{16,20},{17,21},{24,28},{25,29}} | collective-permute-start | bytes 786440 | tf_op jit(solution)/shard_map/ppermute | solution.py:419
  215.8 22.2 %collective-permute-start.49 = (bf16[512,512]{1,0:T(8,128)(2,1)S(1)}, bf16[512,512]{1,0:T(8,128)(2,1)S(1)}, u32[]{:S(2)}, u32[]{:S(2)}) collective-permute-start(bf16[512,512]{1,0:T(8,128)(2,1)S(1)} %get-tuple-element.202.refs_2_), channel_id=1, source_target_pairs={{0,1},{1,0},{2,3},{3,2},{4,5},{5,4},{6,7},{7,6},{8,9},{9,8},{10,11... | collective-permute-start | bytes 1572872 | tf_op jit(solution)/shard_map/ppermute | solution.py:400
  217.6 17.0 %collective-permute-start.33 = (bf16[256,512]{1,0:T(8,128)(2,1)S(1)}, bf16[256,512]{1,0:T(8,128)(2,1)S(1)}, u32[]{:S(2)}, u32[]{:S(2)}) collective-permute-start(bf16[256,512]{1,0:T(8,128)(2,1)S(1)} %get-tuple-element.180.refs_1_), channel_id=1, source_target_pairs={{0,4},{1,5},{8,12},{9,13},{16,20},{17,21},{24,28},{25,29}} | collective-permute-start | bytes 786440 | tf_op jit(solution)/shard_map/ppermute | solution.py:419
  225.8 8.8 %collective-permute-start.46 = (bf16[256,512]{1,0:T(8,128)(2,1)S(1)}, bf16[256,512]{1,0:T(8,128)(2,1)S(1)}, u32[]{:S(2)}, u32[]{:S(2)}) collective-permute-start(bf16[256,512]{1,0:T(8,128)(2,1)S(1)} %get-tuple-element.199.refs_2_), channel_id=1, source_target_pairs={{4,2},{5,3},{12,10},{13,11},{20,18},{21,19},{28,26},{29,27}} | collective-permute-start | bytes 786440 | tf_op jit(solution)/shard_map/ppermute | solution.py:422
  226.4 8.2 %collective-permute-start.47 = (bf16[256,512]{1,0:T(8,128)(2,1)S(1)}, bf16[256,512]{1,0:T(8,128)(2,1)S(1)}, u32[]{:S(2)}, u32[]{:S(2)}) collective-permute-start(bf16[256,512]{1,0:T(8,128)(2,1)S(1)} %get-tuple-element.199.refs_2_), channel_id=1, source_target_pairs={{4,6},{5,7},{12,14},{13,15},{20,22},{21,23},{28,30},{29,31}} | collective-permute-start | bytes 786440 | tf_op jit(solution)/shard_map/ppermute | solution.py:422
  234.7 10.6 %collective-permute-start.48 = (bf16[256,512]{1,0:T(8,128)(2,1)S(1)}, bf16[256,512]{1,0:T(8,128)(2,1)S(1)}, u32[]{:S(2)}, u32[]{:S(2)}) collective-permute-start(bf16[256,512]{1,0:T(8,128)(2,1)S(1)} %get-tuple-element.201.refs_2_), channel_id=1, source_target_pairs={{0,1},{1,0},{2,3},{3,2},{4,5},{5,4},{6,7},{7,6},{8,9},{9,8},{10,11... | collective-permute-start | bytes 786440 | tf_op jit(solution)/shard_map/ppermute | solution.py:400
  236.5 14.1 %collective-permute-start.44 = (bf16[256,512]{1,0:T(8,128)(2,1)S(1)}, bf16[256,512]{1,0:T(8,128)(2,1)S(1)}, u32[]{:S(2)}, u32[]{:S(2)}) collective-permute-start(bf16[256,512]{1,0:T(8,128)(2,1)S(1)} %get-tuple-element.198.refs_2_), channel_id=1, source_target_pairs={{4,2},{5,3},{12,10},{13,11},{20,18},{21,19},{28,26},{29,27}} | collective-permute-start | bytes 786440 | tf_op jit(solution)/shard_map/ppermute | solution.py:422
  237.2 13.5 %collective-permute-start.45 = (bf16[256,512]{1,0:T(8,128)(2,1)S(1)}, bf16[256,512]{1,0:T(8,128)(2,1)S(1)}, u32[]{:S(2)}, u32[]{:S(2)}) collective-permute-start(bf16[256,512]{1,0:T(8,128)(2,1)S(1)} %get-tuple-element.198.refs_2_), channel_id=1, source_target_pairs={{4,6},{5,7},{12,14},{13,15},{20,22},{21,23},{28,30},{29,31}} | collective-permute-start | bytes 786440 | tf_op jit(solution)/shard_map/ppermute | solution.py:422
  237.9 7.4 %collective-permute-start.50 = (f32[4,512]{1,0:T(4,128)S(1)}, f32[4,512]{1,0:T(4,128)S(1)}, u32[]{:S(2)}, u32[]{:S(2)}) collective-permute-start(f32[4,512]{1,0:T(4,128)S(1)} %get-tuple-element.206.refs_0_), channel_id=1, source_target_pairs={{0,2},{1,3},{2,0},{3,1},{4,6},{5,7},{6,4},{7,5},{8,10},{9,11},{10,... | collective-permute-start | bytes 24584 | tf_op jit(solution)/shard_map/ppermute | solution.py:400
  250.7 6.4 %collective-permute-start.51 = (bf16[256,512]{1,0:T(8,128)(2,1)S(1)}, bf16[256,512]{1,0:T(8,128)(2,1)S(1)}, u32[]{:S(2)}, u32[]{:S(2)}) collective-permute-start(bf16[256,512]{1,0:T(8,128)(2,1)S(1)} %get-tuple-element.210.refs_2_), channel_id=1, source_target_pairs={{0,1},{1,0},{2,3},{3,2},{4,5},{5,4},{6,7},{7,6},{8,9},{9,8},{10,11... | collective-permute-start | bytes 786440 | tf_op jit(solution)/shard_map/ppermute | solution.py:400
  251.1 5.3 %collective-permute-start.52 = (f32[4,512]{1,0:T(4,128)S(1)}, f32[4,512]{1,0:T(4,128)S(1)}, u32[]{:S(2)}, u32[]{:S(2)}) collective-permute-start(f32[4,512]{1,0:T(4,128)S(1)} %get-tuple-element.212.refs_0_), channel_id=1, source_target_pairs={{0,4},{1,5},{2,6},{3,7},{4,0},{5,1},{6,2},{7,3},{8,12},{9,13},{10,... | collective-permute-start | bytes 24584 | tf_op jit(solution)/shard_map/ppermute | solution.py:400
  (27 other events, 311.9 us)

commit v2 on v1

--- a/solution.py
+++ b/solution.py
@@ -118,15 +118,21 @@
     return x[0]
 
 
-def extract_kernel(groups, stride, a_ref, sol_ref, col_ref, part_ref, *rest):
-    wide = rest[-1]
-    rows = col_ref.shape[0]
-    if len(rest) > 1:
-        rest[0][...] = a_ref[...]
+def extract_kernel(groups, stride, spans, a_ref, sol_ref, part_ref, *rest):
+    cols, wide = rest[: len(spans)], rest[-1]
+    rows = part_ref.shape[1]
+    if len(rest) > len(spans) + 1:
+        rest[len(spans)][...] = a_ref[...]
     wide[...] = a_ref[...].astype(F32)
-    for g in range(0, groups, stride):
-        piece = wide[pl.ds(g, rows, stride=groups), :]
-        col_ref[:, pl.ds(g // stride * LANES, LANES)] = piece.astype(BF16)
+    i = pl.program_id(0)
+    for col_ref, (start, stop) in zip(cols, spans):
+
+        @pl.when((i >= start) & (i < stop))
+        def _(col_ref=col_ref):
+            for g in range(0, groups, stride):
+                piece = wide[pl.ds(g, rows, stride=groups), :]
+                col_ref[:, pl.ds(g // stride * LANES, LANES)] = piece.astype(BF16)
+
     if groups % 16 == 0:
         sol = sol_ref[...].astype(F32)
         totals = []
@@ -150,23 +156,24 @@
     part_ref[...] = sums[0:1, :]
 
 
-def extract(chain, flat, sol, first, rows, groups, stride, width, with_band):
-    sub = min(rows, 128)
+def extract(chain, flat, sol, sizes, first, groups, stride, width, with_band):
+    sub = min(min(sizes), 256)
     size = sub * groups
     at = first // sub
-    out_specs = [
-        pl.BlockSpec((sub, width), lambda i: (i, 0)),
-        pl.BlockSpec((1, sub), lambda i: (0, i)),
-    ]
-    out_shape = [
-        jax.ShapeDtypeStruct((rows, width), BF16),
-        jax.ShapeDtypeStruct((1, rows), F32),
-    ]
+    rows = sum(sizes)
+    spans, out_specs, out_shape = [], [pl.BlockSpec((1, sub), lambda i: (0, i))], [jax.ShapeDtypeStruct((1, rows), F32)]
+    start = 0
+    for n in sizes:
+        stop = start + n // sub
+        spans.append((start, stop))
+        out_specs.append(pl.BlockSpec((sub, width), lambda i, a=start, b=stop: (jnp.clip(i - a, 0, b - a - 1), 0)))
+        out_shape.append(jax.ShapeDtypeStruct((n, width), BF16))
+        start = stop
     if with_band:
         out_specs.append(pl.BlockSpec((size, LANES), lambda i: (i, 0)))
         out_shape.append(jax.ShapeDtypeStruct((rows * groups, LANES), BF16))
     return chain(
-        lambda *refs: extract_kernel(groups, stride, *refs),
+        lambda *refs: extract_kernel(groups, stride, spans, *refs),
         [flat, sol],
         [
             pl.BlockSpec((size, LANES), lambda i: (at + i, 0)),
@@ -183,28 +190,36 @@
 
 def factor_kernel(groups, n_x, where_ref, *refs):
     core, lane, x = where_ref[0], where_ref[1], where_ref[2]
-    given, (up_ref, low_ref, v_ref, raws, bands, blocks, sems, *rest) = refs[: 4 * n_x], refs[4 * n_x :]
+    given, (mine_ref, other_ref, up_ref, low_ref, v_ref, raws, bands, blocks, sems, *rest) = refs[: 2 * n_x], refs[2 * n_x :]
     width = up_ref.shape[1]
+
+    def both(copies):
+        for copy in copies:
+            copy.start()
+        for copy in copies:
+            copy.wait()
+
     for i in range(n_x):
 
         @pl.when(x == i)
         def _(i=i):
-            pairs = [(raws, given[2 * i], given[2 * i + 1]), (blocks, given[2 * n_x + 2 * i], given[2 * n_x + 2 * i + 1])]
-            copies = []
-            for kind, (target, mine, other) in enumerate(pairs):
-                copies.append(pltpu.make_async_copy(mine, target.at[core], sems.at[kind, 0]))
-                copies.append(pltpu.make_async_copy(other, target.at[1 - core], sems.at[kind, 1]))
-            for copy in copies:
-                copy.start()
-            for copy in copies:
-                copy.wait()
+            both([pltpu.make_async_copy(given[2 * i + k], raws.at[k], sems.at[k]) for k in range(2)])
+
+    for i, (ref_01, ref_10) in enumerate([(other_ref, mine_ref), (mine_ref, other_ref)]):
+
+        @pl.when(lane == i)
+        def _(ref_01=ref_01, ref_10=ref_10):
+            both([
+                pltpu.make_async_copy(ref_01.at[0], blocks.at[0], sems.at[2]),
+                pltpu.make_async_copy(ref_10.at[1], blocks.at[1], sems.at[3]),
+            ])
 
     for slot in range(2):
         if groups % 16 == 0:
 
             def one(block, carry, slot=slot):
                 here = pl.ds(pl.multiple_of(block * 16 * groups, 16 * groups), 16 * groups)
-                raw = raws[slot, here, :].astype(F32).reshape(2, 8, groups, LANES)
+                raw = raws[slot ^ core, here, :].astype(F32).reshape(2, 8, groups, LANES)
                 rows = pl.ds(pl.multiple_of(block * 16, 16), 16)
                 for h in range(groups // 8):
                     turned = transpose8([raw[:, r, 8 * h : 8 * h + 8] for r in range(8)])
@@ -216,7 +231,7 @@
             lax.fori_loop(0, width // 16, one, 0, unroll=2)
         else:
             wide = rest[0]
-            wide[...] = raws[slot].astype(F32)
+            wide[...] = raws[slot ^ core].astype(F32)
             for g in range(groups):
                 at = pl.ds(g * LANES, LANES)
                 bands[slot, :, at] = wide[pl.ds(g, width, stride=groups), :].astype(BF16)
@@ -250,14 +265,14 @@
         pltpu.VMEM((2, width * groups, LANES), BF16),
         pltpu.VMEM((2, width, cols), BF16),
         pltpu.VMEM((2, width, width), BF16),
-        pltpu.SemaphoreType.DMA((2, 2)),
+        pltpu.SemaphoreType.DMA((4,)),
     ]
     if groups % 16:
         scratch.append(pltpu.VMEM((width * groups, LANES), F32))
     return chain(
         lambda *refs: factor_kernel(groups, n_x, *refs),
         [where, *bands, *blocks, upper, lower],
-        [pl.BlockSpec(memory_space=pltpu.SMEM)] + [anywhere] * (4 * n_x) + [vmem] * 2,
+        [pl.BlockSpec(memory_space=pltpu.SMEM)] + [anywhere] * (2 * n_x + 2) + [vmem] * 2,
         [jax.ShapeDtypeStruct((2 * width, cols), BF16)],
         [vmem],
         "factors",
@@ -333,38 +348,44 @@
     )
 
 
-def solve_kernel(place_ref, state_ref, res_ref, inv_ref, *rest):
+def solve_kernel(lane_ref, res_ref, inv_ref, *rest):
     cols, out_ref = rest[:-1], rest[-1]
-    place, lane = place_ref[0], place_ref[1]
-    width = inv_ref.shape[0]
+    lane = lane_ref[0]
+    count, width = out_ref.shape
     nt = (((1,), (1,)), ((), ()))
-    pending = jnp.zeros((8, width), F32)
-    for j, col in enumerate(cols):
-        at = (j + lane) % 2 if j < 2 else j
-        known = jnp.where(at < place, state_ref[pl.ds(at, 1), :], 0.0)
-        pending = pending + lax.dot_general(
-            jnp.broadcast_to(known, (8, width)).astype(BF16), col[...], nt, preferred_element_type=F32
-        )
-    left = res_ref[...] - pending[0:1, :]
-    high = left.astype(BF16)
-    rest_1 = left - high.astype(F32)
-    mid = rest_1.astype(BF16)
-    low = (rest_1 - mid.astype(F32)).astype(BF16)
-    total = jnp.zeros((8, width), F32)
-    for piece in (low, mid, high):
-        wide = jnp.broadcast_to(piece.astype(F32), (8, width)).astype(BF16)
-        total = total + lax.dot_general(wide, inv_ref[...], nt, preferred_element_type=F32)
-    row = lax.broadcasted_iota(jnp.int32, state_ref.shape, 0)
-    out_ref[...] = jnp.where(row == place, jnp.broadcast_to(total[0:1, :], state_ref.shape), state_ref[...])
-
-
-def solve_step(chain, place, state, res, inv, cols):
+    out_ref[...] = jnp.zeros((count, width), F32)
+    for k in range(count):
+        pending = jnp.zeros((8, width), F32)
+        for j, col in enumerate(cols):
+            if j >= max(k, 2) or k == 0:
+                continue
+            if j < 2:
+                at = (j + lane) % 2
+                known = jnp.where(at < k, out_ref[pl.ds(at, 1), :], 0.0)
+            else:
+                known = out_ref[j : j + 1, :]
+            pending = pending + lax.dot_general(
+                jnp.broadcast_to(known, (8, width)).astype(BF16), col[k], nt, preferred_element_type=F32
+            )
+        left = res_ref[k : k + 1, :] - pending[0:1, :]
+        high = left.astype(BF16)
+        rest_1 = left - high.astype(F32)
+        mid = rest_1.astype(BF16)
+        low = (rest_1 - mid.astype(F32)).astype(BF16)
+        total = jnp.zeros((8, width), F32)
+        for piece in (low, mid, high):
+            wide = jnp.broadcast_to(piece.astype(F32), (8, width)).astype(BF16)
+            total = total + lax.dot_general(wide, inv_ref[k], nt, preferred_element_type=F32)
+        out_ref[k : k + 1, :] = total[0:1, :]
+
+
+def solve_all(chain, lane, res, inv, cols):
     vmem = pl.BlockSpec(memory_space=pltpu.VMEM)
     return chain(
         solve_kernel,
-        [place, state, res, inv, *cols],
-        [pl.BlockSpec(memory_space=pltpu.SMEM)] + [vmem] * (3 + len(cols)),
-        [jax.ShapeDtypeStruct(state.shape, F32)],
+        [lane, res, inv, *cols],
+        [pl.BlockSpec(memory_space=pltpu.SMEM)] + [vmem] * (2 + len(cols)),
+        [jax.ShapeDtypeStruct(res.shape, F32)],
         [vmem],
         "solve",
         (2 * inv.size * (len(cols) + 3), 2 * inv.size * (len(cols) + 1)),
@@ -443,123 +464,77 @@
     assert diagonal_block_inverses.shape[0] == 1
     home = count - 2
     inv = diagonal_block_inverses.reshape(width, width)
-    place = jnp.stack([prow, lane]).astype(jnp.int32)
     where = jnp.stack([core, lane, prow // 2]).astype(jnp.int32)
-    flag = jnp.where(core != lane, 0, 1).astype(jnp.int32).reshape(1)
-    bits = [1 << b for b in range(n_pcol.bit_length() - 1)]
-
-    cuts = [(c * width, width) for c in range(slots - 1)]
-    cuts += [((slots - 1) * width + h * width // 2, width // 2) for h in range(2)]
-    chunks = len(cuts)
-    column, parts, first, outward, mine, other, box = {}, {}, {}, {}, {}, {}, {"out": None}
-    for c in [0, 2, 3, 1, *range(4, slots)]:
-        col, part, *band = extract(chain, flat, sol, c * width, width, groups, col_slots, width, c == 0)
-        parts[c] = part
-        if c < slots - 1:
-            column[c] = col
-        else:
-            column[c], column[c + 1] = col[: width // 2], col[width // 2 :]
-        if c < 2:
-            first[c] = first_stage(col)
-        if c == 0:
-            box["bands"] = spread(band[0], "prow", n_prow)
-
-    def total_step(bit):
-        def run():
-            if bit == 1:
-                box["total"] = jnp.concatenate([parts[c] for c in range(slots)], axis=0)
-            box["total"] = chain.add(box["total"], swap(box["total"], "pcol", n_pcol, bit))
-            if bit == bits[-1]:
-                box["residual"] = right_side.reshape(slots, width) - box["total"]
-
-        return run
-
-    def solve(k):
-        def run():
-            if k == 0:
-                needed = [mine[0], other[0]]
-                for j in range(2, home):
-                    needed.append(lax.ppermute(column[0], "pcol", [(j, home)]))
-                box["needed"] = needed + [column[0]]
-                state = jnp.zeros((count, width), F32)
-            else:
-                state = lax.ppermute(box["state"], "prow", [(i, i + 1) for i in range(n_prow - 1)])
-            state = solve_step(chain, place, state, box["residual"][0:1], inv, box["needed"])
-            if k == count - 1:
-                state = jnp.where((prow == n_prow - 1) & (pcol == home), state, 0.0)
-            box["state"] = state
-
-        return run
-
-    def share(axis, size, bit):
-        def run():
-            box["state"] = chain.add(box["state"], swap(box["state"], axis, size, bit))
-
-        return run
-
-    def blocks_out():
-        box["blks"] = spread(chain.choose(flag, [mine[0], other[0]]), "prow", n_prow)
-        box["bands"] = [v for b in box["bands"] for v in (b, swap(b, "prow", n_prow))]
-
-    def blocks_swap():
-        box["blks"] = [v for b in box["blks"] for v in (b, swap(b, "prow", n_prow))]
-
-    def make_factors():
-        box["v"] = factors(chain, where, box["bands"], box["blks"], upper_inv, lower_inv, groups)
-
-    def updates(*which):
-        def run():
-            args = [mine[c] for c in which], [other[c] for c in which]
-            box["out"] = update(chain, flat, *args, box["v"], box["out"], cuts[which[0]][0], groups)
-
-        return run
+
+    sizes = [width] + [2 * width] * ((slots - 2) // 2)
+    sizes += [width // 2] * ((slots * width - sum(sizes)) // (width // 2))
+    starts = [sum(sizes[:c]) for c in range(len(sizes))]
+    chunks = len(sizes)
+    column, first, outward, mine, other, box = {}, {}, {}, {}, {}, {"out": None}
+    part_0, column[0], band = extract(chain, flat, sol, sizes[:1], 0, groups, col_slots, width, True)
+    first[0] = first_stage(column[0])
+    bands = spread(band, "prow", n_prow)
+    part_1, *rest = extract(chain, flat, sol, sizes[1:], width, groups, col_slots, width, False)
+    column.update({c + 1: col for c, col in enumerate(rest)})
+    partial = jnp.concatenate([part_0, part_1], axis=1).reshape(slots, width)
+    residual = right_side.reshape(slots, width) - jnp.sum(lax.all_gather(partial, "pcol"), axis=0)
 
     def take(c):
         mine[c] = settle(column[c], first[c], outward[c])
         other[c] = swap(mine[c], "pcol", n_pcol)
 
-    total = [total_step(b) for b in bits]
-    line = [solve(k) for k in range(count)]
-    line += [share("prow", n_prow, 1 << b) for b in range(n_prow.bit_length() - 1)]
-    line += [share("pcol", n_pcol, b) for b in bits]
-    if slots == 8 and len(line) == 9:
-        plan = {
-            0: total[:1],
-            1: total[1:2],
-            2: [blocks_out, total[2]],
-            3: [blocks_swap, line[0]],
-            4: [make_factors, line[1], updates(0, 1, 2)],
-            5: [line[2], updates(3), line[3]],
-            6: [line[4], updates(4, 5)],
-            7: [line[5], line[6]],
-            8: [updates(6), line[7]],
-        }
-        tail = []
+    def swap_bands():
+        box["bands"] = [v for b in bands for v in (b, swap(b, "prow", n_prow))]
+
+    def gather_blocks():
+        box["blocks"] = [lax.all_gather(mine[0], "prow"), lax.all_gather(other[0], "prow")]
+
+    def gather_rest():
+        own, below, _ = chain.gate([column[0], inv, box["blocks"][0]], [])
+        cols = [lax.ppermute(own, "pcol", [(j, home)]) for j in range(2, home)] + [own]
+        box["cols"] = box["blocks"] + [lax.all_gather(col, "prow") for col in cols]
+        box["inv"] = lax.all_gather(below, "prow")
+        box["res"] = lax.all_gather(residual[0:1], "prow", tiled=True)
+
+    def make_factors():
+        box["v"] = factors(chain, where, box["bands"], box["blocks"], upper_inv, lower_inv, groups)
+
+    def solve():
+        state = solve_all(chain, where[1:2], box["res"], box["inv"], box["cols"])
+        box["state"] = lax.all_gather(state, "pcol")[home]
+
+    def updates(*which):
+        def run():
+            for c in which:
+                box["out"] = update(chain, flat, [mine[c]], [other[c]], box["v"], box["out"], starts[c], groups)
+
+        return run
+
+    plan = {0: [swap_bands], 1: [gather_blocks]}
+    if chunks == 6:
+        plan[2] = [gather_rest, make_factors, updates(0)]
+        plan[3] = [updates(1)]
+        plan[4] = [updates(2), solve]
+        plan[5] = [updates(3)]
     else:
-        plan = {0: total, slots - 1: [blocks_out, blocks_swap, make_factors] + line}
-        tail = [updates(c) for c in range(chunks - 2)]
-        line = []
+        plan[chunks - 1] = plan.pop(chunks - 1, []) + [gather_rest, make_factors, solve, updates(*range(chunks - 2))]
 
     for k in range(chunks):
-        ahead = [column[k + 2]] if k + 2 < chunks else []
+        ahead = [column[k + 1]] if k + 1 < chunks else []
         got = chain.gate([first[k], *ahead], [])
         first[k] = got[0] if ahead else got
+        if ahead:
+            column[k + 1] = got[1]
+            first[k + 1] = first_stage(column[k + 1])
         outward[k] = second_stage(first[k])
-        if ahead:
-            column[k + 2] = got[1]
-            first[k + 2] = first_stage(column[k + 2])
         if k:
             take(k - 1)
         for task in plan.get(k, []):
             task()
-    for task in tail:
-        task()
     updates(chunks - 2)()
     take(chunks - 1)
-    if line:
-        line[-1]()
     updates(chunks - 1)()
-    residual, out, state = box["residual"], box["out"], box["state"]
+    out, state = box["out"], box["state"]
     updated = out.reshape(rows, lane_tiles, col_slots, LANES).transpose(0, 2, 1, 3).reshape(matrix.shape)
     return (updated, residual.reshape(right_side.shape), state)
 

time: 264 us -> 400 us (1.52)
  blocking collectives: 0 us -> 138 us
  starting transfers between devices: 111 us -> 48.9 us
  waiting for transfers between devices: 30.2 us -> 81.6 us
  between operations: 1.32 us -> 14.2 us
  Pallas kernels: 106 us -> 97.6 us
    all_gather x0 -> x3, blocking collectives: none -> 138 us  [the longest x1 102 us: shards(): lax.all_gather(partial, 'pcol')]
    ppermute x9 -> x6, starting transfers between devices: 57.9 us -> 26.3 us  [first_stage(): return lax.ppermute(local, 'pcol', along_z(stages[0][0]))]
    ppermute x2 -> x1, waiting for transfers between devices: 3.11 us -> 32.6 us  [spread(): values.append(lax.ppermute(values[-1], axis, pairs))]
    ppermute x9 -> x6, waiting for transfers between devices: 11.4 us -> 37.2 us  [first_stage(): return lax.ppermute(local, 'pcol', along_z(stages[0][0]))]
    ppermute x21 -> x8, starting transfers between devices: 25.2 us -> 9.03 us  [swap(): return lax.ppermute(value, axis, [(i, i ^ bit) for i in range(size)])]
    pallas_call x46 -> x23, Pallas kernels: 106 us -> 97.6 us  [__call__(): pl.pallas_call(body, in_specs=list(in_specs) + [anywhere] * n_dep, out_sp...]
    ppermute x3 -> x0, starting transfers between devices: 7.23 us -> none  [run(): lax.ppermute(box['state'], 'prow', [(i, i + 1) for i in range(n_prow - 1)])]
    ppermute x18 -> x12, starting transfers between devices: 17.2 us -> 11.9 us  [second_stage(): lax.ppermute(arrived, 'pcol', along_z(moves))]
  transfers between devices with their start and end apart: 53 -> 31, of which waited for: 10 -> 4; matrix products, arithmetic and copies ran while one was open for 1% -> 1% of each run, Pallas kernels for 37% -> 22%
where the time goes in v2:
time: 400 us; the launch traced here: 399 us
  blocking collectives  138 us (34%)
  Pallas kernels  97.6 us (24%)
  waiting for transfers between devices  81.6 us (20%)
  starting transfers between devices  48.9 us (12%)
  local copies, waits for them, and re-layouts  17.3 us (4%)
  between operations  14.2 us (4%)
    all_gather x1, blocking collectives, shards(): lax.all_gather(partial, 'pcol')  102 us
    pallas_call x23, Pallas kernels, __call__(): pl.pallas_call(body, in_specs=list(in_specs) + [anywhere] * n_dep, out_sp...  97.6 us
    ppermute x6, waiting for transfers between devices, first_stage(): return lax.ppermute(local, 'pcol', along_z(stages[0][0]))  37.2 us
    ppermute x1, waiting for transfers between devices, spread(): values.append(lax.ppermute(values[-1], axis, pairs))  32.6 us
    all_gather x1, blocking collectives, solve(): box['state'] = lax.all_gather(state, 'pcol')[home]  30.8 us
    ppermute x6, starting transfers between devices, first_stage(): return lax.ppermute(local, 'pcol', along_z(stages[0][0]))  26.3 us
    unnamed x50, local copies, waits for them, and re-layouts  16.7 us
    ppermute x12, starting transfers between devices, second_stage(): lax.ppermute(arrived, 'pcol', along_z(moves))  11.9 us
  transfers between devices with their start and end apart: 31, of which 4 were waited for; matrix products, arithmetic and copies ran while one was open for 1% of the time, Pallas kernels for 22%

profile of v2, /device:TPU:0, one launch (start us, length us, event | category | flops | bytes accessed | tf_op | source)
XLA Modules:
  0.0 398.6 jit_solution(573731641260758915)
XLA Ops:
  7.2 1.9 copy.60
  9.8 3.3 extract.2
  13.1 1.3 copy-done.15
  14.4 6.8 %collective-permute-start.3 = (bf16[512,512]{1,0:T(8,128)(2,1)}, bf16[512,512]{1,0:T(8,128)(2,1)}, u32[]{:S(2)}, u32[]{:S(2)}) collective-permute-start(bf16[512,512]{1,0:T(8,128)(2,1)} %get-tuple-element.62.refs_1_.refs_0_), channel_id=1, source_target_pairs={{0,4},{1,5},{8,12},{9,13},{16,20},{17,21},{24,28},{25,29}} | collective-permute-start | bytes 1572872 | tf_op jit(solution)/shard_map/ppermute | solution.py:440
  21.1 16.0 %extract.3 = (f32[1,3584]{1,0:T(1,128)S(1)}, bf16[1024,512]{1,0:T(8,128)(2,1)}, bf16[1024,512]{1,0:T(8,128)(2,1)S(1)}, bf16[1024,512]{1,0:T(8,128)(2,1)S(1)}, bf...) custom-call(bf16[65536,128]{1,0:T(8,128)(2,1)} %bitcast.41, ...), custom_call_target="tpu_custom_call" | custom-call | flops 29360128 | bytes 14680064 | tf_op jit(solution)/shard_map/extract/pallas_call | solution.py:32
  37.8 1.3 collective-permute-start.6
  39.2 1.5 collective-permute-start.4
  40.6 1.5 collective-permute-start.5
  42.1 19.7 %collective-permute-done.6.refs_0_ = bf16[1024,512]{1,0:T(8,128)(2,1)S(1)} collective-permute-done((bf16[1024,512]{1,0:T(8,128)(2,1)}, bf16[1024,512]{1,0:T(8,128)(2,1)S(1)}, u32[]{:S(2)}, u32[]{:S(2)}) %collective-permute-start.6) | collective-permute-done | bytes 1048608 | tf_op jit(solution)/shard_map/ppermute | solution.py:440
  61.8 1.1 choose.6
  62.9 0.8 copy-done.3
  63.8 1.6 collective-permute-start.7
  65.4 11.6 %collective-permute-done.7.refs_3_ = bf16[512,512]{1,0:T(8,128)(2,1)} collective-permute-done((bf16[512,512]{1,0:T(8,128)(2,1)}, bf16[512,512]{1,0:T(8,128)(2,1)}, u32[]{:S(2)}, u32[]{:S(2)}) %collective-permute-start.7) | collective-permute-done | bytes 524320 | tf_op jit(solution)/shard_map/ppermute | solution.py:421
  77.0 5.2 %collective-permute-start.10 = (bf16[1024,512]{1,0:T(8,128)(2,1)S(1)}, bf16[1024,512]{1,0:T(8,128)(2,1)S(1)}, u32[]{:S(2)}, u32[]{:S(2)}) collective-permute-start(bf16[1024,512]{1,0:T(8,128)(2,1)S(1)} %get-tuple-element.73.refs_1_), channel_id=1, source_target_pairs={{0,4},{1,5},{8,12},{9,13},{16,20},{17,21},{24,28},{25,29}} | collective-permute-start | bytes 3145736 | tf_op jit(solution)/shard_map/ppermute | solution.py:440
  82.3 0.7 collective-permute-start.8
  83.7 1.6 collective-permute-start.1
  85.3 17.5 %collective-permute-done.10.refs_0_ = bf16[1024,512]{1,0:T(8,128)(2,1)S(1)} collective-permute-done((bf16[1024,512]{1,0:T(8,128)(2,1)S(1)}, bf16[1024,512]{1,0:T(8,128)(2,1)S(1)}, u32[]{:S(2)}, u32[]{:S(2)}) %collective-permute-start.10) | collective-permute-done | bytes 1048608 | tf_op jit(solution)/shard_map/ppermute | solution.py:440
  102.8 1.0 copy-done
  103.8 1.0 copy-done.20
  105.1 1.3 choose.7
  106.4 1.0 copy-done.5
  107.4 1.9 copy.48.refs_2_
  109.5 32.6 %collective-permute-done.1.refs_3_ = bf16[8192,128]{1,0:T(8,128)(2,1)} collective-permute-done((bf16[8192,128]{1,0:T(8,128)(2,1)}, bf16[8192,128]{1,0:T(8,128)(2,1)}, u32[]{:S(2)}, u32[]{:S(2)}) %collective-permute-start.1) | collective-permute-done | bytes 2097184 | tf_op jit(solution)/shard_map/ppermute | solution.py:417
  142.2 4.4 %collective-permute-start.11 = (bf16[1024,512]{1,0:T(8,128)(2,1)S(1)}, bf16[1024,512]{1,0:T(8,128)(2,1)S(1)}, u32[]{:S(2)}, u32[]{:S(2)}) collective-permute-start(bf16[1024,512]{1,0:T(8,128)(2,1)S(1)} %get-tuple-element.80.refs_1_), channel_id=1, source_target_pairs={{0,4},{1,5},{8,12},{9,13},{16,20},{17,21},{24,28},{25,29}} | collective-permute-start | bytes 3145736 | tf_op jit(solution)/shard_map/ppermute | solution.py:440
  146.7 1.7 collective-permute-start.14
  148.3 1.7 collective-permute-start.15
  150.0 1.5 collective-permute-start.13
  151.5 1.2 copy-done.16
  152.7 1.2 copy-done.17
  154.0 15.8 %factors.1 = (bf16[1024,2048]{1,0:T(8,128)(2,1)}, f32[8,128]{1,0:T(8,128)S(1)}) custom-call(s32[3]{0:T(128)S(1)} %pad_add_fusion.refs_0_, bf16[8192,128]{1,0:T(8,128)(2,1)} %copy-done.15, bf16[8192,128]{1,0:T(8,128)(2,1)} %collective-permute-done.refs_2_, bf16[8192,128]{1,0:T(8,128)(2,1)} %collective-permute-done.1.refs_3_, ...), custom_call_target="tpu_custom_call" | custom-call | flops 6442450944 | bytes 12582912 | tf_op jit(solution)/shard_map/factors/pallas_call | solution.py:32
  169.8 7.4 %update.6 = (bf16[65536,128]{1,0:T(8,128)(2,1)}, f32[8,128]{1,0:T(8,128)S(1)}) custom-call(bf16[65536,128]{1,0:T(8,128)(2,1)} %bitcast.42, bf16[1024,2048]{1,0:T(8,128)(2,1)} %get-tuple-element.79.refs_1_, bf16[512,512]{1,0:T(8,128)(2,1)S(1)} %copy-done.4, bf16[512,512]{1,0:T(8,128)(2,1)} %collective-permute-done.7.refs_3_, ...), custom_call_target="tpu_custom_call" | custom-call | flops 2147483648 | bytes 5242880 | tf_op jit(solution)/shard_map/update/pallas_call | solution.py:32
  178.7 1.0 choose.8
  180.4 4.1 %collective-permute-start.12 = (bf16[256,512]{1,0:T(8,128)(2,1)S(1)}, bf16[256,512]{1,0:T(8,128)(2,1)S(1)}, u32[]{:S(2)}, u32[]{:S(2)}) collective-permute-start(bf16[256,512]{1,0:T(8,128)(2,1)S(1)} %get-tuple-element.84.refs_1_), channel_id=1, source_target_pairs={{0,4},{1,5},{8,12},{9,13},{16,20},{17,21},{24,28},{25,29}} | collective-permute-start | bytes 786440 | tf_op jit(solution)/shard_map/ppermute | solution.py:440
  184.5 11.3 %update.7 = (bf16[65536,128]{1,0:T(8,128)(2,1)}, f32[8,128]{1,0:T(8,128)S(1)}) custom-call(bf16[65536,128]{1,0:T(8,128)(2,1)} %bitcast.43, bf16[1024,2048]{1,0:T(8,128)(2,1)} %get-tuple-element.79.refs_1_, bf16[1024,512]{1,0:T(8,128)(2,1)S(1)} %copy-done.6, bf16[1024,512]{1,0:T(8,128)(2,1)} %collective-permute-done.13.refs_3_, ...), custom_call_target="tpu_custom_call", output_to_operand_aliasing={{0}: (4, {})} | custom-call | flops 4294967296 | bytes 10485760 | tf_op jit(solution)/shard_map/update/pallas_call | solution.py:32
  196.5 1.0 copy-done.18
  197.8 1.0 choose.9
  198.9 1.2 collective-permute-start.25
  200.1 102.2 %all_gather.40 = f32[8,8,512]{2,1,0:T(8,128)S(1)} all-gather(f32[1,8,512]{2,1,0:T(8,128)S(1)} %all_gather_reshape.3), channel_id=1, replica_groups=mesh['prow'=4,'pcol'=8] {'pcol'}, dimensions={0}, use_global_device_ids=true | all-gather | bytes 147456 | tf_op jit(solution)/shard_map/all_gather | solution.py:480
  302.4 5.2 %all-gather.5 = f32[4,1,512]{2,1,0:T(1,128)S(1)} all-gather(f32[1,1,512]{2,1,0:T(1,128)S(1)} %fusion), channel_id=1, replica_groups=mesh['prow'=4,'pcol'=8] {'prow'}, dimensions={0}, use_global_device_ids=true | all-gather | bytes 10240 | tf_op jit(solution)/shard_map/all_gather | solution.py:497
  308.9 4.5 %collective-permute-start.16 = (bf16[256,512]{1,0:T(8,128)(2,1)}, bf16[256,512]{1,0:T(8,128)(2,1)S(1)}, u32[]{:S(2)}, u32[]{:S(2)}) collective-permute-start(bf16[256,512]{1,0:T(8,128)(2,1)} %copy-done.9), channel_id=1, source_target_pairs={{0,4},{1,5},{8,12},{9,13},{16,20},{17,21},{24,28},{25,29}} | collective-permute-start | bytes 786440 | tf_op jit(solution)/shard_map/ppermute | solution.py:440
  313.4 11.4 %update.8 = (bf16[65536,128]{1,0:T(8,128)(2,1)}, f32[8,128]{1,0:T(8,128)S(1)}) custom-call(bf16[65536,128]{1,0:T(8,128)(2,1)} %bitcast.44, bf16[1024,2048]{1,0:T(8,128)(2,1)} %get-tuple-element.79.refs_1_, bf16[1024,512]{1,0:T(8,128)(2,1)} %get-tuple-element.97.refs_2_, ...), custom_call_target="tpu_custom_call", output_to_operand_aliasing={{0}: (4, {})} | custom-call | flops 4294967296 | bytes 10485760 | tf_op jit(solution)/shard_map/update/pallas_call | solution.py:32
  324.8 1.6 copy-done.2
  326.4 5.9 %solve.1 = (f32[4,512]{1,0:T(4,128)S(1)}, f32[8,128]{1,0:T(8,128)S(1)}) custom-call(s32[1]{0:T(128)} %bitcast.4.refs_0_, f32[4,512]{1,0:T(4,128)S(1)} %bitcast.36, bf16[4,512,512]{2,1,0:T(8,128)(2,1)S(1)} %bitcast.35, bf16[4,512,512]{2,1,0:T(8,128)(2,1)} %bitcast.51, bf16[4,512,512]{2,1,0:T(8,128)(2,1)} %bitcast.53, bf16[4,512,512]{2,1,0:T(8,128)(2,1)} %bitcast.54, ...), custom_call_target="tpu_custom_call" | custom-call | flops 12582912 | bytes 8388608 | tf_op jit(solution)/shard_map/solve/pallas_call | solution.py:32
  333.9 3.9 collective-permute-start.24
  337.8 11.2 %update.9 = (bf16[65536,128]{1,0:T(8,128)(2,1)}, f32[8,128]{1,0:T(8,128)S(1)}) custom-call(bf16[65536,128]{1,0:T(8,128)(2,1)} %bitcast.45, bf16[1024,2048]{1,0:T(8,128)(2,1)} %get-tuple-element.79.refs_1_, bf16[1024,512]{1,0:T(8,128)(2,1)} %get-tuple-element.108.refs_2_, ...), custom_call_target="tpu_custom_call", output_to_operand_aliasing={{0}: (4, {})} | custom-call | flops 4294967296 | bytes 10485760 | tf_op jit(solution)/shard_map/update/pallas_call | solution.py:32
  349.0 5.5 %update.10 = (bf16[65536,128]{1,0:T(8,128)(2,1)}, f32[8,128]{1,0:T(8,128)S(1)}) custom-call(bf16[65536,128]{1,0:T(8,128)(2,1)} %bitcast.46, bf16[1024,2048]{1,0:T(8,128)(2,1)} %get-tuple-element.79.refs_1_, bf16[256,512]{1,0:T(8,128)(2,1)S(1)} %get-tuple-element.107.refs_2_, ...), custom_call_target="tpu_custom_call", output_to_operand_aliasing={{0}: (4, {})} | custom-call | flops 1073741824 | bytes 2621440 | tf_op jit(solution)/shard_map/update/pallas_call | solution.py:32
  355.3 30.8 %all-gather.6 = f32[8,4,512]{2,1,0:T(4,128)S(1)} all-gather(f32[1,4,512]{2,1,0:T(4,128)S(1)} %bitcast.39), channel_id=6, replica_groups=mesh['prow'=4,'pcol'=8] {'pcol'}, dimensions={0}, use_global_device_ids=true | all-gather | bytes 73728 | tf_op jit(solution)/shard_map/all_gather | solution.py:504
  386.7 5.4 %update.11 = (bf16[65536,128]{1,0:T(8,128)(2,1)}, f32[8,128]{1,0:T(8,128)}) custom-call(bf16[65536,128]{1,0:T(8,128)(2,1)} %bitcast.47, bf16[1024,2048]{1,0:T(8,128)(2,1)} %get-tuple-element.79.refs_1_, bf16[256,512]{1,0:T(8,128)(2,1)S(1)} %get-tuple-element.114.refs_2_, ...), custom_call_target="tpu_custom_call", output_to_operand_aliasing={{0}: (4, {})} | custom-call | flops 1073741824 | bytes 2621440 | tf_op jit(solution)/shard_map/update/pallas_call | solution.py:32
  (101 shorter events, 10.4 us)
Async XLA Ops:
  7.2 100.2 %all-gather.12.cloned.1.call-start = ((), (), s32[]{:S(2)}) async-start(), calls=%async_computation | async-start | bytes 2621440 | tf_op jit(solution)/shard_map/all_gather | solution.py:490
  9.8 11.4 %copy-start.14 = (bf16[4,1,512]{2,0,1:T(4,128)(2,1)S(1)}, bf16[4,1,512]{2,0,1:T(4,128)(2,1)}, u32[]{:S(2)}) copy-start(bf16[4,1,512]{2,0,1:T(4,128)(2,1)} %param.9) | copy-start | bytes 12292
  13.1 1.3 copy-start.15
  14.4 23.4 %collective-permute-start.3 = (bf16[512,512]{1,0:T(8,128)(2,1)}, bf16[512,512]{1,0:T(8,128)(2,1)}, u32[]{:S(2)}, u32[]{:S(2)}) collective-permute-start(bf16[512,512]{1,0:T(8,128)(2,1)} %get-tuple-element.62.refs_1_.refs_0_), channel_id=1, source_target_pairs={{0,4},{1,5},{8,12},{9,13},{16,20},{17,21},{24,28},{25,29}} | collective-permute-start | bytes 1572872 | tf_op jit(solution)/shard_map/ppermute | solution.py:440
  37.8 24.0 %collective-permute-start.6 = (bf16[1024,512]{1,0:T(8,128)(2,1)}, bf16[1024,512]{1,0:T(8,128)(2,1)S(1)}, u32[]{:S(2)}, u32[]{:S(2)}) collective-permute-start(bf16[1024,512]{1,0:T(8,128)(2,1)} %get-tuple-element.67.refs_1_), channel_id=1, source_target_pairs={{0,4},{1,5},{8,12},{9,13},{16,20},{17,21},{24,28},{25,29}} | collective-permute-start | bytes 3145736 | tf_op jit(solution)/shard_map/ppermute | solution.py:440
  39.2 22.7 %collective-permute-start.4 = (bf16[512,512]{1,0:T(8,128)(2,1)}, bf16[512,512]{1,0:T(8,128)(2,1)}, u32[]{:S(2)}, u32[]{:S(2)}) collective-permute-start(bf16[512,512]{1,0:T(8,128)(2,1)} %get-tuple-element.66.refs_2_), channel_id=1, source_target_pairs={{4,2},{5,3},{12,10},{13,11},{20,18},{21,19},{28,26},{29,27}} | collective-permute-start | bytes 1572872 | tf_op jit(solution)/shard_map/ppermute | solution.py:443
  40.6 21.2 %collective-permute-start.5 = (bf16[512,512]{1,0:T(8,128)(2,1)}, bf16[512,512]{1,0:T(8,128)(2,1)}, u32[]{:S(2)}, u32[]{:S(2)}) collective-permute-start(bf16[512,512]{1,0:T(8,128)(2,1)} %get-tuple-element.66.refs_2_), channel_id=1, source_target_pairs={{4,6},{5,7},{12,14},{13,15},{20,22},{21,23},{28,30},{29,31}} | collective-permute-start | bytes 1572872 | tf_op jit(solution)/shard_map/ppermute | solution.py:443
  63.7 87.8 %all-gather.14.cloned.1.call-start = ((), (), s32[]{:S(2)}) async-start(), calls=%async_computation.1 | async-start | bytes 2621440 | tf_op jit(solution)/shard_map/all_gather | solution.py:490
  63.8 13.2 %collective-permute-start.7 = (bf16[512,512]{1,0:T(8,128)(2,1)}, bf16[512,512]{1,0:T(8,128)(2,1)}, u32[]{:S(2)}, u32[]{:S(2)}) collective-permute-start(bf16[512,512]{1,0:T(8,128)(2,1)} %copy-done.3), channel_id=1, source_target_pairs={{0,1},{1,0},{2,3},{3,2},{4,5},{5,4},{6,7},{7,6},{8,9},{9,8},{10,11... | collective-permute-start | bytes 1572872 | tf_op jit(solution)/shard_map/ppermute | solution.py:421
  77.0 247.9 %all-gather.16.cloned.1.call-start = ((), (), s32[]{:S(2)}) async-start(), calls=%async_computation.2 | async-start | bytes 2621440 | tf_op jit(solution)/shard_map/all_gather | solution.py:496
  77.0 25.8 %collective-permute-start.10 = (bf16[1024,512]{1,0:T(8,128)(2,1)S(1)}, bf16[1024,512]{1,0:T(8,128)(2,1)S(1)}, u32[]{:S(2)}, u32[]{:S(2)}) collective-permute-start(bf16[1024,512]{1,0:T(8,128)(2,1)S(1)} %get-tuple-element.73.refs_1_), channel_id=1, source_target_pairs={{0,4},{1,5},{8,12},{9,13},{16,20},{17,21},{24,28},{25,29}} | collective-permute-start | bytes 3145736 | tf_op jit(solution)/shard_map/ppermute | solution.py:440
  82.3 21.6 %collective-permute-start.8 = (bf16[1024,512]{1,0:T(8,128)(2,1)S(1)}, bf16[1024,512]{1,0:T(8,128)(2,1)S(1)}, u32[]{:S(2)}, u32[]{:S(2)}) collective-permute-start(bf16[1024,512]{1,0:T(8,128)(2,1)S(1)} %get-tuple-element.72.refs_2_), channel_id=1, source_target_pairs={{4,2},{5,3},{12,10},{13,11},{20,18},{21,19},{28,26},{29,27}} | collective-permute-start | bytes 3145736 | tf_op jit(solution)/shard_map/ppermute | solution.py:443
  83.0 20.8 %collective-permute-start.9 = (bf16[1024,512]{1,0:T(8,128)(2,1)S(1)}, bf16[1024,512]{1,0:T(8,128)(2,1)S(1)}, u32[]{:S(2)}, u32[]{:S(2)}) collective-permute-start(bf16[1024,512]{1,0:T(8,128)(2,1)S(1)} %get-tuple-element.72.refs_2_), channel_id=1, source_target_pairs={{4,6},{5,7},{12,14},{13,15},{20,22},{21,23},{28,30},{29,31}} | collective-permute-start | bytes 3145736 | tf_op jit(solution)/shard_map/ppermute | solution.py:443
  83.7 58.4 %collective-permute-start.1 = (bf16[8192,128]{1,0:T(8,128)(2,1)}, bf16[8192,128]{1,0:T(8,128)(2,1)}, u32[]{:S(2)}, u32[]{:S(2)}) collective-permute-start(bf16[8192,128]{1,0:T(8,128)(2,1)} %copy-done.15), channel_id=1, source_target_pairs={{0,16},{8,24},{16,0},{24,8},{1,17},{9,25},{17,1},{25,9},{2,18},{10... | collective-permute-start | bytes 6291464 | tf_op jit(solution)/shard_map/ppermute | solution.py:417
  102.8 1.0 copy-start
  103.8 1.3 copy-start.21
  109.4 215.5 %all-gather.18.cloned.1.call-start = ((), (), s32[]{:S(2)}) async-start(), calls=%async_computation.3 | async-start | bytes 2621440 | tf_op jit(solution)/shard_map/all_gather | solution.py:495
  109.4 40.6 %collective-permute-start = (bf16[8192,128]{1,0:T(8,128)(2,1)}, bf16[8192,128]{1,0:T(8,128)(2,1)}, u32[]{:S(2)}, u32[]{:S(2)}) collective-permute-start(bf16[8192,128]{1,0:T(8,128)(2,1)} %copy-done.15), channel_id=1, source_target_pairs={{0,8},{8,0},{16,24},{24,16},{1,9},{9,1},{17,25},{25,17},{2,10},{10... | collective-permute-start | bytes 6291464 | tf_op jit(solution)/shard_map/ppermute | solution.py:421
  142.1 9.4 %collective-permute-start.2 = (bf16[8192,128]{1,0:T(8,128)(2,1)}, bf16[8192,128]{1,0:T(8,128)(2,1)}, u32[]{:S(2)}, u32[]{:S(2)}) collective-permute-start(bf16[8192,128]{1,0:T(8,128)(2,1)} %collective-permute-done.1.refs_3_), channel_id=1, source_target_pairs={{0,8},{8,0},{16,24},{24,16},{1,9},{9,1},{17,25},{25,17},{2,10},{10... | collective-permute-start | bytes 6291464 | tf_op jit(solution)/shard_map/ppermute | solution.py:421
  142.2 35.0 %collective-permute-start.11 = (bf16[1024,512]{1,0:T(8,128)(2,1)S(1)}, bf16[1024,512]{1,0:T(8,128)(2,1)S(1)}, u32[]{:S(2)}, u32[]{:S(2)}) collective-permute-start(bf16[1024,512]{1,0:T(8,128)(2,1)S(1)} %get-tuple-element.80.refs_1_), channel_id=1, source_target_pairs={{0,4},{1,5},{8,12},{9,13},{16,20},{17,21},{24,28},{25,29}} | collective-permute-start | bytes 3145736 | tf_op jit(solution)/shard_map/ppermute | solution.py:440
  146.7 32.0 %collective-permute-start.14 = (bf16[1024,512]{1,0:T(8,128)(2,1)}, bf16[1024,512]{1,0:T(8,128)(2,1)}, u32[]{:S(2)}, u32[]{:S(2)}) collective-permute-start(bf16[1024,512]{1,0:T(8,128)(2,1)} %copy-done), channel_id=1, source_target_pairs={{4,2},{5,3},{12,10},{13,11},{20,18},{21,19},{28,26},{29,27}} | collective-permute-start | bytes 3145736 | tf_op jit(solution)/shard_map/ppermute | solution.py:443
  148.3 30.4 %collective-permute-start.15 = (bf16[1024,512]{1,0:T(8,128)(2,1)}, bf16[1024,512]{1,0:T(8,128)(2,1)}, u32[]{:S(2)}, u32[]{:S(2)}) collective-permute-start(bf16[1024,512]{1,0:T(8,128)(2,1)} %copy-done), channel_id=1, source_target_pairs={{4,6},{5,7},{12,14},{13,15},{20,22},{21,23},{28,30},{29,31}} | collective-permute-start | bytes 3145736 | tf_op jit(solution)/shard_map/ppermute | solution.py:443
  150.0 34.4 %collective-permute-start.13 = (bf16[1024,512]{1,0:T(8,128)(2,1)}, bf16[1024,512]{1,0:T(8,128)(2,1)}, u32[]{:S(2)}, u32[]{:S(2)}) collective-permute-start(bf16[1024,512]{1,0:T(8,128)(2,1)} %copy-done.5), channel_id=1, source_target_pairs={{0,1},{1,0},{2,3},{3,2},{4,5},{5,4},{6,7},{7,6},{8,9},{9,8},{10,11... | collective-permute-start | bytes 3145736 | tf_op jit(solution)/shard_map/ppermute | solution.py:421
  151.5 1.2 copy-start.16
  152.7 1.2 copy-start.17
  154.0 15.8 %copy-start.4 = (bf16[512,512]{1,0:T(8,128)(2,1)S(1)}, bf16[512,512]{1,0:T(8,128)(2,1)}, u32[]{:S(2)}) copy-start(bf16[512,512]{1,0:T(8,128)(2,1)} %copy-done.3) | copy-start | bytes 1572868
  169.8 8.9 %copy-start.1 = (bf16[1024,512]{1,0:T(8,128)(2,1)S(1)}, bf16[1024,512]{1,0:T(8,128)(2,1)}, u32[]{:S(2)}) copy-start(bf16[1024,512]{1,0:T(8,128)(2,1)} %copy-done) | copy-start | bytes 3145732
  177.2 19.3 %collective-permute-start.18 = (bf16[1024,512]{1,0:T(8,128)(2,1)S(1)}, bf16[1024,512]{1,0:T(8,128)(2,1)S(1)}, u32[]{:S(2)}, u32[]{:S(2)}) collective-permute-start(bf16[1024,512]{1,0:T(8,128)(2,1)S(1)} %get-tuple-element.99.refs_2_), channel_id=1, source_target_pairs={{4,2},{5,3},{12,10},{13,11},{20,18},{21,19},{28,26},{29,27}} | collective-permute-start | bytes 3145736 | tf_op jit(solution)/shard_map/ppermute | solution.py:443
  177.9 18.5 %collective-permute-start.19 = (bf16[1024,512]{1,0:T(8,128)(2,1)S(1)}, bf16[1024,512]{1,0:T(8,128)(2,1)S(1)}, u32[]{:S(2)}, u32[]{:S(2)}) collective-permute-start(bf16[1024,512]{1,0:T(8,128)(2,1)S(1)} %get-tuple-element.99.refs_2_), channel_id=1, source_target_pairs={{4,6},{5,7},{12,14},{13,15},{20,22},{21,23},{28,30},{29,31}} | collective-permute-start | bytes 3145736 | tf_op jit(solution)/shard_map/ppermute | solution.py:443
  178.7 5.8 %copy-start.6 = (bf16[1024,512]{1,0:T(8,128)(2,1)S(1)}, bf16[1024,512]{1,0:T(8,128)(2,1)}, u32[]{:S(2)}) copy-start(bf16[1024,512]{1,0:T(8,128)(2,1)} %copy-done.5) | copy-start | bytes 3145732
  179.7 133.7 %collective-permute-start.17 = (bf16[1024,512]{1,0:T(8,128)(2,1)}, bf16[1024,512]{1,0:T(8,128)(2,1)}, u32[]{:S(2)}, u32[]{:S(2)}) collective-permute-start(bf16[1024,512]{1,0:T(8,128)(2,1)} %get-tuple-element.97.refs_2_), channel_id=1, source_target_pairs={{0,1},{1,0},{2,3},{3,2},{4,5},{5,4},{6,7},{7,6},{8,9},{9,8},{10,11... | collective-permute-start | bytes 3145736 | tf_op jit(solution)/shard_map/ppermute | solution.py:421
  180.4 15.4 %collective-permute-start.12 = (bf16[256,512]{1,0:T(8,128)(2,1)S(1)}, bf16[256,512]{1,0:T(8,128)(2,1)S(1)}, u32[]{:S(2)}, u32[]{:S(2)}) collective-permute-start(bf16[256,512]{1,0:T(8,128)(2,1)S(1)} %get-tuple-element.84.refs_1_), channel_id=1, source_target_pairs={{0,4},{1,5},{8,12},{9,13},{16,20},{17,21},{24,28},{25,29}} | collective-permute-start | bytes 786440 | tf_op jit(solution)/shard_map/ppermute | solution.py:440
  184.5 11.3 %copy-start.8 = (bf16[256,512]{1,0:T(8,128)(2,1)S(1)}, bf16[256,512]{1,0:T(8,128)(2,1)}, u32[]{:S(2)}) copy-start(bf16[256,512]{1,0:T(8,128)(2,1)} %copy-done.7) | copy-start | bytes 786436
  196.5 2.4 copy-start.11
  196.5 1.0 copy-start.18
  196.5 1.3 copy-start.19
  197.8 2.3 copy-start.22
  198.9 138.9 %collective-permute-start.25 = (bf16[1024,512]{1,0:T(8,128)(2,1)}, bf16[1024,512]{1,0:T(8,128)(2,1)S(1)}, u32[]{:S(2)}, u32[]{:S(2)}) collective-permute-start(bf16[1024,512]{1,0:T(8,128)(2,1)} %get-tuple-element.108.refs_2_), channel_id=1, source_target_pairs={{0,1},{1,0},{2,3},{3,2},{4,5},{5,4},{6,7},{7,6},{8,9},{9,8},{10,11... | collective-permute-start | bytes 3145736 | tf_op jit(solution)/shard_map/ppermute | solution.py:421
  307.5 26.2 %collective-permute-start.22 = (bf16[256,512]{1,0:T(8,128)(2,1)}, bf16[256,512]{1,0:T(8,128)(2,1)S(1)}, u32[]{:S(2)}, u32[]{:S(2)}) collective-permute-start(bf16[256,512]{1,0:T(8,128)(2,1)} %copy-done.11), channel_id=1, source_target_pairs={{4,2},{5,3},{12,10},{13,11},{20,18},{21,19},{28,26},{29,27}} | collective-permute-start | bytes 786440 | tf_op jit(solution)/shard_map/ppermute | solution.py:443
  308.2 25.6 %collective-permute-start.23 = (bf16[256,512]{1,0:T(8,128)(2,1)}, bf16[256,512]{1,0:T(8,128)(2,1)S(1)}, u32[]{:S(2)}, u32[]{:S(2)}) collective-permute-start(bf16[256,512]{1,0:T(8,128)(2,1)} %copy-done.11), channel_id=1, source_target_pairs={{4,6},{5,7},{12,14},{13,15},{20,22},{21,23},{28,30},{29,31}} | collective-permute-start | bytes 786440 | tf_op jit(solution)/shard_map/ppermute | solution.py:443
  308.9 23.5 %collective-permute-start.16 = (bf16[256,512]{1,0:T(8,128)(2,1)}, bf16[256,512]{1,0:T(8,128)(2,1)S(1)}, u32[]{:S(2)}, u32[]{:S(2)}) collective-permute-start(bf16[256,512]{1,0:T(8,128)(2,1)} %copy-done.9), channel_id=1, source_target_pairs={{0,4},{1,5},{8,12},{9,13},{16,20},{17,21},{24,28},{25,29}} | collective-permute-start | bytes 786440 | tf_op jit(solution)/shard_map/ppermute | solution.py:440
  324.8 1.6 copy-start.2
  326.4 7.3 %copy-start.12 = (bf16[256,512]{1,0:T(8,128)(2,1)S(1)}, bf16[256,512]{1,0:T(8,128)(2,1)}, u32[]{:S(2)}) copy-start(bf16[256,512]{1,0:T(8,128)(2,1)} %copy-done.11) | copy-start | bytes 786436
  332.4 22.1 %collective-permute-start.20 = (bf16[256,512]{1,0:T(8,128)(2,1)S(1)}, bf16[256,512]{1,0:T(8,128)(2,1)S(1)}, u32[]{:S(2)}, u32[]{:S(2)}) collective-permute-start(bf16[256,512]{1,0:T(8,128)(2,1)S(1)} %get-tuple-element.104.refs_2_), channel_id=1, source_target_pairs={{4,2},{5,3},{12,10},{13,11},{20,18},{21,19},{28,26},{29,27}} | collective-permute-start | bytes 786440 | tf_op jit(solution)/shard_map/ppermute | solution.py:443
  333.1 21.4 %collective-permute-start.21 = (bf16[256,512]{1,0:T(8,128)(2,1)S(1)}, bf16[256,512]{1,0:T(8,128)(2,1)S(1)}, u32[]{:S(2)}, u32[]{:S(2)}) collective-permute-start(bf16[256,512]{1,0:T(8,128)(2,1)S(1)} %get-tuple-element.104.refs_2_), channel_id=1, source_target_pairs={{4,6},{5,7},{12,14},{13,15},{20,22},{21,23},{28,30},{29,31}} | collective-permute-start | bytes 786440 | tf_op jit(solution)/shard_map/ppermute | solution.py:443
  333.9 15.1 %collective-permute-start.24 = (bf16[256,512]{1,0:T(8,128)(2,1)S(1)}, bf16[256,512]{1,0:T(8,128)(2,1)S(1)}, u32[]{:S(2)}, u32[]{:S(2)}) collective-permute-start(bf16[256,512]{1,0:T(8,128)(2,1)S(1)} %get-tuple-element.107.refs_2_), channel_id=1, source_target_pairs={{0,1},{1,0},{2,3},{3,2},{4,5},{5,4},{6,7},{7,6},{8,9},{9,8},{10,11... | collective-permute-start | bytes 786440 | tf_op jit(solution)/shard_map/ppermute | solution.py:421
  349.0 5.5 %copy-start.10 = (bf16[256,512]{1,0:T(8,128)(2,1)S(1)}, bf16[256,512]{1,0:T(8,128)(2,1)}, u32[]{:S(2)}) copy-start(bf16[256,512]{1,0:T(8,128)(2,1)} %copy-done.9) | copy-start | bytes 786436
  354.6 32.1 %collective-permute-start.26 = (bf16[256,512]{1,0:T(8,128)(2,1)S(1)}, bf16[256,512]{1,0:T(8,128)(2,1)S(1)}, u32[]{:S(2)}, u32[]{:S(2)}) collective-permute-start(bf16[256,512]{1,0:T(8,128)(2,1)S(1)} %get-tuple-element.114.refs_2_), channel_id=1, source_target_pairs={{0,1},{1,0},{2,3},{3,2},{4,5},{5,4},{6,7},{7,6},{8,9},{9,8},{10,11... | collective-permute-start | bytes 786440 | tf_op jit(solution)/shard_map/ppermute | solution.py:421
  (6 other events, 4.9 us)
Sparse Core Ops, SparseCore 0:
  63.8 24.3 all-gather.11
  89.8 44.3 all-gather.13
  135.8 22.5 all-gather.15
  159.8 22.5 all-gather.17

commit v3 on v1

--- a/solution.py
+++ b/solution.py
@@ -82,7 +82,7 @@
             [index, *values],
             [pl.BlockSpec(memory_space=pltpu.SMEM)] + [anywhere] * len(values),
             [jax.ShapeDtypeStruct(value.shape, value.dtype)],
-            [anywhere],
+            [pl.BlockSpec(memory_space=pltpu.VMEM)],
             "choose",
             (0, 4 * value.size),
             scratch=[pltpu.SemaphoreType.DMA],
@@ -118,15 +118,21 @@
     return x[0]
 
 
-def extract_kernel(groups, stride, a_ref, sol_ref, col_ref, part_ref, *rest):
-    wide = rest[-1]
-    rows = col_ref.shape[0]
-    if len(rest) > 1:
-        rest[0][...] = a_ref[...]
+def extract_kernel(groups, stride, spans, a_ref, sol_ref, part_ref, *rest):
+    cols, wide = rest[: len(spans)], rest[-1]
+    rows = part_ref.shape[1]
+    if len(rest) > len(spans) + 1:
+        rest[len(spans)][...] = a_ref[...]
     wide[...] = a_ref[...].astype(F32)
-    for g in range(0, groups, stride):
-        piece = wide[pl.ds(g, rows, stride=groups), :]
-        col_ref[:, pl.ds(g // stride * LANES, LANES)] = piece.astype(BF16)
+    i = pl.program_id(0)
+    for col_ref, (start, stop) in zip(cols, spans):
+
+        @pl.when((i >= start) & (i < stop))
+        def _(col_ref=col_ref):
+            for g in range(0, groups, stride):
+                piece = wide[pl.ds(g, rows, stride=groups), :]
+                col_ref[:, pl.ds(g // stride * LANES, LANES)] = piece.astype(BF16)
+
     if groups % 16 == 0:
         sol = sol_ref[...].astype(F32)
         totals = []
@@ -150,23 +156,24 @@
     part_ref[...] = sums[0:1, :]
 
 
-def extract(chain, flat, sol, first, rows, groups, stride, width, with_band):
-    sub = min(rows, 128)
+def extract(chain, flat, sol, sizes, first, groups, stride, width, with_band):
+    sub = min(min(sizes), 256)
     size = sub * groups
     at = first // sub
-    out_specs = [
-        pl.BlockSpec((sub, width), lambda i: (i, 0)),
-        pl.BlockSpec((1, sub), lambda i: (0, i)),
-    ]
-    out_shape = [
-        jax.ShapeDtypeStruct((rows, width), BF16),
-        jax.ShapeDtypeStruct((1, rows), F32),
-    ]
+    rows = sum(sizes)
+    spans, out_specs, out_shape = [], [pl.BlockSpec((1, sub), lambda i: (0, i))], [jax.ShapeDtypeStruct((1, rows), F32)]
+    start = 0
+    for n in sizes:
+        stop = start + n // sub
+        spans.append((start, stop))
+        out_specs.append(pl.BlockSpec((sub, width), lambda i, a=start, b=stop: (jnp.clip(i - a, 0, b - a - 1), 0)))
+        out_shape.append(jax.ShapeDtypeStruct((n, width), BF16))
+        start = stop
     if with_band:
         out_specs.append(pl.BlockSpec((size, LANES), lambda i: (i, 0)))
         out_shape.append(jax.ShapeDtypeStruct((rows * groups, LANES), BF16))
     return chain(
-        lambda *refs: extract_kernel(groups, stride, *refs),
+        lambda *refs: extract_kernel(groups, stride, spans, *refs),
         [flat, sol],
         [
             pl.BlockSpec((size, LANES), lambda i: (at + i, 0)),
@@ -266,13 +273,13 @@
     )
 
 
-def update_kernel(groups, chunks, steps, a_ref, v_ref, *rest):
+def update_kernel(groups, spans, a_ref, v_ref, *rest):
     out_ref, both, *wide = rest[-3 if groups % 16 else -2 :]
     rows, width = both.shape[0], both.shape[1] // 2
     i = pl.program_id(0)
-    for c in range(chunks):
-
-        @pl.when(i // steps == c)
+    for c, (start, stop) in enumerate(spans):
+
+        @pl.when((i >= start) & (i < stop))
         def _(c=c):
             both[:, :width] = rest[2 * c][...]
             both[:, width:] = rest[2 * c + 1][...]
@@ -299,18 +306,19 @@
 
 
 def update(chain, flat, mine, other, v, out, first, groups):
-    rows, width = mine[0].shape
-    chunks = len(mine)
-    sub = min(rows, 256)
-    steps = rows // sub
+    rows, width = sum(m.shape[0] for m in mine), mine[0].shape[1]
+    sub = min(256, *(m.shape[0] for m in mine))
     size = sub * groups
     base = first // sub
     cols = groups * LANES
     in_specs = [pl.BlockSpec((size, LANES), lambda i: (base + i, 0)), pl.BlockSpec(memory_space=pltpu.VMEM)]
-    args = [flat, v]
-    for c in range(chunks):
-        args += [mine[c], other[c]]
-        in_specs += [pl.BlockSpec((sub, width), lambda i, c=c: (jnp.clip(i - c * steps, 0, steps - 1), 0))] * 2
+    args, spans, start = [flat, v], [], 0
+    for m, o in zip(mine, other):
+        stop = start + m.shape[0] // sub
+        args += [m, o]
+        in_specs += [pl.BlockSpec((sub, width), lambda i, a=start, b=stop: (jnp.clip(i - a, 0, b - a - 1), 0))] * 2
+        spans.append((start, stop))
+        start = stop
     aliases = {}
     if out is not None:
         aliases = {len(args): 0}
@@ -320,14 +328,14 @@
     if groups % 16:
         scratch.append(pltpu.VMEM((size, LANES), F32))
     return chain(
-        lambda *refs: update_kernel(groups, chunks, steps, *refs),
+        lambda *refs: update_kernel(groups, spans, *refs),
         args,
         in_specs,
         [jax.ShapeDtypeStruct(flat.shape, BF16)],
         [pl.BlockSpec((size, LANES), lambda i: (base + i, 0))],
         "update",
-        (4 * chunks * rows * width * cols, chunks * (4 * rows * cols + 4 * rows * width)),
-        grid=(chunks * steps,),
+        (4 * rows * width * cols, 4 * rows * cols + 4 * rows * width),
+        grid=(rows // sub,),
         scratch=scratch,
         aliases=aliases,
     )
@@ -448,26 +456,28 @@
     flag = jnp.where(core != lane, 0, 1).astype(jnp.int32).reshape(1)
     bits = [1 << b for b in range(n_pcol.bit_length() - 1)]
 
-    cuts = [(c * width, width) for c in range(slots - 1)]
-    cuts += [((slots - 1) * width + h * width // 2, width // 2) for h in range(2)]
-    chunks = len(cuts)
-    column, parts, first, outward, mine, other, box = {}, {}, {}, {}, {}, {}, {"out": None}
-    for c in [0, 2, 3, 1, *range(4, slots)]:
-        col, part, *band = extract(chain, flat, sol, c * width, width, groups, col_slots, width, c == 0)
-        parts[c] = part
-        if c < slots - 1:
-            column[c] = col
-        else:
-            column[c], column[c + 1] = col[: width // 2], col[width // 2 :]
-        if c < 2:
-            first[c] = first_stage(col)
-        if c == 0:
-            box["bands"] = spread(band[0], "prow", n_prow)
+    sizes = [width] + [2 * width] * ((slots - 2) // 2)
+    sizes += [width] * (slots - sum(sizes) // width)
+    starts = [sum(sizes[:c]) for c in range(len(sizes) + 1)]
+    chunks = len(sizes)
+    column, first, outward, mine, other, box = {}, {}, {}, {}, {}, {"out": None}
+
+    def extracts(a, b, with_band=False):
+        part, *cols = extract(chain, flat, sol, sizes[a:b], starts[a], groups, col_slots, width, with_band)
+        column.update(zip(range(a, b), cols))
+        return part, cols[-1]
+
+    parts = []
+    part, band = extracts(0, 1, True)
+    parts.append(part)
+    first[0] = first_stage(column[0])
+    box["bands"] = spread(band, "prow", n_prow)
+    parts.append(extracts(1, 2)[0])
 
     def total_step(bit):
         def run():
             if bit == 1:
-                box["total"] = jnp.concatenate([parts[c] for c in range(slots)], axis=0)
+                box["total"] = jnp.concatenate(parts, axis=1).reshape(slots, width)
             box["total"] = chain.add(box["total"], swap(box["total"], "pcol", n_pcol, bit))
             if bit == bits[-1]:
                 box["residual"] = right_side.reshape(slots, width) - box["total"]
@@ -510,7 +520,7 @@
     def updates(*which):
         def run():
             args = [mine[c] for c in which], [other[c] for c in which]
-            box["out"] = update(chain, flat, *args, box["v"], box["out"], cuts[which[0]][0], groups)
+            box["out"] = update(chain, flat, *args, box["v"], box["out"], starts[which[0]], groups)
 
         return run
 
@@ -522,42 +532,34 @@
     line = [solve(k) for k in range(count)]
     line += [share("prow", n_prow, 1 << b) for b in range(n_prow.bit_length() - 1)]
     line += [share("pcol", n_pcol, b) for b in bits]
-    if slots == 8 and len(line) == 9:
+    def rest_extracted():
+        if chunks > 2:
+            parts.append(extracts(2, chunks)[0])
+
+    if chunks == 5 and len(line) == 9:
         plan = {
-            0: total[:1],
-            1: total[1:2],
-            2: [blocks_out, total[2]],
-            3: [blocks_swap, line[0]],
-            4: [make_factors, line[1], updates(0, 1, 2)],
-            5: [line[2], updates(3), line[3]],
-            6: [line[4], updates(4, 5)],
-            7: [line[5], line[6]],
-            8: [updates(6), line[7]],
+            0: [rest_extracted, *total],
+            1: [blocks_out, *line[:3], blocks_swap, *line[3:5]],
+            2: [make_factors, line[5], updates(0, 1), line[6]],
+            3: [updates(2), line[7]],
+            4: [updates(3), line[8]],
         }
-        tail = []
     else:
-        plan = {0: total, slots - 1: [blocks_out, blocks_swap, make_factors] + line}
-        tail = [updates(c) for c in range(chunks - 2)]
-        line = []
+        plan = {0: [rest_extracted, *total], chunks - 1: [blocks_out, blocks_swap, make_factors, *line, updates(*range(chunks - 1))]}
 
     for k in range(chunks):
-        ahead = [column[k + 2]] if k + 2 < chunks else []
+        ahead = [column[k + 1]] if k + 1 < chunks else []
         got = chain.gate([first[k], *ahead], [])
         first[k] = got[0] if ahead else got
+        if ahead:
+            column[k + 1] = got[1]
+            first[k + 1] = first_stage(column[k + 1])
         outward[k] = second_stage(first[k])
-        if ahead:
-            column[k + 2] = got[1]
-            first[k + 2] = first_stage(column[k + 2])
         if k:
             take(k - 1)
         for task in plan.get(k, []):
             task()
-    for task in tail:
-        task()
-    updates(chunks - 2)()
     take(chunks - 1)
-    if line:
-        line[-1]()
     updates(chunks - 1)()
     residual, out, state = box["residual"], box["out"], box["state"]
     updated = out.reshape(rows, lane_tiles, col_slots, LANES).transpose(0, 2, 1, 3).reshape(matrix.shape)

time: 264 us -> 257 us (0.973)
  waiting for transfers between devices: 30.2 us -> 72.9 us
  starting transfers between devices: 111 us -> 79.2 us
  Pallas kernels: 106 us -> 88.4 us
    ppermute x21 -> x17, waiting for transfers between devices: 15.7 us -> 53.8 us  [swap(): return lax.ppermute(value, axis, [(i, i ^ bit) for i in range(size)])]
    ppermute x9 -> x5, starting transfers between devices: 57.9 us -> 37.7 us  [first_stage(): return lax.ppermute(local, 'pcol', along_z(stages[0][0]))]
    pallas_call x46 -> x31, Pallas kernels: 106 us -> 88.4 us  [__call__(): pl.pallas_call(body, in_specs=list(in_specs) + [anywhere] * n_dep, out_sp...]
    ppermute x2, waiting for transfers between devices: 3.11 us -> 12.6 us  [spread(): values.append(lax.ppermute(values[-1], axis, pairs))]
    ppermute x18 -> x10, starting transfers between devices: 17.2 us -> 8.84 us  [second_stage(): lax.ppermute(arrived, 'pcol', along_z(moves))]
    ppermute x9 -> x5, waiting for transfers between devices: 11.4 us -> 4.79 us  [first_stage(): return lax.ppermute(local, 'pcol', along_z(stages[0][0]))]
    ppermute x21 -> x17, starting transfers between devices: 25.2 us -> 18.6 us  [swap(): return lax.ppermute(value, axis, [(i, i ^ bit) for i in range(size)])]
    unnamed x45 -> x43, local copies, waits for them, and re-layouts: 12.4 us -> 14.1 us
  transfers between devices with their start and end apart: 53 -> 37, of which waited for: 10 -> 13; matrix products, arithmetic and copies ran while one was open for 1% -> 0% of each run, Pallas kernels for 37% -> 30%
where the time goes in v3:
time: 257 us; the launch traced here: 256 us
  Pallas kernels  88.4 us (34%)
  starting transfers between devices  79.2 us (31%)
  waiting for transfers between devices  72.9 us (28%)
  local copies, waits for them, and re-layouts  14.1 us (5%)
    pallas_call x31, Pallas kernels, __call__(): pl.pallas_call(body, in_specs=list(in_specs) + [anywhere] * n_dep, out_sp...  88.4 us
    ppermute x17, waiting for transfers between devices, swap(): return lax.ppermute(value, axis, [(i, i ^ bit) for i in range(size)])  53.8 us
    ppermute x5, starting transfers between devices, first_stage(): return lax.ppermute(local, 'pcol', along_z(stages[0][0]))  37.7 us
    ppermute x17, starting transfers between devices, swap(): return lax.ppermute(value, axis, [(i, i ^ bit) for i in range(size)])  18.6 us
    unnamed x43, local copies, waits for them, and re-layouts  14.1 us
    ppermute x2, waiting for transfers between devices, spread(): values.append(lax.ppermute(values[-1], axis, pairs))  12.6 us
    ppermute x10, starting transfers between devices, second_stage(): lax.ppermute(arrived, 'pcol', along_z(moves))  8.84 us
    ppermute x3, starting transfers between devices, run(): lax.ppermute(box['state'], 'prow', [(i, i + 1) for i in range(n_prow - 1)])  8.6 us
  transfers between devices with their start and end apart: 37, of which 13 were waited for; matrix products, arithmetic and copies ran while one was open for 0% of the time, Pallas kernels for 30%

profile of v3, /device:TPU:0, one launch (start us, length us, event | category | flops | bytes accessed | tf_op | source)
XLA Modules:
  0.0 255.9 jit_solution(12937569669837959362)
XLA Ops:
  1.3 3.5 %extract.3 = (f32[1,512]{1,0:T(1,128)S(1)}, bf16[512,512]{1,0:T(8,128)(2,1)S(1)}, bf16[8192,128]{1,0:T(8,128)(2,1)}, f32[8,128]{1,0:T(8,128)S(1)}) custom-call(bf16[65536,128]{1,0:T(8,128)(2,1)} %bitcast.32, bf16[16,128]{1,0:T(8,128)(2,1)S(1)} %bitcast.29), custom_call_target="tpu_custom_call" | custom-call | flops 4194304 | bytes 2097152 | tf_op jit(solution)/shard_map/extract/pallas_call | solution.py:32
  4.8 2.9 %collective-permute-start.1 = (bf16[8192,128]{1,0:T(8,128)(2,1)}, bf16[8192,128]{1,0:T(8,128)(2,1)}, u32[]{:S(2)}, u32[]{:S(2)}) collective-permute-start(bf16[8192,128]{1,0:T(8,128)(2,1)} %get-tuple-element.74.refs_1_), channel_id=1, source_target_pairs={{0,16},{8,24},{16,0},{24,8},{1,17},{9,25},{17,1},{25,9},{2,18},{10... | collective-permute-start | bytes 6291464 | tf_op jit(solution)/shard_map/ppermute | solution.py:404
  7.8 5.3 %collective-permute-start.3 = (bf16[512,512]{1,0:T(8,128)(2,1)S(1)}, bf16[512,512]{1,0:T(8,128)(2,1)}, u32[]{:S(2)}, u32[]{:S(2)}) collective-permute-start(bf16[512,512]{1,0:T(8,128)(2,1)S(1)} %get-tuple-element.75.refs_1_.refs_6_), channel_id=1, source_target_pairs={{0,4},{1,5},{8,12},{9,13},{16,20},{17,21},{24,28},{25,29}} | collective-permute-start | bytes 1572872 | tf_op jit(solution)/shard_map/ppermute | solution.py:427
  13.1 5.3 %extract.4 = (f32[1,1024]{1,0:T(1,128)S(1)}, bf16[1024,512]{1,0:T(8,128)(2,1)}, f32[8,128]{1,0:T(8,128)S(1)}) custom-call(bf16[65536,128]{1,0:T(8,128)(2,1)} %bitcast.33, bf16[16,128]{1,0:T(8,128)(2,1)S(1)} %bitcast.30, f32[8,128]{1,0:T(8,128)S(1)} %get-tuple-element.76.refs_2_), custom_call_target="tpu_custom_call" | custom-call | flops 8388608 | bytes 4194304 | tf_op jit(solution)/shard_map/extract/pallas_call | solution.py:32
  18.4 4.8 %collective-permute-done.3.refs_0_ = bf16[512,512]{1,0:T(8,128)(2,1)} collective-permute-done((bf16[512,512]{1,0:T(8,128)(2,1)S(1)}, bf16[512,512]{1,0:T(8,128)(2,1)}, u32[]{:S(2)}, u32[]{:S(2)}) %collective-permute-start.3) | collective-permute-done | bytes 524320 | tf_op jit(solution)/shard_map/ppermute | solution.py:427
  23.2 5.4 %collective-permute-start.6 = (bf16[1024,512]{1,0:T(8,128)(2,1)}, bf16[1024,512]{1,0:T(8,128)(2,1)S(1)}, u32[]{:S(2)}, u32[]{:S(2)}) collective-permute-start(bf16[1024,512]{1,0:T(8,128)(2,1)} %get-tuple-element.80.refs_1_), channel_id=1, source_target_pairs={{0,4},{1,5},{8,12},{9,13},{16,20},{17,21},{24,28},{25,29}} | collective-permute-start | bytes 3145736 | tf_op jit(solution)/shard_map/ppermute | solution.py:427
  28.6 1.5 collective-permute-start.4
  30.1 1.4 collective-permute-start.5
  31.5 11.3 %extract.5 = (f32[1,2560]{1,0:T(1,128)S(1)}, bf16[1024,512]{1,0:T(8,128)(2,1)S(1)}, bf16[1024,512]{1,0:T(8,128)(2,1)S(1)}, bf16[512,512]{1,0:T(8,128)(2,1)S(1)}, f32[8,128]{1,0:T(8,128)S(1)}) custom-call(bf16[65536,128]{1,0:T(8,128)(2,1)} %bitcast.34, bf16[16,128]{1,0:T(8,128)(2,1)S(1)} %bitcast.31, f32[8,128]{1,0:T(8,128)S(1)} %get-tuple-element.81.refs_2_), custom_call_target="tpu_custom_call" | custom-call | flops 20971520 | bytes 10485760 | tf_op jit(solution)/shard_map/extract/pallas_call | solution.py:32
  42.9 1.0 copy-done.3
  44.7 1.6 collective-permute-start.7
  46.3 2.2 collective-permute-done.7.refs_1_
  48.5 3.7 %collective-permute-done.8.refs_1_ = f32[8,512]{1,0:T(8,128)S(1)} collective-permute-done((f32[8,512]{1,0:T(8,128)S(1)}, f32[8,512]{1,0:T(8,128)S(1)}, u32[]{:S(2)}, u32[]{:S(2)}) %collective-permute-start.8) | collective-permute-done | bytes 16416 | tf_op jit(solution)/shard_map/ppermute | solution.py:408
  52.9 4.1 %collective-permute-done.9.refs_1_ = f32[8,512]{1,0:T(8,128)S(1)} collective-permute-done((f32[8,512]{1,0:T(8,128)S(1)}, f32[8,512]{1,0:T(8,128)S(1)}, u32[]{:S(2)}, u32[]{:S(2)}) %collective-permute-start.9) | collective-permute-done | bytes 16416 | tf_op jit(solution)/shard_map/ppermute | solution.py:408
  56.9 1.2 copy-done.4
  60.2 1.6 collective-permute-start.10
  61.8 4.5 %collective-permute-start.16 = (bf16[1024,512]{1,0:T(8,128)(2,1)}, bf16[1024,512]{1,0:T(8,128)(2,1)}, u32[]{:S(2)}, u32[]{:S(2)}) collective-permute-start(bf16[1024,512]{1,0:T(8,128)(2,1)} %copy-done.5), channel_id=1, source_target_pairs={{0,4},{1,5},{8,12},{9,13},{16,20},{17,21},{24,28},{25,29}} | collective-permute-start | bytes 3145736 | tf_op jit(solution)/shard_map/ppermute | solution.py:427
  66.5 3.2 %collective-permute-done.10.refs_2_.refs_5_.refs_3_ = bf16[512,512]{1,0:T(8,128)(2,1)S(1)} collective-permute-done((bf16[512,512]{1,0:T(8,128)(2,1)S(1)}, bf16[512,512]{1,0:T(8,128)(2,1)S(1)}, u32[]{:S(2)}, u32[]{:S(2)}) %collective-permute-start.10) | collective-permute-done | bytes 524320 | tf_op jit(solution)/shard_map/ppermute | solution.py:408
  70.6 1.5 solve.4
  72.2 1.3 collective-permute-start.17
  74.3 1.5 solve.5
  75.8 3.1 %collective-permute-start.18 = (f32[4,512]{1,0:T(4,128)S(1)}, f32[4,512]{1,0:T(4,128)S(1)}, u32[]{:S(2)}, u32[]{:S(2)}) collective-permute-start(f32[4,512]{1,0:T(4,128)S(1)} %get-tuple-element.103), channel_id=1, source_target_pairs={{0,8},{8,16},{16,24},{1,9},{9,17},{17,25},{2,10},{10,18},{18,26},{... | collective-permute-start | bytes 24584 | tf_op jit(solution)/shard_map/ppermute | solution.py:496
  79.8 1.5 solve.6
  81.3 4.2 %collective-permute-start.19 = (f32[4,512]{1,0:T(4,128)S(1)}, f32[4,512]{1,0:T(4,128)S(1)}, u32[]{:S(2)}, u32[]{:S(2)}) collective-permute-start(f32[4,512]{1,0:T(4,128)S(1)} %get-tuple-element.105), channel_id=1, source_target_pairs={{0,8},{8,16},{16,24},{1,9},{9,17},{17,25},{2,10},{10,18},{18,26},{... | collective-permute-start | bytes 24584 | tf_op jit(solution)/shard_map/ppermute | solution.py:496
  86.2 1.5 solve.7
  87.8 2.3 collective-permute-start.20
  91.7 2.6 %collective-permute-start.12 = (bf16[512,512]{1,0:T(8,128)(2,1)}, bf16[512,512]{1,0:T(8,128)(2,1)}, u32[]{:S(2)}, u32[]{:S(2)}) collective-permute-start(bf16[512,512]{1,0:T(8,128)(2,1)} %copy-done.12), channel_id=1, source_target_pairs={{0,16},{8,24},{16,0},{24,8},{1,17},{9,25},{17,1},{25,9},{2,18},{10... | collective-permute-start | bytes 1572872 | tf_op jit(solution)/shard_map/ppermute | solution.py:404
  94.2 12.6 %collective-permute-done.12.refs_7_ = bf16[512,512]{1,0:T(8,128)(2,1)} collective-permute-done((bf16[512,512]{1,0:T(8,128)(2,1)}, bf16[512,512]{1,0:T(8,128)(2,1)}, u32[]{:S(2)}, u32[]{:S(2)}) %collective-permute-start.12) | collective-permute-done | bytes 524320 | tf_op jit(solution)/shard_map/ppermute | solution.py:404
  107.8 1.2 copy-done.2
  109.0 1.2 choose.8
  110.3 1.6 collective-permute-start.24
  111.9 1.7 collective-permute-start.22
  115.2 18.9 %collective-permute-start.21 = (bf16[1024,512]{1,0:T(8,128)(2,1)S(1)}, bf16[1024,512]{1,0:T(8,128)(2,1)S(1)}, u32[]{:S(2)}, u32[]{:S(2)}) collective-permute-start(bf16[1024,512]{1,0:T(8,128)(2,1)S(1)} %get-tuple-element.113.refs_1_), channel_id=1, source_target_pairs={{0,4},{1,5},{8,12},{9,13},{16,20},{17,21},{24,28},{25,29}} | collective-permute-start | bytes 3145736 | tf_op jit(solution)/shard_map/ppermute | solution.py:427
  134.1 1.2 copy-done.11
  135.3 1.0 copy-done.13
  136.3 15.4 %factors.1 = (bf16[1024,2048]{1,0:T(8,128)(2,1)}, f32[8,128]{1,0:T(8,128)S(1)}) custom-call(s32[3]{0:T(128)S(1)} %pad_add_fusion.refs_0_, bf16[8192,128]{1,0:T(8,128)(2,1)} %get-tuple-element.74.refs_1_, bf16[8192,128]{1,0:T(8,128)(2,1)} %collective-permute-done.refs_2_, bf16[8192,128]{1,0:T(8,128)(2,1)} %collective-permute-done.1.refs_3_, ...), custom_call_target="tpu_custom_call" | custom-call | flops 6442450944 | bytes 12582912 | tf_op jit(solution)/shard_map/factors/pallas_call | solution.py:32
  152.3 15.1 %update.4 = (bf16[65536,128]{1,0:T(8,128)(2,1)}, f32[8,128]{1,0:T(8,128)S(1)}) custom-call(bf16[65536,128]{1,0:T(8,128)(2,1)} %bitcast.35, bf16[1024,2048]{1,0:T(8,128)(2,1)} %get-tuple-element.112.refs_1_, bf16[512,512]{1,0:T(8,128)(2,1)S(1)} %get-tuple-element.93.refs_1_.refs_4_.refs_2_, ...), custom_call_target="tpu_custom_call" | custom-call | flops 6442450944 | bytes 15728640 | tf_op jit(solution)/shard_map/update/pallas_call | solution.py:32
  168.9 1.6 collective-permute-start.29
  171.9 3.7 %collective-permute-start.25 = (bf16[512,512]{1,0:T(8,128)(2,1)S(1)}, bf16[512,512]{1,0:T(8,128)(2,1)S(1)}, u32[]{:S(2)}, u32[]{:S(2)}) collective-permute-start(bf16[512,512]{1,0:T(8,128)(2,1)S(1)} %get-tuple-element.122.refs_1_), channel_id=1, source_target_pairs={{0,4},{1,5},{8,12},{9,13},{16,20},{17,21},{24,28},{25,29}} | collective-permute-start | bytes 1572872 | tf_op jit(solution)/shard_map/ppermute | solution.py:427
  175.7 16.4 %collective-permute-done.29.refs_3_ = bf16[1024,512]{1,0:T(8,128)(2,1)S(1)} collective-permute-done((bf16[1024,512]{1,0:T(8,128)(2,1)S(1)}, bf16[1024,512]{1,0:T(8,128)(2,1)S(1)}, u32[]{:S(2)}, u32[]{:S(2)}) %collective-permute-start.29) | collective-permute-done | bytes 1048608 | tf_op jit(solution)/shard_map/ppermute | solution.py:408
  192.0 11.1 %update.5 = (bf16[65536,128]{1,0:T(8,128)(2,1)}, f32[8,128]{1,0:T(8,128)S(1)}) custom-call(bf16[65536,128]{1,0:T(8,128)(2,1)} %bitcast.36, bf16[1024,2048]{1,0:T(8,128)(2,1)} %get-tuple-element.112.refs_1_, bf16[1024,512]{1,0:T(8,128)(2,1)S(1)} %get-tuple-element.126.refs_2_, ...), custom_call_target="tpu_custom_call", output_to_operand_aliasing={{0}: (4, {})} | custom-call | flops 4294967296 | bytes 10485760 | tf_op jit(solution)/shard_map/update/pallas_call | solution.py:32
  204.5 1.5 collective-permute-start.35
  207.6 3.9 %collective-permute-start.32 = (f32[4,512]{1,0:T(4,128)S(1)}, f32[4,512]{1,0:T(4,128)S(1)}, u32[]{:S(2)}, u32[]{:S(2)}) collective-permute-start(f32[4,512]{1,0:T(4,128)S(1)} %get-tuple-element.132.refs_0_), channel_id=1, source_target_pairs={{0,4},{1,5},{2,6},{3,7},{4,0},{5,1},{6,2},{7,3},{8,12},{9,13},{10,... | collective-permute-start | bytes 24584 | tf_op jit(solution)/shard_map/ppermute | solution.py:408
  211.5 15.3 %collective-permute-done.35.refs_3_ = bf16[1024,512]{1,0:T(8,128)(2,1)S(1)} collective-permute-done((bf16[1024,512]{1,0:T(8,128)(2,1)S(1)}, bf16[1024,512]{1,0:T(8,128)(2,1)S(1)}, u32[]{:S(2)}, u32[]{:S(2)}) %collective-permute-start.35) | collective-permute-done | bytes 1048608 | tf_op jit(solution)/shard_map/ppermute | solution.py:408
  226.8 11.1 %update.6 = (bf16[65536,128]{1,0:T(8,128)(2,1)}, f32[8,128]{1,0:T(8,128)S(1)}) custom-call(bf16[65536,128]{1,0:T(8,128)(2,1)} %bitcast.37, bf16[1024,2048]{1,0:T(8,128)(2,1)} %get-tuple-element.112.refs_1_, bf16[1024,512]{1,0:T(8,128)(2,1)S(1)} %get-tuple-element.135.refs_2_, ...), custom_call_target="tpu_custom_call", output_to_operand_aliasing={{0}: (4, {})} | custom-call | flops 4294967296 | bytes 10485760 | tf_op jit(solution)/shard_map/update/pallas_call | solution.py:32
  238.5 1.4 collective-permute-start.36
  240.5 8.1 %collective-permute-done.36.refs_3_ = bf16[512,512]{1,0:T(8,128)(2,1)S(1)} collective-permute-done((bf16[512,512]{1,0:T(8,128)(2,1)S(1)}, bf16[512,512]{1,0:T(8,128)(2,1)S(1)}, u32[]{:S(2)}, u32[]{:S(2)}) %collective-permute-start.36) | collective-permute-done | bytes 524320 | tf_op jit(solution)/shard_map/ppermute | solution.py:408
  248.6 7.3 %update.7 = (bf16[65536,128]{1,0:T(8,128)(2,1)}, f32[8,128]{1,0:T(8,128)}) custom-call(bf16[65536,128]{1,0:T(8,128)(2,1)} %bitcast.38, bf16[1024,2048]{1,0:T(8,128)(2,1)} %get-tuple-element.112.refs_1_, bf16[512,512]{1,0:T(8,128)(2,1)S(1)} %get-tuple-element.140.refs_2_, ...), custom_call_target="tpu_custom_call", output_to_operand_aliasing={{0}: (4, {})} | custom-call | flops 2147483648 | bytes 5242880 | tf_op jit(solution)/shard_map/update/pallas_call | solution.py:32
  (108 shorter events, 19.6 us)
Async XLA Ops:
  1.3 11.7 %copy-start.10 = (bf16[4,1,512]{2,0,1:T(4,128)(2,1)S(1)}, bf16[4,1,512]{2,0,1:T(4,128)(2,1)}, u32[]{:S(2)}) copy-start(bf16[4,1,512]{2,0,1:T(4,128)(2,1)} %param.9) | copy-start | bytes 12292
  4.8 61.4 %collective-permute-start.1 = (bf16[8192,128]{1,0:T(8,128)(2,1)}, bf16[8192,128]{1,0:T(8,128)(2,1)}, u32[]{:S(2)}, u32[]{:S(2)}) collective-permute-start(bf16[8192,128]{1,0:T(8,128)(2,1)} %get-tuple-element.74.refs_1_), channel_id=1, source_target_pairs={{0,16},{8,24},{16,0},{24,8},{1,17},{9,25},{17,1},{25,9},{2,18},{10... | collective-permute-start | bytes 6291464 | tf_op jit(solution)/shard_map/ppermute | solution.py:404
  7.8 15.4 %collective-permute-start.3 = (bf16[512,512]{1,0:T(8,128)(2,1)S(1)}, bf16[512,512]{1,0:T(8,128)(2,1)}, u32[]{:S(2)}, u32[]{:S(2)}) collective-permute-start(bf16[512,512]{1,0:T(8,128)(2,1)S(1)} %get-tuple-element.75.refs_1_.refs_6_), channel_id=1, source_target_pairs={{0,4},{1,5},{8,12},{9,13},{16,20},{17,21},{24,28},{25,29}} | collective-permute-start | bytes 1572872 | tf_op jit(solution)/shard_map/ppermute | solution.py:427
  13.1 53.5 %copy-start.20 = (f32[8,1,512]{2,1,0:T(1,128)S(1)}, f32[8,1,512]{2,1,0:T(1,128)}, u32[]{:S(2)}) copy-start(f32[8,1,512]{2,1,0:T(1,128)} %param.10) | copy-start | bytes 49156
  13.1 57.6 %copy-start = (bf16[1,1,512,512]{3,2,1,0:T(8,128)(2,1)S(1)}, bf16[1,1,512,512]{3,2,1,0:T(8,128)(2,1)}, u32[]{:S(2)}) copy-start(bf16[1,1,512,512]{3,2,1,0:T(8,128)(2,1)} %param.11) | copy-start | bytes 1572868
  23.2 33.8 %collective-permute-start.6 = (bf16[1024,512]{1,0:T(8,128)(2,1)}, bf16[1024,512]{1,0:T(8,128)(2,1)S(1)}, u32[]{:S(2)}, u32[]{:S(2)}) collective-permute-start(bf16[1024,512]{1,0:T(8,128)(2,1)} %get-tuple-element.80.refs_1_), channel_id=1, source_target_pairs={{0,4},{1,5},{8,12},{9,13},{16,20},{17,21},{24,28},{25,29}} | collective-permute-start | bytes 3145736 | tf_op jit(solution)/shard_map/ppermute | solution.py:427
  28.6 31.5 %collective-permute-start.4 = (bf16[512,512]{1,0:T(8,128)(2,1)}, bf16[512,512]{1,0:T(8,128)(2,1)}, u32[]{:S(2)}, u32[]{:S(2)}) collective-permute-start(bf16[512,512]{1,0:T(8,128)(2,1)} %get-tuple-element.79.refs_2_), channel_id=1, source_target_pairs={{4,2},{5,3},{12,10},{13,11},{20,18},{21,19},{28,26},{29,27}} | collective-permute-start | bytes 1572872 | tf_op jit(solution)/shard_map/ppermute | solution.py:430
  30.1 30.0 %collective-permute-start.5 = (bf16[512,512]{1,0:T(8,128)(2,1)}, bf16[512,512]{1,0:T(8,128)(2,1)}, u32[]{:S(2)}, u32[]{:S(2)}) collective-permute-start(bf16[512,512]{1,0:T(8,128)(2,1)} %get-tuple-element.79.refs_2_), channel_id=1, source_target_pairs={{4,6},{5,7},{12,14},{13,15},{20,22},{21,23},{28,30},{29,31}} | collective-permute-start | bytes 1572872 | tf_op jit(solution)/shard_map/ppermute | solution.py:430
  44.7 3.8 %collective-permute-start.7 = (f32[8,512]{1,0:T(8,128)S(1)}, f32[8,512]{1,0:T(8,128)S(1)}, u32[]{:S(2)}, u32[]{:S(2)}) collective-permute-start(f32[8,512]{1,0:T(8,128)S(1)} %reshape.48.refs_0_), channel_id=1, source_target_pairs={{0,1},{1,0},{2,3},{3,2},{4,5},{5,4},{6,7},{7,6},{8,9},{9,8},{10,11... | collective-permute-start | bytes 49160 | tf_op jit(solution)/shard_map/ppermute | solution.py:408
  48.5 3.7 %collective-permute-start.8 = (f32[8,512]{1,0:T(8,128)S(1)}, f32[8,512]{1,0:T(8,128)S(1)}, u32[]{:S(2)}, u32[]{:S(2)}) collective-permute-start(f32[8,512]{1,0:T(8,128)S(1)} %get-tuple-element.87.refs_0_), channel_id=1, source_target_pairs={{0,2},{1,3},{2,0},{3,1},{4,6},{5,7},{6,4},{7,5},{8,10},{9,11},{10,... | collective-permute-start | bytes 49160 | tf_op jit(solution)/shard_map/ppermute | solution.py:408
  52.3 4.6 %collective-permute-start.9 = (f32[8,512]{1,0:T(8,128)S(1)}, f32[8,512]{1,0:T(8,128)S(1)}, u32[]{:S(2)}, u32[]{:S(2)}) collective-permute-start(f32[8,512]{1,0:T(8,128)S(1)} %get-tuple-element.89.refs_0_), channel_id=1, source_target_pairs={{0,4},{1,5},{2,6},{3,7},{4,0},{5,1},{6,2},{7,3},{8,12},{9,13},{10,... | collective-permute-start | bytes 49160 | tf_op jit(solution)/shard_map/ppermute | solution.py:408
  56.9 1.2 copy-start.4
  60.2 9.6 %collective-permute-start.10 = (bf16[512,512]{1,0:T(8,128)(2,1)S(1)}, bf16[512,512]{1,0:T(8,128)(2,1)S(1)}, u32[]{:S(2)}, u32[]{:S(2)}) collective-permute-start(bf16[512,512]{1,0:T(8,128)(2,1)S(1)} %get-tuple-element.93.refs_1_.refs_4_.refs_2_), channel_id=1, source_target_pairs={{0,1},{1,0},{2,3},{3,2},{4,5},{5,4},{6,7},{7,6},{8,9},{9,8},{10,11... | collective-permute-start | bytes 1572872 | tf_op jit(solution)/shard_map/ppermute | solution.py:408
  61.8 50.2 %collective-permute-start = (bf16[8192,128]{1,0:T(8,128)(2,1)}, bf16[8192,128]{1,0:T(8,128)(2,1)}, u32[]{:S(2)}, u32[]{:S(2)}) collective-permute-start(bf16[8192,128]{1,0:T(8,128)(2,1)} %get-tuple-element.74.refs_1_), channel_id=1, source_target_pairs={{0,8},{8,0},{16,24},{24,16},{1,9},{9,1},{17,25},{25,17},{2,10},{10... | collective-permute-start | bytes 6291464 | tf_op jit(solution)/shard_map/ppermute | solution.py:408
  61.8 29.9 %collective-permute-start.16 = (bf16[1024,512]{1,0:T(8,128)(2,1)}, bf16[1024,512]{1,0:T(8,128)(2,1)}, u32[]{:S(2)}, u32[]{:S(2)}) collective-permute-start(bf16[1024,512]{1,0:T(8,128)(2,1)} %copy-done.5), channel_id=1, source_target_pairs={{0,4},{1,5},{8,12},{9,13},{16,20},{17,21},{24,28},{25,29}} | collective-permute-start | bytes 3145736 | tf_op jit(solution)/shard_map/ppermute | solution.py:427
  66.2 48.9 %collective-permute-start.2 = (bf16[8192,128]{1,0:T(8,128)(2,1)}, bf16[8192,128]{1,0:T(8,128)(2,1)}, u32[]{:S(2)}, u32[]{:S(2)}) collective-permute-start(bf16[8192,128]{1,0:T(8,128)(2,1)} %collective-permute-done.1.refs_3_), channel_id=1, source_target_pairs={{0,8},{8,0},{16,24},{24,16},{1,9},{9,1},{17,25},{25,17},{2,10},{10... | collective-permute-start | bytes 6291464 | tf_op jit(solution)/shard_map/ppermute | solution.py:408
  72.2 2.1 collective-permute-start.17
  75.8 4.0 %collective-permute-start.18 = (f32[4,512]{1,0:T(4,128)S(1)}, f32[4,512]{1,0:T(4,128)S(1)}, u32[]{:S(2)}, u32[]{:S(2)}) collective-permute-start(f32[4,512]{1,0:T(4,128)S(1)} %get-tuple-element.103), channel_id=1, source_target_pairs={{0,8},{8,16},{16,24},{1,9},{9,17},{17,25},{2,10},{10,18},{18,26},{... | collective-permute-start | bytes 24584 | tf_op jit(solution)/shard_map/ppermute | solution.py:496
  81.3 5.0 %collective-permute-start.19 = (f32[4,512]{1,0:T(4,128)S(1)}, f32[4,512]{1,0:T(4,128)S(1)}, u32[]{:S(2)}, u32[]{:S(2)}) collective-permute-start(f32[4,512]{1,0:T(4,128)S(1)} %get-tuple-element.105), channel_id=1, source_target_pairs={{0,8},{8,16},{16,24},{1,9},{9,17},{17,25},{2,10},{10,18},{18,26},{... | collective-permute-start | bytes 24584 | tf_op jit(solution)/shard_map/ppermute | solution.py:496
  85.4 8.8 %collective-permute-start.14 = (bf16[1024,512]{1,0:T(8,128)(2,1)}, bf16[1024,512]{1,0:T(8,128)(2,1)S(1)}, u32[]{:S(2)}, u32[]{:S(2)}) collective-permute-start(bf16[1024,512]{1,0:T(8,128)(2,1)} %copy-done.1), channel_id=1, source_target_pairs={{4,2},{5,3},{12,10},{13,11},{20,18},{21,19},{28,26},{29,27}} | collective-permute-start | bytes 3145736 | tf_op jit(solution)/shard_map/ppermute | solution.py:430
  87.8 3.1 %collective-permute-start.20 = (f32[4,512]{1,0:T(4,128)S(1)}, f32[4,512]{1,0:T(4,128)S(1)}, u32[]{:S(2)}, u32[]{:S(2)}) collective-permute-start(f32[4,512]{1,0:T(4,128)S(1)} %broadcast_select_fusion.refs_0_), channel_id=1, source_target_pairs={{0,8},{8,0},{16,24},{24,16},{1,9},{9,1},{17,25},{25,17},{2,10},{10... | collective-permute-start | bytes 24584 | tf_op jit(solution)/shard_map/ppermute | solution.py:408
  90.9 15.9 %collective-permute-start.15 = (bf16[1024,512]{1,0:T(8,128)(2,1)}, bf16[1024,512]{1,0:T(8,128)(2,1)S(1)}, u32[]{:S(2)}, u32[]{:S(2)}) collective-permute-start(bf16[1024,512]{1,0:T(8,128)(2,1)} %copy-done.1), channel_id=1, source_target_pairs={{4,6},{5,7},{12,14},{13,15},{20,22},{21,23},{28,30},{29,31}} | collective-permute-start | bytes 3145736 | tf_op jit(solution)/shard_map/ppermute | solution.py:430
  91.7 15.1 %collective-permute-start.12 = (bf16[512,512]{1,0:T(8,128)(2,1)}, bf16[512,512]{1,0:T(8,128)(2,1)}, u32[]{:S(2)}, u32[]{:S(2)}) collective-permute-start(bf16[512,512]{1,0:T(8,128)(2,1)} %copy-done.12), channel_id=1, source_target_pairs={{0,16},{8,24},{16,0},{24,8},{1,17},{9,25},{17,1},{25,9},{2,18},{10... | collective-permute-start | bytes 1572872 | tf_op jit(solution)/shard_map/ppermute | solution.py:404
  94.2 12.6 %copy-start.16 = (bf16[1024,512]{1,0:T(8,128)(2,1)}, bf16[1024,512]{1,0:T(8,128)(2,1)S(1)}, u32[]{:S(2)}) copy-start(bf16[1024,512]{1,0:T(8,128)(2,1)S(1)} %collective-permute-done.14.refs_3_) | copy-start | bytes 3145732
  94.2 19.5 %collective-permute-start.11 = (bf16[512,512]{1,0:T(8,128)(2,1)}, bf16[512,512]{1,0:T(8,128)(2,1)}, u32[]{:S(2)}, u32[]{:S(2)}) collective-permute-start(bf16[512,512]{1,0:T(8,128)(2,1)} %copy-done.12), channel_id=1, source_target_pairs={{0,8},{8,0},{16,24},{24,16},{1,9},{9,1},{17,25},{25,17},{2,10},{10... | collective-permute-start | bytes 1572872 | tf_op jit(solution)/shard_map/ppermute | solution.py:408
  106.8 7.6 %collective-permute-start.13 = (bf16[512,512]{1,0:T(8,128)(2,1)}, bf16[512,512]{1,0:T(8,128)(2,1)}, u32[]{:S(2)}, u32[]{:S(2)}) collective-permute-start(bf16[512,512]{1,0:T(8,128)(2,1)} %collective-permute-done.12.refs_7_), channel_id=1, source_target_pairs={{0,8},{8,0},{16,24},{24,16},{1,9},{9,1},{17,25},{25,17},{2,10},{10... | collective-permute-start | bytes 1572872 | tf_op jit(solution)/shard_map/ppermute | solution.py:408
  107.8 1.2 copy-start.2
  110.3 42.1 %collective-permute-start.24 = (bf16[1024,512]{1,0:T(8,128)(2,1)S(1)}, bf16[1024,512]{1,0:T(8,128)(2,1)}, u32[]{:S(2)}, u32[]{:S(2)}) collective-permute-start(bf16[1024,512]{1,0:T(8,128)(2,1)S(1)} %get-tuple-element.118.refs_4_), channel_id=1, source_target_pairs={{0,1},{1,0},{2,3},{3,2},{4,5},{5,4},{6,7},{7,6},{8,9},{9,8},{10,11... | collective-permute-start | bytes 3145736 | tf_op jit(solution)/shard_map/ppermute | solution.py:408
  111.9 39.8 %collective-permute-start.22 = (f32[4,512]{1,0:T(4,128)S(1)}, f32[4,512]{1,0:T(4,128)S(1)}, u32[]{:S(2)}, u32[]{:S(2)}) collective-permute-start(f32[4,512]{1,0:T(4,128)S(1)} %get-tuple-element.115.refs_0_), channel_id=1, source_target_pairs={{0,16},{8,24},{16,0},{24,8},{1,17},{9,25},{17,1},{25,9},{2,18},{10... | collective-permute-start | bytes 24584 | tf_op jit(solution)/shard_map/ppermute | solution.py:408
  113.7 53.8 %collective-permute-start.27 = (bf16[1024,512]{1,0:T(8,128)(2,1)}, bf16[1024,512]{1,0:T(8,128)(2,1)S(1)}, u32[]{:S(2)}, u32[]{:S(2)}) collective-permute-start(bf16[1024,512]{1,0:T(8,128)(2,1)} %get-tuple-element.124.refs_2_), channel_id=1, source_target_pairs={{4,2},{5,3},{12,10},{13,11},{20,18},{21,19},{28,26},{29,27}} | collective-permute-start | bytes 3145736 | tf_op jit(solution)/shard_map/ppermute | solution.py:430
  114.4 53.1 %collective-permute-start.28 = (bf16[1024,512]{1,0:T(8,128)(2,1)}, bf16[1024,512]{1,0:T(8,128)(2,1)S(1)}, u32[]{:S(2)}, u32[]{:S(2)}) collective-permute-start(bf16[1024,512]{1,0:T(8,128)(2,1)} %get-tuple-element.124.refs_2_), channel_id=1, source_target_pairs={{4,6},{5,7},{12,14},{13,15},{20,22},{21,23},{28,30},{29,31}} | collective-permute-start | bytes 3145736 | tf_op jit(solution)/shard_map/ppermute | solution.py:430
  115.2 52.3 %collective-permute-start.21 = (bf16[1024,512]{1,0:T(8,128)(2,1)S(1)}, bf16[1024,512]{1,0:T(8,128)(2,1)S(1)}, u32[]{:S(2)}, u32[]{:S(2)}) collective-permute-start(bf16[1024,512]{1,0:T(8,128)(2,1)S(1)} %get-tuple-element.113.refs_1_), channel_id=1, source_target_pairs={{0,4},{1,5},{8,12},{9,13},{16,20},{17,21},{24,28},{25,29}} | collective-permute-start | bytes 3145736 | tf_op jit(solution)/shard_map/ppermute | solution.py:427
  134.1 1.2 copy-start.11
  151.7 15.7 %copy-start.8 = (bf16[512,512]{1,0:T(8,128)(2,1)S(1)}, bf16[512,512]{1,0:T(8,128)(2,1)}, u32[]{:S(2)}) copy-start(bf16[512,512]{1,0:T(8,128)(2,1)} %copy-done.7) | copy-start | bytes 1572868
  151.7 17.0 %copy-start.6 = (bf16[1024,512]{1,0:T(8,128)(2,1)S(1)}, bf16[1024,512]{1,0:T(8,128)(2,1)}, u32[]{:S(2)}) copy-start(bf16[1024,512]{1,0:T(8,128)(2,1)} %copy-done.5) | copy-start | bytes 3145732
  151.8 15.7 %collective-permute-start.23 = (f32[4,512]{1,0:T(4,128)S(1)}, f32[4,512]{1,0:T(4,128)S(1)}, u32[]{:S(2)}, u32[]{:S(2)}) collective-permute-start(f32[4,512]{1,0:T(4,128)S(1)} %get-tuple-element.117.refs_0_), channel_id=1, source_target_pairs={{0,1},{1,0},{2,3},{3,2},{4,5},{5,4},{6,7},{7,6},{8,9},{9,8},{10,11... | collective-permute-start | bytes 24584 | tf_op jit(solution)/shard_map/ppermute | solution.py:408
  167.5 1.3 copy-start.15
  168.9 23.1 %collective-permute-start.29 = (bf16[1024,512]{1,0:T(8,128)(2,1)S(1)}, bf16[1024,512]{1,0:T(8,128)(2,1)S(1)}, u32[]{:S(2)}, u32[]{:S(2)}) collective-permute-start(bf16[1024,512]{1,0:T(8,128)(2,1)S(1)} %get-tuple-element.126.refs_2_), channel_id=1, source_target_pairs={{0,1},{1,0},{2,3},{3,2},{4,5},{5,4},{6,7},{7,6},{8,9},{9,8},{10,11... | collective-permute-start | bytes 3145736 | tf_op jit(solution)/shard_map/ppermute | solution.py:408
  170.5 32.7 %collective-permute-start.33 = (bf16[1024,512]{1,0:T(8,128)(2,1)S(1)}, bf16[1024,512]{1,0:T(8,128)(2,1)S(1)}, u32[]{:S(2)}, u32[]{:S(2)}) collective-permute-start(bf16[1024,512]{1,0:T(8,128)(2,1)S(1)} %get-tuple-element.133.refs_2_), channel_id=1, source_target_pairs={{4,2},{5,3},{12,10},{13,11},{20,18},{21,19},{28,26},{29,27}} | collective-permute-start | bytes 3145736 | tf_op jit(solution)/shard_map/ppermute | solution.py:430
  171.2 32.0 %collective-permute-start.34 = (bf16[1024,512]{1,0:T(8,128)(2,1)S(1)}, bf16[1024,512]{1,0:T(8,128)(2,1)S(1)}, u32[]{:S(2)}, u32[]{:S(2)}) collective-permute-start(bf16[1024,512]{1,0:T(8,128)(2,1)S(1)} %get-tuple-element.133.refs_2_), channel_id=1, source_target_pairs={{4,6},{5,7},{12,14},{13,15},{20,22},{21,23},{28,30},{29,31}} | collective-permute-start | bytes 3145736 | tf_op jit(solution)/shard_map/ppermute | solution.py:430
  171.9 31.2 %collective-permute-start.25 = (bf16[512,512]{1,0:T(8,128)(2,1)S(1)}, bf16[512,512]{1,0:T(8,128)(2,1)S(1)}, u32[]{:S(2)}, u32[]{:S(2)}) collective-permute-start(bf16[512,512]{1,0:T(8,128)(2,1)S(1)} %get-tuple-element.122.refs_1_), channel_id=1, source_target_pairs={{0,4},{1,5},{8,12},{9,13},{16,20},{17,21},{24,28},{25,29}} | collective-permute-start | bytes 1572872 | tf_op jit(solution)/shard_map/ppermute | solution.py:427
  175.6 27.5 %collective-permute-start.26 = (f32[4,512]{1,0:T(4,128)S(1)}, f32[4,512]{1,0:T(4,128)S(1)}, u32[]{:S(2)}, u32[]{:S(2)}) collective-permute-start(f32[4,512]{1,0:T(4,128)S(1)} %get-tuple-element.123.refs_0_), channel_id=1, source_target_pairs={{0,2},{1,3},{2,0},{3,1},{4,6},{5,7},{6,4},{7,5},{8,10},{9,11},{10,... | collective-permute-start | bytes 24584 | tf_op jit(solution)/shard_map/ppermute | solution.py:408
  203.2 1.3 copy-start.18
  204.5 22.2 %collective-permute-start.35 = (bf16[1024,512]{1,0:T(8,128)(2,1)S(1)}, bf16[1024,512]{1,0:T(8,128)(2,1)S(1)}, u32[]{:S(2)}, u32[]{:S(2)}) collective-permute-start(bf16[1024,512]{1,0:T(8,128)(2,1)S(1)} %get-tuple-element.135.refs_2_), channel_id=1, source_target_pairs={{0,1},{1,0},{2,3},{3,2},{4,5},{5,4},{6,7},{7,6},{8,9},{9,8},{10,11... | collective-permute-start | bytes 3145736 | tf_op jit(solution)/shard_map/ppermute | solution.py:408
  206.0 32.4 %collective-permute-start.30 = (bf16[512,512]{1,0:T(8,128)(2,1)S(1)}, bf16[512,512]{1,0:T(8,128)(2,1)S(1)}, u32[]{:S(2)}, u32[]{:S(2)}) collective-permute-start(bf16[512,512]{1,0:T(8,128)(2,1)S(1)} %get-tuple-element.131.refs_2_), channel_id=1, source_target_pairs={{4,2},{5,3},{12,10},{13,11},{20,18},{21,19},{28,26},{29,27}} | collective-permute-start | bytes 1572872 | tf_op jit(solution)/shard_map/ppermute | solution.py:430
  206.7 31.7 %collective-permute-start.31 = (bf16[512,512]{1,0:T(8,128)(2,1)S(1)}, bf16[512,512]{1,0:T(8,128)(2,1)S(1)}, u32[]{:S(2)}, u32[]{:S(2)}) collective-permute-start(bf16[512,512]{1,0:T(8,128)(2,1)S(1)} %get-tuple-element.131.refs_2_), channel_id=1, source_target_pairs={{4,6},{5,7},{12,14},{13,15},{20,22},{21,23},{28,30},{29,31}} | collective-permute-start | bytes 1572872 | tf_op jit(solution)/shard_map/ppermute | solution.py:430
  207.6 30.2 %collective-permute-start.32 = (f32[4,512]{1,0:T(4,128)S(1)}, f32[4,512]{1,0:T(4,128)S(1)}, u32[]{:S(2)}, u32[]{:S(2)}) collective-permute-start(f32[4,512]{1,0:T(4,128)S(1)} %get-tuple-element.132.refs_0_), channel_id=1, source_target_pairs={{0,4},{1,5},{2,6},{3,7},{4,0},{5,1},{6,2},{7,3},{8,12},{9,13},{10,... | collective-permute-start | bytes 24584 | tf_op jit(solution)/shard_map/ppermute | solution.py:408
  238.5 10.1 %collective-permute-start.36 = (bf16[512,512]{1,0:T(8,128)(2,1)S(1)}, bf16[512,512]{1,0:T(8,128)(2,1)S(1)}, u32[]{:S(2)}, u32[]{:S(2)}) collective-permute-start(bf16[512,512]{1,0:T(8,128)(2,1)S(1)} %get-tuple-element.140.refs_2_), channel_id=1, source_target_pairs={{0,1},{1,0},{2,3},{3,2},{4,5},{5,4},{6,7},{7,6},{8,9},{9,8},{10,11... | collective-permute-start | bytes 1572872 | tf_op jit(solution)/shard_map/ppermute | solution.py:408
  (10 other events, 9.2 us)

commit v4 on v3

--- a/solution.py
+++ b/solution.py
@@ -37,7 +37,7 @@
             scratch_shapes=list(scratch),
             input_output_aliases=aliases or {},
             compiler_params=pltpu.CompilerParams(vmem_limit_bytes=VMEM_BYTES),
-            cost_estimate=pl.CostEstimate(flops=work[0], bytes_accessed=work[1], transcendentals=0),
+            cost_estimate=pl.CostEstimate(flops=0, bytes_accessed=0, transcendentals=0),
             name=name,
             **params,
         )(*inputs, *deps)
@@ -190,13 +190,13 @@
 
 def factor_kernel(groups, n_x, where_ref, *refs):
     core, lane, x = where_ref[0], where_ref[1], where_ref[2]
-    given, (up_ref, low_ref, v_ref, raws, bands, blocks, sems, *rest) = refs[: 4 * n_x], refs[4 * n_x :]
+    given, (blk_mine_ref, blk_other_ref, up_ref, low_ref, v_ref, raws, bands, blocks, sems, *rest) = refs[: 2 * n_x], refs[2 * n_x :]
     width = up_ref.shape[1]
     for i in range(n_x):
 
         @pl.when(x == i)
         def _(i=i):
-            pairs = [(raws, given[2 * i], given[2 * i + 1]), (blocks, given[2 * n_x + 2 * i], given[2 * n_x + 2 * i + 1])]
+            pairs = [(raws, given[2 * i], given[2 * i + 1]), (blocks, blk_mine_ref, blk_other_ref)]
             copies = []
             for kind, (target, mine, other) in enumerate(pairs):
                 copies.append(pltpu.make_async_copy(mine, target.at[core], sems.at[kind, 0]))
@@ -264,7 +264,7 @@
     return chain(
         lambda *refs: factor_kernel(groups, n_x, *refs),
         [where, *bands, *blocks, upper, lower],
-        [pl.BlockSpec(memory_space=pltpu.SMEM)] + [anywhere] * (4 * n_x) + [vmem] * 2,
+        [pl.BlockSpec(memory_space=pltpu.SMEM)] + [anywhere] * (2 * n_x + 2) + [vmem] * 2,
         [jax.ShapeDtypeStruct((2 * width, cols), BF16)],
         [vmem],
         "factors",
@@ -471,7 +471,8 @@
     part, band = extracts(0, 1, True)
     parts.append(part)
     first[0] = first_stage(column[0])
-    box["bands"] = spread(band, "prow", n_prow)
+    bands = spread(band, "prow", n_prow)
+    swaps = {0: swap(band, "prow", n_prow)}
     parts.append(extracts(1, 2)[0])
 
     def total_step(bit):
@@ -507,12 +508,27 @@
 
         return run
 
+    def arrive(values):
+        got = chain.gate(list(values), [])
+        return got if len(values) > 1 else [got]
+
     def blocks_out():
-        box["blks"] = spread(chain.choose(flag, [mine[0], other[0]]), "prow", n_prow)
-        box["bands"] = [v for b in box["bands"] for v in (b, swap(b, "prow", n_prow))]
+        box["pick"] = spread(chain.choose(flag, [mine[0], other[0]]), "prow", n_prow)
+        bands[1:] = arrive(bands[1:])
+        for i, value in enumerate(bands[1:]):
+            swaps[i + 1] = swap(value, "prow", n_prow)
+
+    def bands_in():
+        for i, value in zip(range(1, len(bands)), arrive([swaps[i] for i in range(1, len(bands))])):
+            swaps[i] = value
+        box["bands"] = [v for i, b in enumerate(bands) for v in (b, swaps[i])]
 
     def blocks_swap():
-        box["blks"] = [v for b in box["blks"] for v in (b, swap(b, "prow", n_prow))]
+        blk = chain.choose(where[2:3], box["pick"])
+        box["blks"] = [blk, swap(blk, "prow", n_prow)]
+
+    def blocks_in():
+        box["blks"][1:] = arrive(box["blks"][1:])
 
     def make_factors():
         box["v"] = factors(chain, where, box["bands"], box["blks"], upper_inv, lower_inv, groups)
@@ -538,24 +554,29 @@
 
     if chunks == 5 and len(line) == 9:
         plan = {
-            0: [rest_extracted, *total],
-            1: [blocks_out, *line[:3], blocks_swap, *line[3:5]],
-            2: [make_factors, line[5], updates(0, 1), line[6]],
-            3: [updates(2), line[7]],
+            0: [rest_extracted, lambda: take(0), *total],
+            1: [blocks_out, line[0], bands_in, *line[1:3], blocks_swap, line[3], blocks_in],
+            2: [make_factors, line[4], updates(0, 1), line[5]],
+            3: [line[6], updates(2), line[7]],
             4: [updates(3), line[8]],
         }
     else:
-        plan = {0: [rest_extracted, *total], chunks - 1: [blocks_out, blocks_swap, make_factors, *line, updates(*range(chunks - 1))]}
+        plan = {0: [rest_extracted, lambda: take(0), *total], chunks - 1: [blocks_out, bands_in, blocks_swap, blocks_in, make_factors, *line, updates(*range(chunks - 1))]}
 
     for k in range(chunks):
         ahead = [column[k + 1]] if k + 1 < chunks else []
-        got = chain.gate([first[k], *ahead], [])
-        first[k] = got[0] if ahead else got
+        extra = [swaps[0]] if k == 0 else []
+        got = chain.gate([first[k], *ahead, *extra], [])
+        got = got if ahead or extra else [got]
+        first[k] = got[0]
         if ahead:
             column[k + 1] = got[1]
             first[k + 1] = first_stage(column[k + 1])
+        extra = got[1 + len(ahead) :]
+        if k == 0:
+            swaps[0] = extra[0]
         outward[k] = second_stage(first[k])
-        if k:
+        if k > 1:
             take(k - 1)
         for task in plan.get(k, []):
             task()

time: 257 us -> 245 us (0.953)
  starting transfers between devices: 79.2 us -> 66.2 us
  Pallas kernels: 88.4 us -> 91.9 us
    ppermute x2, waiting for transfers between devices: 12.6 us -> 0.01 us  [spread(): values.append(lax.ppermute(values[-1], axis, pairs))]
    ppermute x5, starting transfers between devices: 37.7 us -> 25.3 us  [first_stage(): return lax.ppermute(local, 'pcol', along_z(stages[0][0]))]
    ppermute x17 -> x16, waiting for transfers between devices: 53.8 us -> 63.8 us  [swap(): return lax.ppermute(value, axis, [(i, i ^ bit) for i in range(size)])]
    pallas_call x31 -> x35, Pallas kernels: 88.4 us -> 91.9 us  [__call__(): pl.pallas_call(body, in_specs=list(in_specs) + [anywhere] * n_dep, out_sp...]
    ppermute x10, starting transfers between devices: 8.84 us -> 11.7 us  [second_stage(): lax.ppermute(arrived, 'pcol', along_z(moves))]
    unnamed x43 -> x37, local copies, waits for them, and re-layouts: 14.1 us -> 12.5 us
    ppermute x17 -> x16, starting transfers between devices: 18.6 us -> 18.7 us  [swap(): return lax.ppermute(value, axis, [(i, i ^ bit) for i in range(size)])]
  transfers between devices with their start and end apart: 37 -> 36, of which waited for: 13 -> 9; matrix products, arithmetic and copies ran while one was open for 0% -> 0% of each run, Pallas kernels for 30% -> 32%
where the time goes in v4:
time: 245 us; the launch traced here: 244 us
  Pallas kernels  91.9 us (38%)
  waiting for transfers between devices  71.8 us (29%)
  starting transfers between devices  66.2 us (27%)
  local copies, waits for them, and re-layouts  12.5 us (5%)
    pallas_call x35, Pallas kernels, __call__(): pl.pallas_call(body, in_specs=list(in_specs) + [anywhere] * n_dep, out_sp...  91.9 us
    ppermute x16, waiting for transfers between devices, swap(): return lax.ppermute(value, axis, [(i, i ^ bit) for i in range(size)])  63.8 us
    ppermute x5, starting transfers between devices, first_stage(): return lax.ppermute(local, 'pcol', along_z(stages[0][0]))  25.3 us
    ppermute x16, starting transfers between devices, swap(): return lax.ppermute(value, axis, [(i, i ^ bit) for i in range(size)])  18.7 us
    unnamed x37, local copies, waits for them, and re-layouts  12.5 us
    ppermute x10, starting transfers between devices, second_stage(): lax.ppermute(arrived, 'pcol', along_z(moves))  11.7 us
    ppermute x3, starting transfers between devices, run(): lax.ppermute(box['state'], 'prow', [(i, i + 1) for i in range(n_prow - 1)])  7.35 us
    ppermute x5, waiting for transfers between devices, first_stage(): return lax.ppermute(local, 'pcol', along_z(stages[0][0]))  6.28 us
  transfers between devices with their start and end apart: 36, of which 9 were waited for; matrix products, arithmetic and copies ran while one was open for 0% of the time, Pallas kernels for 32%

profile of v4, /device:TPU:0, one launch (start us, length us, event | category | flops | bytes accessed | tf_op | source)
XLA Modules:
  0.0 243.8 jit_solution(13733379725941661349)
XLA Ops:
  1.3 3.5 %extract.3 = (f32[1,512]{1,0:T(1,128)S(1)}, bf16[512,512]{1,0:T(8,128)(2,1)S(1)}, bf16[8192,128]{1,0:T(8,128)(2,1)}, f32[8,128]{1,0:T(8,128)S(1)}) custom-call(bf16[65536,128]{1,0:T(8,128)(2,1)} %bitcast.32, bf16[16,128]{1,0:T(8,128)(2,1)S(1)} %bitcast.29), custom_call_target="tpu_custom_call" | custom-call | tf_op jit(solution)/shard_map/extract/pallas_call | solution.py:32
  5.3 2.5 %collective-permute-start.2 = (bf16[8192,128]{1,0:T(8,128)(2,1)}, bf16[8192,128]{1,0:T(8,128)(2,1)}, u32[]{:S(2)}, u32[]{:S(2)}) collective-permute-start(bf16[8192,128]{1,0:T(8,128)(2,1)} %get-tuple-element.83.refs_1_), channel_id=1, source_target_pairs={{0,16},{8,24},{16,0},{24,8},{1,17},{9,25},{17,1},{25,9},{2,18},{10... | collective-permute-start | bytes 6291464 | tf_op jit(solution)/shard_map/ppermute | solution.py:404
  7.8 4.5 %collective-permute-start = (bf16[512,512]{1,0:T(8,128)(2,1)S(1)}, bf16[512,512]{1,0:T(8,128)(2,1)S(1)}, u32[]{:S(2)}, u32[]{:S(2)}) collective-permute-start(bf16[512,512]{1,0:T(8,128)(2,1)S(1)} %get-tuple-element.84.refs_1_.refs_6_), channel_id=1, source_target_pairs={{0,4},{1,5},{8,12},{9,13},{16,20},{17,21},{24,28},{25,29}} | collective-permute-start | bytes 1572872 | tf_op jit(solution)/shard_map/ppermute | solution.py:427
  12.3 5.3 %extract.4 = (f32[1,1024]{1,0:T(1,128)S(1)}, bf16[1024,512]{1,0:T(8,128)(2,1)}, f32[8,128]{1,0:T(8,128)S(1)}) custom-call(bf16[65536,128]{1,0:T(8,128)(2,1)} %bitcast.33, bf16[16,128]{1,0:T(8,128)(2,1)S(1)} %bitcast.30, f32[8,128]{1,0:T(8,128)S(1)} %get-tuple-element.85.refs_2_), custom_call_target="tpu_custom_call" | custom-call | tf_op jit(solution)/shard_map/extract/pallas_call | solution.py:32
  17.5 6.3 %collective-permute-done.refs_0_ = bf16[512,512]{1,0:T(8,128)(2,1)S(1)} collective-permute-done((bf16[512,512]{1,0:T(8,128)(2,1)S(1)}, bf16[512,512]{1,0:T(8,128)(2,1)S(1)}, u32[]{:S(2)}, u32[]{:S(2)}) %collective-permute-start) | collective-permute-done | bytes 524320 | tf_op jit(solution)/shard_map/ppermute | solution.py:427
  23.8 1.3 copy-done.1
  25.9 1.5 collective-permute-start.4
  27.4 7.5 %collective-permute-start.6 = (bf16[1024,512]{1,0:T(8,128)(2,1)}, bf16[1024,512]{1,0:T(8,128)(2,1)}, u32[]{:S(2)}, u32[]{:S(2)}) collective-permute-start(bf16[1024,512]{1,0:T(8,128)(2,1)} %get-tuple-element.93.refs_1_), channel_id=1, source_target_pairs={{0,4},{1,5},{8,12},{9,13},{16,20},{17,21},{24,28},{25,29}} | collective-permute-start | bytes 3145736 | tf_op jit(solution)/shard_map/ppermute | solution.py:427
  34.9 11.6 %extract.5 = (f32[1,2560]{1,0:T(1,128)S(1)}, bf16[1024,512]{1,0:T(8,128)(2,1)}, bf16[1024,512]{1,0:T(8,128)(2,1)S(1)}, bf16[512,512]{1,0:T(8,128)(2,1)S(1)}, f32[8,128]{1,0:T(8,128)S(1)}) custom-call(bf16[65536,128]{1,0:T(8,128)(2,1)} %bitcast.34, bf16[16,128]{1,0:T(8,128)(2,1)S(1)} %bitcast.31, f32[8,128]{1,0:T(8,128)S(1)} %get-tuple-element.90.refs_2_), custom_call_target="tpu_custom_call" | custom-call | tf_op jit(solution)/shard_map/extract/pallas_call | solution.py:32
  47.4 1.0 copy-done.10
  48.5 1.6 collective-permute-start.5
  50.7 11.2 %collective-permute-done.7.refs_1_ = f32[8,512]{1,0:T(8,128)S(1)} collective-permute-done((f32[8,512]{1,0:T(8,128)S(1)}, f32[8,512]{1,0:T(8,128)S(1)}, u32[]{:S(2)}, u32[]{:S(2)}) %collective-permute-start.7) | collective-permute-done | bytes 16416 | tf_op jit(solution)/shard_map/ppermute | solution.py:408
  61.9 3.7 %collective-permute-done.8.refs_1_ = f32[8,512]{1,0:T(8,128)S(1)} collective-permute-done((f32[8,512]{1,0:T(8,128)S(1)}, f32[8,512]{1,0:T(8,128)S(1)}, u32[]{:S(2)}, u32[]{:S(2)}) %collective-permute-start.8) | collective-permute-done | bytes 16416 | tf_op jit(solution)/shard_map/ppermute | solution.py:408
  65.7 4.6 %collective-permute-done.9.refs_1_ = f32[8,512]{1,0:T(8,128)S(1)} collective-permute-done((f32[8,512]{1,0:T(8,128)S(1)}, f32[8,512]{1,0:T(8,128)S(1)}, u32[]{:S(2)}, u32[]{:S(2)}) %collective-permute-start.9) | collective-permute-done | bytes 16416 | tf_op jit(solution)/shard_map/ppermute | solution.py:408
  71.9 2.9 %collective-permute-start.18 = (bf16[1024,512]{1,0:T(8,128)(2,1)}, bf16[1024,512]{1,0:T(8,128)(2,1)}, u32[]{:S(2)}, u32[]{:S(2)}) collective-permute-start(bf16[1024,512]{1,0:T(8,128)(2,1)} %get-tuple-element.123.refs_1_), channel_id=1, source_target_pairs={{0,4},{1,5},{8,12},{9,13},{16,20},{17,21},{24,28},{25,29}} | collective-permute-start | bytes 3145736 | tf_op jit(solution)/shard_map/ppermute | solution.py:427
  74.8 1.6 collective-permute-start.16
  76.5 1.6 collective-permute-start.17
  78.2 1.5 solve.4
  79.7 1.8 collective-permute-start.12
  81.6 1.3 copy-done
  82.9 1.5 solve.5
  84.4 3.6 %collective-permute-start.13 = (f32[4,512]{1,0:T(4,128)S(1)}, f32[4,512]{1,0:T(4,128)S(1)}, u32[]{:S(2)}, u32[]{:S(2)}) collective-permute-start(f32[4,512]{1,0:T(4,128)S(1)} %get-tuple-element.114), channel_id=1, source_target_pairs={{0,8},{8,16},{16,24},{1,9},{9,17},{17,25},{2,10},{10,18},{18,26},{... | collective-permute-start | bytes 24584 | tf_op jit(solution)/shard_map/ppermute | solution.py:497
  88.8 1.5 solve.6
  90.3 1.1 choose.9
  91.4 1.9 collective-permute-start.14
  93.4 1.9 collective-permute-start.15
  96.1 1.5 solve.7
  98.5 2.2 choose.10
  100.7 1.6 collective-permute-start.22
  102.3 5.8 %collective-permute-start.19 = (bf16[1024,512]{1,0:T(8,128)(2,1)S(1)}, bf16[1024,512]{1,0:T(8,128)(2,1)S(1)}, u32[]{:S(2)}, u32[]{:S(2)}) collective-permute-start(bf16[1024,512]{1,0:T(8,128)(2,1)S(1)} %get-tuple-element.129.refs_1_), channel_id=1, source_target_pairs={{0,4},{1,5},{8,12},{9,13},{16,20},{17,21},{24,28},{25,29}} | collective-permute-start | bytes 3145736 | tf_op jit(solution)/shard_map/ppermute | solution.py:427
  108.1 1.6 collective-permute-start.25
  109.7 1.6 collective-permute-start.26
  111.4 1.0 copy-done.6
  112.5 1.2 copy-done.7
  113.7 1.2 copy-done.8
  116.0 14.5 %factors.1 = (bf16[1024,2048]{1,0:T(8,128)(2,1)}, f32[8,128]{1,0:T(8,128)S(1)}) custom-call(s32[3]{0:T(128)S(1)} %pad_add_fusion.refs_0_, bf16[8192,128]{1,0:T(8,128)(2,1)} %get-tuple-element.83.refs_1_, bf16[8192,128]{1,0:T(8,128)(2,1)} %copy-done.1, bf16[8192,128]{1,0:T(8,128)(2,1)} %get-tuple-element.106.refs_3_, bf16[8192,128]{1,0:T(8,128)(2,1)} %copy-done, ...), custom_call_target="tpu_custom_call" | custom-call | tf_op jit(solution)/shard_map/factors/pallas_call | solution.py:32
  130.5 2.7 %collective-permute-start.21 = (f32[4,512]{1,0:T(4,128)S(1)}, f32[4,512]{1,0:T(4,128)S(1)}, u32[]{:S(2)}, u32[]{:S(2)}) collective-permute-start(f32[4,512]{1,0:T(4,128)S(1)} %get-tuple-element.133.refs_0_), channel_id=1, source_target_pairs={{0,16},{8,24},{16,0},{24,8},{1,17},{9,25},{17,1},{25,9},{2,18},{10... | collective-permute-start | bytes 24584 | tf_op jit(solution)/shard_map/ppermute | solution.py:408
  133.2 15.2 %update.4 = (bf16[65536,128]{1,0:T(8,128)(2,1)}, f32[8,128]{1,0:T(8,128)S(1)}) custom-call(bf16[65536,128]{1,0:T(8,128)(2,1)} %bitcast.35, bf16[1024,2048]{1,0:T(8,128)(2,1)} %get-tuple-element.128.refs_1_, bf16[512,512]{1,0:T(8,128)(2,1)S(1)} %get-tuple-element.92.refs_1_.refs_4_.refs_2_, ...), custom_call_target="tpu_custom_call" | custom-call | tf_op jit(solution)/shard_map/update/pallas_call | solution.py:32
  148.5 1.2 choose.11
  151.8 4.6 %collective-permute-start.23 = (bf16[512,512]{1,0:T(8,128)(2,1)S(1)}, bf16[512,512]{1,0:T(8,128)(2,1)S(1)}, u32[]{:S(2)}, u32[]{:S(2)}) collective-permute-start(bf16[512,512]{1,0:T(8,128)(2,1)S(1)} %get-tuple-element.138.refs_1_), channel_id=1, source_target_pairs={{0,4},{1,5},{8,12},{9,13},{16,20},{17,21},{24,28},{25,29}} | collective-permute-start | bytes 1572872 | tf_op jit(solution)/shard_map/ppermute | solution.py:427
  156.3 1.6 collective-permute-start.24
  157.9 17.3 %collective-permute-done.24.refs_1_ = f32[4,512]{1,0:T(4,128)S(1)} collective-permute-done((f32[4,512]{1,0:T(4,128)S(1)}, f32[4,512]{1,0:T(4,128)S(1)}, u32[]{:S(2)}, u32[]{:S(2)}) %collective-permute-start.24) | collective-permute-done | bytes 8224 | tf_op jit(solution)/shard_map/ppermute | solution.py:408
  175.3 11.1 %update.5 = (bf16[65536,128]{1,0:T(8,128)(2,1)}, f32[8,128]{1,0:T(8,128)S(1)}) custom-call(bf16[65536,128]{1,0:T(8,128)(2,1)} %bitcast.36, bf16[1024,2048]{1,0:T(8,128)(2,1)} %get-tuple-element.128.refs_1_, bf16[1024,512]{1,0:T(8,128)(2,1)S(1)} %get-tuple-element.144.refs_2_, ...), custom_call_target="tpu_custom_call", output_to_operand_aliasing={{0}: (4, {})} | custom-call | tf_op jit(solution)/shard_map/update/pallas_call | solution.py:32
  190.0 6.5 %collective-permute-start.31 = (f32[4,512]{1,0:T(4,128)S(1)}, f32[4,512]{1,0:T(4,128)S(1)}, u32[]{:S(2)}, u32[]{:S(2)}) collective-permute-start(f32[4,512]{1,0:T(4,128)S(1)} %get-tuple-element.150.refs_0_), channel_id=1, source_target_pairs={{0,4},{1,5},{2,6},{3,7},{4,0},{5,1},{6,2},{7,3},{8,12},{9,13},{10,... | collective-permute-start | bytes 24584 | tf_op jit(solution)/shard_map/ppermute | solution.py:408
  196.6 15.8 %collective-permute-done.34.refs_3_ = bf16[1024,512]{1,0:T(8,128)(2,1)S(1)} collective-permute-done((bf16[1024,512]{1,0:T(8,128)(2,1)S(1)}, bf16[1024,512]{1,0:T(8,128)(2,1)S(1)}, u32[]{:S(2)}, u32[]{:S(2)}) %collective-permute-start.34) | collective-permute-done | bytes 1048608 | tf_op jit(solution)/shard_map/ppermute | solution.py:408
  212.4 11.1 %update.6 = (bf16[65536,128]{1,0:T(8,128)(2,1)}, f32[8,128]{1,0:T(8,128)S(1)}) custom-call(bf16[65536,128]{1,0:T(8,128)(2,1)} %bitcast.37, bf16[1024,2048]{1,0:T(8,128)(2,1)} %get-tuple-element.128.refs_1_, bf16[1024,512]{1,0:T(8,128)(2,1)S(1)} %get-tuple-element.153.refs_2_, ...), custom_call_target="tpu_custom_call", output_to_operand_aliasing={{0}: (4, {})} | custom-call | tf_op jit(solution)/shard_map/update/pallas_call | solution.py:32
  225.3 11.2 %collective-permute-done.35.refs_3_ = bf16[512,512]{1,0:T(8,128)(2,1)S(1)} collective-permute-done((bf16[512,512]{1,0:T(8,128)(2,1)S(1)}, bf16[512,512]{1,0:T(8,128)(2,1)S(1)}, u32[]{:S(2)}, u32[]{:S(2)}) %collective-permute-start.35) | collective-permute-done | bytes 524320 | tf_op jit(solution)/shard_map/ppermute | solution.py:408
  236.5 7.3 %update.7 = (bf16[65536,128]{1,0:T(8,128)(2,1)}, f32[8,128]{1,0:T(8,128)}) custom-call(bf16[65536,128]{1,0:T(8,128)(2,1)} %bitcast.38, bf16[1024,2048]{1,0:T(8,128)(2,1)} %get-tuple-element.128.refs_1_, bf16[512,512]{1,0:T(8,128)(2,1)S(1)} %get-tuple-element.158.refs_2_, ...), custom_call_target="tpu_custom_call", output_to_operand_aliasing={{0}: (4, {})} | custom-call | tf_op jit(solution)/shard_map/update/pallas_call | solution.py:32
  (104 shorter events, 16.2 us)
Async XLA Ops:
  4.8 19.0 %collective-permute-start.1 = (bf16[8192,128]{1,0:T(8,128)(2,1)}, bf16[8192,128]{1,0:T(8,128)(2,1)S(1)}, u32[]{:S(2)}, u32[]{:S(2)}) collective-permute-start(bf16[8192,128]{1,0:T(8,128)(2,1)} %get-tuple-element.83.refs_1_), channel_id=1, source_target_pairs={{0,8},{8,0},{16,24},{24,16},{1,9},{9,1},{17,25},{25,17},{2,10},{10... | collective-permute-start | bytes 6291464 | tf_op jit(solution)/shard_map/ppermute | solution.py:408
  5.3 65.9 %collective-permute-start.2 = (bf16[8192,128]{1,0:T(8,128)(2,1)}, bf16[8192,128]{1,0:T(8,128)(2,1)}, u32[]{:S(2)}, u32[]{:S(2)}) collective-permute-start(bf16[8192,128]{1,0:T(8,128)(2,1)} %get-tuple-element.83.refs_1_), channel_id=1, source_target_pairs={{0,16},{8,24},{16,0},{24,8},{1,17},{9,25},{17,1},{25,9},{2,18},{10... | collective-permute-start | bytes 6291464 | tf_op jit(solution)/shard_map/ppermute | solution.py:404
  7.8 16.0 %collective-permute-start = (bf16[512,512]{1,0:T(8,128)(2,1)S(1)}, bf16[512,512]{1,0:T(8,128)(2,1)S(1)}, u32[]{:S(2)}, u32[]{:S(2)}) collective-permute-start(bf16[512,512]{1,0:T(8,128)(2,1)S(1)} %get-tuple-element.84.refs_1_.refs_6_), channel_id=1, source_target_pairs={{0,4},{1,5},{8,12},{9,13},{16,20},{17,21},{24,28},{25,29}} | collective-permute-start | bytes 1572872 | tf_op jit(solution)/shard_map/ppermute | solution.py:427
  17.5 17.3 %copy-start.14 = (bf16[4,1,512]{2,0,1:T(4,128)(2,1)S(1)}, bf16[4,1,512]{2,0,1:T(4,128)(2,1)}, u32[]{:S(2)}) copy-start(bf16[4,1,512]{2,0,1:T(4,128)(2,1)} %param.9) | copy-start | bytes 12292
  23.8 1.3 copy-start.1
  25.2 21.3 %collective-permute-start.3 = (bf16[512,512]{1,0:T(8,128)(2,1)S(1)}, bf16[512,512]{1,0:T(8,128)(2,1)S(1)}, u32[]{:S(2)}, u32[]{:S(2)}) collective-permute-start(bf16[512,512]{1,0:T(8,128)(2,1)S(1)} %get-tuple-element.89.refs_2_), channel_id=1, source_target_pairs={{4,2},{5,3},{12,10},{13,11},{20,18},{21,19},{28,26},{29,27}} | collective-permute-start | bytes 1572872 | tf_op jit(solution)/shard_map/ppermute | solution.py:430
  25.9 21.5 %collective-permute-start.4 = (bf16[512,512]{1,0:T(8,128)(2,1)S(1)}, bf16[512,512]{1,0:T(8,128)(2,1)}, u32[]{:S(2)}, u32[]{:S(2)}) collective-permute-start(bf16[512,512]{1,0:T(8,128)(2,1)S(1)} %get-tuple-element.89.refs_2_), channel_id=1, source_target_pairs={{4,6},{5,7},{12,14},{13,15},{20,22},{21,23},{28,30},{29,31}} | collective-permute-start | bytes 1572872 | tf_op jit(solution)/shard_map/ppermute | solution.py:430
  27.4 42.9 %collective-permute-start.6 = (bf16[1024,512]{1,0:T(8,128)(2,1)}, bf16[1024,512]{1,0:T(8,128)(2,1)}, u32[]{:S(2)}, u32[]{:S(2)}) collective-permute-start(bf16[1024,512]{1,0:T(8,128)(2,1)} %get-tuple-element.93.refs_1_), channel_id=1, source_target_pairs={{0,4},{1,5},{8,12},{9,13},{16,20},{17,21},{24,28},{25,29}} | collective-permute-start | bytes 3145736 | tf_op jit(solution)/shard_map/ppermute | solution.py:427
  46.5 23.8 %copy-start.3 = (bf16[512,512]{1,0:T(8,128)(2,1)}, bf16[512,512]{1,0:T(8,128)(2,1)S(1)}, u32[]{:S(2)}) copy-start(bf16[512,512]{1,0:T(8,128)(2,1)S(1)} %get-tuple-element.130.refs_1_) | copy-start | bytes 1572868
  48.5 21.8 %collective-permute-start.5 = (bf16[512,512]{1,0:T(8,128)(2,1)S(1)}, bf16[512,512]{1,0:T(8,128)(2,1)S(1)}, u32[]{:S(2)}, u32[]{:S(2)}) collective-permute-start(bf16[512,512]{1,0:T(8,128)(2,1)S(1)} %get-tuple-element.92.refs_1_.refs_4_.refs_2_), channel_id=1, source_target_pairs={{0,1},{1,0},{2,3},{3,2},{4,5},{5,4},{6,7},{7,6},{8,9},{9,8},{10,11... | collective-permute-start | bytes 1572872 | tf_op jit(solution)/shard_map/ppermute | solution.py:408
  50.1 11.7 %collective-permute-start.7 = (f32[8,512]{1,0:T(8,128)S(1)}, f32[8,512]{1,0:T(8,128)S(1)}, u32[]{:S(2)}, u32[]{:S(2)}) collective-permute-start(f32[8,512]{1,0:T(8,128)S(1)} %reshape.48.refs_0_), channel_id=1, source_target_pairs={{0,1},{1,0},{2,3},{3,2},{4,5},{5,4},{6,7},{7,6},{8,9},{9,8},{10,11... | collective-permute-start | bytes 49160 | tf_op jit(solution)/shard_map/ppermute | solution.py:408
  61.9 3.7 %collective-permute-start.8 = (f32[8,512]{1,0:T(8,128)S(1)}, f32[8,512]{1,0:T(8,128)S(1)}, u32[]{:S(2)}, u32[]{:S(2)}) collective-permute-start(f32[8,512]{1,0:T(8,128)S(1)} %get-tuple-element.99.refs_0_), channel_id=1, source_target_pairs={{0,2},{1,3},{2,0},{3,1},{4,6},{5,7},{6,4},{7,5},{8,10},{9,11},{10,... | collective-permute-start | bytes 49160 | tf_op jit(solution)/shard_map/ppermute | solution.py:408
  65.6 4.6 %collective-permute-start.9 = (f32[8,512]{1,0:T(8,128)S(1)}, f32[8,512]{1,0:T(8,128)S(1)}, u32[]{:S(2)}, u32[]{:S(2)}) collective-permute-start(f32[8,512]{1,0:T(8,128)S(1)} %get-tuple-element.101.refs_0_), channel_id=1, source_target_pairs={{0,4},{1,5},{2,6},{3,7},{4,0},{5,1},{6,2},{7,3},{8,12},{9,13},{10,... | collective-permute-start | bytes 49160 | tf_op jit(solution)/shard_map/ppermute | solution.py:408
  70.3 7.9 %copy-start.17 = (f32[8,1,512]{2,1,0:T(1,128)S(1)}, f32[8,1,512]{2,1,0:T(1,128)}, u32[]{:S(2)}) copy-start(f32[8,1,512]{2,1,0:T(1,128)} %param.10) | copy-start | bytes 49156
  70.3 7.9 %copy-start.2 = (bf16[1,1,512,512]{3,2,1,0:T(8,128)(2,1)S(1)}, bf16[1,1,512,512]{3,2,1,0:T(8,128)(2,1)}, u32[]{:S(2)}) copy-start(bf16[1,1,512,512]{3,2,1,0:T(8,128)(2,1)} %param.11) | copy-start | bytes 1572868
  71.2 8.5 %collective-permute-start.10 = (bf16[8192,128]{1,0:T(8,128)(2,1)}, bf16[8192,128]{1,0:T(8,128)(2,1)S(1)}, u32[]{:S(2)}, u32[]{:S(2)}) collective-permute-start(bf16[8192,128]{1,0:T(8,128)(2,1)} %get-tuple-element.106.refs_3_), channel_id=1, source_target_pairs={{0,8},{8,0},{16,24},{24,16},{1,9},{9,1},{17,25},{25,17},{2,10},{10... | collective-permute-start | bytes 6291464 | tf_op jit(solution)/shard_map/ppermute | solution.py:408
  71.3 19.0 %collective-permute-start.11 = (bf16[512,512]{1,0:T(8,128)(2,1)}, bf16[512,512]{1,0:T(8,128)(2,1)}, u32[]{:S(2)}, u32[]{:S(2)}) collective-permute-start(bf16[512,512]{1,0:T(8,128)(2,1)} %get-tuple-element.111.refs_1_), channel_id=1, source_target_pairs={{0,16},{8,24},{16,0},{24,8},{1,17},{9,25},{17,1},{25,9},{2,18},{10... | collective-permute-start | bytes 1572872 | tf_op jit(solution)/shard_map/ppermute | solution.py:404
  71.9 26.6 %collective-permute-start.18 = (bf16[1024,512]{1,0:T(8,128)(2,1)}, bf16[1024,512]{1,0:T(8,128)(2,1)}, u32[]{:S(2)}, u32[]{:S(2)}) collective-permute-start(bf16[1024,512]{1,0:T(8,128)(2,1)} %get-tuple-element.123.refs_1_), channel_id=1, source_target_pairs={{0,4},{1,5},{8,12},{9,13},{16,20},{17,21},{24,28},{25,29}} | collective-permute-start | bytes 3145736 | tf_op jit(solution)/shard_map/ppermute | solution.py:427
  74.8 23.7 %collective-permute-start.16 = (bf16[1024,512]{1,0:T(8,128)(2,1)}, bf16[1024,512]{1,0:T(8,128)(2,1)}, u32[]{:S(2)}, u32[]{:S(2)}) collective-permute-start(bf16[1024,512]{1,0:T(8,128)(2,1)} %get-tuple-element.122.refs_2_), channel_id=1, source_target_pairs={{4,2},{5,3},{12,10},{13,11},{20,18},{21,19},{28,26},{29,27}} | collective-permute-start | bytes 3145736 | tf_op jit(solution)/shard_map/ppermute | solution.py:430
  76.5 22.0 %collective-permute-start.17 = (bf16[1024,512]{1,0:T(8,128)(2,1)}, bf16[1024,512]{1,0:T(8,128)(2,1)}, u32[]{:S(2)}, u32[]{:S(2)}) collective-permute-start(bf16[1024,512]{1,0:T(8,128)(2,1)} %get-tuple-element.122.refs_2_), channel_id=1, source_target_pairs={{4,6},{5,7},{12,14},{13,15},{20,22},{21,23},{28,30},{29,31}} | collective-permute-start | bytes 3145736 | tf_op jit(solution)/shard_map/ppermute | solution.py:430
  79.7 3.1 %collective-permute-start.12 = (f32[4,512]{1,0:T(4,128)S(1)}, f32[4,512]{1,0:T(4,128)S(1)}, u32[]{:S(2)}, u32[]{:S(2)}) collective-permute-start(f32[4,512]{1,0:T(4,128)S(1)} %get-tuple-element.112), channel_id=1, source_target_pairs={{0,8},{8,16},{16,24},{1,9},{9,17},{17,25},{2,10},{10,18},{18,26},{... | collective-permute-start | bytes 24584 | tf_op jit(solution)/shard_map/ppermute | solution.py:497
  81.6 1.3 copy-start
  84.4 4.5 %collective-permute-start.13 = (f32[4,512]{1,0:T(4,128)S(1)}, f32[4,512]{1,0:T(4,128)S(1)}, u32[]{:S(2)}, u32[]{:S(2)}) collective-permute-start(f32[4,512]{1,0:T(4,128)S(1)} %get-tuple-element.114), channel_id=1, source_target_pairs={{0,8},{8,16},{16,24},{1,9},{9,17},{17,25},{2,10},{10,18},{18,26},{... | collective-permute-start | bytes 24584 | tf_op jit(solution)/shard_map/ppermute | solution.py:497
  91.4 7.1 %copy-start.11 = (bf16[512,512]{1,0:T(8,128)(2,1)}, bf16[512,512]{1,0:T(8,128)(2,1)S(1)}, u32[]{:S(2)}) copy-start(bf16[512,512]{1,0:T(8,128)(2,1)S(1)} %get-tuple-element.117.refs_5_) | copy-start | bytes 1572868
  91.4 6.2 %collective-permute-start.14 = (bf16[512,512]{1,0:T(8,128)(2,1)S(1)}, bf16[512,512]{1,0:T(8,128)(2,1)S(1)}, u32[]{:S(2)}, u32[]{:S(2)}) collective-permute-start(bf16[512,512]{1,0:T(8,128)(2,1)S(1)} %get-tuple-element.117.refs_5_), channel_id=1, source_target_pairs={{0,8},{8,0},{16,24},{24,16},{1,9},{9,1},{17,25},{25,17},{2,10},{10... | collective-permute-start | bytes 1572872 | tf_op jit(solution)/shard_map/ppermute | solution.py:408
  93.4 2.7 %collective-permute-start.15 = (f32[4,512]{1,0:T(4,128)S(1)}, f32[4,512]{1,0:T(4,128)S(1)}, u32[]{:S(2)}, u32[]{:S(2)}) collective-permute-start(f32[4,512]{1,0:T(4,128)S(1)} %get-tuple-element.118), channel_id=1, source_target_pairs={{0,8},{8,16},{16,24},{1,9},{9,17},{17,25},{2,10},{10,18},{18,26},{... | collective-permute-start | bytes 24584 | tf_op jit(solution)/shard_map/ppermute | solution.py:497
  100.7 32.5 %collective-permute-start.22 = (bf16[1024,512]{1,0:T(8,128)(2,1)}, bf16[1024,512]{1,0:T(8,128)(2,1)}, u32[]{:S(2)}, u32[]{:S(2)}) collective-permute-start(bf16[1024,512]{1,0:T(8,128)(2,1)} %get-tuple-element.134.refs_4_), channel_id=1, source_target_pairs={{0,1},{1,0},{2,3},{3,2},{4,5},{5,4},{6,7},{7,6},{8,9},{9,8},{10,11... | collective-permute-start | bytes 3145736 | tf_op jit(solution)/shard_map/ppermute | solution.py:408
  102.3 46.1 %collective-permute-start.19 = (bf16[1024,512]{1,0:T(8,128)(2,1)S(1)}, bf16[1024,512]{1,0:T(8,128)(2,1)S(1)}, u32[]{:S(2)}, u32[]{:S(2)}) collective-permute-start(bf16[1024,512]{1,0:T(8,128)(2,1)S(1)} %get-tuple-element.129.refs_1_), channel_id=1, source_target_pairs={{0,4},{1,5},{8,12},{9,13},{16,20},{17,21},{24,28},{25,29}} | collective-permute-start | bytes 3145736 | tf_op jit(solution)/shard_map/ppermute | solution.py:427
  108.1 40.4 %collective-permute-start.25 = (bf16[1024,512]{1,0:T(8,128)(2,1)}, bf16[1024,512]{1,0:T(8,128)(2,1)}, u32[]{:S(2)}, u32[]{:S(2)}) collective-permute-start(bf16[1024,512]{1,0:T(8,128)(2,1)} %get-tuple-element.140.refs_2_), channel_id=1, source_target_pairs={{4,2},{5,3},{12,10},{13,11},{20,18},{21,19},{28,26},{29,27}} | collective-permute-start | bytes 3145736 | tf_op jit(solution)/shard_map/ppermute | solution.py:430
  109.7 38.7 %collective-permute-start.26 = (bf16[1024,512]{1,0:T(8,128)(2,1)}, bf16[1024,512]{1,0:T(8,128)(2,1)}, u32[]{:S(2)}, u32[]{:S(2)}) collective-permute-start(bf16[1024,512]{1,0:T(8,128)(2,1)} %get-tuple-element.140.refs_2_), channel_id=1, source_target_pairs={{4,6},{5,7},{12,14},{13,15},{20,22},{21,23},{28,30},{29,31}} | collective-permute-start | bytes 3145736 | tf_op jit(solution)/shard_map/ppermute | solution.py:430
  111.4 19.1 %collective-permute-start.20 = (f32[4,512]{1,0:T(4,128)S(1)}, f32[4,512]{1,0:T(4,128)S(1)}, u32[]{:S(2)}, u32[]{:S(2)}) collective-permute-start(f32[4,512]{1,0:T(4,128)S(1)} %broadcast_select_fusion.refs_0_), channel_id=1, source_target_pairs={{0,8},{8,0},{16,24},{24,16},{1,9},{9,1},{17,25},{25,17},{2,10},{10... | collective-permute-start | bytes 24584 | tf_op jit(solution)/shard_map/ppermute | solution.py:408
  111.4 1.0 copy-start.6
  112.5 1.2 copy-start.7
  113.7 1.2 copy-start.8
  130.5 17.9 %collective-permute-start.21 = (f32[4,512]{1,0:T(4,128)S(1)}, f32[4,512]{1,0:T(4,128)S(1)}, u32[]{:S(2)}, u32[]{:S(2)}) collective-permute-start(f32[4,512]{1,0:T(4,128)S(1)} %get-tuple-element.133.refs_0_), channel_id=1, source_target_pairs={{0,16},{8,24},{16,0},{24,8},{1,17},{9,25},{17,1},{25,9},{2,18},{10... | collective-permute-start | bytes 24584 | tf_op jit(solution)/shard_map/ppermute | solution.py:408
  133.2 15.2 %copy-start.4 = (bf16[512,512]{1,0:T(8,128)(2,1)S(1)}, bf16[512,512]{1,0:T(8,128)(2,1)}, u32[]{:S(2)}) copy-start(bf16[512,512]{1,0:T(8,128)(2,1)} %copy-done.3) | copy-start | bytes 1572868
  149.7 25.5 %collective-permute-start.28 = (bf16[1024,512]{1,0:T(8,128)(2,1)S(1)}, bf16[1024,512]{1,0:T(8,128)(2,1)S(1)}, u32[]{:S(2)}, u32[]{:S(2)}) collective-permute-start(bf16[1024,512]{1,0:T(8,128)(2,1)S(1)} %get-tuple-element.144.refs_2_), channel_id=1, source_target_pairs={{0,1},{1,0},{2,3},{3,2},{4,5},{5,4},{6,7},{7,6},{8,9},{9,8},{10,11... | collective-permute-start | bytes 3145736 | tf_op jit(solution)/shard_map/ppermute | solution.py:408
  150.3 36.1 %collective-permute-start.32 = (bf16[1024,512]{1,0:T(8,128)(2,1)S(1)}, bf16[1024,512]{1,0:T(8,128)(2,1)S(1)}, u32[]{:S(2)}, u32[]{:S(2)}) collective-permute-start(bf16[1024,512]{1,0:T(8,128)(2,1)S(1)} %get-tuple-element.151.refs_2_), channel_id=1, source_target_pairs={{4,2},{5,3},{12,10},{13,11},{20,18},{21,19},{28,26},{29,27}} | collective-permute-start | bytes 3145736 | tf_op jit(solution)/shard_map/ppermute | solution.py:430
  151.0 35.4 %collective-permute-start.33 = (bf16[1024,512]{1,0:T(8,128)(2,1)S(1)}, bf16[1024,512]{1,0:T(8,128)(2,1)S(1)}, u32[]{:S(2)}, u32[]{:S(2)}) collective-permute-start(bf16[1024,512]{1,0:T(8,128)(2,1)S(1)} %get-tuple-element.151.refs_2_), channel_id=1, source_target_pairs={{4,6},{5,7},{12,14},{13,15},{20,22},{21,23},{28,30},{29,31}} | collective-permute-start | bytes 3145736 | tf_op jit(solution)/shard_map/ppermute | solution.py:430
  151.8 34.6 %collective-permute-start.23 = (bf16[512,512]{1,0:T(8,128)(2,1)S(1)}, bf16[512,512]{1,0:T(8,128)(2,1)S(1)}, u32[]{:S(2)}, u32[]{:S(2)}) collective-permute-start(bf16[512,512]{1,0:T(8,128)(2,1)S(1)} %get-tuple-element.138.refs_1_), channel_id=1, source_target_pairs={{0,4},{1,5},{8,12},{9,13},{16,20},{17,21},{24,28},{25,29}} | collective-permute-start | bytes 1572872 | tf_op jit(solution)/shard_map/ppermute | solution.py:427
  156.3 18.9 %collective-permute-start.24 = (f32[4,512]{1,0:T(4,128)S(1)}, f32[4,512]{1,0:T(4,128)S(1)}, u32[]{:S(2)}, u32[]{:S(2)}) collective-permute-start(f32[4,512]{1,0:T(4,128)S(1)} %get-tuple-element.139.refs_0_), channel_id=1, source_target_pairs={{0,1},{1,0},{2,3},{3,2},{4,5},{5,4},{6,7},{7,6},{8,9},{9,8},{10,11... | collective-permute-start | bytes 24584 | tf_op jit(solution)/shard_map/ppermute | solution.py:408
  175.3 11.1 %collective-permute-start.27 = (f32[4,512]{1,0:T(4,128)S(1)}, f32[4,512]{1,0:T(4,128)S(1)}, u32[]{:S(2)}, u32[]{:S(2)}) collective-permute-start(f32[4,512]{1,0:T(4,128)S(1)} %get-tuple-element.143.refs_0_), channel_id=1, source_target_pairs={{0,2},{1,3},{2,0},{3,1},{4,6},{5,7},{6,4},{7,5},{8,10},{9,11},{10,... | collective-permute-start | bytes 24584 | tf_op jit(solution)/shard_map/ppermute | solution.py:408
  186.4 1.3 copy-start.16
  187.8 24.5 %collective-permute-start.34 = (bf16[1024,512]{1,0:T(8,128)(2,1)S(1)}, bf16[1024,512]{1,0:T(8,128)(2,1)S(1)}, u32[]{:S(2)}, u32[]{:S(2)}) collective-permute-start(bf16[1024,512]{1,0:T(8,128)(2,1)S(1)} %get-tuple-element.153.refs_2_), channel_id=1, source_target_pairs={{0,1},{1,0},{2,3},{3,2},{4,5},{5,4},{6,7},{7,6},{8,9},{9,8},{10,11... | collective-permute-start | bytes 3145736 | tf_op jit(solution)/shard_map/ppermute | solution.py:408
  188.4 35.6 %collective-permute-start.29 = (bf16[512,512]{1,0:T(8,128)(2,1)S(1)}, bf16[512,512]{1,0:T(8,128)(2,1)S(1)}, u32[]{:S(2)}, u32[]{:S(2)}) collective-permute-start(bf16[512,512]{1,0:T(8,128)(2,1)S(1)} %get-tuple-element.149.refs_2_), channel_id=1, source_target_pairs={{4,2},{5,3},{12,10},{13,11},{20,18},{21,19},{28,26},{29,27}} | collective-permute-start | bytes 1572872 | tf_op jit(solution)/shard_map/ppermute | solution.py:430
  189.1 35.0 %collective-permute-start.30 = (bf16[512,512]{1,0:T(8,128)(2,1)S(1)}, bf16[512,512]{1,0:T(8,128)(2,1)S(1)}, u32[]{:S(2)}, u32[]{:S(2)}) collective-permute-start(bf16[512,512]{1,0:T(8,128)(2,1)S(1)} %get-tuple-element.149.refs_2_), channel_id=1, source_target_pairs={{4,6},{5,7},{12,14},{13,15},{20,22},{21,23},{28,30},{29,31}} | collective-permute-start | bytes 1572872 | tf_op jit(solution)/shard_map/ppermute | solution.py:430
  190.0 33.4 %collective-permute-start.31 = (f32[4,512]{1,0:T(4,128)S(1)}, f32[4,512]{1,0:T(4,128)S(1)}, u32[]{:S(2)}, u32[]{:S(2)}) collective-permute-start(f32[4,512]{1,0:T(4,128)S(1)} %get-tuple-element.150.refs_0_), channel_id=1, source_target_pairs={{0,4},{1,5},{2,6},{3,7},{4,0},{5,1},{6,2},{7,3},{8,12},{9,13},{10,... | collective-permute-start | bytes 24584 | tf_op jit(solution)/shard_map/ppermute | solution.py:408
  224.1 12.4 %collective-permute-start.35 = (bf16[512,512]{1,0:T(8,128)(2,1)S(1)}, bf16[512,512]{1,0:T(8,128)(2,1)S(1)}, u32[]{:S(2)}, u32[]{:S(2)}) collective-permute-start(bf16[512,512]{1,0:T(8,128)(2,1)S(1)} %get-tuple-element.158.refs_2_), channel_id=1, source_target_pairs={{0,1},{1,0},{2,3},{3,2},{4,5},{5,4},{6,7},{7,6},{8,9},{9,8},{10,11... | collective-permute-start | bytes 1572872 | tf_op jit(solution)/shard_map/ppermute | solution.py:408
  (6 other events, 5.5 us)

commit v5 on v4

--- a/solution.py
+++ b/solution.py
@@ -455,6 +455,7 @@
     where = jnp.stack([core, lane, prow // 2]).astype(jnp.int32)
     flag = jnp.where(core != lane, 0, 1).astype(jnp.int32).reshape(1)
     bits = [1 << b for b in range(n_pcol.bit_length() - 1)]
+    order = bits[1:] + bits[:1]
 
     sizes = [width] + [2 * width] * ((slots - 2) // 2)
     sizes += [width] * (slots - sum(sizes) // width)
@@ -477,10 +478,10 @@
 
     def total_step(bit):
         def run():
-            if bit == 1:
+            if bit == order[0]:
                 box["total"] = jnp.concatenate(parts, axis=1).reshape(slots, width)
             box["total"] = chain.add(box["total"], swap(box["total"], "pcol", n_pcol, bit))
-            if bit == bits[-1]:
+            if bit == order[-1]:
                 box["residual"] = right_side.reshape(slots, width) - box["total"]
 
         return run
@@ -544,26 +545,15 @@
         mine[c] = settle(column[c], first[c], outward[c])
         other[c] = swap(mine[c], "pcol", n_pcol)
 
-    total = [total_step(b) for b in bits]
+    total = [total_step(b) for b in order]
     line = [solve(k) for k in range(count)]
     line += [share("prow", n_prow, 1 << b) for b in range(n_prow.bit_length() - 1)]
     line += [share("pcol", n_pcol, b) for b in bits]
-    def rest_extracted():
-        if chunks > 2:
-            parts.append(extracts(2, chunks)[0])
-
-    if chunks == 5 and len(line) == 9:
-        plan = {
-            0: [rest_extracted, lambda: take(0), *total],
-            1: [blocks_out, line[0], bands_in, *line[1:3], blocks_swap, line[3], blocks_in],
-            2: [make_factors, line[4], updates(0, 1), line[5]],
-            3: [line[6], updates(2), line[7]],
-            4: [updates(3), line[8]],
-        }
-    else:
-        plan = {0: [rest_extracted, lambda: take(0), *total], chunks - 1: [blocks_out, bands_in, blocks_swap, blocks_in, make_factors, *line, updates(*range(chunks - 1))]}
-
-    for k in range(chunks):
+    def extracted(a, b):
+        if a < b:
+            parts.append(extracts(a, b)[0])
+
+    def advance(k):
         ahead = [column[k + 1]] if k + 1 < chunks else []
         extra = [swaps[0]] if k == 0 else []
         got = chain.gate([first[k], *ahead, *extra], [])
@@ -572,16 +562,40 @@
         if ahead:
             column[k + 1] = got[1]
             first[k + 1] = first_stage(column[k + 1])
-        extra = got[1 + len(ahead) :]
-        if k == 0:
-            swaps[0] = extra[0]
+        if extra:
+            swaps[0] = got[-1]
         outward[k] = second_stage(first[k])
-        if k > 1:
-            take(k - 1)
-        for task in plan.get(k, []):
+
+    def each(tasks):
+        for task in tasks:
             task()
-    take(chunks - 1)
-    updates(chunks - 1)()
+
+    advance(0)
+    extracted(2, min(3, chunks))
+    take(0)
+    extracted(3, chunks)
+    if chunks == 5 and len(line) == 9:
+        each(total[:2])
+        advance(1)
+        each([blocks_out, total[2], bands_in, line[0], blocks_swap, blocks_in, make_factors])
+        advance(2)
+        take(1)
+        updates(0)()
+        other[1] = arrive([other[1]])[0]
+        advance(3)
+        take(2)
+        each([updates(1), *line[1:6]])
+        advance(4)
+        take(3)
+        each([line[6], updates(2)])
+        take(4)
+        each([line[7], updates(3), line[8], updates(4)])
+    else:
+        each([*total, blocks_out, bands_in, blocks_swap, blocks_in, make_factors, *line])
+        for k in range(1, chunks):
+            advance(k)
+            take(k)
+        updates(*range(chunks))()
     residual, out, state = box["residual"], box["out"], box["state"]
     updated = out.reshape(rows, lane_tiles, col_slots, LANES).transpose(0, 2, 1, 3).reshape(matrix.shape)
     return (updated, residual.reshape(right_side.shape), state)

time: 245 us -> 236 us (0.963)
  waiting for transfers between devices: 71.8 us -> 56.5 us
  Pallas kernels: 91.9 us -> 96 us
  starting transfers between devices: 66.2 us -> 69.9 us
    ppermute x16, waiting for transfers between devices: 63.8 us -> 42.9 us  [swap(): return lax.ppermute(value, axis, [(i, i ^ bit) for i in range(size)])]
    ppermute x5, starting transfers between devices: 25.3 us -> 30.4 us  [first_stage(): return lax.ppermute(local, 'pcol', along_z(stages[0][0]))]
    pallas_call x35 -> x38, Pallas kernels: 91.9 us -> 96 us  [__call__(): pl.pallas_call(body, in_specs=list(in_specs) + [anywhere] * n_dep, out_sp...]
    ppermute x2, waiting for transfers between devices: 0.01 us -> 3.76 us  [spread(): values.append(lax.ppermute(values[-1], axis, pairs))]
    unnamed x37 -> x35, local copies, waits for them, and re-layouts: 12.5 us -> 10.9 us
  transfers between devices with their start and end apart: 36 -> 36, of which waited for: 9 -> 13; matrix products, arithmetic and copies ran while one was open for 0% -> 0% of each run, Pallas kernels for 32% -> 36%
where the time goes in v5:
time: 236 us; the launch traced here: 235 us
  Pallas kernels  96 us (41%)
  starting transfers between devices  69.9 us (30%)
  waiting for transfers between devices  56.5 us (24%)
  local copies, waits for them, and re-layouts  10.9 us (5%)
    pallas_call x38, Pallas kernels, __call__(): pl.pallas_call(body, in_specs=list(in_specs) + [anywhere] * n_dep, out_sp...  96 us
    ppermute x16, waiting for transfers between devices, swap(): return lax.ppermute(value, axis, [(i, i ^ bit) for i in range(size)])  42.9 us
    ppermute x5, starting transfers between devices, first_stage(): return lax.ppermute(local, 'pcol', along_z(stages[0][0]))  30.4 us
    ppermute x16, starting transfers between devices, swap(): return lax.ppermute(value, axis, [(i, i ^ bit) for i in range(size)])  18.7 us
    ppermute x10, starting transfers between devices, second_stage(): lax.ppermute(arrived, 'pcol', along_z(moves))  11.1 us
    unnamed x35, local copies, waits for them, and re-layouts  10.9 us
    ppermute x5, waiting for transfers between devices, first_stage(): return lax.ppermute(local, 'pcol', along_z(stages[0][0]))  8.25 us
    ppermute x3, starting transfers between devices, run(): lax.ppermute(box['state'], 'prow', [(i, i + 1) for i in range(n_prow - 1)])  6.71 us
  transfers between devices with their start and end apart: 36, of which 13 were waited for; matrix products, arithmetic and copies ran while one was open for 0% of the time, Pallas kernels for 36%

profile of v5, /device:TPU:0, one launch (start us, length us, event | category | flops | bytes accessed | tf_op | source)
XLA Modules:
  0.0 234.6 jit_solution(4379905198385086804)
XLA Ops:
  1.3 3.5 %extract.4 = (f32[1,512]{1,0:T(1,128)S(1)}, bf16[512,512]{1,0:T(8,128)(2,1)S(1)}, bf16[8192,128]{1,0:T(8,128)(2,1)}, f32[8,128]{1,0:T(8,128)S(1)}) custom-call(bf16[65536,128]{1,0:T(8,128)(2,1)} %bitcast.33, bf16[16,128]{1,0:T(8,128)(2,1)S(1)} %bitcast.29), custom_call_target="tpu_custom_call" | custom-call | tf_op jit(solution)/shard_map/extract/pallas_call | solution.py:32
  5.3 2.5 %collective-permute-start.2 = (bf16[8192,128]{1,0:T(8,128)(2,1)}, bf16[8192,128]{1,0:T(8,128)(2,1)}, u32[]{:S(2)}, u32[]{:S(2)}) collective-permute-start(bf16[8192,128]{1,0:T(8,128)(2,1)} %get-tuple-element.89.refs_1_), channel_id=1, source_target_pairs={{0,16},{8,24},{16,0},{24,8},{1,17},{9,25},{17,1},{25,9},{2,18},{10... | collective-permute-start | bytes 6291464 | tf_op jit(solution)/shard_map/ppermute | solution.py:404
  7.8 5.3 %collective-permute-start = (bf16[512,512]{1,0:T(8,128)(2,1)S(1)}, bf16[512,512]{1,0:T(8,128)(2,1)}, u32[]{:S(2)}, u32[]{:S(2)}) collective-permute-start(bf16[512,512]{1,0:T(8,128)(2,1)S(1)} %get-tuple-element.90.refs_1_.refs_6_), channel_id=1, source_target_pairs={{0,4},{1,5},{8,12},{9,13},{16,20},{17,21},{24,28},{25,29}} | collective-permute-start | bytes 1572872 | tf_op jit(solution)/shard_map/ppermute | solution.py:427
  13.1 5.3 %extract.5 = (f32[1,1024]{1,0:T(1,128)S(1)}, bf16[1024,512]{1,0:T(8,128)(2,1)}, f32[8,128]{1,0:T(8,128)S(1)}) custom-call(bf16[65536,128]{1,0:T(8,128)(2,1)} %bitcast.34, bf16[16,128]{1,0:T(8,128)(2,1)S(1)} %bitcast.30, f32[8,128]{1,0:T(8,128)S(1)} %get-tuple-element.91.refs_2_), custom_call_target="tpu_custom_call" | custom-call | tf_op jit(solution)/shard_map/extract/pallas_call | solution.py:32
  18.3 5.5 %collective-permute-done.refs_0_ = bf16[512,512]{1,0:T(8,128)(2,1)} collective-permute-done((bf16[512,512]{1,0:T(8,128)(2,1)S(1)}, bf16[512,512]{1,0:T(8,128)(2,1)}, u32[]{:S(2)}, u32[]{:S(2)}) %collective-permute-start) | collective-permute-done | bytes 524320 | tf_op jit(solution)/shard_map/ppermute | solution.py:427
  23.8 1.3 copy-done
  26.6 7.6 %collective-permute-start.6 = (bf16[1024,512]{1,0:T(8,128)(2,1)}, bf16[1024,512]{1,0:T(8,128)(2,1)}, u32[]{:S(2)}, u32[]{:S(2)}) collective-permute-start(bf16[1024,512]{1,0:T(8,128)(2,1)} %get-tuple-element.99.refs_1_), channel_id=1, source_target_pairs={{0,4},{1,5},{8,12},{9,13},{16,20},{17,21},{24,28},{25,29}} | collective-permute-start | bytes 3145736 | tf_op jit(solution)/shard_map/ppermute | solution.py:427
  34.2 4.9 %extract.6 = (f32[1,1024]{1,0:T(1,128)S(1)}, bf16[1024,512]{1,0:T(8,128)(2,1)S(1)}, f32[8,128]{1,0:T(8,128)S(1)}) custom-call(bf16[65536,128]{1,0:T(8,128)(2,1)} %bitcast.35, bf16[16,128]{1,0:T(8,128)(2,1)S(1)} %bitcast.31, f32[8,128]{1,0:T(8,128)S(1)} %get-tuple-element.96.refs_2_), custom_call_target="tpu_custom_call" | custom-call | tf_op jit(solution)/shard_map/extract/pallas_call | solution.py:32
  43.9 1.6 collective-permute-start.5
  45.5 7.4 %extract.7 = (f32[1,1536]{1,0:T(1,128)S(1)}, bf16[1024,512]{1,0:T(8,128)(2,1)S(1)}, bf16[512,512]{1,0:T(8,128)(2,1)}, f32[8,128]{1,0:T(8,128)S(1)}) custom-call(bf16[65536,128]{1,0:T(8,128)(2,1)} %bitcast.36, bf16[16,128]{1,0:T(8,128)(2,1)S(1)} %bitcast.32, f32[8,128]{1,0:T(8,128)S(1)} %get-tuple-element.104.refs_2_), custom_call_target="tpu_custom_call" | custom-call | tf_op jit(solution)/shard_map/extract/pallas_call | solution.py:32
  52.9 2.6 %collective-permute-start.7 = (f32[8,512]{1,0:T(8,128)S(1)}, f32[8,512]{1,0:T(8,128)S(1)}, u32[]{:S(2)}, u32[]{:S(2)}) collective-permute-start(f32[8,512]{1,0:T(8,128)S(1)} %reshape.48.refs_0_), channel_id=1, source_target_pairs={{0,2},{1,3},{2,0},{3,1},{4,6},{5,7},{6,4},{7,5},{8,10},{9,11},{10,... | collective-permute-start | bytes 49160 | tf_op jit(solution)/shard_map/ppermute | solution.py:408
  55.5 1.7 collective-permute-done.7.refs_1_
  57.3 2.1 collective-permute-start.8
  59.4 2.5 %collective-permute-done.8.refs_1_ = f32[8,512]{1,0:T(8,128)S(1)} collective-permute-done((f32[8,512]{1,0:T(8,128)S(1)}, f32[8,512]{1,0:T(8,128)S(1)}, u32[]{:S(2)}, u32[]{:S(2)}) %collective-permute-start.8) | collective-permute-done | bytes 16416 | tf_op jit(solution)/shard_map/ppermute | solution.py:408
  61.9 1.2 copy-done.3
  66.2 5.0 %collective-permute-start.13 = (bf16[1024,512]{1,0:T(8,128)(2,1)}, bf16[1024,512]{1,0:T(8,128)(2,1)}, u32[]{:S(2)}, u32[]{:S(2)}) collective-permute-start(bf16[1024,512]{1,0:T(8,128)(2,1)} %copy-done.4), channel_id=1, source_target_pairs={{0,4},{1,5},{8,12},{9,13},{16,20},{17,21},{24,28},{25,29}} | collective-permute-start | bytes 3145736 | tf_op jit(solution)/shard_map/ppermute | solution.py:427
  71.2 1.6 collective-permute-start.16
  72.9 1.7 collective-permute-start.15
  74.7 1.5 solve.4
  76.2 3.8 %collective-permute-done.11.refs_2_ = bf16[512,512]{1,0:T(8,128)(2,1)} collective-permute-done((bf16[512,512]{1,0:T(8,128)(2,1)}, bf16[512,512]{1,0:T(8,128)(2,1)}, u32[]{:S(2)}, u32[]{:S(2)}) %collective-permute-start.11) | collective-permute-done | bytes 524320 | tf_op jit(solution)/shard_map/ppermute | solution.py:404
  81.2 1.8 collective-permute-done.12.refs_0_
  83.0 14.6 %factors.1 = (bf16[1024,2048]{1,0:T(8,128)(2,1)}, f32[8,128]{1,0:T(8,128)S(1)}) custom-call(s32[3]{0:T(128)S(1)} %pad_add_fusion.refs_0_, bf16[8192,128]{1,0:T(8,128)(2,1)} %get-tuple-element.89.refs_1_, bf16[8192,128]{1,0:T(8,128)(2,1)} %copy-done, bf16[8192,128]{1,0:T(8,128)(2,1)} %get-tuple-element.112.refs_3_, ...), custom_call_target="tpu_custom_call" | custom-call | tf_op jit(solution)/shard_map/factors/pallas_call | solution.py:32
  97.7 1.2 choose.10
  99.0 1.6 collective-permute-start.17
  100.5 5.1 %collective-permute-start.14 = (bf16[1024,512]{1,0:T(8,128)(2,1)S(1)}, bf16[1024,512]{1,0:T(8,128)(2,1)}, u32[]{:S(2)}, u32[]{:S(2)}) collective-permute-start(bf16[1024,512]{1,0:T(8,128)(2,1)S(1)} %get-tuple-element.129.refs_1_), channel_id=1, source_target_pairs={{0,4},{1,5},{8,12},{9,13},{16,20},{17,21},{24,28},{25,29}} | collective-permute-start | bytes 3145736 | tf_op jit(solution)/shard_map/ppermute | solution.py:427
  107.2 7.4 %update.5 = (bf16[65536,128]{1,0:T(8,128)(2,1)}, f32[8,128]{1,0:T(8,128)S(1)}) custom-call(bf16[65536,128]{1,0:T(8,128)(2,1)} %bitcast.37, bf16[1024,2048]{1,0:T(8,128)(2,1)} %get-tuple-element.125.refs_1_, bf16[512,512]{1,0:T(8,128)(2,1)S(1)} %get-tuple-element.98.refs_1_.refs_4_.refs_2_, ...), custom_call_target="tpu_custom_call" | custom-call | tf_op jit(solution)/shard_map/update/pallas_call | solution.py:32
  114.6 9.6 %collective-permute-done.17.refs_0_ = bf16[1024,512]{1,0:T(8,128)(2,1)S(1)} collective-permute-done((bf16[1024,512]{1,0:T(8,128)(2,1)S(1)}, bf16[1024,512]{1,0:T(8,128)(2,1)S(1)}, u32[]{:S(2)}, u32[]{:S(2)}) %collective-permute-start.17) | collective-permute-done | bytes 1048608 | tf_op jit(solution)/shard_map/ppermute | solution.py:408
  124.2 2.7 %collective-permute-done.14.refs_0_ = bf16[1024,512]{1,0:T(8,128)(2,1)} collective-permute-done((bf16[1024,512]{1,0:T(8,128)(2,1)S(1)}, bf16[1024,512]{1,0:T(8,128)(2,1)}, u32[]{:S(2)}, u32[]{:S(2)}) %collective-permute-start.14) | collective-permute-done | bytes 1048608 | tf_op jit(solution)/shard_map/ppermute | solution.py:427
  127.0 1.6 collective-permute-start.31
  128.6 1.7 collective-permute-start.30
  130.3 7.4 %collective-permute-start.18 = (bf16[512,512]{1,0:T(8,128)(2,1)}, bf16[512,512]{1,0:T(8,128)(2,1)}, u32[]{:S(2)}, u32[]{:S(2)}) collective-permute-start(bf16[512,512]{1,0:T(8,128)(2,1)} %get-tuple-element.137.refs_1_), channel_id=1, source_target_pairs={{0,4},{1,5},{8,12},{9,13},{16,20},{17,21},{24,28},{25,29}} | collective-permute-start | bytes 1572872 | tf_op jit(solution)/shard_map/ppermute | solution.py:427
  140.8 1.3 collective-permute-start.19
  142.0 11.1 %update.6 = (bf16[65536,128]{1,0:T(8,128)(2,1)}, f32[8,128]{1,0:T(8,128)S(1)}) custom-call(bf16[65536,128]{1,0:T(8,128)(2,1)} %bitcast.38, bf16[1024,2048]{1,0:T(8,128)(2,1)} %get-tuple-element.125.refs_1_, bf16[1024,512]{1,0:T(8,128)(2,1)S(1)} %get-tuple-element.133.refs_2_, ...), custom_call_target="tpu_custom_call", output_to_operand_aliasing={{0}: (4, {})} | custom-call | tf_op jit(solution)/shard_map/update/pallas_call | solution.py:32
  153.1 1.5 solve.5
  154.7 3.2 %collective-permute-start.22 = (f32[4,512]{1,0:T(4,128)S(1)}, f32[4,512]{1,0:T(4,128)S(1)}, u32[]{:S(2)}, u32[]{:S(2)}) collective-permute-start(f32[4,512]{1,0:T(4,128)S(1)} %get-tuple-element.145), channel_id=1, source_target_pairs={{0,8},{8,16},{16,24},{1,9},{9,17},{17,25},{2,10},{10,18},{18,26},{... | collective-permute-start | bytes 24584 | tf_op jit(solution)/shard_map/ppermute | solution.py:498
  158.7 1.5 solve.6
  160.2 2.3 collective-permute-start.23
  163.3 1.5 solve.7
  164.8 1.9 collective-permute-start.24
  167.6 2.5 %collective-permute-start.25 = (f32[4,512]{1,0:T(4,128)S(1)}, f32[4,512]{1,0:T(4,128)S(1)}, u32[]{:S(2)}, u32[]{:S(2)}) collective-permute-start(f32[4,512]{1,0:T(4,128)S(1)} %get-tuple-element.151.refs_0_), channel_id=1, source_target_pairs={{0,16},{8,24},{16,0},{24,8},{1,17},{9,25},{17,1},{25,9},{2,18},{10... | collective-permute-start | bytes 24584 | tf_op jit(solution)/shard_map/ppermute | solution.py:408
  170.1 1.6 collective-permute-done.25.refs_1_
  171.8 1.6 collective-permute-start.33
  175.4 21.1 %collective-permute-done.29.refs_1_ = f32[4,512]{1,0:T(4,128)S(1)} collective-permute-done((f32[4,512]{1,0:T(4,128)S(1)}, f32[4,512]{1,0:T(4,128)S(1)}, u32[]{:S(2)}, u32[]{:S(2)}) %collective-permute-start.29) | collective-permute-done | bytes 8224 | tf_op jit(solution)/shard_map/ppermute | solution.py:408
  196.4 11.4 %update.7 = (bf16[65536,128]{1,0:T(8,128)(2,1)}, f32[8,128]{1,0:T(8,128)S(1)}) custom-call(bf16[65536,128]{1,0:T(8,128)(2,1)} %bitcast.39, bf16[1024,2048]{1,0:T(8,128)(2,1)} %get-tuple-element.125.refs_1_, bf16[1024,512]{1,0:T(8,128)(2,1)} %get-tuple-element.155.refs_2_, ...), custom_call_target="tpu_custom_call", output_to_operand_aliasing={{0}: (4, {})} | custom-call | tf_op jit(solution)/shard_map/update/pallas_call | solution.py:32
  208.9 1.6 collective-permute-start.32
  210.5 3.6 %collective-permute-done.34.refs_1_ = f32[4,512]{1,0:T(4,128)S(1)} collective-permute-done((f32[4,512]{1,0:T(4,128)S(1)}, f32[4,512]{1,0:T(4,128)S(1)}, u32[]{:S(2)}, u32[]{:S(2)}) %collective-permute-start.34) | collective-permute-done | bytes 8224 | tf_op jit(solution)/shard_map/ppermute | solution.py:408
  215.6 11.1 %update.8 = (bf16[65536,128]{1,0:T(8,128)(2,1)}, f32[8,128]{1,0:T(8,128)S(1)}) custom-call(bf16[65536,128]{1,0:T(8,128)(2,1)} %bitcast.40, bf16[1024,2048]{1,0:T(8,128)(2,1)} %get-tuple-element.125.refs_1_, bf16[1024,512]{1,0:T(8,128)(2,1)S(1)} %get-tuple-element.164.refs_2_, ...), custom_call_target="tpu_custom_call", output_to_operand_aliasing={{0}: (4, {})} | custom-call | tf_op jit(solution)/shard_map/update/pallas_call | solution.py:32
  227.3 7.3 %update.9 = (bf16[65536,128]{1,0:T(8,128)(2,1)}, f32[8,128]{1,0:T(8,128)}) custom-call(bf16[65536,128]{1,0:T(8,128)(2,1)} %bitcast.41, bf16[1024,2048]{1,0:T(8,128)(2,1)} %get-tuple-element.125.refs_1_, bf16[512,512]{1,0:T(8,128)(2,1)S(1)} %get-tuple-element.163.refs_2_, ...), custom_call_target="tpu_custom_call", output_to_operand_aliasing={{0}: (4, {})} | custom-call | tf_op jit(solution)/shard_map/update/pallas_call | solution.py:32
  (105 shorter events, 24.0 us)
Async XLA Ops:
  4.8 19.0 %collective-permute-start.1 = (bf16[8192,128]{1,0:T(8,128)(2,1)}, bf16[8192,128]{1,0:T(8,128)(2,1)S(1)}, u32[]{:S(2)}, u32[]{:S(2)}) collective-permute-start(bf16[8192,128]{1,0:T(8,128)(2,1)} %get-tuple-element.89.refs_1_), channel_id=1, source_target_pairs={{0,8},{8,0},{16,24},{24,16},{1,9},{9,1},{17,25},{25,17},{2,10},{10... | collective-permute-start | bytes 6291464 | tf_op jit(solution)/shard_map/ppermute | solution.py:408
  5.3 59.7 %collective-permute-start.2 = (bf16[8192,128]{1,0:T(8,128)(2,1)}, bf16[8192,128]{1,0:T(8,128)(2,1)}, u32[]{:S(2)}, u32[]{:S(2)}) collective-permute-start(bf16[8192,128]{1,0:T(8,128)(2,1)} %get-tuple-element.89.refs_1_), channel_id=1, source_target_pairs={{0,16},{8,24},{16,0},{24,8},{1,17},{9,25},{17,1},{25,9},{2,18},{10... | collective-permute-start | bytes 6291464 | tf_op jit(solution)/shard_map/ppermute | solution.py:404
  7.8 16.0 %collective-permute-start = (bf16[512,512]{1,0:T(8,128)(2,1)S(1)}, bf16[512,512]{1,0:T(8,128)(2,1)}, u32[]{:S(2)}, u32[]{:S(2)}) collective-permute-start(bf16[512,512]{1,0:T(8,128)(2,1)S(1)} %get-tuple-element.90.refs_1_.refs_6_), channel_id=1, source_target_pairs={{0,4},{1,5},{8,12},{9,13},{16,20},{17,21},{24,28},{25,29}} | collective-permute-start | bytes 1572872 | tf_op jit(solution)/shard_map/ppermute | solution.py:427
  13.1 21.1 %copy-start.13 = (bf16[4,1,512]{2,0,1:T(4,128)(2,1)S(1)}, bf16[4,1,512]{2,0,1:T(4,128)(2,1)}, u32[]{:S(2)}) copy-start(bf16[4,1,512]{2,0,1:T(4,128)(2,1)} %param.9) | copy-start | bytes 12292
  23.8 1.3 copy-start
  25.2 15.0 %collective-permute-start.4 = (bf16[512,512]{1,0:T(8,128)(2,1)}, bf16[512,512]{1,0:T(8,128)(2,1)S(1)}, u32[]{:S(2)}, u32[]{:S(2)}) collective-permute-start(bf16[512,512]{1,0:T(8,128)(2,1)} %get-tuple-element.95.refs_2_), channel_id=1, source_target_pairs={{4,6},{5,7},{12,14},{13,15},{20,22},{21,23},{28,30},{29,31}} | collective-permute-start | bytes 1572872 | tf_op jit(solution)/shard_map/ppermute | solution.py:430
  25.9 15.1 %collective-permute-start.3 = (bf16[512,512]{1,0:T(8,128)(2,1)}, bf16[512,512]{1,0:T(8,128)(2,1)S(1)}, u32[]{:S(2)}, u32[]{:S(2)}) collective-permute-start(bf16[512,512]{1,0:T(8,128)(2,1)} %get-tuple-element.95.refs_2_), channel_id=1, source_target_pairs={{4,2},{5,3},{12,10},{13,11},{20,18},{21,19},{28,26},{29,27}} | collective-permute-start | bytes 1572872 | tf_op jit(solution)/shard_map/ppermute | solution.py:430
  26.6 35.4 %collective-permute-start.6 = (bf16[1024,512]{1,0:T(8,128)(2,1)}, bf16[1024,512]{1,0:T(8,128)(2,1)}, u32[]{:S(2)}, u32[]{:S(2)}) collective-permute-start(bf16[1024,512]{1,0:T(8,128)(2,1)} %get-tuple-element.99.refs_1_), channel_id=1, source_target_pairs={{0,4},{1,5},{8,12},{9,13},{16,20},{17,21},{24,28},{25,29}} | collective-permute-start | bytes 3145736 | tf_op jit(solution)/shard_map/ppermute | solution.py:427
  41.7 1.0 copy-start.9
  42.8 1.0 copy-start.11
  43.9 20.3 %collective-permute-start.5 = (bf16[512,512]{1,0:T(8,128)(2,1)S(1)}, bf16[512,512]{1,0:T(8,128)(2,1)S(1)}, u32[]{:S(2)}, u32[]{:S(2)}) collective-permute-start(bf16[512,512]{1,0:T(8,128)(2,1)S(1)} %get-tuple-element.98.refs_1_.refs_4_.refs_2_), channel_id=1, source_target_pairs={{0,1},{1,0},{2,3},{3,2},{4,5},{5,4},{6,7},{7,6},{8,9},{9,8},{10,11... | collective-permute-start | bytes 1572872 | tf_op jit(solution)/shard_map/ppermute | solution.py:408
  45.5 29.2 %copy-start.16 = (f32[8,1,512]{2,1,0:T(1,128)S(1)}, f32[8,1,512]{2,1,0:T(1,128)}, u32[]{:S(2)}) copy-start(f32[8,1,512]{2,1,0:T(1,128)} %param.10) | copy-start | bytes 49156
  52.9 21.8 %copy-start.1 = (bf16[1,1,512,512]{3,2,1,0:T(8,128)(2,1)S(1)}, bf16[1,1,512,512]{3,2,1,0:T(8,128)(2,1)}, u32[]{:S(2)}) copy-start(bf16[1,1,512,512]{3,2,1,0:T(8,128)(2,1)} %param.11) | copy-start | bytes 1572868
  52.9 4.3 %collective-permute-start.7 = (f32[8,512]{1,0:T(8,128)S(1)}, f32[8,512]{1,0:T(8,128)S(1)}, u32[]{:S(2)}, u32[]{:S(2)}) collective-permute-start(f32[8,512]{1,0:T(8,128)S(1)} %reshape.48.refs_0_), channel_id=1, source_target_pairs={{0,2},{1,3},{2,0},{3,1},{4,6},{5,7},{6,4},{7,5},{8,10},{9,11},{10,... | collective-permute-start | bytes 49160 | tf_op jit(solution)/shard_map/ppermute | solution.py:408
  57.3 4.6 %collective-permute-start.8 = (f32[8,512]{1,0:T(8,128)S(1)}, f32[8,512]{1,0:T(8,128)S(1)}, u32[]{:S(2)}, u32[]{:S(2)}) collective-permute-start(f32[8,512]{1,0:T(8,128)S(1)} %get-tuple-element.107.refs_0_), channel_id=1, source_target_pairs={{0,4},{1,5},{2,6},{3,7},{4,0},{5,1},{6,2},{7,3},{8,12},{9,13},{10,... | collective-permute-start | bytes 49160 | tf_op jit(solution)/shard_map/ppermute | solution.py:408
  61.9 1.2 copy-start.3
  65.0 9.7 %collective-permute-start.9 = (bf16[8192,128]{1,0:T(8,128)(2,1)}, bf16[8192,128]{1,0:T(8,128)(2,1)}, u32[]{:S(2)}, u32[]{:S(2)}) collective-permute-start(bf16[8192,128]{1,0:T(8,128)(2,1)} %get-tuple-element.112.refs_3_), channel_id=1, source_target_pairs={{0,8},{8,0},{16,24},{24,16},{1,9},{9,1},{17,25},{25,17},{2,10},{10... | collective-permute-start | bytes 6291464 | tf_op jit(solution)/shard_map/ppermute | solution.py:408
  65.1 7.8 %collective-permute-start.10 = (f32[8,512]{1,0:T(8,128)S(1)}, f32[8,512]{1,0:T(8,128)S(1)}, u32[]{:S(2)}, u32[]{:S(2)}) collective-permute-start(f32[8,512]{1,0:T(8,128)S(1)} %get-tuple-element.113.refs_0_), channel_id=1, source_target_pairs={{0,1},{1,0},{2,3},{3,2},{4,5},{5,4},{6,7},{7,6},{8,9},{9,8},{10,11... | collective-permute-start | bytes 49160 | tf_op jit(solution)/shard_map/ppermute | solution.py:408
  65.7 14.3 %collective-permute-start.11 = (bf16[512,512]{1,0:T(8,128)(2,1)}, bf16[512,512]{1,0:T(8,128)(2,1)}, u32[]{:S(2)}, u32[]{:S(2)}) collective-permute-start(bf16[512,512]{1,0:T(8,128)(2,1)} %get-tuple-element.117.refs_1_), channel_id=1, source_target_pairs={{0,16},{8,24},{16,0},{24,8},{1,17},{9,25},{17,1},{25,9},{2,18},{10... | collective-permute-start | bytes 1572872 | tf_op jit(solution)/shard_map/ppermute | solution.py:404
  66.2 31.5 %collective-permute-start.13 = (bf16[1024,512]{1,0:T(8,128)(2,1)}, bf16[1024,512]{1,0:T(8,128)(2,1)}, u32[]{:S(2)}, u32[]{:S(2)}) collective-permute-start(bf16[1024,512]{1,0:T(8,128)(2,1)} %copy-done.4), channel_id=1, source_target_pairs={{0,4},{1,5},{8,12},{9,13},{16,20},{17,21},{24,28},{25,29}} | collective-permute-start | bytes 3145736 | tf_op jit(solution)/shard_map/ppermute | solution.py:427
  71.2 26.5 %collective-permute-start.16 = (bf16[1024,512]{1,0:T(8,128)(2,1)}, bf16[1024,512]{1,0:T(8,128)(2,1)}, u32[]{:S(2)}, u32[]{:S(2)}) collective-permute-start(bf16[1024,512]{1,0:T(8,128)(2,1)} %get-tuple-element.131.refs_2_), channel_id=1, source_target_pairs={{4,6},{5,7},{12,14},{13,15},{20,22},{21,23},{28,30},{29,31}} | collective-permute-start | bytes 3145736 | tf_op jit(solution)/shard_map/ppermute | solution.py:430
  72.9 24.8 %collective-permute-start.15 = (bf16[1024,512]{1,0:T(8,128)(2,1)}, bf16[1024,512]{1,0:T(8,128)(2,1)}, u32[]{:S(2)}, u32[]{:S(2)}) collective-permute-start(bf16[1024,512]{1,0:T(8,128)(2,1)} %get-tuple-element.131.refs_2_), channel_id=1, source_target_pairs={{4,2},{5,3},{12,10},{13,11},{20,18},{21,19},{28,26},{29,27}} | collective-permute-start | bytes 3145736 | tf_op jit(solution)/shard_map/ppermute | solution.py:430
  74.6 8.5 %copy-start.6 = (bf16[2,512,512]{2,1,0:T(8,128)(2,1)S(1)}, bf16[2,512,512]{2,1,0:T(8,128)(2,1)}, u32[]{:S(2)}) copy-start(bf16[2,512,512]{2,1,0:T(8,128)(2,1)} %refs_7_.1) | copy-start | bytes 3145732
  74.6 8.5 %copy-start.7 = (bf16[2,512,512]{2,1,0:T(8,128)(2,1)S(1)}, bf16[2,512,512]{2,1,0:T(8,128)(2,1)}, u32[]{:S(2)}) copy-start(bf16[2,512,512]{2,1,0:T(8,128)(2,1)} %refs_8_.1) | copy-start | bytes 3145732
  81.0 2.0 collective-permute-start.12
  99.0 25.3 %collective-permute-start.17 = (bf16[1024,512]{1,0:T(8,128)(2,1)S(1)}, bf16[1024,512]{1,0:T(8,128)(2,1)S(1)}, u32[]{:S(2)}, u32[]{:S(2)}) collective-permute-start(bf16[1024,512]{1,0:T(8,128)(2,1)S(1)} %get-tuple-element.133.refs_2_), channel_id=1, source_target_pairs={{0,1},{1,0},{2,3},{3,2},{4,5},{5,4},{6,7},{7,6},{8,9},{9,8},{10,11... | collective-permute-start | bytes 3145736 | tf_op jit(solution)/shard_map/ppermute | solution.py:408
  100.5 26.4 %collective-permute-start.14 = (bf16[1024,512]{1,0:T(8,128)(2,1)S(1)}, bf16[1024,512]{1,0:T(8,128)(2,1)}, u32[]{:S(2)}, u32[]{:S(2)}) collective-permute-start(bf16[1024,512]{1,0:T(8,128)(2,1)S(1)} %get-tuple-element.129.refs_1_), channel_id=1, source_target_pairs={{0,4},{1,5},{8,12},{9,13},{16,20},{17,21},{24,28},{25,29}} | collective-permute-start | bytes 3145736 | tf_op jit(solution)/shard_map/ppermute | solution.py:427
  105.6 32.2 %collective-permute-start.21 = (bf16[1024,512]{1,0:T(8,128)(2,1)}, bf16[1024,512]{1,0:T(8,128)(2,1)S(1)}, u32[]{:S(2)}, u32[]{:S(2)}) collective-permute-start(bf16[1024,512]{1,0:T(8,128)(2,1)} %get-tuple-element.141.refs_2_), channel_id=1, source_target_pairs={{4,6},{5,7},{12,14},{13,15},{20,22},{21,23},{28,30},{29,31}} | collective-permute-start | bytes 3145736 | tf_op jit(solution)/shard_map/ppermute | solution.py:430
  106.5 31.3 %collective-permute-start.20 = (bf16[1024,512]{1,0:T(8,128)(2,1)}, bf16[1024,512]{1,0:T(8,128)(2,1)S(1)}, u32[]{:S(2)}, u32[]{:S(2)}) collective-permute-start(bf16[1024,512]{1,0:T(8,128)(2,1)} %get-tuple-element.141.refs_2_), channel_id=1, source_target_pairs={{4,2},{5,3},{12,10},{13,11},{20,18},{21,19},{28,26},{29,27}} | collective-permute-start | bytes 3145736 | tf_op jit(solution)/shard_map/ppermute | solution.py:430
  107.2 31.9 %copy-start.5 = (bf16[1024,512]{1,0:T(8,128)(2,1)S(1)}, bf16[1024,512]{1,0:T(8,128)(2,1)}, u32[]{:S(2)}) copy-start(bf16[1024,512]{1,0:T(8,128)(2,1)} %copy-done.4) | copy-start | bytes 3145732
  127.0 44.7 %collective-permute-start.31 = (bf16[1024,512]{1,0:T(8,128)(2,1)}, bf16[1024,512]{1,0:T(8,128)(2,1)}, u32[]{:S(2)}, u32[]{:S(2)}) collective-permute-start(bf16[1024,512]{1,0:T(8,128)(2,1)} %get-tuple-element.158.refs_2_), channel_id=1, source_target_pairs={{4,6},{5,7},{12,14},{13,15},{20,22},{21,23},{28,30},{29,31}} | collective-permute-start | bytes 3145736 | tf_op jit(solution)/shard_map/ppermute | solution.py:430
  128.6 43.1 %collective-permute-start.30 = (bf16[1024,512]{1,0:T(8,128)(2,1)}, bf16[1024,512]{1,0:T(8,128)(2,1)}, u32[]{:S(2)}, u32[]{:S(2)}) collective-permute-start(bf16[1024,512]{1,0:T(8,128)(2,1)} %get-tuple-element.158.refs_2_), channel_id=1, source_target_pairs={{4,2},{5,3},{12,10},{13,11},{20,18},{21,19},{28,26},{29,27}} | collective-permute-start | bytes 3145736 | tf_op jit(solution)/shard_map/ppermute | solution.py:430
  130.3 41.4 %collective-permute-start.18 = (bf16[512,512]{1,0:T(8,128)(2,1)}, bf16[512,512]{1,0:T(8,128)(2,1)}, u32[]{:S(2)}, u32[]{:S(2)}) collective-permute-start(bf16[512,512]{1,0:T(8,128)(2,1)} %get-tuple-element.137.refs_1_), channel_id=1, source_target_pairs={{0,4},{1,5},{8,12},{9,13},{16,20},{17,21},{24,28},{25,29}} | collective-permute-start | bytes 1572872 | tf_op jit(solution)/shard_map/ppermute | solution.py:427
  137.8 1.1 copy-start.14
  137.8 1.3 copy-start.15
  140.2 56.3 %collective-permute-start.28 = (bf16[1024,512]{1,0:T(8,128)(2,1)}, bf16[1024,512]{1,0:T(8,128)(2,1)}, u32[]{:S(2)}, u32[]{:S(2)}) collective-permute-start(bf16[1024,512]{1,0:T(8,128)(2,1)} %get-tuple-element.155.refs_2_), channel_id=1, source_target_pairs={{0,1},{1,0},{2,3},{3,2},{4,5},{5,4},{6,7},{7,6},{8,9},{9,8},{10,11... | collective-permute-start | bytes 3145736 | tf_op jit(solution)/shard_map/ppermute | solution.py:408
  140.8 12.4 %collective-permute-start.19 = (f32[4,512]{1,0:T(4,128)S(1)}, f32[4,512]{1,0:T(4,128)S(1)}, u32[]{:S(2)}, u32[]{:S(2)}) collective-permute-start(f32[4,512]{1,0:T(4,128)S(1)} %get-tuple-element.138), channel_id=1, source_target_pairs={{0,8},{8,16},{16,24},{1,9},{9,17},{17,25},{2,10},{10,18},{18,26},{... | collective-permute-start | bytes 24584 | tf_op jit(solution)/shard_map/ppermute | solution.py:498
  154.7 4.0 %collective-permute-start.22 = (f32[4,512]{1,0:T(4,128)S(1)}, f32[4,512]{1,0:T(4,128)S(1)}, u32[]{:S(2)}, u32[]{:S(2)}) collective-permute-start(f32[4,512]{1,0:T(4,128)S(1)} %get-tuple-element.145), channel_id=1, source_target_pairs={{0,8},{8,16},{16,24},{1,9},{9,17},{17,25},{2,10},{10,18},{18,26},{... | collective-permute-start | bytes 24584 | tf_op jit(solution)/shard_map/ppermute | solution.py:498
  160.2 3.1 %collective-permute-start.23 = (f32[4,512]{1,0:T(4,128)S(1)}, f32[4,512]{1,0:T(4,128)S(1)}, u32[]{:S(2)}, u32[]{:S(2)}) collective-permute-start(f32[4,512]{1,0:T(4,128)S(1)} %get-tuple-element.147), channel_id=1, source_target_pairs={{0,8},{8,16},{16,24},{1,9},{9,17},{17,25},{2,10},{10,18},{18,26},{... | collective-permute-start | bytes 24584 | tf_op jit(solution)/shard_map/ppermute | solution.py:498
  164.8 2.8 %collective-permute-start.24 = (f32[4,512]{1,0:T(4,128)S(1)}, f32[4,512]{1,0:T(4,128)S(1)}, u32[]{:S(2)}, u32[]{:S(2)}) collective-permute-start(f32[4,512]{1,0:T(4,128)S(1)} %broadcast_select_fusion.refs_0_), channel_id=1, source_target_pairs={{0,8},{8,0},{16,24},{24,16},{1,9},{9,1},{17,25},{25,17},{2,10},{10... | collective-permute-start | bytes 24584 | tf_op jit(solution)/shard_map/ppermute | solution.py:408
  167.6 4.1 %collective-permute-start.25 = (f32[4,512]{1,0:T(4,128)S(1)}, f32[4,512]{1,0:T(4,128)S(1)}, u32[]{:S(2)}, u32[]{:S(2)}) collective-permute-start(f32[4,512]{1,0:T(4,128)S(1)} %get-tuple-element.151.refs_0_), channel_id=1, source_target_pairs={{0,16},{8,24},{16,0},{24,8},{1,17},{9,25},{17,1},{25,9},{2,18},{10... | collective-permute-start | bytes 24584 | tf_op jit(solution)/shard_map/ppermute | solution.py:408
  171.8 43.8 %collective-permute-start.33 = (bf16[1024,512]{1,0:T(8,128)(2,1)S(1)}, bf16[1024,512]{1,0:T(8,128)(2,1)S(1)}, u32[]{:S(2)}, u32[]{:S(2)}) collective-permute-start(bf16[1024,512]{1,0:T(8,128)(2,1)S(1)} %get-tuple-element.164.refs_2_), channel_id=1, source_target_pairs={{0,1},{1,0},{2,3},{3,2},{4,5},{5,4},{6,7},{7,6},{8,9},{9,8},{10,11... | collective-permute-start | bytes 3145736 | tf_op jit(solution)/shard_map/ppermute | solution.py:408
  173.4 34.4 %collective-permute-start.27 = (bf16[512,512]{1,0:T(8,128)(2,1)}, bf16[512,512]{1,0:T(8,128)(2,1)S(1)}, u32[]{:S(2)}, u32[]{:S(2)}) collective-permute-start(bf16[512,512]{1,0:T(8,128)(2,1)} %get-tuple-element.154.refs_2_), channel_id=1, source_target_pairs={{4,6},{5,7},{12,14},{13,15},{20,22},{21,23},{28,30},{29,31}} | collective-permute-start | bytes 1572872 | tf_op jit(solution)/shard_map/ppermute | solution.py:430
  174.1 33.7 %collective-permute-start.26 = (bf16[512,512]{1,0:T(8,128)(2,1)}, bf16[512,512]{1,0:T(8,128)(2,1)S(1)}, u32[]{:S(2)}, u32[]{:S(2)}) collective-permute-start(bf16[512,512]{1,0:T(8,128)(2,1)} %get-tuple-element.154.refs_2_), channel_id=1, source_target_pairs={{4,2},{5,3},{12,10},{13,11},{20,18},{21,19},{28,26},{29,27}} | collective-permute-start | bytes 1572872 | tf_op jit(solution)/shard_map/ppermute | solution.py:430
  174.8 21.6 %collective-permute-start.29 = (f32[4,512]{1,0:T(4,128)S(1)}, f32[4,512]{1,0:T(4,128)S(1)}, u32[]{:S(2)}, u32[]{:S(2)}) collective-permute-start(f32[4,512]{1,0:T(4,128)S(1)} %get-tuple-element.157.refs_0_), channel_id=1, source_target_pairs={{0,1},{1,0},{2,3},{3,2},{4,5},{5,4},{6,7},{7,6},{8,9},{9,8},{10,11... | collective-permute-start | bytes 24584 | tf_op jit(solution)/shard_map/ppermute | solution.py:408
  208.9 18.4 %collective-permute-start.32 = (bf16[512,512]{1,0:T(8,128)(2,1)S(1)}, bf16[512,512]{1,0:T(8,128)(2,1)S(1)}, u32[]{:S(2)}, u32[]{:S(2)}) collective-permute-start(bf16[512,512]{1,0:T(8,128)(2,1)S(1)} %get-tuple-element.163.refs_2_), channel_id=1, source_target_pairs={{0,1},{1,0},{2,3},{3,2},{4,5},{5,4},{6,7},{7,6},{8,9},{9,8},{10,11... | collective-permute-start | bytes 1572872 | tf_op jit(solution)/shard_map/ppermute | solution.py:408
  210.5 3.7 %collective-permute-start.34 = (f32[4,512]{1,0:T(4,128)S(1)}, f32[4,512]{1,0:T(4,128)S(1)}, u32[]{:S(2)}, u32[]{:S(2)}) collective-permute-start(f32[4,512]{1,0:T(4,128)S(1)} %get-tuple-element.166.refs_0_), channel_id=1, source_target_pairs={{0,2},{1,3},{2,0},{3,1},{4,6},{5,7},{6,4},{7,5},{8,10},{9,11},{10,... | collective-permute-start | bytes 24584 | tf_op jit(solution)/shard_map/ppermute | solution.py:408
  214.1 12.6 %collective-permute-start.35 = (f32[4,512]{1,0:T(4,128)S(1)}, f32[4,512]{1,0:T(4,128)S(1)}, u32[]{:S(2)}, u32[]{:S(2)}) collective-permute-start(f32[4,512]{1,0:T(4,128)S(1)} %get-tuple-element.170.refs_0_), channel_id=1, source_target_pairs={{0,4},{1,5},{2,6},{3,7},{4,0},{5,1},{6,2},{7,3},{8,12},{9,13},{10,... | collective-permute-start | bytes 24584 | tf_op jit(solution)/shard_map/ppermute | solution.py:408
  (5 other events, 4.3 us)

commit v6 on v5

--- a/solution.py
+++ b/solution.py
@@ -580,16 +580,17 @@
         each([blocks_out, total[2], bands_in, line[0], blocks_swap, blocks_in, make_factors])
         advance(2)
         take(1)
-        updates(0)()
+        each([updates(0), *line[1:4]])
         other[1] = arrive([other[1]])[0]
         advance(3)
         take(2)
-        each([updates(1), *line[1:6]])
+        updates(1)()
         advance(4)
+        each(line[4:7])
         take(3)
-        each([line[6], updates(2)])
+        each([line[7], updates(2), line[8]])
         take(4)
-        each([line[7], updates(3), line[8], updates(4)])
+        each([updates(3), updates(4)])
     else:
         each([*total, blocks_out, bands_in, blocks_swap, blocks_in, make_factors, *line])
         for k in range(1, chunks):

time: 236 us -> 211 us (0.89)
  waiting for transfers between devices: 56.5 us -> 32.6 us
    ppermute x16, waiting for transfers between devices: 42.9 us -> 18.8 us  [swap(): return lax.ppermute(value, axis, [(i, i ^ bit) for i in range(size)])]
    ppermute x5, starting transfers between devices: 30.4 us -> 24.1 us  [first_stage(): return lax.ppermute(local, 'pcol', along_z(stages[0][0]))]
    ppermute x16, starting transfers between devices: 18.7 us -> 21.4 us  [swap(): return lax.ppermute(value, axis, [(i, i ^ bit) for i in range(size)])]
    unnamed x35 -> x43, local copies, waits for them, and re-layouts: 10.9 us -> 12.2 us
  transfers between devices with their start and end apart: 36 -> 36, of which waited for: 13 -> 11; matrix products, arithmetic and copies ran while one was open for 0% -> 0% of each run, Pallas kernels for 36% -> 40%
where the time goes in v6:
time: 211 us; the launch traced here: 210 us
  Pallas kernels  96 us (45%)
  starting transfers between devices  68.1 us (32%)
  waiting for transfers between devices  32.6 us (15%)
  local copies, waits for them, and re-layouts  12.2 us (6%)
    pallas_call x38, Pallas kernels, __call__(): pl.pallas_call(body, in_specs=list(in_specs) + [anywhere] * n_dep, out_sp...  96 us
    ppermute x5, starting transfers between devices, first_stage(): return lax.ppermute(local, 'pcol', along_z(stages[0][0]))  24.1 us
    ppermute x16, starting transfers between devices, swap(): return lax.ppermute(value, axis, [(i, i ^ bit) for i in range(size)])  21.4 us
    ppermute x16, waiting for transfers between devices, swap(): return lax.ppermute(value, axis, [(i, i ^ bit) for i in range(size)])  18.8 us
    unnamed x43, local copies, waits for them, and re-layouts  12.2 us
    ppermute x10, starting transfers between devices, second_stage(): lax.ppermute(arrived, 'pcol', along_z(moves))  12 us
    ppermute x3, starting transfers between devices, run(): lax.ppermute(box['state'], 'prow', [(i, i + 1) for i in range(n_prow - 1)])  7.69 us
    ppermute x5, waiting for transfers between devices, first_stage(): return lax.ppermute(local, 'pcol', along_z(stages[0][0]))  6.25 us
  transfers between devices with their start and end apart: 36, of which 11 were waited for; matrix products, arithmetic and copies ran while one was open for 0% of the time, Pallas kernels for 40%

profile of v6, /device:TPU:0, one launch (start us, length us, event | category | flops | bytes accessed | tf_op | source)
XLA Modules:
  0.0 210.2 jit_solution(7164117640070991829)
XLA Ops:
  1.3 3.5 %extract.4 = (f32[1,512]{1,0:T(1,128)S(1)}, bf16[512,512]{1,0:T(8,128)(2,1)S(1)}, bf16[8192,128]{1,0:T(8,128)(2,1)}, f32[8,128]{1,0:T(8,128)S(1)}) custom-call(bf16[65536,128]{1,0:T(8,128)(2,1)} %bitcast.33, bf16[16,128]{1,0:T(8,128)(2,1)S(1)} %bitcast.29), custom_call_target="tpu_custom_call" | custom-call | tf_op jit(solution)/shard_map/extract/pallas_call | solution.py:32
  5.3 2.5 %collective-permute-start.2 = (bf16[8192,128]{1,0:T(8,128)(2,1)}, bf16[8192,128]{1,0:T(8,128)(2,1)}, u32[]{:S(2)}, u32[]{:S(2)}) collective-permute-start(bf16[8192,128]{1,0:T(8,128)(2,1)} %get-tuple-element.89.refs_1_), channel_id=1, source_target_pairs={{0,16},{8,24},{16,0},{24,8},{1,17},{9,25},{17,1},{25,9},{2,18},{10... | collective-permute-start | bytes 6291464 | tf_op jit(solution)/shard_map/ppermute | solution.py:404
  7.8 4.5 %collective-permute-start = (bf16[512,512]{1,0:T(8,128)(2,1)S(1)}, bf16[512,512]{1,0:T(8,128)(2,1)S(1)}, u32[]{:S(2)}, u32[]{:S(2)}) collective-permute-start(bf16[512,512]{1,0:T(8,128)(2,1)S(1)} %get-tuple-element.90.refs_1_.refs_6_), channel_id=1, source_target_pairs={{0,4},{1,5},{8,12},{9,13},{16,20},{17,21},{24,28},{25,29}} | collective-permute-start | bytes 1572872 | tf_op jit(solution)/shard_map/ppermute | solution.py:427
  12.3 5.3 %extract.5 = (f32[1,1024]{1,0:T(1,128)S(1)}, bf16[1024,512]{1,0:T(8,128)(2,1)}, f32[8,128]{1,0:T(8,128)S(1)}) custom-call(bf16[65536,128]{1,0:T(8,128)(2,1)} %bitcast.34, bf16[16,128]{1,0:T(8,128)(2,1)S(1)} %bitcast.30, f32[8,128]{1,0:T(8,128)S(1)} %get-tuple-element.91.refs_2_), custom_call_target="tpu_custom_call" | custom-call | tf_op jit(solution)/shard_map/extract/pallas_call | solution.py:32
  17.6 6.2 %collective-permute-done.refs_0_ = bf16[512,512]{1,0:T(8,128)(2,1)S(1)} collective-permute-done((bf16[512,512]{1,0:T(8,128)(2,1)S(1)}, bf16[512,512]{1,0:T(8,128)(2,1)S(1)}, u32[]{:S(2)}, u32[]{:S(2)}) %collective-permute-start) | collective-permute-done | bytes 524320 | tf_op jit(solution)/shard_map/ppermute | solution.py:427
  23.8 1.3 copy-done
  25.9 1.5 collective-permute-start.3
  27.3 7.5 %collective-permute-start.6 = (bf16[1024,512]{1,0:T(8,128)(2,1)}, bf16[1024,512]{1,0:T(8,128)(2,1)}, u32[]{:S(2)}, u32[]{:S(2)}) collective-permute-start(bf16[1024,512]{1,0:T(8,128)(2,1)} %get-tuple-element.99.refs_1_), channel_id=1, source_target_pairs={{0,4},{1,5},{8,12},{9,13},{16,20},{17,21},{24,28},{25,29}} | collective-permute-start | bytes 3145736 | tf_op jit(solution)/shard_map/ppermute | solution.py:427
  34.9 4.9 %extract.6 = (f32[1,1024]{1,0:T(1,128)S(1)}, bf16[1024,512]{1,0:T(8,128)(2,1)S(1)}, f32[8,128]{1,0:T(8,128)S(1)}) custom-call(bf16[65536,128]{1,0:T(8,128)(2,1)} %bitcast.35, bf16[16,128]{1,0:T(8,128)(2,1)S(1)} %bitcast.31, f32[8,128]{1,0:T(8,128)S(1)} %get-tuple-element.96.refs_2_), custom_call_target="tpu_custom_call" | custom-call | tf_op jit(solution)/shard_map/extract/pallas_call | solution.py:32
  40.9 1.6 collective-permute-start.5
  42.5 7.4 %extract.7 = (f32[1,1536]{1,0:T(1,128)S(1)}, bf16[1024,512]{1,0:T(8,128)(2,1)S(1)}, bf16[512,512]{1,0:T(8,128)(2,1)}, f32[8,128]{1,0:T(8,128)S(1)}) custom-call(bf16[65536,128]{1,0:T(8,128)(2,1)} %bitcast.36, bf16[16,128]{1,0:T(8,128)(2,1)S(1)} %bitcast.32, f32[8,128]{1,0:T(8,128)S(1)} %get-tuple-element.104.refs_2_), custom_call_target="tpu_custom_call" | custom-call | tf_op jit(solution)/shard_map/extract/pallas_call | solution.py:32
  49.9 3.5 %collective-permute-start.7 = (f32[8,512]{1,0:T(8,128)S(1)}, f32[8,512]{1,0:T(8,128)S(1)}, u32[]{:S(2)}, u32[]{:S(2)}) collective-permute-start(f32[8,512]{1,0:T(8,128)S(1)} %reshape.48.refs_0_), channel_id=1, source_target_pairs={{0,2},{1,3},{2,0},{3,1},{4,6},{5,7},{6,4},{7,5},{8,10},{9,11},{10,... | collective-permute-start | bytes 49160 | tf_op jit(solution)/shard_map/ppermute | solution.py:408
  53.5 3.1 %collective-permute-done.7.refs_1_ = f32[8,512]{1,0:T(8,128)S(1)} collective-permute-done((f32[8,512]{1,0:T(8,128)S(1)}, f32[8,512]{1,0:T(8,128)S(1)}, u32[]{:S(2)}, u32[]{:S(2)}) %collective-permute-start.7) | collective-permute-done | bytes 16416 | tf_op jit(solution)/shard_map/ppermute | solution.py:408
  56.6 4.6 %collective-permute-done.8.refs_1_ = f32[8,512]{1,0:T(8,128)S(1)} collective-permute-done((f32[8,512]{1,0:T(8,128)S(1)}, f32[8,512]{1,0:T(8,128)S(1)}, u32[]{:S(2)}, u32[]{:S(2)}) %collective-permute-start.8) | collective-permute-done | bytes 16416 | tf_op jit(solution)/shard_map/ppermute | solution.py:408
  64.4 1.6 collective-permute-start.10
  66.5 2.9 %collective-permute-start.13 = (bf16[1024,512]{1,0:T(8,128)(2,1)}, bf16[1024,512]{1,0:T(8,128)(2,1)}, u32[]{:S(2)}, u32[]{:S(2)}) collective-permute-start(bf16[1024,512]{1,0:T(8,128)(2,1)} %copy-done.4), channel_id=1, source_target_pairs={{0,4},{1,5},{8,12},{9,13},{16,20},{17,21},{24,28},{25,29}} | collective-permute-start | bytes 3145736 | tf_op jit(solution)/shard_map/ppermute | solution.py:427
  69.5 1.6 collective-permute-start.16
  71.1 1.7 collective-permute-start.15
  72.9 1.5 solve.4
  74.4 5.9 %collective-permute-done.11.refs_2_ = bf16[512,512]{1,0:T(8,128)(2,1)} collective-permute-done((bf16[512,512]{1,0:T(8,128)(2,1)}, bf16[512,512]{1,0:T(8,128)(2,1)}, u32[]{:S(2)}, u32[]{:S(2)}) %collective-permute-start.11) | collective-permute-done | bytes 524320 | tf_op jit(solution)/shard_map/ppermute | solution.py:404
  81.5 1.8 collective-permute-done.12.refs_0_
  83.4 14.6 %factors.1 = (bf16[1024,2048]{1,0:T(8,128)(2,1)}, f32[8,128]{1,0:T(8,128)S(1)}) custom-call(s32[3]{0:T(128)S(1)} %pad_add_fusion.refs_0_, bf16[8192,128]{1,0:T(8,128)(2,1)} %get-tuple-element.89.refs_1_, bf16[8192,128]{1,0:T(8,128)(2,1)} %copy-done, bf16[8192,128]{1,0:T(8,128)(2,1)} %get-tuple-element.112.refs_3_, ...), custom_call_target="tpu_custom_call" | custom-call | tf_op jit(solution)/shard_map/factors/pallas_call | solution.py:32
  98.0 1.2 choose.10
  99.8 3.3 %collective-permute-start.14 = (bf16[1024,512]{1,0:T(8,128)(2,1)S(1)}, bf16[1024,512]{1,0:T(8,128)(2,1)}, u32[]{:S(2)}, u32[]{:S(2)}) collective-permute-start(bf16[1024,512]{1,0:T(8,128)(2,1)S(1)} %get-tuple-element.129.refs_1_), channel_id=1, source_target_pairs={{0,4},{1,5},{8,12},{9,13},{16,20},{17,21},{24,28},{25,29}} | collective-permute-start | bytes 3145736 | tf_op jit(solution)/shard_map/ppermute | solution.py:427
  104.8 1.3 collective-permute-start.18
  106.1 7.3 %update.5 = (bf16[65536,128]{1,0:T(8,128)(2,1)}, f32[8,128]{1,0:T(8,128)S(1)}) custom-call(bf16[65536,128]{1,0:T(8,128)(2,1)} %bitcast.37, bf16[1024,2048]{1,0:T(8,128)(2,1)} %get-tuple-element.125.refs_1_, bf16[512,512]{1,0:T(8,128)(2,1)S(1)} %get-tuple-element.98.refs_1_.refs_4_.refs_2_, ...), custom_call_target="tpu_custom_call" | custom-call | tf_op jit(solution)/shard_map/update/pallas_call | solution.py:32
  113.4 1.5 solve.5
  115.0 4.1 %collective-permute-start.19 = (f32[4,512]{1,0:T(4,128)S(1)}, f32[4,512]{1,0:T(4,128)S(1)}, u32[]{:S(2)}, u32[]{:S(2)}) collective-permute-start(f32[4,512]{1,0:T(4,128)S(1)} %get-tuple-element.137), channel_id=1, source_target_pairs={{0,8},{8,16},{16,24},{1,9},{9,17},{17,25},{2,10},{10,18},{18,26},{... | collective-permute-start | bytes 24584 | tf_op jit(solution)/shard_map/ppermute | solution.py:498
  119.9 1.5 solve.6
  121.4 2.3 %collective-permute-start.20 = (f32[4,512]{1,0:T(4,128)S(1)}, f32[4,512]{1,0:T(4,128)S(1)}, u32[]{:S(2)}, u32[]{:S(2)}) collective-permute-start(f32[4,512]{1,0:T(4,128)S(1)} %get-tuple-element.139), channel_id=1, source_target_pairs={{0,8},{8,16},{16,24},{1,9},{9,17},{17,25},{2,10},{10,18},{18,26},{... | collective-permute-start | bytes 24584 | tf_op jit(solution)/shard_map/ppermute | solution.py:498
  124.5 1.5 solve.7
  127.1 1.9 collective-permute-start.31
  129.0 1.6 collective-permute-start.30
  130.6 5.7 %collective-permute-start.21 = (bf16[512,512]{1,0:T(8,128)(2,1)}, bf16[512,512]{1,0:T(8,128)(2,1)S(1)}, u32[]{:S(2)}, u32[]{:S(2)}) collective-permute-start(bf16[512,512]{1,0:T(8,128)(2,1)} %get-tuple-element.143.refs_1_), channel_id=1, source_target_pairs={{0,4},{1,5},{8,12},{9,13},{16,20},{17,21},{24,28},{25,29}} | collective-permute-start | bytes 1572872 | tf_op jit(solution)/shard_map/ppermute | solution.py:427
  138.8 1.6 collective-permute-start.33
  140.4 1.3 collective-permute-start.26
  143.0 11.1 %update.6 = (bf16[65536,128]{1,0:T(8,128)(2,1)}, f32[8,128]{1,0:T(8,128)S(1)}) custom-call(bf16[65536,128]{1,0:T(8,128)(2,1)} %bitcast.38, bf16[1024,2048]{1,0:T(8,128)(2,1)} %get-tuple-element.125.refs_1_, bf16[1024,512]{1,0:T(8,128)(2,1)S(1)} %copy-done.13, bf16[1024,512]{1,0:T(8,128)(2,1)S(1)} %copy-done.7, ...), custom_call_target="tpu_custom_call", output_to_operand_aliasing={{0}: (4, {})} | custom-call | tf_op jit(solution)/shard_map/update/pallas_call | solution.py:32
  156.8 2.7 %collective-permute-start.27 = (f32[4,512]{1,0:T(4,128)S(1)}, f32[4,512]{1,0:T(4,128)S(1)}, u32[]{:S(2)}, u32[]{:S(2)}) collective-permute-start(f32[4,512]{1,0:T(4,128)S(1)} %get-tuple-element.153.refs_0_), channel_id=1, source_target_pairs={{0,16},{8,24},{16,0},{24,8},{1,17},{9,25},{17,1},{25,9},{2,18},{10... | collective-permute-start | bytes 24584 | tf_op jit(solution)/shard_map/ppermute | solution.py:408
  159.5 1.6 collective-permute-done.27.refs_1_
  162.3 2.6 %collective-permute-done.28.refs_1_ = f32[4,512]{1,0:T(4,128)S(1)} collective-permute-done((f32[4,512]{1,0:T(4,128)S(1)}, f32[4,512]{1,0:T(4,128)S(1)}, u32[]{:S(2)}, u32[]{:S(2)}) %collective-permute-start.28) | collective-permute-done | bytes 8224 | tf_op jit(solution)/shard_map/ppermute | solution.py:408
  165.8 1.4 collective-permute-start.35
  167.2 3.6 %collective-permute-done.29.refs_1_ = f32[4,512]{1,0:T(4,128)S(1)} collective-permute-done((f32[4,512]{1,0:T(4,128)S(1)}, f32[4,512]{1,0:T(4,128)S(1)}, u32[]{:S(2)}, u32[]{:S(2)}) %collective-permute-start.29) | collective-permute-done | bytes 8224 | tf_op jit(solution)/shard_map/ppermute | solution.py:408
  170.8 4.3 %collective-permute-start.32 = (f32[4,512]{1,0:T(4,128)S(1)}, f32[4,512]{1,0:T(4,128)S(1)}, u32[]{:S(2)}, u32[]{:S(2)}) collective-permute-start(f32[4,512]{1,0:T(4,128)S(1)} %get-tuple-element.161.refs_0_), channel_id=1, source_target_pairs={{0,4},{1,5},{2,6},{3,7},{4,0},{5,1},{6,2},{7,3},{8,12},{9,13},{10,... | collective-permute-start | bytes 24584 | tf_op jit(solution)/shard_map/ppermute | solution.py:408
  175.2 11.4 %update.7 = (bf16[65536,128]{1,0:T(8,128)(2,1)}, f32[8,128]{1,0:T(8,128)S(1)}) custom-call(bf16[65536,128]{1,0:T(8,128)(2,1)} %bitcast.39, bf16[1024,2048]{1,0:T(8,128)(2,1)} %get-tuple-element.125.refs_1_, bf16[1024,512]{1,0:T(8,128)(2,1)} %get-tuple-element.162.refs_2_, ...), custom_call_target="tpu_custom_call", output_to_operand_aliasing={{0}: (4, {})} | custom-call | tf_op jit(solution)/shard_map/update/pallas_call | solution.py:32
  188.3 1.6 collective-permute-start.34
  190.5 1.3 collective-permute-done.35.refs_3_
  191.8 11.1 %update.8 = (bf16[65536,128]{1,0:T(8,128)(2,1)}, f32[8,128]{1,0:T(8,128)S(1)}) custom-call(bf16[65536,128]{1,0:T(8,128)(2,1)} %bitcast.40, bf16[1024,2048]{1,0:T(8,128)(2,1)} %get-tuple-element.125.refs_1_, bf16[1024,512]{1,0:T(8,128)(2,1)S(1)} %get-tuple-element.168.refs_2_, ...), custom_call_target="tpu_custom_call", output_to_operand_aliasing={{0}: (4, {})} | custom-call | tf_op jit(solution)/shard_map/update/pallas_call | solution.py:32
  202.9 7.3 %update.9 = (bf16[65536,128]{1,0:T(8,128)(2,1)}, f32[8,128]{1,0:T(8,128)}) custom-call(bf16[65536,128]{1,0:T(8,128)(2,1)} %bitcast.41, bf16[1024,2048]{1,0:T(8,128)(2,1)} %get-tuple-element.125.refs_1_, bf16[512,512]{1,0:T(8,128)(2,1)S(1)} %get-tuple-element.167.refs_2_, ...), custom_call_target="tpu_custom_call", output_to_operand_aliasing={{0}: (4, {})} | custom-call | tf_op jit(solution)/shard_map/update/pallas_call | solution.py:32
  (113 shorter events, 23.5 us)
Async XLA Ops:
  1.3 11.0 %copy-start.17 = (bf16[4,1,512]{2,0,1:T(4,128)(2,1)S(1)}, bf16[4,1,512]{2,0,1:T(4,128)(2,1)}, u32[]{:S(2)}) copy-start(bf16[4,1,512]{2,0,1:T(4,128)(2,1)} %param.9) | copy-start | bytes 12292
  4.8 19.0 %collective-permute-start.1 = (bf16[8192,128]{1,0:T(8,128)(2,1)}, bf16[8192,128]{1,0:T(8,128)(2,1)S(1)}, u32[]{:S(2)}, u32[]{:S(2)}) collective-permute-start(bf16[8192,128]{1,0:T(8,128)(2,1)} %get-tuple-element.89.refs_1_), channel_id=1, source_target_pairs={{0,8},{8,0},{16,24},{24,16},{1,9},{9,1},{17,25},{25,17},{2,10},{10... | collective-permute-start | bytes 6291464 | tf_op jit(solution)/shard_map/ppermute | solution.py:408
  5.3 59.0 %collective-permute-start.2 = (bf16[8192,128]{1,0:T(8,128)(2,1)}, bf16[8192,128]{1,0:T(8,128)(2,1)}, u32[]{:S(2)}, u32[]{:S(2)}) collective-permute-start(bf16[8192,128]{1,0:T(8,128)(2,1)} %get-tuple-element.89.refs_1_), channel_id=1, source_target_pairs={{0,16},{8,24},{16,0},{24,8},{1,17},{9,25},{17,1},{25,9},{2,18},{10... | collective-permute-start | bytes 6291464 | tf_op jit(solution)/shard_map/ppermute | solution.py:404
  7.8 16.0 %collective-permute-start = (bf16[512,512]{1,0:T(8,128)(2,1)S(1)}, bf16[512,512]{1,0:T(8,128)(2,1)S(1)}, u32[]{:S(2)}, u32[]{:S(2)}) collective-permute-start(bf16[512,512]{1,0:T(8,128)(2,1)S(1)} %get-tuple-element.90.refs_1_.refs_6_), channel_id=1, source_target_pairs={{0,4},{1,5},{8,12},{9,13},{16,20},{17,21},{24,28},{25,29}} | collective-permute-start | bytes 1572872 | tf_op jit(solution)/shard_map/ppermute | solution.py:427
  23.8 1.3 copy-start
  25.2 15.6 %collective-permute-start.4 = (bf16[512,512]{1,0:T(8,128)(2,1)S(1)}, bf16[512,512]{1,0:T(8,128)(2,1)S(1)}, u32[]{:S(2)}, u32[]{:S(2)}) collective-permute-start(bf16[512,512]{1,0:T(8,128)(2,1)S(1)} %get-tuple-element.95.refs_2_), channel_id=1, source_target_pairs={{4,6},{5,7},{12,14},{13,15},{20,22},{21,23},{28,30},{29,31}} | collective-permute-start | bytes 1572872 | tf_op jit(solution)/shard_map/ppermute | solution.py:430
  25.9 14.9 %collective-permute-start.3 = (bf16[512,512]{1,0:T(8,128)(2,1)S(1)}, bf16[512,512]{1,0:T(8,128)(2,1)}, u32[]{:S(2)}, u32[]{:S(2)}) collective-permute-start(bf16[512,512]{1,0:T(8,128)(2,1)S(1)} %get-tuple-element.95.refs_2_), channel_id=1, source_target_pairs={{4,2},{5,3},{12,10},{13,11},{20,18},{21,19},{28,26},{29,27}} | collective-permute-start | bytes 1572872 | tf_op jit(solution)/shard_map/ppermute | solution.py:430
  27.3 33.9 %collective-permute-start.6 = (bf16[1024,512]{1,0:T(8,128)(2,1)}, bf16[1024,512]{1,0:T(8,128)(2,1)}, u32[]{:S(2)}, u32[]{:S(2)}) collective-permute-start(bf16[1024,512]{1,0:T(8,128)(2,1)} %get-tuple-element.99.refs_1_), channel_id=1, source_target_pairs={{0,4},{1,5},{8,12},{9,13},{16,20},{17,21},{24,28},{25,29}} | collective-permute-start | bytes 3145736 | tf_op jit(solution)/shard_map/ppermute | solution.py:427
  40.9 22.6 %collective-permute-start.5 = (bf16[512,512]{1,0:T(8,128)(2,1)S(1)}, bf16[512,512]{1,0:T(8,128)(2,1)S(1)}, u32[]{:S(2)}, u32[]{:S(2)}) collective-permute-start(bf16[512,512]{1,0:T(8,128)(2,1)S(1)} %get-tuple-element.98.refs_1_.refs_4_.refs_2_), channel_id=1, source_target_pairs={{0,1},{1,0},{2,3},{3,2},{4,5},{5,4},{6,7},{7,6},{8,9},{9,8},{10,11... | collective-permute-start | bytes 1572872 | tf_op jit(solution)/shard_map/ppermute | solution.py:408
  42.5 30.4 %copy-start.20 = (f32[8,1,512]{2,1,0:T(1,128)S(1)}, f32[8,1,512]{2,1,0:T(1,128)}, u32[]{:S(2)}) copy-start(f32[8,1,512]{2,1,0:T(1,128)} %param.10) | copy-start | bytes 49156
  49.9 23.0 %copy-start.1 = (bf16[1,1,512,512]{3,2,1,0:T(8,128)(2,1)S(1)}, bf16[1,1,512,512]{3,2,1,0:T(8,128)(2,1)}, u32[]{:S(2)}) copy-start(bf16[1,1,512,512]{3,2,1,0:T(8,128)(2,1)} %param.11) | copy-start | bytes 1572868
  49.9 6.7 %collective-permute-start.7 = (f32[8,512]{1,0:T(8,128)S(1)}, f32[8,512]{1,0:T(8,128)S(1)}, u32[]{:S(2)}, u32[]{:S(2)}) collective-permute-start(f32[8,512]{1,0:T(8,128)S(1)} %reshape.48.refs_0_), channel_id=1, source_target_pairs={{0,2},{1,3},{2,0},{3,1},{4,6},{5,7},{6,4},{7,5},{8,10},{9,11},{10,... | collective-permute-start | bytes 49160 | tf_op jit(solution)/shard_map/ppermute | solution.py:408
  56.6 4.6 %collective-permute-start.8 = (f32[8,512]{1,0:T(8,128)S(1)}, f32[8,512]{1,0:T(8,128)S(1)}, u32[]{:S(2)}, u32[]{:S(2)}) collective-permute-start(f32[8,512]{1,0:T(8,128)S(1)} %get-tuple-element.107.refs_0_), channel_id=1, source_target_pairs={{0,4},{1,5},{2,6},{3,7},{4,0},{5,1},{6,2},{7,3},{8,12},{9,13},{10,... | collective-permute-start | bytes 49160 | tf_op jit(solution)/shard_map/ppermute | solution.py:408
  61.2 1.2 copy-start.3
  64.3 8.5 %collective-permute-start.9 = (bf16[8192,128]{1,0:T(8,128)(2,1)}, bf16[8192,128]{1,0:T(8,128)(2,1)}, u32[]{:S(2)}, u32[]{:S(2)}) collective-permute-start(bf16[8192,128]{1,0:T(8,128)(2,1)} %get-tuple-element.112.refs_3_), channel_id=1, source_target_pairs={{0,8},{8,0},{16,24},{24,16},{1,9},{9,1},{17,25},{25,17},{2,10},{10... | collective-permute-start | bytes 6291464 | tf_op jit(solution)/shard_map/ppermute | solution.py:408
  64.4 6.7 %collective-permute-start.10 = (f32[8,512]{1,0:T(8,128)S(1)}, f32[8,512]{1,0:T(8,128)S(1)}, u32[]{:S(2)}, u32[]{:S(2)}) collective-permute-start(f32[8,512]{1,0:T(8,128)S(1)} %get-tuple-element.113.refs_0_), channel_id=1, source_target_pairs={{0,1},{1,0},{2,3},{3,2},{4,5},{5,4},{6,7},{7,6},{8,9},{9,8},{10,11... | collective-permute-start | bytes 49160 | tf_op jit(solution)/shard_map/ppermute | solution.py:408
  66.0 14.3 %collective-permute-start.11 = (bf16[512,512]{1,0:T(8,128)(2,1)}, bf16[512,512]{1,0:T(8,128)(2,1)}, u32[]{:S(2)}, u32[]{:S(2)}) collective-permute-start(bf16[512,512]{1,0:T(8,128)(2,1)} %get-tuple-element.117.refs_1_), channel_id=1, source_target_pairs={{0,16},{8,24},{16,0},{24,8},{1,17},{9,25},{17,1},{25,9},{2,18},{10... | collective-permute-start | bytes 1572872 | tf_op jit(solution)/shard_map/ppermute | solution.py:404
  66.5 31.4 %collective-permute-start.13 = (bf16[1024,512]{1,0:T(8,128)(2,1)}, bf16[1024,512]{1,0:T(8,128)(2,1)}, u32[]{:S(2)}, u32[]{:S(2)}) collective-permute-start(bf16[1024,512]{1,0:T(8,128)(2,1)} %copy-done.4), channel_id=1, source_target_pairs={{0,4},{1,5},{8,12},{9,13},{16,20},{17,21},{24,28},{25,29}} | collective-permute-start | bytes 3145736 | tf_op jit(solution)/shard_map/ppermute | solution.py:427
  69.5 28.5 %collective-permute-start.16 = (bf16[1024,512]{1,0:T(8,128)(2,1)}, bf16[1024,512]{1,0:T(8,128)(2,1)}, u32[]{:S(2)}, u32[]{:S(2)}) collective-permute-start(bf16[1024,512]{1,0:T(8,128)(2,1)} %get-tuple-element.131.refs_2_), channel_id=1, source_target_pairs={{4,6},{5,7},{12,14},{13,15},{20,22},{21,23},{28,30},{29,31}} | collective-permute-start | bytes 3145736 | tf_op jit(solution)/shard_map/ppermute | solution.py:430
  71.1 26.9 %collective-permute-start.15 = (bf16[1024,512]{1,0:T(8,128)(2,1)}, bf16[1024,512]{1,0:T(8,128)(2,1)}, u32[]{:S(2)}, u32[]{:S(2)}) collective-permute-start(bf16[1024,512]{1,0:T(8,128)(2,1)} %get-tuple-element.131.refs_2_), channel_id=1, source_target_pairs={{4,2},{5,3},{12,10},{13,11},{20,18},{21,19},{28,26},{29,27}} | collective-permute-start | bytes 3145736 | tf_op jit(solution)/shard_map/ppermute | solution.py:430
  72.8 10.6 %copy-start.14 = (bf16[2,512,512]{2,1,0:T(8,128)(2,1)S(1)}, bf16[2,512,512]{2,1,0:T(8,128)(2,1)}, u32[]{:S(2)}) copy-start(bf16[2,512,512]{2,1,0:T(8,128)(2,1)} %refs_7_.1) | copy-start | bytes 3145732
  72.8 10.6 %copy-start.15 = (bf16[2,512,512]{2,1,0:T(8,128)(2,1)S(1)}, bf16[2,512,512]{2,1,0:T(8,128)(2,1)}, u32[]{:S(2)}) copy-start(bf16[2,512,512]{2,1,0:T(8,128)(2,1)} %refs_8_.1) | copy-start | bytes 3145732
  81.4 2.0 collective-permute-start.12
  99.3 14.2 %copy-start.12 = (bf16[1024,512]{1,0:T(8,128)(2,1)}, bf16[1024,512]{1,0:T(8,128)(2,1)S(1)}, u32[]{:S(2)}) copy-start(bf16[1024,512]{1,0:T(8,128)(2,1)S(1)} %get-tuple-element.133.refs_2_) | copy-start | bytes 3145732
  99.3 26.7 %collective-permute-start.17 = (bf16[1024,512]{1,0:T(8,128)(2,1)S(1)}, bf16[1024,512]{1,0:T(8,128)(2,1)S(1)}, u32[]{:S(2)}, u32[]{:S(2)}) collective-permute-start(bf16[1024,512]{1,0:T(8,128)(2,1)S(1)} %get-tuple-element.133.refs_2_), channel_id=1, source_target_pairs={{0,1},{1,0},{2,3},{3,2},{4,5},{5,4},{6,7},{7,6},{8,9},{9,8},{10,11... | collective-permute-start | bytes 3145736 | tf_op jit(solution)/shard_map/ppermute | solution.py:408
  99.8 27.3 %collective-permute-start.14 = (bf16[1024,512]{1,0:T(8,128)(2,1)S(1)}, bf16[1024,512]{1,0:T(8,128)(2,1)}, u32[]{:S(2)}, u32[]{:S(2)}) collective-permute-start(bf16[1024,512]{1,0:T(8,128)(2,1)S(1)} %get-tuple-element.129.refs_1_), channel_id=1, source_target_pairs={{0,4},{1,5},{8,12},{9,13},{16,20},{17,21},{24,28},{25,29}} | collective-permute-start | bytes 3145736 | tf_op jit(solution)/shard_map/ppermute | solution.py:427
  103.2 33.2 %collective-permute-start.23 = (bf16[1024,512]{1,0:T(8,128)(2,1)}, bf16[1024,512]{1,0:T(8,128)(2,1)S(1)}, u32[]{:S(2)}, u32[]{:S(2)}) collective-permute-start(bf16[1024,512]{1,0:T(8,128)(2,1)} %get-tuple-element.146.refs_2_), channel_id=1, source_target_pairs={{4,6},{5,7},{12,14},{13,15},{20,22},{21,23},{28,30},{29,31}} | collective-permute-start | bytes 3145736 | tf_op jit(solution)/shard_map/ppermute | solution.py:430
  104.1 32.3 %collective-permute-start.22 = (bf16[1024,512]{1,0:T(8,128)(2,1)}, bf16[1024,512]{1,0:T(8,128)(2,1)S(1)}, u32[]{:S(2)}, u32[]{:S(2)}) collective-permute-start(bf16[1024,512]{1,0:T(8,128)(2,1)} %get-tuple-element.146.refs_2_), channel_id=1, source_target_pairs={{4,2},{5,3},{12,10},{13,11},{20,18},{21,19},{28,26},{29,27}} | collective-permute-start | bytes 3145736 | tf_op jit(solution)/shard_map/ppermute | solution.py:430
  104.8 8.6 %collective-permute-start.18 = (f32[4,512]{1,0:T(4,128)S(1)}, f32[4,512]{1,0:T(4,128)S(1)}, u32[]{:S(2)}, u32[]{:S(2)}) collective-permute-start(f32[4,512]{1,0:T(4,128)S(1)} %get-tuple-element.134), channel_id=1, source_target_pairs={{0,8},{8,16},{16,24},{1,9},{9,17},{17,25},{2,10},{10,18},{18,26},{... | collective-permute-start | bytes 24584 | tf_op jit(solution)/shard_map/ppermute | solution.py:498
  113.4 24.3 %copy-start.5 = (bf16[1024,512]{1,0:T(8,128)(2,1)S(1)}, bf16[1024,512]{1,0:T(8,128)(2,1)}, u32[]{:S(2)}) copy-start(bf16[1024,512]{1,0:T(8,128)(2,1)} %copy-done.4) | copy-start | bytes 3145732
  115.0 5.0 %collective-permute-start.19 = (f32[4,512]{1,0:T(4,128)S(1)}, f32[4,512]{1,0:T(4,128)S(1)}, u32[]{:S(2)}, u32[]{:S(2)}) collective-permute-start(f32[4,512]{1,0:T(4,128)S(1)} %get-tuple-element.137), channel_id=1, source_target_pairs={{0,8},{8,16},{16,24},{1,9},{9,17},{17,25},{2,10},{10,18},{18,26},{... | collective-permute-start | bytes 24584 | tf_op jit(solution)/shard_map/ppermute | solution.py:498
  121.4 3.1 %collective-permute-start.20 = (f32[4,512]{1,0:T(4,128)S(1)}, f32[4,512]{1,0:T(4,128)S(1)}, u32[]{:S(2)}, u32[]{:S(2)}) collective-permute-start(f32[4,512]{1,0:T(4,128)S(1)} %get-tuple-element.139), channel_id=1, source_target_pairs={{0,8},{8,16},{16,24},{1,9},{9,17},{17,25},{2,10},{10,18},{18,26},{... | collective-permute-start | bytes 24584 | tf_op jit(solution)/shard_map/ppermute | solution.py:498
  127.1 14.6 %copy-start.7 = (bf16[1024,512]{1,0:T(8,128)(2,1)S(1)}, bf16[1024,512]{1,0:T(8,128)(2,1)}, u32[]{:S(2)}) copy-start(bf16[1024,512]{1,0:T(8,128)(2,1)} %copy-done.6) | copy-start | bytes 3145732
  127.1 38.5 %collective-permute-start.31 = (bf16[1024,512]{1,0:T(8,128)(2,1)}, bf16[1024,512]{1,0:T(8,128)(2,1)}, u32[]{:S(2)}, u32[]{:S(2)}) collective-permute-start(bf16[1024,512]{1,0:T(8,128)(2,1)} %get-tuple-element.158.refs_2_), channel_id=1, source_target_pairs={{4,6},{5,7},{12,14},{13,15},{20,22},{21,23},{28,30},{29,31}} | collective-permute-start | bytes 3145736 | tf_op jit(solution)/shard_map/ppermute | solution.py:430
  129.0 36.6 %collective-permute-start.30 = (bf16[1024,512]{1,0:T(8,128)(2,1)}, bf16[1024,512]{1,0:T(8,128)(2,1)}, u32[]{:S(2)}, u32[]{:S(2)}) collective-permute-start(bf16[1024,512]{1,0:T(8,128)(2,1)} %get-tuple-element.158.refs_2_), channel_id=1, source_target_pairs={{4,2},{5,3},{12,10},{13,11},{20,18},{21,19},{28,26},{29,27}} | collective-permute-start | bytes 3145736 | tf_op jit(solution)/shard_map/ppermute | solution.py:430
  130.6 23.5 %collective-permute-start.21 = (bf16[512,512]{1,0:T(8,128)(2,1)}, bf16[512,512]{1,0:T(8,128)(2,1)S(1)}, u32[]{:S(2)}, u32[]{:S(2)}) collective-permute-start(bf16[512,512]{1,0:T(8,128)(2,1)} %get-tuple-element.143.refs_1_), channel_id=1, source_target_pairs={{0,4},{1,5},{8,12},{9,13},{16,20},{17,21},{24,28},{25,29}} | collective-permute-start | bytes 1572872 | tf_op jit(solution)/shard_map/ppermute | solution.py:427
  136.4 1.3 copy-start.19
  138.8 36.3 %collective-permute-start.33 = (bf16[1024,512]{1,0:T(8,128)(2,1)}, bf16[1024,512]{1,0:T(8,128)(2,1)}, u32[]{:S(2)}, u32[]{:S(2)}) collective-permute-start(bf16[1024,512]{1,0:T(8,128)(2,1)} %get-tuple-element.162.refs_2_), channel_id=1, source_target_pairs={{0,1},{1,0},{2,3},{3,2},{4,5},{5,4},{6,7},{7,6},{8,9},{9,8},{10,11... | collective-permute-start | bytes 3145736 | tf_op jit(solution)/shard_map/ppermute | solution.py:408
  140.4 16.3 %collective-permute-start.26 = (f32[4,512]{1,0:T(4,128)S(1)}, f32[4,512]{1,0:T(4,128)S(1)}, u32[]{:S(2)}, u32[]{:S(2)}) collective-permute-start(f32[4,512]{1,0:T(4,128)S(1)} %broadcast_select_fusion.refs_0_), channel_id=1, source_target_pairs={{0,8},{8,0},{16,24},{24,16},{1,9},{9,1},{17,25},{25,17},{2,10},{10... | collective-permute-start | bytes 24584 | tf_op jit(solution)/shard_map/ppermute | solution.py:408
  156.8 4.4 %collective-permute-start.27 = (f32[4,512]{1,0:T(4,128)S(1)}, f32[4,512]{1,0:T(4,128)S(1)}, u32[]{:S(2)}, u32[]{:S(2)}) collective-permute-start(f32[4,512]{1,0:T(4,128)S(1)} %get-tuple-element.153.refs_0_), channel_id=1, source_target_pairs={{0,16},{8,24},{16,0},{24,8},{1,17},{9,25},{17,1},{25,9},{2,18},{10... | collective-permute-start | bytes 24584 | tf_op jit(solution)/shard_map/ppermute | solution.py:408
  161.1 3.8 %collective-permute-start.28 = (f32[4,512]{1,0:T(4,128)S(1)}, f32[4,512]{1,0:T(4,128)S(1)}, u32[]{:S(2)}, u32[]{:S(2)}) collective-permute-start(f32[4,512]{1,0:T(4,128)S(1)} %get-tuple-element.155.refs_0_), channel_id=1, source_target_pairs={{0,1},{1,0},{2,3},{3,2},{4,5},{5,4},{6,7},{7,6},{8,9},{9,8},{10,11... | collective-permute-start | bytes 24584 | tf_op jit(solution)/shard_map/ppermute | solution.py:408
  161.6 25.6 %collective-permute-start.25 = (bf16[512,512]{1,0:T(8,128)(2,1)}, bf16[512,512]{1,0:T(8,128)(2,1)S(1)}, u32[]{:S(2)}, u32[]{:S(2)}) collective-permute-start(bf16[512,512]{1,0:T(8,128)(2,1)} %copy-done.10), channel_id=1, source_target_pairs={{4,6},{5,7},{12,14},{13,15},{20,22},{21,23},{28,30},{29,31}} | collective-permute-start | bytes 1572872 | tf_op jit(solution)/shard_map/ppermute | solution.py:430
  164.9 22.3 %collective-permute-start.24 = (bf16[512,512]{1,0:T(8,128)(2,1)}, bf16[512,512]{1,0:T(8,128)(2,1)S(1)}, u32[]{:S(2)}, u32[]{:S(2)}) collective-permute-start(bf16[512,512]{1,0:T(8,128)(2,1)} %copy-done.10), channel_id=1, source_target_pairs={{4,2},{5,3},{12,10},{13,11},{20,18},{21,19},{28,26},{29,27}} | collective-permute-start | bytes 1572872 | tf_op jit(solution)/shard_map/ppermute | solution.py:430
  165.8 26.1 %collective-permute-start.35 = (bf16[1024,512]{1,0:T(8,128)(2,1)S(1)}, bf16[1024,512]{1,0:T(8,128)(2,1)S(1)}, u32[]{:S(2)}, u32[]{:S(2)}) collective-permute-start(bf16[1024,512]{1,0:T(8,128)(2,1)S(1)} %get-tuple-element.168.refs_2_), channel_id=1, source_target_pairs={{0,1},{1,0},{2,3},{3,2},{4,5},{5,4},{6,7},{7,6},{8,9},{9,8},{10,11... | collective-permute-start | bytes 3145736 | tf_op jit(solution)/shard_map/ppermute | solution.py:408
  167.2 3.7 %collective-permute-start.29 = (f32[4,512]{1,0:T(4,128)S(1)}, f32[4,512]{1,0:T(4,128)S(1)}, u32[]{:S(2)}, u32[]{:S(2)}) collective-permute-start(f32[4,512]{1,0:T(4,128)S(1)} %get-tuple-element.157.refs_0_), channel_id=1, source_target_pairs={{0,2},{1,3},{2,0},{3,1},{4,6},{5,7},{6,4},{7,5},{8,10},{9,11},{10,... | collective-permute-start | bytes 24584 | tf_op jit(solution)/shard_map/ppermute | solution.py:408
  170.8 15.8 %collective-permute-start.32 = (f32[4,512]{1,0:T(4,128)S(1)}, f32[4,512]{1,0:T(4,128)S(1)}, u32[]{:S(2)}, u32[]{:S(2)}) collective-permute-start(f32[4,512]{1,0:T(4,128)S(1)} %get-tuple-element.161.refs_0_), channel_id=1, source_target_pairs={{0,4},{1,5},{2,6},{3,7},{4,0},{5,1},{6,2},{7,3},{8,12},{9,13},{10,... | collective-permute-start | bytes 24584 | tf_op jit(solution)/shard_map/ppermute | solution.py:408
  175.2 12.0 %copy-start.11 = (bf16[512,512]{1,0:T(8,128)(2,1)S(1)}, bf16[512,512]{1,0:T(8,128)(2,1)}, u32[]{:S(2)}) copy-start(bf16[512,512]{1,0:T(8,128)(2,1)} %copy-done.10) | copy-start | bytes 1572868
  188.3 14.6 %collective-permute-start.34 = (bf16[512,512]{1,0:T(8,128)(2,1)S(1)}, bf16[512,512]{1,0:T(8,128)(2,1)S(1)}, u32[]{:S(2)}, u32[]{:S(2)}) collective-permute-start(bf16[512,512]{1,0:T(8,128)(2,1)S(1)} %get-tuple-element.167.refs_2_), channel_id=1, source_target_pairs={{0,1},{1,0},{2,3},{3,2},{4,5},{5,4},{6,7},{7,6},{8,9},{9,8},{10,11... | collective-permute-start | bytes 1572872 | tf_op jit(solution)/shard_map/ppermute | solution.py:408
  (9 other events, 8.6 us)

commit v7 on v6

--- a/solution.py
+++ b/solution.py
@@ -588,9 +588,9 @@
         advance(4)
         each(line[4:7])
         take(3)
-        each([line[7], updates(2), line[8]])
+        updates(2)()
         take(4)
-        each([updates(3), updates(4)])
+        each([line[7], line[8], updates(3), updates(4)])
     else:
         each([*total, blocks_out, bands_in, blocks_swap, blocks_in, make_factors, *line])
         for k in range(1, chunks):

time: 211 us -> 211 us (level)
  starting transfers between devices: 68.1 us -> 65.1 us
  waiting for transfers between devices: 32.6 us -> 35.6 us
    ppermute x16, starting transfers between devices: 21.4 us -> 18.4 us  [swap(): return lax.ppermute(value, axis, [(i, i ^ bit) for i in range(size)])]
    ppermute x16, waiting for transfers between devices: 18.8 us -> 21.8 us  [swap(): return lax.ppermute(value, axis, [(i, i ^ bit) for i in range(size)])]
  transfers between devices with their start and end apart: 36 -> 36, of which waited for: 11 -> 12; matrix products, arithmetic and copies ran while one was open for 0% -> 0% of each run, Pallas kernels for 40% -> 40%
where the time goes in v7:
time: 211 us; the launch traced here: 210 us
  Pallas kernels  96 us (45%)
  starting transfers between devices  65.1 us (31%)
  waiting for transfers between devices  35.6 us (17%)
  local copies, waits for them, and re-layouts  12.2 us (6%)
    pallas_call x38, Pallas kernels, __call__(): pl.pallas_call(body, in_specs=list(in_specs) + [anywhere] * n_dep, out_sp...  96 us
    ppermute x5, starting transfers between devices, first_stage(): return lax.ppermute(local, 'pcol', along_z(stages[0][0]))  24.1 us
    ppermute x16, waiting for transfers between devices, swap(): return lax.ppermute(value, axis, [(i, i ^ bit) for i in range(size)])  21.8 us
    ppermute x16, starting transfers between devices, swap(): return lax.ppermute(value, axis, [(i, i ^ bit) for i in range(size)])  18.4 us
    unnamed x43, local copies, waits for them, and re-layouts  12.2 us
    ppermute x10, starting transfers between devices, second_stage(): lax.ppermute(arrived, 'pcol', along_z(moves))  12 us
    ppermute x3, starting transfers between devices, run(): lax.ppermute(box['state'], 'prow', [(i, i + 1) for i in range(n_prow - 1)])  7.69 us
    ppermute x5, waiting for transfers between devices, first_stage(): return lax.ppermute(local, 'pcol', along_z(stages[0][0]))  6.25 us
  transfers between devices with their start and end apart: 36, of which 12 were waited for; matrix products, arithmetic and copies ran while one was open for 0% of the time, Pallas kernels for 40%

profile of v7, /device:TPU:0, one launch (start us, length us, event | category | flops | bytes accessed | tf_op | source)
XLA Modules:
  0.0 210.2 jit_solution(8667972804280146750)
XLA Ops:
  1.3 3.5 %extract.4 = (f32[1,512]{1,0:T(1,128)S(1)}, bf16[512,512]{1,0:T(8,128)(2,1)S(1)}, bf16[8192,128]{1,0:T(8,128)(2,1)}, f32[8,128]{1,0:T(8,128)S(1)}) custom-call(bf16[65536,128]{1,0:T(8,128)(2,1)} %bitcast.33, bf16[16,128]{1,0:T(8,128)(2,1)S(1)} %bitcast.29), custom_call_target="tpu_custom_call" | custom-call | tf_op jit(solution)/shard_map/extract/pallas_call | solution.py:32
  5.3 2.5 %collective-permute-start.2 = (bf16[8192,128]{1,0:T(8,128)(2,1)}, bf16[8192,128]{1,0:T(8,128)(2,1)}, u32[]{:S(2)}, u32[]{:S(2)}) collective-permute-start(bf16[8192,128]{1,0:T(8,128)(2,1)} %get-tuple-element.89.refs_1_), channel_id=1, source_target_pairs={{0,16},{8,24},{16,0},{24,8},{1,17},{9,25},{17,1},{25,9},{2,18},{10... | collective-permute-start | bytes 6291464 | tf_op jit(solution)/shard_map/ppermute | solution.py:404
  7.8 4.5 %collective-permute-start = (bf16[512,512]{1,0:T(8,128)(2,1)S(1)}, bf16[512,512]{1,0:T(8,128)(2,1)S(1)}, u32[]{:S(2)}, u32[]{:S(2)}) collective-permute-start(bf16[512,512]{1,0:T(8,128)(2,1)S(1)} %get-tuple-element.90.refs_1_.refs_6_), channel_id=1, source_target_pairs={{0,4},{1,5},{8,12},{9,13},{16,20},{17,21},{24,28},{25,29}} | collective-permute-start | bytes 1572872 | tf_op jit(solution)/shard_map/ppermute | solution.py:427
  12.3 5.3 %extract.5 = (f32[1,1024]{1,0:T(1,128)S(1)}, bf16[1024,512]{1,0:T(8,128)(2,1)}, f32[8,128]{1,0:T(8,128)S(1)}) custom-call(bf16[65536,128]{1,0:T(8,128)(2,1)} %bitcast.34, bf16[16,128]{1,0:T(8,128)(2,1)S(1)} %bitcast.30, f32[8,128]{1,0:T(8,128)S(1)} %get-tuple-element.91.refs_2_), custom_call_target="tpu_custom_call" | custom-call | tf_op jit(solution)/shard_map/extract/pallas_call | solution.py:32
  17.6 6.2 %collective-permute-done.refs_0_ = bf16[512,512]{1,0:T(8,128)(2,1)S(1)} collective-permute-done((bf16[512,512]{1,0:T(8,128)(2,1)S(1)}, bf16[512,512]{1,0:T(8,128)(2,1)S(1)}, u32[]{:S(2)}, u32[]{:S(2)}) %collective-permute-start) | collective-permute-done | bytes 524320 | tf_op jit(solution)/shard_map/ppermute | solution.py:427
  23.8 1.3 copy-done
  25.9 1.5 collective-permute-start.3
  27.3 7.5 %collective-permute-start.6 = (bf16[1024,512]{1,0:T(8,128)(2,1)}, bf16[1024,512]{1,0:T(8,128)(2,1)}, u32[]{:S(2)}, u32[]{:S(2)}) collective-permute-start(bf16[1024,512]{1,0:T(8,128)(2,1)} %get-tuple-element.99.refs_1_), channel_id=1, source_target_pairs={{0,4},{1,5},{8,12},{9,13},{16,20},{17,21},{24,28},{25,29}} | collective-permute-start | bytes 3145736 | tf_op jit(solution)/shard_map/ppermute | solution.py:427
  34.9 4.9 %extract.6 = (f32[1,1024]{1,0:T(1,128)S(1)}, bf16[1024,512]{1,0:T(8,128)(2,1)S(1)}, f32[8,128]{1,0:T(8,128)S(1)}) custom-call(bf16[65536,128]{1,0:T(8,128)(2,1)} %bitcast.35, bf16[16,128]{1,0:T(8,128)(2,1)S(1)} %bitcast.31, f32[8,128]{1,0:T(8,128)S(1)} %get-tuple-element.96.refs_2_), custom_call_target="tpu_custom_call" | custom-call | tf_op jit(solution)/shard_map/extract/pallas_call | solution.py:32
  40.9 1.6 collective-permute-start.5
  42.5 7.4 %extract.7 = (f32[1,1536]{1,0:T(1,128)S(1)}, bf16[1024,512]{1,0:T(8,128)(2,1)S(1)}, bf16[512,512]{1,0:T(8,128)(2,1)}, f32[8,128]{1,0:T(8,128)S(1)}) custom-call(bf16[65536,128]{1,0:T(8,128)(2,1)} %bitcast.36, bf16[16,128]{1,0:T(8,128)(2,1)S(1)} %bitcast.32, f32[8,128]{1,0:T(8,128)S(1)} %get-tuple-element.104.refs_2_), custom_call_target="tpu_custom_call" | custom-call | tf_op jit(solution)/shard_map/extract/pallas_call | solution.py:32
  49.9 3.5 %collective-permute-start.7 = (f32[8,512]{1,0:T(8,128)S(1)}, f32[8,512]{1,0:T(8,128)S(1)}, u32[]{:S(2)}, u32[]{:S(2)}) collective-permute-start(f32[8,512]{1,0:T(8,128)S(1)} %reshape.48.refs_0_), channel_id=1, source_target_pairs={{0,2},{1,3},{2,0},{3,1},{4,6},{5,7},{6,4},{7,5},{8,10},{9,11},{10,... | collective-permute-start | bytes 49160 | tf_op jit(solution)/shard_map/ppermute | solution.py:408
  53.5 3.1 %collective-permute-done.7.refs_1_ = f32[8,512]{1,0:T(8,128)S(1)} collective-permute-done((f32[8,512]{1,0:T(8,128)S(1)}, f32[8,512]{1,0:T(8,128)S(1)}, u32[]{:S(2)}, u32[]{:S(2)}) %collective-permute-start.7) | collective-permute-done | bytes 16416 | tf_op jit(solution)/shard_map/ppermute | solution.py:408
  56.6 4.6 %collective-permute-done.8.refs_1_ = f32[8,512]{1,0:T(8,128)S(1)} collective-permute-done((f32[8,512]{1,0:T(8,128)S(1)}, f32[8,512]{1,0:T(8,128)S(1)}, u32[]{:S(2)}, u32[]{:S(2)}) %collective-permute-start.8) | collective-permute-done | bytes 16416 | tf_op jit(solution)/shard_map/ppermute | solution.py:408
  64.4 1.6 collective-permute-start.10
  66.5 2.9 %collective-permute-start.13 = (bf16[1024,512]{1,0:T(8,128)(2,1)}, bf16[1024,512]{1,0:T(8,128)(2,1)}, u32[]{:S(2)}, u32[]{:S(2)}) collective-permute-start(bf16[1024,512]{1,0:T(8,128)(2,1)} %copy-done.4), channel_id=1, source_target_pairs={{0,4},{1,5},{8,12},{9,13},{16,20},{17,21},{24,28},{25,29}} | collective-permute-start | bytes 3145736 | tf_op jit(solution)/shard_map/ppermute | solution.py:427
  69.5 1.6 collective-permute-start.16
  71.1 1.7 collective-permute-start.15
  72.9 1.5 solve.4
  74.4 5.9 %collective-permute-done.11.refs_2_ = bf16[512,512]{1,0:T(8,128)(2,1)} collective-permute-done((bf16[512,512]{1,0:T(8,128)(2,1)}, bf16[512,512]{1,0:T(8,128)(2,1)}, u32[]{:S(2)}, u32[]{:S(2)}) %collective-permute-start.11) | collective-permute-done | bytes 524320 | tf_op jit(solution)/shard_map/ppermute | solution.py:404
  81.5 1.8 collective-permute-done.12.refs_0_
  83.4 14.6 %factors.1 = (bf16[1024,2048]{1,0:T(8,128)(2,1)}, f32[8,128]{1,0:T(8,128)S(1)}) custom-call(s32[3]{0:T(128)S(1)} %pad_add_fusion.refs_0_, bf16[8192,128]{1,0:T(8,128)(2,1)} %get-tuple-element.89.refs_1_, bf16[8192,128]{1,0:T(8,128)(2,1)} %copy-done, bf16[8192,128]{1,0:T(8,128)(2,1)} %get-tuple-element.112.refs_3_, ...), custom_call_target="tpu_custom_call" | custom-call | tf_op jit(solution)/shard_map/factors/pallas_call | solution.py:32
  98.0 1.2 choose.10
  99.8 3.3 %collective-permute-start.14 = (bf16[1024,512]{1,0:T(8,128)(2,1)S(1)}, bf16[1024,512]{1,0:T(8,128)(2,1)}, u32[]{:S(2)}, u32[]{:S(2)}) collective-permute-start(bf16[1024,512]{1,0:T(8,128)(2,1)S(1)} %get-tuple-element.129.refs_1_), channel_id=1, source_target_pairs={{0,4},{1,5},{8,12},{9,13},{16,20},{17,21},{24,28},{25,29}} | collective-permute-start | bytes 3145736 | tf_op jit(solution)/shard_map/ppermute | solution.py:427
  104.8 1.3 collective-permute-start.18
  106.1 7.3 %update.5 = (bf16[65536,128]{1,0:T(8,128)(2,1)}, f32[8,128]{1,0:T(8,128)S(1)}) custom-call(bf16[65536,128]{1,0:T(8,128)(2,1)} %bitcast.37, bf16[1024,2048]{1,0:T(8,128)(2,1)} %get-tuple-element.125.refs_1_, bf16[512,512]{1,0:T(8,128)(2,1)S(1)} %get-tuple-element.98.refs_1_.refs_4_.refs_2_, ...), custom_call_target="tpu_custom_call" | custom-call | tf_op jit(solution)/shard_map/update/pallas_call | solution.py:32
  113.4 1.5 solve.5
  115.0 4.1 %collective-permute-start.19 = (f32[4,512]{1,0:T(4,128)S(1)}, f32[4,512]{1,0:T(4,128)S(1)}, u32[]{:S(2)}, u32[]{:S(2)}) collective-permute-start(f32[4,512]{1,0:T(4,128)S(1)} %get-tuple-element.137), channel_id=1, source_target_pairs={{0,8},{8,16},{16,24},{1,9},{9,17},{17,25},{2,10},{10,18},{18,26},{... | collective-permute-start | bytes 24584 | tf_op jit(solution)/shard_map/ppermute | solution.py:498
  119.9 1.5 solve.6
  121.4 2.3 %collective-permute-start.20 = (f32[4,512]{1,0:T(4,128)S(1)}, f32[4,512]{1,0:T(4,128)S(1)}, u32[]{:S(2)}, u32[]{:S(2)}) collective-permute-start(f32[4,512]{1,0:T(4,128)S(1)} %get-tuple-element.139), channel_id=1, source_target_pairs={{0,8},{8,16},{16,24},{1,9},{9,17},{17,25},{2,10},{10,18},{18,26},{... | collective-permute-start | bytes 24584 | tf_op jit(solution)/shard_map/ppermute | solution.py:498
  124.5 1.5 solve.7
  127.1 1.9 collective-permute-start.28
  129.0 1.6 collective-permute-start.27
  130.6 5.7 %collective-permute-start.21 = (bf16[512,512]{1,0:T(8,128)(2,1)}, bf16[512,512]{1,0:T(8,128)(2,1)S(1)}, u32[]{:S(2)}, u32[]{:S(2)}) collective-permute-start(bf16[512,512]{1,0:T(8,128)(2,1)} %get-tuple-element.143.refs_1_), channel_id=1, source_target_pairs={{0,4},{1,5},{8,12},{9,13},{16,20},{17,21},{24,28},{25,29}} | collective-permute-start | bytes 1572872 | tf_op jit(solution)/shard_map/ppermute | solution.py:427
  138.8 1.6 collective-permute-start.26
  140.4 1.3 collective-permute-start.29
  143.0 11.1 %update.6 = (bf16[65536,128]{1,0:T(8,128)(2,1)}, f32[8,128]{1,0:T(8,128)S(1)}) custom-call(bf16[65536,128]{1,0:T(8,128)(2,1)} %bitcast.38, bf16[1024,2048]{1,0:T(8,128)(2,1)} %get-tuple-element.125.refs_1_, bf16[1024,512]{1,0:T(8,128)(2,1)S(1)} %copy-done.13, bf16[1024,512]{1,0:T(8,128)(2,1)S(1)} %copy-done.7, ...), custom_call_target="tpu_custom_call", output_to_operand_aliasing={{0}: (4, {})} | custom-call | tf_op jit(solution)/shard_map/update/pallas_call | solution.py:32
  156.8 2.7 %collective-permute-start.30 = (f32[4,512]{1,0:T(4,128)S(1)}, f32[4,512]{1,0:T(4,128)S(1)}, u32[]{:S(2)}, u32[]{:S(2)}) collective-permute-start(f32[4,512]{1,0:T(4,128)S(1)} %get-tuple-element.156.refs_0_), channel_id=1, source_target_pairs={{0,16},{8,24},{16,0},{24,8},{1,17},{9,25},{17,1},{25,9},{2,18},{10... | collective-permute-start | bytes 24584 | tf_op jit(solution)/shard_map/ppermute | solution.py:408
  159.5 1.6 collective-permute-done.30.refs_1_
  162.3 2.6 %collective-permute-done.31.refs_1_ = f32[4,512]{1,0:T(4,128)S(1)} collective-permute-done((f32[4,512]{1,0:T(4,128)S(1)}, f32[4,512]{1,0:T(4,128)S(1)}, u32[]{:S(2)}, u32[]{:S(2)}) %collective-permute-start.31) | collective-permute-done | bytes 8224 | tf_op jit(solution)/shard_map/ppermute | solution.py:408
  165.8 1.4 collective-permute-start.33
  167.2 11.4 %update.7 = (bf16[65536,128]{1,0:T(8,128)(2,1)}, f32[8,128]{1,0:T(8,128)S(1)}) custom-call(bf16[65536,128]{1,0:T(8,128)(2,1)} %bitcast.39, bf16[1024,2048]{1,0:T(8,128)(2,1)} %get-tuple-element.125.refs_1_, bf16[1024,512]{1,0:T(8,128)(2,1)} %get-tuple-element.151.refs_2_, ...), custom_call_target="tpu_custom_call", output_to_operand_aliasing={{0}: (4, {})} | custom-call | tf_op jit(solution)/shard_map/update/pallas_call | solution.py:32
  181.3 2.7 %collective-permute-done.34.refs_1_ = f32[4,512]{1,0:T(4,128)S(1)} collective-permute-done((f32[4,512]{1,0:T(4,128)S(1)}, f32[4,512]{1,0:T(4,128)S(1)}, u32[]{:S(2)}, u32[]{:S(2)}) %collective-permute-start.34) | collective-permute-done | bytes 8224 | tf_op jit(solution)/shard_map/ppermute | solution.py:408
  184.1 1.3 collective-permute-start.35
  186.0 2.7 %collective-permute-done.35.refs_1_ = f32[4,512]{1,0:T(4,128)S(1)} collective-permute-done((f32[4,512]{1,0:T(4,128)S(1)}, f32[4,512]{1,0:T(4,128)S(1)}, u32[]{:S(2)}, u32[]{:S(2)}) %collective-permute-start.35) | collective-permute-done | bytes 8224 | tf_op jit(solution)/shard_map/ppermute | solution.py:408
  189.2 2.6 %collective-permute-done.33.refs_3_ = bf16[1024,512]{1,0:T(8,128)(2,1)S(1)} collective-permute-done((bf16[1024,512]{1,0:T(8,128)(2,1)S(1)}, bf16[1024,512]{1,0:T(8,128)(2,1)S(1)}, u32[]{:S(2)}, u32[]{:S(2)}) %collective-permute-start.33) | collective-permute-done | bytes 1048608 | tf_op jit(solution)/shard_map/ppermute | solution.py:408
  191.8 11.1 %update.8 = (bf16[65536,128]{1,0:T(8,128)(2,1)}, f32[8,128]{1,0:T(8,128)S(1)}) custom-call(bf16[65536,128]{1,0:T(8,128)(2,1)} %bitcast.40, bf16[1024,2048]{1,0:T(8,128)(2,1)} %get-tuple-element.125.refs_1_, bf16[1024,512]{1,0:T(8,128)(2,1)S(1)} %get-tuple-element.164.refs_2_, ...), custom_call_target="tpu_custom_call", output_to_operand_aliasing={{0}: (4, {})} | custom-call | tf_op jit(solution)/shard_map/update/pallas_call | solution.py:32
  202.9 7.3 %update.9 = (bf16[65536,128]{1,0:T(8,128)(2,1)}, f32[8,128]{1,0:T(8,128)}) custom-call(bf16[65536,128]{1,0:T(8,128)(2,1)} %bitcast.41, bf16[1024,2048]{1,0:T(8,128)(2,1)} %get-tuple-element.125.refs_1_, bf16[512,512]{1,0:T(8,128)(2,1)S(1)} %get-tuple-element.163.refs_2_, ...), custom_call_target="tpu_custom_call", output_to_operand_aliasing={{0}: (4, {})} | custom-call | tf_op jit(solution)/shard_map/update/pallas_call | solution.py:32
  (113 shorter events, 25.1 us)
Async XLA Ops:
  1.3 11.0 %copy-start.17 = (bf16[4,1,512]{2,0,1:T(4,128)(2,1)S(1)}, bf16[4,1,512]{2,0,1:T(4,128)(2,1)}, u32[]{:S(2)}) copy-start(bf16[4,1,512]{2,0,1:T(4,128)(2,1)} %param.9) | copy-start | bytes 12292
  4.8 19.0 %collective-permute-start.1 = (bf16[8192,128]{1,0:T(8,128)(2,1)}, bf16[8192,128]{1,0:T(8,128)(2,1)S(1)}, u32[]{:S(2)}, u32[]{:S(2)}) collective-permute-start(bf16[8192,128]{1,0:T(8,128)(2,1)} %get-tuple-element.89.refs_1_), channel_id=1, source_target_pairs={{0,8},{8,0},{16,24},{24,16},{1,9},{9,1},{17,25},{25,17},{2,10},{10... | collective-permute-start | bytes 6291464 | tf_op jit(solution)/shard_map/ppermute | solution.py:408
  5.3 59.0 %collective-permute-start.2 = (bf16[8192,128]{1,0:T(8,128)(2,1)}, bf16[8192,128]{1,0:T(8,128)(2,1)}, u32[]{:S(2)}, u32[]{:S(2)}) collective-permute-start(bf16[8192,128]{1,0:T(8,128)(2,1)} %get-tuple-element.89.refs_1_), channel_id=1, source_target_pairs={{0,16},{8,24},{16,0},{24,8},{1,17},{9,25},{17,1},{25,9},{2,18},{10... | collective-permute-start | bytes 6291464 | tf_op jit(solution)/shard_map/ppermute | solution.py:404
  7.8 16.0 %collective-permute-start = (bf16[512,512]{1,0:T(8,128)(2,1)S(1)}, bf16[512,512]{1,0:T(8,128)(2,1)S(1)}, u32[]{:S(2)}, u32[]{:S(2)}) collective-permute-start(bf16[512,512]{1,0:T(8,128)(2,1)S(1)} %get-tuple-element.90.refs_1_.refs_6_), channel_id=1, source_target_pairs={{0,4},{1,5},{8,12},{9,13},{16,20},{17,21},{24,28},{25,29}} | collective-permute-start | bytes 1572872 | tf_op jit(solution)/shard_map/ppermute | solution.py:427
  23.8 1.3 copy-start
  25.2 15.6 %collective-permute-start.4 = (bf16[512,512]{1,0:T(8,128)(2,1)S(1)}, bf16[512,512]{1,0:T(8,128)(2,1)S(1)}, u32[]{:S(2)}, u32[]{:S(2)}) collective-permute-start(bf16[512,512]{1,0:T(8,128)(2,1)S(1)} %get-tuple-element.95.refs_2_), channel_id=1, source_target_pairs={{4,6},{5,7},{12,14},{13,15},{20,22},{21,23},{28,30},{29,31}} | collective-permute-start | bytes 1572872 | tf_op jit(solution)/shard_map/ppermute | solution.py:430
  25.9 14.9 %collective-permute-start.3 = (bf16[512,512]{1,0:T(8,128)(2,1)S(1)}, bf16[512,512]{1,0:T(8,128)(2,1)}, u32[]{:S(2)}, u32[]{:S(2)}) collective-permute-start(bf16[512,512]{1,0:T(8,128)(2,1)S(1)} %get-tuple-element.95.refs_2_), channel_id=1, source_target_pairs={{4,2},{5,3},{12,10},{13,11},{20,18},{21,19},{28,26},{29,27}} | collective-permute-start | bytes 1572872 | tf_op jit(solution)/shard_map/ppermute | solution.py:430
  27.3 33.9 %collective-permute-start.6 = (bf16[1024,512]{1,0:T(8,128)(2,1)}, bf16[1024,512]{1,0:T(8,128)(2,1)}, u32[]{:S(2)}, u32[]{:S(2)}) collective-permute-start(bf16[1024,512]{1,0:T(8,128)(2,1)} %get-tuple-element.99.refs_1_), channel_id=1, source_target_pairs={{0,4},{1,5},{8,12},{9,13},{16,20},{17,21},{24,28},{25,29}} | collective-permute-start | bytes 3145736 | tf_op jit(solution)/shard_map/ppermute | solution.py:427
  40.9 22.6 %collective-permute-start.5 = (bf16[512,512]{1,0:T(8,128)(2,1)S(1)}, bf16[512,512]{1,0:T(8,128)(2,1)S(1)}, u32[]{:S(2)}, u32[]{:S(2)}) collective-permute-start(bf16[512,512]{1,0:T(8,128)(2,1)S(1)} %get-tuple-element.98.refs_1_.refs_4_.refs_2_), channel_id=1, source_target_pairs={{0,1},{1,0},{2,3},{3,2},{4,5},{5,4},{6,7},{7,6},{8,9},{9,8},{10,11... | collective-permute-start | bytes 1572872 | tf_op jit(solution)/shard_map/ppermute | solution.py:408
  42.5 30.4 %copy-start.20 = (f32[8,1,512]{2,1,0:T(1,128)S(1)}, f32[8,1,512]{2,1,0:T(1,128)}, u32[]{:S(2)}) copy-start(f32[8,1,512]{2,1,0:T(1,128)} %param.10) | copy-start | bytes 49156
  49.9 23.0 %copy-start.1 = (bf16[1,1,512,512]{3,2,1,0:T(8,128)(2,1)S(1)}, bf16[1,1,512,512]{3,2,1,0:T(8,128)(2,1)}, u32[]{:S(2)}) copy-start(bf16[1,1,512,512]{3,2,1,0:T(8,128)(2,1)} %param.11) | copy-start | bytes 1572868
  49.9 6.7 %collective-permute-start.7 = (f32[8,512]{1,0:T(8,128)S(1)}, f32[8,512]{1,0:T(8,128)S(1)}, u32[]{:S(2)}, u32[]{:S(2)}) collective-permute-start(f32[8,512]{1,0:T(8,128)S(1)} %reshape.48.refs_0_), channel_id=1, source_target_pairs={{0,2},{1,3},{2,0},{3,1},{4,6},{5,7},{6,4},{7,5},{8,10},{9,11},{10,... | collective-permute-start | bytes 49160 | tf_op jit(solution)/shard_map/ppermute | solution.py:408
  56.6 4.6 %collective-permute-start.8 = (f32[8,512]{1,0:T(8,128)S(1)}, f32[8,512]{1,0:T(8,128)S(1)}, u32[]{:S(2)}, u32[]{:S(2)}) collective-permute-start(f32[8,512]{1,0:T(8,128)S(1)} %get-tuple-element.107.refs_0_), channel_id=1, source_target_pairs={{0,4},{1,5},{2,6},{3,7},{4,0},{5,1},{6,2},{7,3},{8,12},{9,13},{10,... | collective-permute-start | bytes 49160 | tf_op jit(solution)/shard_map/ppermute | solution.py:408
  61.2 1.2 copy-start.3
  64.3 8.5 %collective-permute-start.9 = (bf16[8192,128]{1,0:T(8,128)(2,1)}, bf16[8192,128]{1,0:T(8,128)(2,1)}, u32[]{:S(2)}, u32[]{:S(2)}) collective-permute-start(bf16[8192,128]{1,0:T(8,128)(2,1)} %get-tuple-element.112.refs_3_), channel_id=1, source_target_pairs={{0,8},{8,0},{16,24},{24,16},{1,9},{9,1},{17,25},{25,17},{2,10},{10... | collective-permute-start | bytes 6291464 | tf_op jit(solution)/shard_map/ppermute | solution.py:408
  64.4 6.7 %collective-permute-start.10 = (f32[8,512]{1,0:T(8,128)S(1)}, f32[8,512]{1,0:T(8,128)S(1)}, u32[]{:S(2)}, u32[]{:S(2)}) collective-permute-start(f32[8,512]{1,0:T(8,128)S(1)} %get-tuple-element.113.refs_0_), channel_id=1, source_target_pairs={{0,1},{1,0},{2,3},{3,2},{4,5},{5,4},{6,7},{7,6},{8,9},{9,8},{10,11... | collective-permute-start | bytes 49160 | tf_op jit(solution)/shard_map/ppermute | solution.py:408
  66.0 14.3 %collective-permute-start.11 = (bf16[512,512]{1,0:T(8,128)(2,1)}, bf16[512,512]{1,0:T(8,128)(2,1)}, u32[]{:S(2)}, u32[]{:S(2)}) collective-permute-start(bf16[512,512]{1,0:T(8,128)(2,1)} %get-tuple-element.117.refs_1_), channel_id=1, source_target_pairs={{0,16},{8,24},{16,0},{24,8},{1,17},{9,25},{17,1},{25,9},{2,18},{10... | collective-permute-start | bytes 1572872 | tf_op jit(solution)/shard_map/ppermute | solution.py:404
  66.5 31.4 %collective-permute-start.13 = (bf16[1024,512]{1,0:T(8,128)(2,1)}, bf16[1024,512]{1,0:T(8,128)(2,1)}, u32[]{:S(2)}, u32[]{:S(2)}) collective-permute-start(bf16[1024,512]{1,0:T(8,128)(2,1)} %copy-done.4), channel_id=1, source_target_pairs={{0,4},{1,5},{8,12},{9,13},{16,20},{17,21},{24,28},{25,29}} | collective-permute-start | bytes 3145736 | tf_op jit(solution)/shard_map/ppermute | solution.py:427
  69.5 28.5 %collective-permute-start.16 = (bf16[1024,512]{1,0:T(8,128)(2,1)}, bf16[1024,512]{1,0:T(8,128)(2,1)}, u32[]{:S(2)}, u32[]{:S(2)}) collective-permute-start(bf16[1024,512]{1,0:T(8,128)(2,1)} %get-tuple-element.131.refs_2_), channel_id=1, source_target_pairs={{4,6},{5,7},{12,14},{13,15},{20,22},{21,23},{28,30},{29,31}} | collective-permute-start | bytes 3145736 | tf_op jit(solution)/shard_map/ppermute | solution.py:430
  71.1 26.9 %collective-permute-start.15 = (bf16[1024,512]{1,0:T(8,128)(2,1)}, bf16[1024,512]{1,0:T(8,128)(2,1)}, u32[]{:S(2)}, u32[]{:S(2)}) collective-permute-start(bf16[1024,512]{1,0:T(8,128)(2,1)} %get-tuple-element.131.refs_2_), channel_id=1, source_target_pairs={{4,2},{5,3},{12,10},{13,11},{20,18},{21,19},{28,26},{29,27}} | collective-permute-start | bytes 3145736 | tf_op jit(solution)/shard_map/ppermute | solution.py:430
  72.8 10.6 %copy-start.14 = (bf16[2,512,512]{2,1,0:T(8,128)(2,1)S(1)}, bf16[2,512,512]{2,1,0:T(8,128)(2,1)}, u32[]{:S(2)}) copy-start(bf16[2,512,512]{2,1,0:T(8,128)(2,1)} %refs_7_.1) | copy-start | bytes 3145732
  72.8 10.6 %copy-start.15 = (bf16[2,512,512]{2,1,0:T(8,128)(2,1)S(1)}, bf16[2,512,512]{2,1,0:T(8,128)(2,1)}, u32[]{:S(2)}) copy-start(bf16[2,512,512]{2,1,0:T(8,128)(2,1)} %refs_8_.1) | copy-start | bytes 3145732
  81.4 2.0 collective-permute-start.12
  99.3 14.2 %copy-start.12 = (bf16[1024,512]{1,0:T(8,128)(2,1)}, bf16[1024,512]{1,0:T(8,128)(2,1)S(1)}, u32[]{:S(2)}) copy-start(bf16[1024,512]{1,0:T(8,128)(2,1)S(1)} %get-tuple-element.133.refs_2_) | copy-start | bytes 3145732
  99.3 26.7 %collective-permute-start.17 = (bf16[1024,512]{1,0:T(8,128)(2,1)S(1)}, bf16[1024,512]{1,0:T(8,128)(2,1)S(1)}, u32[]{:S(2)}, u32[]{:S(2)}) collective-permute-start(bf16[1024,512]{1,0:T(8,128)(2,1)S(1)} %get-tuple-element.133.refs_2_), channel_id=1, source_target_pairs={{0,1},{1,0},{2,3},{3,2},{4,5},{5,4},{6,7},{7,6},{8,9},{9,8},{10,11... | collective-permute-start | bytes 3145736 | tf_op jit(solution)/shard_map/ppermute | solution.py:408
  99.8 27.3 %collective-permute-start.14 = (bf16[1024,512]{1,0:T(8,128)(2,1)S(1)}, bf16[1024,512]{1,0:T(8,128)(2,1)}, u32[]{:S(2)}, u32[]{:S(2)}) collective-permute-start(bf16[1024,512]{1,0:T(8,128)(2,1)S(1)} %get-tuple-element.129.refs_1_), channel_id=1, source_target_pairs={{0,4},{1,5},{8,12},{9,13},{16,20},{17,21},{24,28},{25,29}} | collective-permute-start | bytes 3145736 | tf_op jit(solution)/shard_map/ppermute | solution.py:427
  103.2 33.2 %collective-permute-start.23 = (bf16[1024,512]{1,0:T(8,128)(2,1)}, bf16[1024,512]{1,0:T(8,128)(2,1)S(1)}, u32[]{:S(2)}, u32[]{:S(2)}) collective-permute-start(bf16[1024,512]{1,0:T(8,128)(2,1)} %get-tuple-element.146.refs_2_), channel_id=1, source_target_pairs={{4,6},{5,7},{12,14},{13,15},{20,22},{21,23},{28,30},{29,31}} | collective-permute-start | bytes 3145736 | tf_op jit(solution)/shard_map/ppermute | solution.py:430
  104.1 32.3 %collective-permute-start.22 = (bf16[1024,512]{1,0:T(8,128)(2,1)}, bf16[1024,512]{1,0:T(8,128)(2,1)S(1)}, u32[]{:S(2)}, u32[]{:S(2)}) collective-permute-start(bf16[1024,512]{1,0:T(8,128)(2,1)} %get-tuple-element.146.refs_2_), channel_id=1, source_target_pairs={{4,2},{5,3},{12,10},{13,11},{20,18},{21,19},{28,26},{29,27}} | collective-permute-start | bytes 3145736 | tf_op jit(solution)/shard_map/ppermute | solution.py:430
  104.8 8.6 %collective-permute-start.18 = (f32[4,512]{1,0:T(4,128)S(1)}, f32[4,512]{1,0:T(4,128)S(1)}, u32[]{:S(2)}, u32[]{:S(2)}) collective-permute-start(f32[4,512]{1,0:T(4,128)S(1)} %get-tuple-element.134), channel_id=1, source_target_pairs={{0,8},{8,16},{16,24},{1,9},{9,17},{17,25},{2,10},{10,18},{18,26},{... | collective-permute-start | bytes 24584 | tf_op jit(solution)/shard_map/ppermute | solution.py:498
  113.4 24.3 %copy-start.5 = (bf16[1024,512]{1,0:T(8,128)(2,1)S(1)}, bf16[1024,512]{1,0:T(8,128)(2,1)}, u32[]{:S(2)}) copy-start(bf16[1024,512]{1,0:T(8,128)(2,1)} %copy-done.4) | copy-start | bytes 3145732
  115.0 5.0 %collective-permute-start.19 = (f32[4,512]{1,0:T(4,128)S(1)}, f32[4,512]{1,0:T(4,128)S(1)}, u32[]{:S(2)}, u32[]{:S(2)}) collective-permute-start(f32[4,512]{1,0:T(4,128)S(1)} %get-tuple-element.137), channel_id=1, source_target_pairs={{0,8},{8,16},{16,24},{1,9},{9,17},{17,25},{2,10},{10,18},{18,26},{... | collective-permute-start | bytes 24584 | tf_op jit(solution)/shard_map/ppermute | solution.py:498
  121.4 3.1 %collective-permute-start.20 = (f32[4,512]{1,0:T(4,128)S(1)}, f32[4,512]{1,0:T(4,128)S(1)}, u32[]{:S(2)}, u32[]{:S(2)}) collective-permute-start(f32[4,512]{1,0:T(4,128)S(1)} %get-tuple-element.139), channel_id=1, source_target_pairs={{0,8},{8,16},{16,24},{1,9},{9,17},{17,25},{2,10},{10,18},{18,26},{... | collective-permute-start | bytes 24584 | tf_op jit(solution)/shard_map/ppermute | solution.py:498
  127.1 14.6 %copy-start.7 = (bf16[1024,512]{1,0:T(8,128)(2,1)S(1)}, bf16[1024,512]{1,0:T(8,128)(2,1)}, u32[]{:S(2)}) copy-start(bf16[1024,512]{1,0:T(8,128)(2,1)} %copy-done.6) | copy-start | bytes 3145732
  127.1 38.5 %collective-permute-start.28 = (bf16[1024,512]{1,0:T(8,128)(2,1)}, bf16[1024,512]{1,0:T(8,128)(2,1)}, u32[]{:S(2)}, u32[]{:S(2)}) collective-permute-start(bf16[1024,512]{1,0:T(8,128)(2,1)} %get-tuple-element.153.refs_2_), channel_id=1, source_target_pairs={{4,6},{5,7},{12,14},{13,15},{20,22},{21,23},{28,30},{29,31}} | collective-permute-start | bytes 3145736 | tf_op jit(solution)/shard_map/ppermute | solution.py:430
  129.0 36.6 %collective-permute-start.27 = (bf16[1024,512]{1,0:T(8,128)(2,1)}, bf16[1024,512]{1,0:T(8,128)(2,1)}, u32[]{:S(2)}, u32[]{:S(2)}) collective-permute-start(bf16[1024,512]{1,0:T(8,128)(2,1)} %get-tuple-element.153.refs_2_), channel_id=1, source_target_pairs={{4,2},{5,3},{12,10},{13,11},{20,18},{21,19},{28,26},{29,27}} | collective-permute-start | bytes 3145736 | tf_op jit(solution)/shard_map/ppermute | solution.py:430
  130.6 23.5 %collective-permute-start.21 = (bf16[512,512]{1,0:T(8,128)(2,1)}, bf16[512,512]{1,0:T(8,128)(2,1)S(1)}, u32[]{:S(2)}, u32[]{:S(2)}) collective-permute-start(bf16[512,512]{1,0:T(8,128)(2,1)} %get-tuple-element.143.refs_1_), channel_id=1, source_target_pairs={{0,4},{1,5},{8,12},{9,13},{16,20},{17,21},{24,28},{25,29}} | collective-permute-start | bytes 1572872 | tf_op jit(solution)/shard_map/ppermute | solution.py:427
  136.4 1.3 copy-start.19
  138.8 28.3 %collective-permute-start.26 = (bf16[1024,512]{1,0:T(8,128)(2,1)}, bf16[1024,512]{1,0:T(8,128)(2,1)}, u32[]{:S(2)}, u32[]{:S(2)}) collective-permute-start(bf16[1024,512]{1,0:T(8,128)(2,1)} %get-tuple-element.151.refs_2_), channel_id=1, source_target_pairs={{0,1},{1,0},{2,3},{3,2},{4,5},{5,4},{6,7},{7,6},{8,9},{9,8},{10,11... | collective-permute-start | bytes 3145736 | tf_op jit(solution)/shard_map/ppermute | solution.py:408
  140.4 16.3 %collective-permute-start.29 = (f32[4,512]{1,0:T(4,128)S(1)}, f32[4,512]{1,0:T(4,128)S(1)}, u32[]{:S(2)}, u32[]{:S(2)}) collective-permute-start(f32[4,512]{1,0:T(4,128)S(1)} %broadcast_select_fusion.refs_0_), channel_id=1, source_target_pairs={{0,8},{8,0},{16,24},{24,16},{1,9},{9,1},{17,25},{25,17},{2,10},{10... | collective-permute-start | bytes 24584 | tf_op jit(solution)/shard_map/ppermute | solution.py:408
  156.8 4.4 %collective-permute-start.30 = (f32[4,512]{1,0:T(4,128)S(1)}, f32[4,512]{1,0:T(4,128)S(1)}, u32[]{:S(2)}, u32[]{:S(2)}) collective-permute-start(f32[4,512]{1,0:T(4,128)S(1)} %get-tuple-element.156.refs_0_), channel_id=1, source_target_pairs={{0,16},{8,24},{16,0},{24,8},{1,17},{9,25},{17,1},{25,9},{2,18},{10... | collective-permute-start | bytes 24584 | tf_op jit(solution)/shard_map/ppermute | solution.py:408
  161.1 3.8 %collective-permute-start.31 = (f32[4,512]{1,0:T(4,128)S(1)}, f32[4,512]{1,0:T(4,128)S(1)}, u32[]{:S(2)}, u32[]{:S(2)}) collective-permute-start(f32[4,512]{1,0:T(4,128)S(1)} %get-tuple-element.158.refs_0_), channel_id=1, source_target_pairs={{0,1},{1,0},{2,3},{3,2},{4,5},{5,4},{6,7},{7,6},{8,9},{9,8},{10,11... | collective-permute-start | bytes 24584 | tf_op jit(solution)/shard_map/ppermute | solution.py:408
  161.6 17.0 %collective-permute-start.25 = (bf16[512,512]{1,0:T(8,128)(2,1)}, bf16[512,512]{1,0:T(8,128)(2,1)S(1)}, u32[]{:S(2)}, u32[]{:S(2)}) collective-permute-start(bf16[512,512]{1,0:T(8,128)(2,1)} %copy-done.10), channel_id=1, source_target_pairs={{4,6},{5,7},{12,14},{13,15},{20,22},{21,23},{28,30},{29,31}} | collective-permute-start | bytes 1572872 | tf_op jit(solution)/shard_map/ppermute | solution.py:430
  164.9 13.7 %collective-permute-start.24 = (bf16[512,512]{1,0:T(8,128)(2,1)}, bf16[512,512]{1,0:T(8,128)(2,1)S(1)}, u32[]{:S(2)}, u32[]{:S(2)}) collective-permute-start(bf16[512,512]{1,0:T(8,128)(2,1)} %copy-done.10), channel_id=1, source_target_pairs={{4,2},{5,3},{12,10},{13,11},{20,18},{21,19},{28,26},{29,27}} | collective-permute-start | bytes 1572872 | tf_op jit(solution)/shard_map/ppermute | solution.py:430
  165.8 26.1 %collective-permute-start.33 = (bf16[1024,512]{1,0:T(8,128)(2,1)S(1)}, bf16[1024,512]{1,0:T(8,128)(2,1)S(1)}, u32[]{:S(2)}, u32[]{:S(2)}) collective-permute-start(bf16[1024,512]{1,0:T(8,128)(2,1)S(1)} %get-tuple-element.164.refs_2_), channel_id=1, source_target_pairs={{0,1},{1,0},{2,3},{3,2},{4,5},{5,4},{6,7},{7,6},{8,9},{9,8},{10,11... | collective-permute-start | bytes 3145736 | tf_op jit(solution)/shard_map/ppermute | solution.py:408
  167.2 11.4 %copy-start.11 = (bf16[512,512]{1,0:T(8,128)(2,1)S(1)}, bf16[512,512]{1,0:T(8,128)(2,1)}, u32[]{:S(2)}) copy-start(bf16[512,512]{1,0:T(8,128)(2,1)} %copy-done.10) | copy-start | bytes 1572868
  179.7 23.2 %collective-permute-start.32 = (bf16[512,512]{1,0:T(8,128)(2,1)S(1)}, bf16[512,512]{1,0:T(8,128)(2,1)S(1)}, u32[]{:S(2)}, u32[]{:S(2)}) collective-permute-start(bf16[512,512]{1,0:T(8,128)(2,1)S(1)} %get-tuple-element.163.refs_2_), channel_id=1, source_target_pairs={{0,1},{1,0},{2,3},{3,2},{4,5},{5,4},{6,7},{7,6},{8,9},{9,8},{10,11... | collective-permute-start | bytes 1572872 | tf_op jit(solution)/shard_map/ppermute | solution.py:408
  180.4 3.7 %collective-permute-start.34 = (f32[4,512]{1,0:T(4,128)S(1)}, f32[4,512]{1,0:T(4,128)S(1)}, u32[]{:S(2)}, u32[]{:S(2)}) collective-permute-start(f32[4,512]{1,0:T(4,128)S(1)} %get-tuple-element.166.refs_0_), channel_id=1, source_target_pairs={{0,2},{1,3},{2,0},{3,1},{4,6},{5,7},{6,4},{7,5},{8,10},{9,11},{10,... | collective-permute-start | bytes 24584 | tf_op jit(solution)/shard_map/ppermute | solution.py:408
  184.1 4.5 %collective-permute-start.35 = (f32[4,512]{1,0:T(4,128)S(1)}, f32[4,512]{1,0:T(4,128)S(1)}, u32[]{:S(2)}, u32[]{:S(2)}) collective-permute-start(f32[4,512]{1,0:T(4,128)S(1)} %get-tuple-element.168.refs_0_), channel_id=1, source_target_pairs={{0,4},{1,5},{2,6},{3,7},{4,0},{5,1},{6,2},{7,3},{8,12},{9,13},{10,... | collective-permute-start | bytes 24584 | tf_op jit(solution)/shard_map/ppermute | solution.py:408
  (9 other events, 8.6 us)
